TPU v7x, 32 devices: a whole 2x2x4 slice. The times are simulated.
32 devices in a mesh: sub: 8 (over z, x), grp: 4 (over y, core).
Axes of the slice: x: 2, y: 2, z: 4, core: 2. Of those that a mesh axis runs over, the one named last changes fastest.
Arguments:
- rhs: float32 [4, 32, 256, 256], P('grp', 'sub')
- counts: int32 [4, 32], P('grp', 'sub'), may hold values from 64 to 256, as said below
- solve_panel: bfloat16 [4, 32, 512, 512], P('grp', 'sub'), as said below
- dirichlet_panel: bfloat16 [4, 32, 512, 512], P('grp', 'sub'), as said below
- coupling: float32 [4, 32, 32, 512], P('grp', 'sub'), may hold values from -0.25 to 0.25
- corner_map: int32 [4, 32, 32], P('grp', 'sub'), may hold values from 0 to 1023
- coarse_inverse: float32 [8, 1024, 1024], P('sub', 'grp'), as said below
Outputs:
- multipliers: float32 [4, 32, 256, 256], P('grp', 'sub')
- residual: float32 [4, 32, 256, 256], P('grp', 'sub')
Inputs may be any that keep to these rules, and one draw needn't show every extreme that they name: `counts`: some pair has all 256 unknowns constrained. `solve_panel`: each panel is symmetric positive definite. `dirichlet_panel`: each panel is symmetric positive definite. `coarse_inverse`: each slab's matrix is symmetric positive definite.
All inputs are finite; a program needn't handle non-finite values.
Results may differ from a plain program's by a relative error of at most 0.0003.
Values sent between devices are 32-bit elements; how exact they have to be, the bound alone decides.
No kernel may reach another device: no remote copies, remote signals or barrier semaphores. Data moves between devices by JAX's collectives and lax.ppermute only.
A program may use at most 128 MiB of HBM per device.

v0:
```python
import jax
import jax.numpy as jnp
from jax import lax
from jax.sharding import PartitionSpec as P

ITERS = 3


HIGH = lax.Precision.HIGHEST


def passed_along(block, axis, distance):
    devices = range(lax.axis_size(axis))
    route = [(i - distance, i) for i in devices if i - distance in devices]
    return lax.ppermute(block, axis, route)


def spread_faces(values):
    previous = passed_along(values[:, -1:], "sub", 1)
    prior = jnp.concatenate([previous, values[:, :-1]], axis=1)
    return jnp.concatenate([-prior, values], axis=3)


def face_jump(result, live_mask):
    width = result.shape[3] // 2
    following = passed_along(result[:, :1, :, :width], "sub", -1)
    next_left = jnp.concatenate([result[:, 1:, :, :width], following], axis=1)
    return live_mask * (result[..., width:] - next_left)


def panel_apply(panel, face_vals):
    return jnp.einsum(
        "gsrp,gsqp->gsrq", face_vals, panel, precision=HIGH, preferred_element_type=jnp.float32
    )


def inner(first, second):
    return jnp.sum(first * second, axis=(0, 1, 3))


def expand(scalars):
    return scalars[None, None, :, None]


def residual_sum(resid, precond):
    return lax.psum(inner(resid, precond), ("sub", "grp"))


def local(rhs, counts, solve_panel, dirichlet_panel, coupling, corner_map, coarse_inverse):
    local_subs = rhs.shape[1]
    width = rhs.shape[3]
    size = coarse_inverse.shape[2]
    last_device = lax.axis_index("sub") == lax.axis_size("sub") - 1
    slots = jnp.arange(local_subs, dtype=jnp.int32)
    positions = jnp.arange(width, dtype=jnp.int32)
    not_last = jnp.logical_not(last_device & (slots == local_subs - 1))
    live = (positions[None, None, :] < counts[:, :, None]) & not_last[None, :, None]
    live_mask = live.astype(jnp.float32)[:, :, None, :]
    corner_onehot = (corner_map[0][..., None] == jnp.arange(size, dtype=jnp.int32)).astype(
        jnp.float32
    )

    def precondition(values):
        return 0.25 * face_jump(panel_apply(dirichlet_panel, spread_faces(values)), live_mask)

    multipliers = jnp.zeros_like(rhs)
    residual = live_mask * rhs
    precond = precondition(residual)
    direction = precond
    rz_now = residual_sum(residual, precond)
    for step in range(ITERS):
        apply_face_vals = spread_faces(direction)
        corner_vals = jnp.einsum("srp,skp->srk", apply_face_vals[0], coupling[0], precision=HIGH)
        owned_totals = lax.psum_scatter(
            jnp.einsum("skn,srk->nr", corner_onehot, corner_vals, precision=HIGH),
            "grp",
            scatter_dimension=0,
            tiled=True,
        )
        partial_solved = jnp.einsum("mn,mr->nr", coarse_inverse[0], owned_totals, precision=HIGH)
        solved = lax.psum(partial_solved, "grp")
        back = jnp.einsum("skn,nr->srk", corner_onehot, solved, precision=HIGH)
        result = (
            panel_apply(solve_panel, apply_face_vals)
            + jnp.einsum("srk,skp->srp", back, coupling[0], precision=HIGH)[None]
        )
        image = face_jump(result, live_mask)
        alpha = rz_now / lax.psum(inner(direction, image), ("sub", "grp"))
        multipliers = multipliers + expand(alpha) * direction
        residual = residual - expand(alpha) * image
        if step + 1 < ITERS:
            precond = precondition(residual)
            rz_next = residual_sum(residual, precond)
            direction = precond + expand(rz_next / rz_now) * direction
            rz_now = rz_next
    return (multipliers, residual)


def solution(mesh):
    return jax.shard_map(
        local,
        mesh=mesh,
        in_specs=(
            P("grp", "sub", None, None),
            P("grp", "sub"),
            P("grp", "sub", None, None),
            P("grp", "sub", None, None),
            P("grp", "sub", None, None),
            P("grp", "sub", None),
            P("sub", "grp", None),
        ),
        out_specs=(P("grp", "sub", None, None), P("grp", "sub", None, None)),
        check_vma=False,
    )
```

profile of v0, /device:TPU:0, one launch (start us, length us, event | category | flops | bytes accessed | tf_op | source)
XLA Modules:
  0.0 583.0 jit_solution(17739421646902401245)
XLA Ops:
  7.2 0.9 fusion.70
  8.1 1.3 broadcast_multiply_fusion.1
  9.4 4.9 collective-permute-start
  14.4 5.5 collective-permute-done
  19.9 1.8 fusion.33
  21.8 1.3 collective-permute-start.1
  23.2 8.4 %collective-permute-done.1 = f32[1,1,256,256]{3,2,1,0:T(8,128)S(1)} collective-permute-done((f32[1,1,256,256]{3,2,1,0:T(8,128)S(1)}, f32[1,1,256,256]{3,2,1,0:T(8,128)S(1)}, u32[]{:S(2)}, u32[]{:S(2)}) %collective-permute-start.1) | collective-permute-done | bytes 262176 | tf_op jit(solution)/shard_map/ppermute | solution.py:15
  31.9 4.7 collective-permute-start.2
  36.7 3.8 collective-permute-done.2
  40.5 1.9 fusion.20
  42.4 2.3 convolution_bitcast_fusion.2
  44.8 27.2 %reduce-scatter.4.cloned.1.call-done = f32[256,256]{1,0:T(8,128)} async-done(((f32[1024,256]{1,0:T(8,128)}), f32[256,256]{1,0:T(8,128)}) %reduce-scatter.4.cloned.1.call-update) | async-done | bytes 262160 | tf_op jit(solution)/shard_map/reduce_scatter | solution.py:74
  72.0 3.3 convolution_bitcast_fusion.5
  75.4 36.2 %all-reduce.5.cloned.1.call-done = f32[1024,256]{0,1:T(8,128)} async-done(((f32[1024,256]{0,1:T(8,128)}), f32[1024,256]{0,1:T(8,128)}) %all-reduce.5.cloned.1.call-update) | async-done | bytes 1048592 | tf_op jit(solution)/shard_map/psum | solution.py:81
  111.6 2.1 convolution_bitcast_fusion.8
  113.8 1.8 fusion.60
  115.7 3.1 add_bitcast_fusion.2
  118.8 1.6 collective-permute-start.3
  120.4 8.3 %collective-permute-done.3 = f32[1,1,256,256]{3,2,1,0:T(8,128)S(1)} collective-permute-done((f32[1,1,256,256]{3,2,1,0:T(8,128)S(1)}, f32[1,1,256,256]{3,2,1,0:T(8,128)S(1)}, u32[]{:S(2)}, u32[]{:S(2)}) %collective-permute-start.3) | collective-permute-done | bytes 262176 | tf_op jit(solution)/shard_map/ppermute | solution.py:15
  129.5 40.8 %all-reduce = (f32[256]{0:T(256)S(1)}, f32[256]{0:T(256)S(1)}) all-reduce(f32[256]{0:T(256)S(1)} %get-tuple-element.3, f32[256]{0:T(256)S(1)} %get-tuple-element.2), channel_id=1, replica_groups=mesh['sub'=8,'grp'=4] {'sub','grp'}, use_global_device_ids=true, to_apply=%region_1.0 | all-reduce | flops 512 | bytes 4096 | tf_op jit(solution)/shard_map/psum | solution.py:46
  170.3 2.1 multiply_subtract_fusion.2
  172.5 4.2 collective-permute-start.4
  176.7 4.0 collective-permute-done.4
  180.8 1.8 fusion.30
  182.6 1.3 collective-permute-start.5
  184.0 7.3 %collective-permute-done.5 = f32[1,1,256,256]{3,2,1,0:T(8,128)S(1)} collective-permute-done((f32[1,1,256,256]{3,2,1,0:T(8,128)S(1)}, f32[1,1,256,256]{3,2,1,0:T(8,128)S(1)}, u32[]{:S(2)}, u32[]{:S(2)}) %collective-permute-start.5) | collective-permute-done | bytes 262176 | tf_op jit(solution)/shard_map/ppermute | solution.py:15
  192.4 40.4 %psum.66 = f32[256]{0:T(256)S(1)} all-reduce(f32[256]{0:T(256)S(1)} %multiply_reduce_fusion.3), channel_id=1, replica_groups=mesh['sub'=8,'grp'=4] {'sub','grp'}, use_global_device_ids=true, to_apply=%region_7.0 | all-reduce | flops 256 | bytes 2048 | tf_op jit(solution)/shard_map/psum | solution.py:46
  232.8 2.1 multiply_add_fusion.2
  234.9 4.2 collective-permute-start.6
  239.2 4.0 collective-permute-done.6
  243.3 1.0 copy-done.19
  244.3 1.9 fusion.19
  246.1 2.3 convolution_bitcast_fusion.1
  248.5 25.9 %reduce-scatter.6.cloned.1.call-done = f32[256,256]{1,0:T(8,128)} async-done(((f32[1024,256]{1,0:T(8,128)}), f32[256,256]{1,0:T(8,128)}) %reduce-scatter.6.cloned.1.call-update) | async-done | bytes 262160 | tf_op jit(solution)/shard_map/reduce_scatter | solution.py:74
  274.4 3.3 convolution_bitcast_fusion.4
  278.0 36.0 %all-reduce.7.cloned.1.call-done = f32[1024,256]{0,1:T(8,128)} async-done(((f32[1024,256]{0,1:T(8,128)}), f32[1024,256]{0,1:T(8,128)}) %all-reduce.7.cloned.1.call-update) | async-done | bytes 1048592 | tf_op jit(solution)/shard_map/psum | solution.py:81
  314.0 2.1 convolution_bitcast_fusion.7
  316.1 1.8 fusion.57
  318.0 1.8 add_bitcast_fusion.1
  319.9 1.3 collective-permute-start.7
  321.2 8.3 %collective-permute-done.7 = f32[1,1,256,256]{3,2,1,0:T(8,128)S(1)} collective-permute-done((f32[1,1,256,256]{3,2,1,0:T(8,128)S(1)}, f32[1,1,256,256]{3,2,1,0:T(8,128)S(1)}, u32[]{:S(2)}, u32[]{:S(2)}) %collective-permute-start.7) | collective-permute-done | bytes 262176 | tf_op jit(solution)/shard_map/ppermute | solution.py:15
  330.6 40.7 %psum.68 = f32[256]{0:T(256)S(1)} all-reduce(f32[256]{0:T(256)S(1)} %multiply_reduce_fusion.2), channel_id=1, replica_groups=mesh['sub'=8,'grp'=4] {'sub','grp'}, use_global_device_ids=true, to_apply=%region_11.0 | all-reduce | flops 256 | bytes 2048 | tf_op jit(solution)/shard_map/psum | solution.py:88
  371.3 2.1 multiply_subtract_fusion.1
  373.4 4.2 collective-permute-start.8
  377.7 4.0 collective-permute-done.8
  381.7 1.8 fusion.27
  383.6 1.3 collective-permute-start.9
  385.0 7.3 %collective-permute-done.9 = f32[1,1,256,256]{3,2,1,0:T(8,128)S(1)} collective-permute-done((f32[1,1,256,256]{3,2,1,0:T(8,128)S(1)}, f32[1,1,256,256]{3,2,1,0:T(8,128)S(1)}, u32[]{:S(2)}, u32[]{:S(2)}) %collective-permute-start.9) | collective-permute-done | bytes 262176 | tf_op jit(solution)/shard_map/ppermute | solution.py:15
  393.4 40.4 %psum.69 = f32[256]{0:T(256)S(1)} all-reduce(f32[256]{0:T(256)S(1)} %multiply_reduce_fusion.1), channel_id=1, replica_groups=mesh['sub'=8,'grp'=4] {'sub','grp'}, use_global_device_ids=true, to_apply=%region_13.0 | all-reduce | flops 256 | bytes 2048 | tf_op jit(solution)/shard_map/psum | solution.py:46
  433.8 1.8 multiply_add_fusion.1
  435.6 4.2 collective-permute-start.10
  439.8 4.0 collective-permute-done.10
  443.9 1.9 fusion.18
  445.8 2.3 convolution_bitcast_fusion
  448.4 25.6 %reduce-scatter.8.cloned.1.call-done = f32[256,256]{1,0:T(8,128)} async-done(((f32[1024,256]{1,0:T(8,128)}), f32[256,256]{1,0:T(8,128)}) %reduce-scatter.8.cloned.1.call-update) | async-done | bytes 262160 | tf_op jit(solution)/shard_map/reduce_scatter | solution.py:74
  474.1 3.3 convolution_bitcast_fusion.3
  477.4 36.3 %all-reduce.9.cloned.1.call-done = f32[1024,256]{0,1:T(8,128)} async-done(((f32[1024,256]{0,1:T(8,128)}), f32[1024,256]{0,1:T(8,128)}) %all-reduce.9.cloned.1.call-update) | async-done | bytes 1048592 | tf_op jit(solution)/shard_map/psum | solution.py:81
  513.7 2.1 convolution_bitcast_fusion.6
  515.9 1.8 fusion.54
  517.7 3.1 add_bitcast_fusion
  520.8 1.3 collective-permute-start.11
  522.2 8.3 %collective-permute-done.11 = f32[1,1,256,256]{3,2,1,0:T(8,128)S(1)} collective-permute-done((f32[1,1,256,256]{3,2,1,0:T(8,128)S(1)}, f32[1,1,256,256]{3,2,1,0:T(8,128)S(1)}, u32[]{:S(2)}, u32[]{:S(2)}) %collective-permute-start.11) | collective-permute-done | bytes 262176 | tf_op jit(solution)/shard_map/ppermute | solution.py:15
  530.8 40.7 %psum.71 = f32[256]{0:T(256)S(1)} all-reduce(f32[256]{0:T(256)S(1)} %multiply_reduce_fusion), channel_id=1, replica_groups=mesh['sub'=8,'grp'=4] {'sub','grp'}, use_global_device_ids=true, to_apply=%region_17.0 | all-reduce | flops 256 | bytes 2048 | tf_op jit(solution)/shard_map/psum | solution.py:88
  571.5 4.1 multiply_subtract_fusion
  (117 shorter events, 6.6 us)
Async XLA Ops:
  7.2 12.8 %copy-start = (bf16[1,4,512,512]{3,2,1,0:T(8,128)(2,1)S(1)}, bf16[1,4,512,512]{3,2,1,0:T(8,128)(2,1)}, u32[]{:S(2)}) copy-start(bf16[1,4,512,512]{3,2,1,0:T(8,128)(2,1)} %param.10) | copy-start | bytes 6291460
  7.2 64.8 %reduce-scatter.4.cloned.1.call-start = ((), (), s32[]{:S(2)}) async-start(), calls=%async_computation.3 | async-start | bytes 1310720 | tf_op jit(solution)/shard_map/reduce_scatter | solution.py:74
  9.4 10.4 %collective-permute-start = (f32[1,1,256,256]{3,2,1,0:T(8,128)S(1)}, f32[1,1,256,256]{3,2,1,0:T(8,128)S(1)}, u32[]{:S(2)}, u32[]{:S(2)}) collective-permute-start(f32[1,1,256,256]{3,2,1,0:T(8,128)S(1)} %slice.120), channel_id=1, source_target_pairs={{0,4},{4,8},{8,12},{12,16},{16,20},{20,24},{24,28},{1,5},{5,9},{9,... | collective-permute-start | bytes 786440 | tf_op jit(solution)/shard_map/ppermute | solution.py:15
  21.8 9.8 %collective-permute-start.1 = (f32[1,1,256,256]{3,2,1,0:T(8,128)S(1)}, f32[1,1,256,256]{3,2,1,0:T(8,128)S(1)}, u32[]{:S(2)}, u32[]{:S(2)}) collective-permute-start(f32[1,1,256,256]{3,2,1,0:T(8,128)S(1)} %slice.124), channel_id=1, source_target_pairs={{4,0},{8,4},{12,8},{16,12},{20,16},{24,20},{28,24},{5,1},{9,5},{13... | collective-permute-start | bytes 786440 | tf_op jit(solution)/shard_map/ppermute | solution.py:15
  31.8 8.7 %copy-start.9 = (f32[1,4,256,256]{3,2,1,0:T(8,128)}, f32[1,4,256,256]{3,2,1,0:T(8,128)S(1)}, u32[]{:S(2)}) copy-start(f32[1,4,256,256]{3,2,1,0:T(8,128)S(1)} %get-tuple-element.8) | copy-start | bytes 3145732
  31.8 96.9 %copy-start.8 = (f32[1,4,256,256]{3,2,1,0:T(8,128)}, f32[1,4,256,256]{3,2,1,0:T(8,128)S(1)}, u32[]{:S(2)}) copy-start(f32[1,4,256,256]{3,2,1,0:T(8,128)S(1)} %get-tuple-element.9) | copy-start | bytes 3145732
  31.8 8.7 %copy-start.17 = (f32[1,4,32,512]{3,2,1,0:T(8,128)S(1)}, f32[1,4,32,512]{3,2,1,0:T(8,128)}, u32[]{:S(2)}) copy-start(f32[1,4,32,512]{3,2,1,0:T(8,128)} %param.11) | copy-start | bytes 786436
  31.9 8.5 %collective-permute-start.2 = (f32[1,1,256,256]{3,2,1,0:T(8,128)S(1)}, f32[1,1,256,256]{3,2,1,0:T(8,128)S(1)}, u32[]{:S(2)}, u32[]{:S(2)}) collective-permute-start(f32[1,1,256,256]{3,2,1,0:T(8,128)S(1)} %slice.125), channel_id=1, source_target_pairs={{0,4},{4,8},{8,12},{12,16},{16,20},{20,24},{24,28},{1,5},{5,9},{9,... | collective-permute-start | bytes 786440 | tf_op jit(solution)/shard_map/ppermute | solution.py:15
  36.6 5.8 copy-start.31
  40.5 1.9 copy-start.18
  44.7 66.9 %all-reduce.5.cloned.1.call-start = ((), (), s32[]{:S(2)}) async-start(), calls=%async_computation.4 | async-start | bytes 2097152 | tf_op jit(solution)/shard_map/psum | solution.py:81
  75.4 199.0 %reduce-scatter.6.cloned.1.call-start = ((), (), s32[]{:S(2)}) async-start(), calls=%async_computation.5 | async-start | bytes 1310720 | tf_op jit(solution)/shard_map/reduce_scatter | solution.py:74
  111.6 4.0 copy-start.5
  111.6 4.0 copy-start.10
  118.7 10.5 %copy-start.14 = (f32[1,4,256,512]{3,2,1,0:T(8,128)}, f32[1,4,256,512]{3,2,1,0:T(8,128)S(1)}, u32[]{:S(2)}) copy-start(f32[1,4,256,512]{3,2,1,0:T(8,128)S(1)} %add_bitcast_fusion.2) | copy-start | bytes 6291460
  118.7 10.0 %copy-start.16 = (f32[1,4,256,256]{3,2,1,0:T(8,128)S(1)}, f32[1,4,256,256]{3,2,1,0:T(8,128)}, u32[]{:S(2)}) copy-start(f32[1,4,256,256]{3,2,1,0:T(8,128)} %param.7) | copy-start | bytes 3145732
  118.8 10.0 %collective-permute-start.3 = (f32[1,1,256,256]{3,2,1,0:T(8,128)S(1)}, f32[1,1,256,256]{3,2,1,0:T(8,128)S(1)}, u32[]{:S(2)}, u32[]{:S(2)}) collective-permute-start(f32[1,1,256,256]{3,2,1,0:T(8,128)S(1)} %slice.129), channel_id=1, source_target_pairs={{4,0},{8,4},{12,8},{16,12},{20,16},{24,20},{28,24},{5,1},{9,5},{13... | collective-permute-start | bytes 786440 | tf_op jit(solution)/shard_map/ppermute | solution.py:15
  120.4 8.9 %copy-start.23 = (f32[1,3,256,256]{3,2,1,0:T(8,128)}, f32[1,3,256,256]{3,2,1,0:T(8,128)S(1)}, u32[]{:S(2)}) copy-start(f32[1,3,256,256]{3,2,1,0:T(8,128)S(1)} %slice.128) | copy-start | bytes 2359300
  128.8 0.7 copy-start.27
  172.4 19.0 %copy-start.4 = (f32[1,4,256,256]{3,2,1,0:T(8,128)}, f32[1,4,256,256]{3,2,1,0:T(8,128)S(1)}, u32[]{:S(2)}) copy-start(f32[1,4,256,256]{3,2,1,0:T(8,128)S(1)} %multiply_subtract_fusion.2) | copy-start | bytes 3145732
  172.5 8.2 %collective-permute-start.4 = (f32[1,1,256,256]{3,2,1,0:T(8,128)S(1)}, f32[1,1,256,256]{3,2,1,0:T(8,128)S(1)}, u32[]{:S(2)}, u32[]{:S(2)}) collective-permute-start(f32[1,1,256,256]{3,2,1,0:T(8,128)S(1)} %slice.130), channel_id=1, source_target_pairs={{0,4},{4,8},{8,12},{12,16},{16,20},{20,24},{24,28},{1,5},{5,9},{9,... | collective-permute-start | bytes 786440 | tf_op jit(solution)/shard_map/ppermute | solution.py:15
  182.6 8.8 %copy-start.11 = (f32[1,4,256,512]{3,2,1,0:T(8,128)}, f32[1,4,256,512]{3,2,1,0:T(8,128)S(1)}, u32[]{:S(2)}) copy-start(f32[1,4,256,512]{3,2,1,0:T(8,128)S(1)} %fusion.30) | copy-start | bytes 6291460
  182.6 8.7 %collective-permute-start.5 = (f32[1,1,256,256]{3,2,1,0:T(8,128)S(1)}, f32[1,1,256,256]{3,2,1,0:T(8,128)S(1)}, u32[]{:S(2)}, u32[]{:S(2)}) collective-permute-start(f32[1,1,256,256]{3,2,1,0:T(8,128)S(1)} %slice.134), channel_id=1, source_target_pairs={{4,0},{8,4},{12,8},{16,12},{20,16},{24,20},{28,24},{5,1},{9,5},{13... | collective-permute-start | bytes 786440 | tf_op jit(solution)/shard_map/ppermute | solution.py:15
  184.0 7.4 %copy-start.25 = (f32[1,3,256,256]{3,2,1,0:T(8,128)}, f32[1,3,256,256]{3,2,1,0:T(8,128)S(1)}, u32[]{:S(2)}) copy-start(f32[1,3,256,256]{3,2,1,0:T(8,128)S(1)} %slice.133) | copy-start | bytes 2359300
  191.4 0.7 copy-start.29
  234.9 8.3 %collective-permute-start.6 = (f32[1,1,256,256]{3,2,1,0:T(8,128)S(1)}, f32[1,1,256,256]{3,2,1,0:T(8,128)S(1)}, u32[]{:S(2)}, u32[]{:S(2)}) collective-permute-start(f32[1,1,256,256]{3,2,1,0:T(8,128)S(1)} %slice.135), channel_id=1, source_target_pairs={{0,4},{4,8},{8,12},{12,16},{16,20},{20,24},{24,28},{1,5},{5,9},{9,... | collective-permute-start | bytes 786440 | tf_op jit(solution)/shard_map/ppermute | solution.py:15
  243.3 1.0 copy-start.19
  248.4 65.5 %all-reduce.7.cloned.1.call-start = ((), (), s32[]{:S(2)}) async-start(), calls=%async_computation.6 | async-start | bytes 2097152 | tf_op jit(solution)/shard_map/psum | solution.py:81
  277.7 196.4 %reduce-scatter.8.cloned.1.call-start = ((), (), s32[]{:S(2)}) async-start(), calls=%async_computation.7 | async-start | bytes 1310720 | tf_op jit(solution)/shard_map/reduce_scatter | solution.py:74
  314.0 4.0 copy-start.6
  314.0 4.0 copy-start.20
  319.8 9.8 %copy-start.15 = (f32[1,4,256,512]{3,2,1,0:T(8,128)}, f32[1,4,256,512]{3,2,1,0:T(8,128)S(1)}, u32[]{:S(2)}) copy-start(f32[1,4,256,512]{3,2,1,0:T(8,128)S(1)} %add_bitcast_fusion.1) | copy-start | bytes 6291460
  319.9 9.7 %collective-permute-start.7 = (f32[1,1,256,256]{3,2,1,0:T(8,128)S(1)}, f32[1,1,256,256]{3,2,1,0:T(8,128)S(1)}, u32[]{:S(2)}, u32[]{:S(2)}) collective-permute-start(f32[1,1,256,256]{3,2,1,0:T(8,128)S(1)} %slice.139), channel_id=1, source_target_pairs={{4,0},{8,4},{12,8},{16,12},{20,16},{24,20},{28,24},{5,1},{9,5},{13... | collective-permute-start | bytes 786440 | tf_op jit(solution)/shard_map/ppermute | solution.py:15
  321.2 8.3 %copy-start.24 = (f32[1,3,256,256]{3,2,1,0:T(8,128)}, f32[1,3,256,256]{3,2,1,0:T(8,128)S(1)}, u32[]{:S(2)}) copy-start(f32[1,3,256,256]{3,2,1,0:T(8,128)S(1)} %slice.138) | copy-start | bytes 2359300
  329.6 0.7 copy-start.28
  373.4 19.0 %copy-start.3 = (f32[1,4,256,256]{3,2,1,0:T(8,128)}, f32[1,4,256,256]{3,2,1,0:T(8,128)S(1)}, u32[]{:S(2)}) copy-start(f32[1,4,256,256]{3,2,1,0:T(8,128)S(1)} %multiply_subtract_fusion.1) | copy-start | bytes 3145732
  373.4 8.2 %collective-permute-start.8 = (f32[1,1,256,256]{3,2,1,0:T(8,128)S(1)}, f32[1,1,256,256]{3,2,1,0:T(8,128)S(1)}, u32[]{:S(2)}, u32[]{:S(2)}) collective-permute-start(f32[1,1,256,256]{3,2,1,0:T(8,128)S(1)} %slice.140), channel_id=1, source_target_pairs={{0,4},{4,8},{8,12},{12,16},{16,20},{20,24},{24,28},{1,5},{5,9},{9,... | collective-permute-start | bytes 786440 | tf_op jit(solution)/shard_map/ppermute | solution.py:15
  383.6 8.8 %copy-start.12 = (f32[1,4,256,512]{3,2,1,0:T(8,128)}, f32[1,4,256,512]{3,2,1,0:T(8,128)S(1)}, u32[]{:S(2)}) copy-start(f32[1,4,256,512]{3,2,1,0:T(8,128)S(1)} %fusion.27) | copy-start | bytes 6291460
  383.6 8.7 %collective-permute-start.9 = (f32[1,1,256,256]{3,2,1,0:T(8,128)S(1)}, f32[1,1,256,256]{3,2,1,0:T(8,128)S(1)}, u32[]{:S(2)}, u32[]{:S(2)}) collective-permute-start(f32[1,1,256,256]{3,2,1,0:T(8,128)S(1)} %slice.144), channel_id=1, source_target_pairs={{4,0},{8,4},{12,8},{16,12},{20,16},{24,20},{28,24},{5,1},{9,5},{13... | collective-permute-start | bytes 786440 | tf_op jit(solution)/shard_map/ppermute | solution.py:15
  385.0 7.4 %copy-start.26 = (f32[1,3,256,256]{3,2,1,0:T(8,128)}, f32[1,3,256,256]{3,2,1,0:T(8,128)S(1)}, u32[]{:S(2)}) copy-start(f32[1,3,256,256]{3,2,1,0:T(8,128)S(1)} %slice.143) | copy-start | bytes 2359300
  392.4 0.7 copy-start.30
  435.5 8.4 %copy-start.1 = (f32[1,4,256,256]{3,2,1,0:T(8,128)}, f32[1,4,256,256]{3,2,1,0:T(8,128)S(1)}, u32[]{:S(2)}) copy-start(f32[1,4,256,256]{3,2,1,0:T(8,128)S(1)} %multiply_add_fusion.1) | copy-start | bytes 3145732
  435.6 8.3 %collective-permute-start.10 = (f32[1,1,256,256]{3,2,1,0:T(8,128)S(1)}, f32[1,1,256,256]{3,2,1,0:T(8,128)S(1)}, u32[]{:S(2)}, u32[]{:S(2)}) collective-permute-start(f32[1,1,256,256]{3,2,1,0:T(8,128)S(1)} %slice.145), channel_id=1, source_target_pairs={{0,4},{4,8},{8,12},{12,16},{16,20},{20,24},{24,28},{1,5},{5,9},{9,... | collective-permute-start | bytes 786440 | tf_op jit(solution)/shard_map/ppermute | solution.py:15
  443.9 1.9 copy-start.21
  448.1 65.6 %all-reduce.9.cloned.1.call-start = ((), (), s32[]{:S(2)}) async-start(), calls=%async_computation.8 | async-start | bytes 2097152 | tf_op jit(solution)/shard_map/psum | solution.py:81
  513.7 4.0 copy-start.2
  513.7 4.0 copy-start.7
  520.8 9.8 %copy-start.13 = (f32[1,4,256,512]{3,2,1,0:T(8,128)}, f32[1,4,256,512]{3,2,1,0:T(8,128)S(1)}, u32[]{:S(2)}) copy-start(f32[1,4,256,512]{3,2,1,0:T(8,128)S(1)} %add_bitcast_fusion) | copy-start | bytes 6291460
  520.8 9.7 %collective-permute-start.11 = (f32[1,1,256,256]{3,2,1,0:T(8,128)S(1)}, f32[1,1,256,256]{3,2,1,0:T(8,128)S(1)}, u32[]{:S(2)}, u32[]{:S(2)}) collective-permute-start(f32[1,1,256,256]{3,2,1,0:T(8,128)S(1)} %slice.149), channel_id=1, source_target_pairs={{4,0},{8,4},{12,8},{16,12},{20,16},{24,20},{28,24},{5,1},{9,5},{13... | collective-permute-start | bytes 786440 | tf_op jit(solution)/shard_map/ppermute | solution.py:15
  522.2 8.3 %copy-start.22 = (f32[1,3,256,256]{3,2,1,0:T(8,128)}, f32[1,3,256,256]{3,2,1,0:T(8,128)S(1)}, u32[]{:S(2)}) copy-start(f32[1,3,256,256]{3,2,1,0:T(8,128)S(1)} %slice.148) | copy-start | bytes 2359300
Sparse Core Ops, SparseCore 0:
  44.9 27.1 reduce-scatter.3
  75.5 36.1 all-reduce.4
  248.5 25.7 reduce-scatter.5
  277.8 36.0 all-reduce.6
  448.3 25.7 reduce-scatter.7
  477.6 36.1 all-reduce.8
where the time goes:
time: 593 us; the launch traced here: 583 us
  waiting for transfers between devices  261 us (44%)
  blocking collectives  203 us (34%)
  matrix products  47.7 us (8%)
  starting transfers between devices  35.1 us (6%)
  other arithmetic  16.7 us (3%)
  between operations  15.4 us (3%)
    psum x3, blocking collectives, residual_sum(): return lax.psum(inner(resid, precond), ('sub', 'grp'))  122 us
    psum x3, waiting for transfers between devices, local(): solved = lax.psum(partial_solved, 'grp')  109 us
    psum x2, blocking collectives, local(): alpha = rz_now / lax.psum(inner(direction, image), ('sub', 'grp'))  81.5 us
    reduce_scatter x3, waiting for transfers between devices, local(): lax.psum_scatter(jnp.einsum('skn,srk->nr', corner_onehot, corner_vals, pr...  78.8 us
    ppermute x12, waiting for transfers between devices, passed_along(): return lax.ppermute(block, axis, route)  73.3 us
    ppermute x12, starting transfers between devices, passed_along(): return lax.ppermute(block, axis, route)  34.3 us
    dot_general x6, matrix products, panel_apply(): jnp.einsum('gsrp,gsqp->gsrq', face_vals, panel, precision=HIGH, preferred...  13.4 us
  transfers between devices with their start and end apart: 18, of which 18 were waited for; matrix products, arithmetic and copies ran while one was open for 0% of the time, Pallas kernels for 0%

commit v1 on v0

v1 whole, which is shorter than its diff:
```python
import jax
import jax.numpy as jnp
from jax import lax
from jax.sharding import PartitionSpec as P

ITERS = 3


HIGH = lax.Precision.HIGH


def split(values):
    high = lax.reduce_precision(values, exponent_bits=8, mantissa_bits=7)
    return high.astype(jnp.bfloat16), (values - high).astype(jnp.bfloat16)


def neighbour_pairs(size, first):
    pairs = [(i, i + 1) for i in range(first, size - 1, 2)]
    return [route for a, b in pairs for route in ((a, b), (b, a))]


def swap_with_neighbours(to_next, to_prev, even):
    size = lax.axis_size("sub")
    near = lax.ppermute(jnp.where(even, to_next, to_prev), "sub", neighbour_pairs(size, 0))
    far = lax.ppermute(jnp.where(even, to_prev, to_next), "sub", neighbour_pairs(size, 1))
    return jnp.where(even, far, near), jnp.where(even, near, far)


def sum_all(rows):
    size = lax.axis_size("sub") * lax.axis_size("grp")
    copies = jnp.broadcast_to(rows[None], (size,) + rows.shape)
    return jnp.sum(lax.all_to_all(copies, ("sub", "grp"), 0, 0), axis=0)


def spread_faces(edges):
    return jnp.concatenate([-edges[:-1], edges[1:]], axis=2)


def panel_apply(panel, face_vals):
    high, low = split(face_vals)
    dims = (((2,), (2,)), ((0,), (0,)))
    return lax.dot_general(high, panel, dims, preferred_element_type=jnp.float32) + lax.dot_general(
        low, panel, dims, preferred_element_type=jnp.float32
    )


def face_jump(result, live, even):
    width = result.shape[2] // 2
    from_prev, from_next = swap_with_neighbours(result[-1, :, width:], result[0, :, :width], even)
    right = jnp.concatenate([from_prev[None], result[:, :, width:]], axis=0)
    left = jnp.concatenate([result[:, :, :width], from_next[None]], axis=0)
    return live * (right - left)


def coarse_block(corner_map, coarse_inverse):
    rows, size = coarse_inverse.shape
    own = corner_map.size
    grp, group = lax.axis_index("grp"), lax.axis_size("grp")
    everyone = lax.all_gather(corner_map.reshape(own), "grp", tiled=True)
    columns = (everyone[None, :] == jnp.arange(size, dtype=jnp.int32)[:, None]).astype(jnp.float32)
    picked = jnp.dot(coarse_inverse, columns, precision=HIGH)
    owned = jnp.arange(rows, dtype=jnp.int32) + grp * rows

    def rows_for(member):
        wanted = lax.dynamic_slice_in_dim(everyone, member * own, own)
        chosen = (wanted[:, None] == owned[None, :]).astype(jnp.float32)
        return jnp.dot(chosen, picked, precision=HIGH)

    block = rows_for(grp)
    for distance in range(1, group):
        routes = [(i, i ^ distance) for i in range(group)]
        block = block + lax.ppermute(rows_for(grp ^ distance), "grp", routes)
    return block


def inner(first, second):
    return jnp.sum(first * second, axis=(0, 2))


def expand(scalars):
    return scalars[None, :, None]


def local(rhs, counts, solve_panel, dirichlet_panel, coupling, corner_map, coarse_inverse):
    local_subs, loads, width = rhs.shape[1:]
    corners = coupling.shape[2]
    place = lax.axis_index("sub")
    even = place % 2 == 0
    last_device = place == lax.axis_size("sub") - 1
    slots = jnp.arange(local_subs, dtype=jnp.int32)
    positions = jnp.arange(width, dtype=jnp.int32)
    not_last = jnp.logical_not(last_device & (slots == local_subs - 1))
    live = ((positions[None, :] < counts[0][:, None]) & not_last[:, None]).astype(jnp.float32)
    residual = live[:, None, :] * rhs[0]

    size = lax.axis_size("sub")
    tail = jnp.concatenate([residual[-1], jnp.broadcast_to(live[-1:], (8, width))], axis=0)
    head = lax.ppermute(tail, "sub", [(i, i + 1) for i in range(size - 1)])
    residual = jnp.concatenate([head[None, :loads], residual], axis=0)
    live = jnp.concatenate([head[loads : loads + 1], live], axis=0)[:, None, :]

    block = coarse_block(corner_map[0], coarse_inverse[0])

    def precondition(edges):
        return face_jump(panel_apply(dirichlet_panel[0], spread_faces(edges)), 0.25 * live, even)

    def apply_dual(edges):
        faces = spread_faces(edges)
        corner_vals = jnp.einsum("skp,srp->skr", coupling[0], faces, precision=HIGH)
        everyone = lax.all_gather(
            corner_vals.reshape(local_subs * corners, loads), "grp", tiled=True
        )
        back = jnp.dot(block, everyone, precision=HIGH).reshape(local_subs, corners, loads)
        result = panel_apply(solve_panel[0], faces) + jnp.einsum(
            "skr,skp->srp", back, coupling[0], precision=HIGH
        )
        return face_jump(result, live, even)

    multipliers = jnp.zeros_like(rhs[0])
    precond = precondition(residual)
    image = apply_dual(precond)
    for step in range(ITERS):
        sums = sum_all(
            jnp.stack([inner(residual[1:], precond[1:]), inner(image[1:], precond[1:])])
        )
        if step + 1 < ITERS:
            next_precond = precondition(image)
            next_image = apply_dual(next_precond)
        rz_now, curvature = sums[0], sums[1]
        if step == 0:
            alpha = rz_now / curvature
            direction, direction_image = precond, image
            step_precond, step_image = next_precond, next_image
        else:
            beta = rz_now / rz_before
            alpha = rz_now / (curvature - beta * rz_now / alpha)
            direction = precond + expand(beta) * direction
            direction_image = image + expand(beta) * direction_image
            if step + 1 < ITERS:
                step_precond = next_precond + expand(beta) * step_precond
                step_image = next_image + expand(beta) * step_image
        multipliers = multipliers + expand(alpha) * direction[1:]
        residual = residual - expand(alpha) * direction_image
        if step + 1 < ITERS:
            precond = precond - expand(alpha) * step_precond
            image = image - expand(alpha) * step_image
        rz_before = rz_now
    return (multipliers[None], residual[1:][None])


def solution(mesh):
    return jax.shard_map(
        local,
        mesh=mesh,
        in_specs=(
            P("grp", "sub", None, None),
            P("grp", "sub"),
            P("grp", "sub", None, None),
            P("grp", "sub", None, None),
            P("grp", "sub", None, None),
            P("grp", "sub", None),
            P("sub", "grp", None),
        ),
        out_specs=(P("grp", "sub", None, None), P("grp", "sub", None, None)),
        check_vma=False,
    )
```

time: 593 us -> 220 us (0.37); the launches traced: 583 us -> 219 us
  waiting for transfers between devices: 261 us -> 69.6 us
  blocking collectives: 203 us -> 40.1 us
  matrix products: 47.7 us -> 26.7 us
  between operations: 15.4 us -> 1.54 us
  local copies, waits for them, and re-layouts: 4.34 us -> 15.3 us
  starting transfers between devices: 35.1 us -> 42.7 us
  other arithmetic: 16.7 us -> 23.2 us
    psum x5 -> x0, blocking collectives: 203 us -> none  [the longest x3 122 us: residual_sum(): return lax.psum(inner(resid, precond), ('sub', 'grp'))]
    psum x3 -> x0, waiting for transfers between devices: 109 us -> none  [local(): solved = lax.psum(partial_solved, 'grp')]
    reduce_scatter x3 -> x0, waiting for transfers between devices: 78.8 us -> none  [local(): lax.psum_scatter(jnp.einsum('skn,srk->nr', corner_onehot, corner_vals, pr...]
    all_gather x0 -> x4, blocking collectives: none -> 27.5 us  [the longest x3 21.5 us: apply_dual(): lax.all_gather(corner_vals.reshape(local_subs * corners, loads), 'grp', t...]
    dot_general x21 -> x26, matrix products: 47.7 us -> 26.7 us  [the longest x6 7.85 us: panel_apply(): lax.dot_general(low, panel, dims, preferred_element_type=jnp.float32)]
    all_to_all x0 -> x1, blocking collectives: none -> 12.7 us  [sum_all(): return jnp.sum(lax.all_to_all(copies, ('sub', 'grp'), 0, 0), axis=0)]
    all_to_all x0 -> x2, starting transfers between devices: none -> 11 us  [sum_all(): return jnp.sum(lax.all_to_all(copies, ('sub', 'grp'), 0, 0), axis=0)]
    broadcast_in_dim x0 -> x7, other arithmetic: none -> 6.58 us  [the longest x1 4.31 us: local(): return (multipliers[None], residual[1:][None])]
  transfers between devices with their start and end apart: 18 -> 18, of which waited for: 18 -> 8; matrix products, arithmetic and copies ran while one was open for 0% -> 8% of each run, Pallas kernels for 0% -> 0%
where the time goes in v1:
time: 220 us; the launch traced here: 219 us
  waiting for transfers between devices  69.6 us (32%)
  starting transfers between devices  42.7 us (19%)
  blocking collectives  40.1 us (18%)
  matrix products  26.7 us (12%)
  other arithmetic  23.2 us (11%)
  local copies, waits for them, and re-layouts  15.3 us (7%)
    ppermute x6, waiting for transfers between devices, swap_with_neighbours(): lax.ppermute(jnp.where(even, to_next, to_prev), 'sub', neighbour_pairs(si...  64.1 us
    all_gather x3, blocking collectives, apply_dual(): lax.all_gather(corner_vals.reshape(local_subs * corners, loads), 'grp', t...  21.5 us
    ppermute x6, starting transfers between devices, swap_with_neighbours(): lax.ppermute(jnp.where(even, to_next, to_prev), 'sub', neighbour_pairs(si...  19.6 us
    all_to_all x1, blocking collectives, sum_all(): return jnp.sum(lax.all_to_all(copies, ('sub', 'grp'), 0, 0), axis=0)  12.7 us
    all_to_all x2, starting transfers between devices, sum_all(): return jnp.sum(lax.all_to_all(copies, ('sub', 'grp'), 0, 0), axis=0)  11 us
    unnamed x83, local copies, waits for them, and re-layouts  8.4 us
    dot_general x6, matrix products, panel_apply(): lax.dot_general(low, panel, dims, preferred_element_type=jnp.float32)  7.85 us
    all_gather x1, blocking collectives, coarse_block(): everyone = lax.all_gather(corner_map.reshape(own), 'grp', tiled=True)  5.97 us
  transfers between devices with their start and end apart: 18, of which 8 were waited for; matrix products, arithmetic and copies ran while one was open for 8% of the time, Pallas kernels for 0%

profile of v1, /device:TPU:0, one launch (start us, length us, event | category | flops | bytes accessed | tf_op | source)
XLA Modules:
  0.0 219.2 jit_solution(15607745388521065092)
XLA Ops:
  0.7 0.9 reshape.224
  1.6 6.0 %all-gather = s32[4,1,128]{2,1,0:T(1,128)S(1)} all-gather(s32[1,1,128]{2,1,0:T(1,128)S(1)} %reshape.224), channel_id=1, replica_groups=mesh['sub'=8,'grp'=4] {'grp'}, dimensions={0}, use_global_device_ids=true | all-gather | bytes 2560 | tf_op jit(solution)/shard_map/all_gather | solution.py:59
  7.6 2.2 fusion.57
  9.8 1.0 fusion.82
  11.2 1.0 fusion.80
  12.2 2.0 collective-permute-start.4
  14.2 1.0 fusion.78
  15.4 1.3 bitcast_multiply_fusion
  16.8 4.1 %collective-permute-start = (f32[264,256]{1,0:T(8,128)S(1)}, f32[264,256]{1,0:T(8,128)}, u32[]{:S(2)}, u32[]{:S(2)}) collective-permute-start(f32[264,256]{1,0:T(8,128)S(1)} %pad_maximum_fusion.10), channel_id=1, source_target_pairs={{0,4},{4,8},{8,12},{12,16},{16,20},{20,24},{24,28},{1,5},{5,9},{9,... | collective-permute-start | bytes 811016 | tf_op jit(solution)/shard_map/ppermute | solution.py:98
  21.6 4.8 %collective-permute-done.5 = f32[128,512]{1,0:T(8,128)} collective-permute-done((f32[128,512]{1,0:T(8,128)}, f32[128,512]{1,0:T(8,128)}, u32[]{:S(2)}, u32[]{:S(2)}) %collective-permute-start.5) | collective-permute-done | bytes 262176 | tf_op jit(solution)/shard_map/ppermute | solution.py:72
  26.4 1.6 fusion.54
  28.0 0.7 slice.221
  28.8 1.0 slice_bitcast_fusion
  30.6 0.7 fusion.26
  31.3 0.7 fusion.31
  32.1 1.5 collective-permute-start.2
  34.5 11.3 %collective-permute-done.2 = f32[256,256]{1,0:T(8,128)S(1)} collective-permute-done((f32[256,256]{1,0:T(8,128)S(1)}, f32[256,256]{1,0:T(8,128)S(1)}, u32[]{:S(2)}, u32[]{:S(2)}) %collective-permute-start.2) | collective-permute-done | bytes 262176 | tf_op jit(solution)/shard_map/ppermute | solution.py:24
  46.2 1.4 copy-done.1
  49.3 1.0 fusion.42
  50.3 7.2 %all_gather.13 = f32[512,256]{1,0:T(8,128)S(1)} all-gather(f32[128,256]{1,0:T(8,128)S(1)} %bitcast.153), channel_id=1, replica_groups=mesh['sub'=8,'grp'=4] {'grp'}, dimensions={0}, use_global_device_ids=true | all-gather | bytes 655360 | tf_op jit(solution)/shard_map/all_gather | solution.py:110
  57.8 1.2 add_add_fusion.2
  59.1 2.5 %collective-permute-start.7 = (f32[256,256]{1,0:T(8,128)S(1)}, f32[256,256]{1,0:T(8,128)S(1)}, u32[]{:S(2)}, u32[]{:S(2)}) collective-permute-start(f32[256,256]{1,0:T(8,128)S(1)} %get-tuple-element.37), channel_id=1, source_target_pairs={{0,4},{4,0},{8,12},{12,8},{16,20},{20,16},{24,28},{28,24},{1,5},{5... | collective-permute-start | bytes 786440 | tf_op jit(solution)/shard_map/ppermute | solution.py:24
  62.5 10.8 %collective-permute-done.7 = f32[256,256]{1,0:T(8,128)S(1)} collective-permute-done((f32[256,256]{1,0:T(8,128)S(1)}, f32[256,256]{1,0:T(8,128)S(1)}, u32[]{:S(2)}, u32[]{:S(2)}) %collective-permute-start.7) | collective-permute-done | bytes 262176 | tf_op jit(solution)/shard_map/ppermute | solution.py:24
  73.6 1.0 copy-done.33
  74.6 1.7 multiply_reduce_fusion.4
  77.0 5.6 %all-to-all-start = ((f32[32,2,256]{2,1,0:T(2,128)}), f32[32,2,256]{2,1,0:T(2,128)S(1)}, u32[]{:S(2)}, u32[]{:S(2)}) async-start(f32[32,2,256]{2,1,0:T(2,128)} %broadcast_in_dim.47), calls=%async_computation | async-start | bytes 131072 | tf_op jit(solution)/shard_map/all_to_all | solution.py:32
  82.6 2.4 %fusion.22 = f32[4,256,512]{2,1,0:T(8,128)S(1)} fusion(bf16[1,4,512,512]{3,2,1,0:T(8,128)(2,1)S(1)} %copy-done, f32[4,256,256]{2,1,0:T(8,128)} %get-tuple-element.54, f32[4,256,256]{2,1,0:T(8,128)} %get-tuple-element.53), kind=kOutput, calls=%fused_computation.40 | convolution fusion | flops 538968064 | bytes 6291456 | tf_op jit(solution)/shard_map/dot_general | solution.py:42
  85.1 0.7 fusion.34
  85.8 0.8 select_bitcast_fusion.15
  86.7 1.4 collective-permute-start.8
  88.0 4.0 %collective-permute-start.9 = (f32[256,256]{1,0:T(8,128)}, f32[256,256]{1,0:T(8,128)}, u32[]{:S(2)}, u32[]{:S(2)}) collective-permute-start(f32[256,256]{1,0:T(8,128)} %get-tuple-element.34), channel_id=1, source_target_pairs={{0,4},{4,0},{8,12},{12,8},{16,20},{20,16},{24,28},{28,24},{1,5},{5... | collective-permute-start | bytes 786440 | tf_op jit(solution)/shard_map/ppermute | solution.py:24
  92.0 1.5 fusion.116
  93.6 9.4 %collective-permute-done.9 = f32[256,256]{1,0:T(8,128)} collective-permute-done((f32[256,256]{1,0:T(8,128)}, f32[256,256]{1,0:T(8,128)}, u32[]{:S(2)}, u32[]{:S(2)}) %collective-permute-start.9) | collective-permute-done | bytes 262176 | tf_op jit(solution)/shard_map/ppermute | solution.py:24
  103.0 1.1 select_bitcast_fusion.13
  104.1 1.8 multiply_subtract_fusion.3
  106.1 0.9 copy-done.11
  107.1 1.0 fusion.41
  108.6 0.8 fusion.10
  109.4 0.8 fusion.12
  110.2 7.1 %all_gather.14 = f32[512,256]{1,0:T(8,128)S(1)} all-gather(f32[128,256]{1,0:T(8,128)S(1)} %bitcast.148), channel_id=1, replica_groups=mesh['sub'=8,'grp'=4] {'grp'}, dimensions={0}, use_global_device_ids=true | all-gather | bytes 655360 | tf_op jit(solution)/shard_map/all_gather | solution.py:110
  117.6 1.2 add_add_fusion.1
  119.6 5.2 %collective-permute-start.11 = (f32[256,256]{1,0:T(8,128)S(1)}, f32[256,256]{1,0:T(8,128)S(1)}, u32[]{:S(2)}, u32[]{:S(2)}) collective-permute-start(f32[256,256]{1,0:T(8,128)S(1)} %get-tuple-element.30), channel_id=1, source_target_pairs={{0,4},{4,0},{8,12},{12,8},{16,20},{20,16},{24,28},{28,24},{1,5},{5... | collective-permute-start | bytes 786440 | tf_op jit(solution)/shard_map/ppermute | solution.py:24
  125.0 10.8 %collective-permute-done.11 = f32[256,256]{1,0:T(8,128)S(1)} collective-permute-done((f32[256,256]{1,0:T(8,128)S(1)}, f32[256,256]{1,0:T(8,128)S(1)}, u32[]{:S(2)}, u32[]{:S(2)}) %collective-permute-start.11) | collective-permute-done | bytes 262176 | tf_op jit(solution)/shard_map/ppermute | solution.py:24
  136.6 1.9 fusion.69
  139.5 5.5 %all-to-all-start.1 = ((f32[32,2,256]{2,1,0:T(2,128)}), f32[32,2,256]{2,1,0:T(2,128)S(1)}, u32[]{:S(2)}, u32[]{:S(2)}) async-start(f32[32,2,256]{2,1,0:T(2,128)} %broadcast_in_dim.52), calls=%async_computation.1 | async-start | bytes 131072 | tf_op jit(solution)/shard_map/all_to_all | solution.py:32
  145.0 2.4 %fusion.18 = f32[4,256,512]{2,1,0:T(8,128)S(1)} fusion(bf16[1,4,512,512]{3,2,1,0:T(8,128)(2,1)S(1)} %copy-done, f32[4,256,256]{2,1,0:T(8,128)} %get-tuple-element.50, f32[4,256,256]{2,1,0:T(8,128)} %get-tuple-element.49), kind=kOutput, calls=%fused_computation.36 | convolution fusion | flops 538968064 | bytes 6291456 | tf_op jit(solution)/shard_map/dot_general | solution.py:42
  147.4 0.7 fusion.37
  148.2 1.5 fusion.114
  149.7 0.8 select_bitcast_fusion.7
  150.5 1.4 collective-permute-start.12
  151.9 3.8 %collective-permute-start.13 = (f32[256,256]{1,0:T(8,128)}, f32[256,256]{1,0:T(8,128)}, u32[]{:S(2)}, u32[]{:S(2)}) collective-permute-start(f32[256,256]{1,0:T(8,128)} %get-tuple-element.26), channel_id=1, source_target_pairs={{0,4},{4,0},{8,12},{12,8},{16,20},{20,16},{24,28},{28,24},{1,5},{5... | collective-permute-start | bytes 786440 | tf_op jit(solution)/shard_map/ppermute | solution.py:24
  155.8 11.1 %collective-permute-done.13 = f32[256,256]{1,0:T(8,128)} collective-permute-done((f32[256,256]{1,0:T(8,128)}, f32[256,256]{1,0:T(8,128)}, u32[]{:S(2)}, u32[]{:S(2)}) %collective-permute-start.13) | collective-permute-done | bytes 262176 | tf_op jit(solution)/shard_map/ppermute | solution.py:24
  166.9 1.1 select_bitcast_fusion.5
  167.9 4.0 %multiply_subtract_fusion = (f32[5,256,256]{2,1,0:T(8,128)S(1)}, f32[5,256,256]{2,1,0:T(8,128)S(1)}, f32[5,256,256]{2,1,0:T(8,128)}) fusion(f32[5,256,256]{2,1,0:T(8,128)} %copy-done.14, f32[5,256,256]{2,1,0:T(8,128)} %copy-done.11, f32[256]{0:T(256)S(1)} %get-tuple-element.14, f32[256]{0:T(256)S(1)} %get-tuple-element.16, ...), kind=kLoop, calls=%fused_computation.78 | loop fusion | flops 3276800 | bytes 10492928 | tf_op jit(solution)/shard_map/sub | solution.py:145
  172.2 0.9 copy-done.17
  173.1 1.0 fusion.40
  175.6 7.1 %all_gather.15 = f32[512,256]{1,0:T(8,128)S(1)} all-gather(f32[128,256]{1,0:T(8,128)S(1)} %bitcast.149), channel_id=1, replica_groups=mesh['sub'=8,'grp'=4] {'grp'}, dimensions={0}, use_global_device_ids=true | all-gather | bytes 655360 | tf_op jit(solution)/shard_map/all_gather | solution.py:110
  183.1 1.2 add_add_fusion
  184.4 2.5 %collective-permute-start.15 = (f32[256,256]{1,0:T(8,128)S(1)}, f32[256,256]{1,0:T(8,128)S(1)}, u32[]{:S(2)}, u32[]{:S(2)}) collective-permute-start(f32[256,256]{1,0:T(8,128)S(1)} %get-tuple-element.21), channel_id=1, source_target_pairs={{0,4},{4,0},{8,12},{12,8},{16,20},{20,16},{24,28},{28,24},{1,5},{5... | collective-permute-start | bytes 786440 | tf_op jit(solution)/shard_map/ppermute | solution.py:24
  186.9 0.8 collective-permute-start.14
  188.0 10.7 %collective-permute-done.15 = f32[256,256]{1,0:T(8,128)S(1)} collective-permute-done((f32[256,256]{1,0:T(8,128)S(1)}, f32[256,256]{1,0:T(8,128)S(1)}, u32[]{:S(2)}, u32[]{:S(2)}) %collective-permute-start.15) | collective-permute-done | bytes 262176 | tf_op jit(solution)/shard_map/ppermute | solution.py:24
  198.7 1.9 multiply_subtract_fusion.1
  202.1 12.7 %all_to_all.15 = f32[32,2,256]{2,1,0:T(2,128)S(1)} all-to-all(f32[32,2,256]{2,1,0:T(2,128)S(1)} %broadcast_in_dim.57), channel_id=1, replica_groups=mesh['sub'=8,'grp'=4] {'sub','grp'}, dimensions={0} | all-to-all | bytes 131072 | tf_op jit(solution)/shard_map/all_to_all | solution.py:32
  214.8 4.3 %fusion.68 = (f32[1,4,256,256]{3,2,1,0:T(8,128)}, f32[1,4,256,256]{3,2,1,0:T(8,128)}) fusion(f32[5,256,256]{2,1,0:T(8,128)} %get-tuple-element.11, f32[5,256,256]{2,1,0:T(8,128)} %copy-done.28, f32[5,256,256]{2,1,0:T(8,128)} %copy-done.27, f32[256]{0:T(256)S(1)} %get-tuple-element.9, f32[256]{0:T(256)S(1)} %get-tuple-element.8, ...), kind=kLoop, calls=%fused_computation.94 | loop fusion | flops 2883584 | bytes 8392704 | tf_op jit(solution)/shard_map/broadcast_in_dim | solution.py:148
  (145 shorter events, 14.7 us)
Async XLA Ops:
  0.6 29.9 %copy-start = (bf16[1,4,512,512]{3,2,1,0:T(8,128)(2,1)S(1)}, bf16[1,4,512,512]{3,2,1,0:T(8,128)(2,1)}, u32[]{:S(2)}) copy-start(bf16[1,4,512,512]{3,2,1,0:T(8,128)(2,1)} %param.10) | copy-start | bytes 6291460
  0.6 14.6 %copy-start.40 = (s32[1,4]{1,0:T(1,128)S(1)}, s32[1,4]{1,0:T(1,128)}, u32[]{:S(2)}) copy-start(s32[1,4]{1,0:T(1,128)} %param.8) | copy-start | bytes 52
  9.7 4.5 %copy-start.29 = (f32[512,256]{1,0:T(8,128)}, f32[512,256]{1,0:T(8,128)S(1)}, u32[]{:S(2)}) copy-start(f32[512,256]{1,0:T(8,128)S(1)} %fusion.57) | copy-start | bytes 1572868
  10.9 10.0 %collective-permute-start.3 = (f32[128,512]{1,0:T(8,128)}, f32[128,512]{1,0:T(8,128)}, u32[]{:S(2)}, u32[]{:S(2)}) collective-permute-start(f32[128,512]{1,0:T(8,128)} %fusion.82), channel_id=1, source_target_pairs={{0,1},{1,0},{2,3},{3,2},{4,5},{5,4},{6,7},{7,6},{8,9},{9,8},{10,11... | collective-permute-start | bytes 786440 | tf_op jit(solution)/shard_map/ppermute | solution.py:72
  12.2 9.4 %collective-permute-start.4 = (f32[128,512]{1,0:T(8,128)}, f32[128,512]{1,0:T(8,128)}, u32[]{:S(2)}, u32[]{:S(2)}) collective-permute-start(f32[128,512]{1,0:T(8,128)} %fusion.80), channel_id=1, source_target_pairs={{0,2},{1,3},{2,0},{3,1},{4,6},{5,7},{6,4},{7,5},{8,10},{9,11},{10,... | collective-permute-start | bytes 786440 | tf_op jit(solution)/shard_map/ppermute | solution.py:72
  15.2 11.2 %collective-permute-start.5 = (f32[128,512]{1,0:T(8,128)}, f32[128,512]{1,0:T(8,128)}, u32[]{:S(2)}, u32[]{:S(2)}) collective-permute-start(f32[128,512]{1,0:T(8,128)} %fusion.78), channel_id=1, source_target_pairs={{0,3},{1,2},{2,1},{3,0},{4,7},{5,6},{6,5},{7,4},{8,11},{9,10},{10,... | collective-permute-start | bytes 786440 | tf_op jit(solution)/shard_map/ppermute | solution.py:72
  16.7 14.6 %copy-start.4 = (f32[4,256,256]{2,1,0:T(8,128)}, f32[4,256,256]{2,1,0:T(8,128)S(1)}, u32[]{:S(2)}) copy-start(f32[4,256,256]{2,1,0:T(8,128)S(1)} %bitcast_multiply_fusion) | copy-start | bytes 3145732
  16.8 11.3 %collective-permute-start = (f32[264,256]{1,0:T(8,128)S(1)}, f32[264,256]{1,0:T(8,128)}, u32[]{:S(2)}, u32[]{:S(2)}) collective-permute-start(f32[264,256]{1,0:T(8,128)S(1)} %pad_maximum_fusion.10), channel_id=1, source_target_pairs={{0,4},{4,8},{8,12},{12,16},{16,20},{20,24},{24,28},{1,5},{5,9},{9,... | collective-permute-start | bytes 811016 | tf_op jit(solution)/shard_map/ppermute | solution.py:98
  28.0 29.5 %copy-start.30 = (f32[128,512]{1,0:T(8,128)}, f32[128,512]{1,0:T(8,128)S(1)}, u32[]{:S(2)}) copy-start(f32[128,512]{1,0:T(8,128)S(1)} %fusion.54) | copy-start | bytes 786436
  29.8 0.7 copy-start.34
  32.1 13.6 %collective-permute-start.2 = (f32[256,256]{1,0:T(8,128)S(1)}, f32[256,256]{1,0:T(8,128)S(1)}, u32[]{:S(2)}, u32[]{:S(2)}) collective-permute-start(f32[256,256]{1,0:T(8,128)S(1)} %get-tuple-element.41), channel_id=1, source_target_pairs={{0,4},{4,0},{8,12},{12,8},{16,20},{20,16},{24,28},{28,24},{1,5},{5... | collective-permute-start | bytes 786440 | tf_op jit(solution)/shard_map/ppermute | solution.py:24
  33.6 12.2 %collective-permute-start.1 = (f32[256,256]{1,0:T(8,128)S(1)}, f32[256,256]{1,0:T(8,128)S(1)}, u32[]{:S(2)}, u32[]{:S(2)}) collective-permute-start(f32[256,256]{1,0:T(8,128)S(1)} %get-tuple-element.42), channel_id=1, source_target_pairs={{4,8},{8,4},{12,16},{16,12},{20,24},{24,20},{5,9},{9,5},{13,17},{1... | collective-permute-start | bytes 786440 | tf_op jit(solution)/shard_map/ppermute | solution.py:25
  46.0 1.6 copy-start.1
  48.3 1.0 copy-start.15
  59.1 14.2 %collective-permute-start.7 = (f32[256,256]{1,0:T(8,128)S(1)}, f32[256,256]{1,0:T(8,128)S(1)}, u32[]{:S(2)}, u32[]{:S(2)}) collective-permute-start(f32[256,256]{1,0:T(8,128)S(1)} %get-tuple-element.37), channel_id=1, source_target_pairs={{0,4},{4,0},{8,12},{12,8},{16,20},{20,16},{24,28},{28,24},{1,5},{5... | collective-permute-start | bytes 786440 | tf_op jit(solution)/shard_map/ppermute | solution.py:24
  61.6 11.7 %collective-permute-start.6 = (f32[256,256]{1,0:T(8,128)S(1)}, f32[256,256]{1,0:T(8,128)S(1)}, u32[]{:S(2)}, u32[]{:S(2)}) collective-permute-start(f32[256,256]{1,0:T(8,128)S(1)} %get-tuple-element.38), channel_id=1, source_target_pairs={{4,8},{8,4},{12,16},{16,12},{20,24},{24,20},{5,9},{9,5},{13,17},{1... | collective-permute-start | bytes 786440 | tf_op jit(solution)/shard_map/ppermute | solution.py:25
  73.4 1.2 copy-start.33
  74.6 1.7 copy-start.6
  77.0 16.5 %all-to-all-start = ((f32[32,2,256]{2,1,0:T(2,128)}), f32[32,2,256]{2,1,0:T(2,128)S(1)}, u32[]{:S(2)}, u32[]{:S(2)}) async-start(f32[32,2,256]{2,1,0:T(2,128)} %broadcast_in_dim.47), calls=%async_computation | async-start | bytes 131072 | tf_op jit(solution)/shard_map/all_to_all | solution.py:32
  82.6 2.5 %copy-start.22 = (f32[4,256,256]{2,1,0:T(8,128)S(1)}, f32[4,256,256]{2,1,0:T(8,128)}, u32[]{:S(2)}) copy-start(f32[4,256,256]{2,1,0:T(8,128)} %get-tuple-element.53) | copy-start | bytes 3145732
  82.6 2.5 %copy-start.23 = (f32[4,256,256]{2,1,0:T(8,128)S(1)}, f32[4,256,256]{2,1,0:T(8,128)}, u32[]{:S(2)}) copy-start(f32[4,256,256]{2,1,0:T(8,128)} %get-tuple-element.54) | copy-start | bytes 3145732
  86.7 7.0 %collective-permute-start.8 = (f32[256,256]{1,0:T(8,128)}, f32[256,256]{1,0:T(8,128)}, u32[]{:S(2)}, u32[]{:S(2)}) collective-permute-start(f32[256,256]{1,0:T(8,128)} %get-tuple-element.33), channel_id=1, source_target_pairs={{4,8},{8,4},{12,16},{16,12},{20,24},{24,20},{5,9},{9,5},{13,17},{1... | collective-permute-start | bytes 786440 | tf_op jit(solution)/shard_map/ppermute | solution.py:25
  88.0 15.0 %collective-permute-start.9 = (f32[256,256]{1,0:T(8,128)}, f32[256,256]{1,0:T(8,128)}, u32[]{:S(2)}, u32[]{:S(2)}) collective-permute-start(f32[256,256]{1,0:T(8,128)} %get-tuple-element.34), channel_id=1, source_target_pairs={{0,4},{4,0},{8,12},{12,8},{16,20},{20,16},{24,28},{28,24},{1,5},{5... | collective-permute-start | bytes 786440 | tf_op jit(solution)/shard_map/ppermute | solution.py:24
  105.9 1.1 copy-start.11
  105.9 30.7 %copy-start.14 = (f32[5,256,256]{2,1,0:T(8,128)}, f32[5,256,256]{2,1,0:T(8,128)S(1)}, u32[]{:S(2)}) copy-start(f32[5,256,256]{2,1,0:T(8,128)S(1)} %get-tuple-element.17) | copy-start | bytes 3932164
  106.0 1.2 copy-start.16
  107.0 1.6 copy-start.2
  109.4 7.9 %copy-start.31 = (f32[128,512]{1,0:T(8,128)S(1)}, f32[128,512]{1,0:T(8,128)}, u32[]{:S(2)}) copy-start(f32[128,512]{1,0:T(8,128)} %copy-done.30) | copy-start | bytes 786436
  118.8 6.2 %collective-permute-start.10 = (f32[256,256]{1,0:T(8,128)S(1)}, f32[256,256]{1,0:T(8,128)S(1)}, u32[]{:S(2)}, u32[]{:S(2)}) collective-permute-start(f32[256,256]{1,0:T(8,128)S(1)} %get-tuple-element.29), channel_id=1, source_target_pairs={{4,8},{8,4},{12,16},{16,12},{20,24},{24,20},{5,9},{9,5},{13,17},{1... | collective-permute-start | bytes 786440 | tf_op jit(solution)/shard_map/ppermute | solution.py:25
  119.5 16.3 %copy-start.5 = (f32[4,256,256]{2,1,0:T(8,128)S(1)}, f32[4,256,256]{2,1,0:T(8,128)}, u32[]{:S(2)}) copy-start(f32[4,256,256]{2,1,0:T(8,128)} %copy-done.4) | copy-start | bytes 3145732
  119.5 16.3 %copy-start.7 = (f32[5,256,256]{2,1,0:T(8,128)S(1)}, f32[5,256,256]{2,1,0:T(8,128)}, u32[]{:S(2)}) copy-start(f32[5,256,256]{2,1,0:T(8,128)} %copy-done.6) | copy-start | bytes 3932164
  119.5 16.3 %copy-start.35 = (f32[1,256,256]{2,1,0:T(8,128)S(1)}, f32[1,256,256]{2,1,0:T(8,128)}, u32[]{:S(2)}) copy-start(f32[1,256,256]{2,1,0:T(8,128)} %copy-done.34) | copy-start | bytes 786436
  119.6 16.2 %collective-permute-start.11 = (f32[256,256]{1,0:T(8,128)S(1)}, f32[256,256]{1,0:T(8,128)S(1)}, u32[]{:S(2)}, u32[]{:S(2)}) collective-permute-start(f32[256,256]{1,0:T(8,128)S(1)} %get-tuple-element.30), channel_id=1, source_target_pairs={{0,4},{4,0},{8,12},{12,8},{16,20},{20,16},{24,28},{28,24},{1,5},{5... | collective-permute-start | bytes 786440 | tf_op jit(solution)/shard_map/ppermute | solution.py:24
  125.0 11.3 %copy-start.18 = (f32[4,256,256]{2,1,0:T(8,128)}, f32[4,256,256]{2,1,0:T(8,128)S(1)}, u32[]{:S(2)}) copy-start(f32[4,256,256]{2,1,0:T(8,128)S(1)} %get-tuple-element.27) | copy-start | bytes 3145732
  125.0 11.3 %copy-start.20 = (f32[4,256,256]{2,1,0:T(8,128)}, f32[4,256,256]{2,1,0:T(8,128)S(1)}, u32[]{:S(2)}) copy-start(f32[4,256,256]{2,1,0:T(8,128)S(1)} %get-tuple-element.28) | copy-start | bytes 3145732
  135.8 0.7 copy-start.36
  135.8 0.8 copy-start.38
  136.6 1.9 copy-start.9
  136.6 2.2 copy-start.12
  139.5 16.2 %all-to-all-start.1 = ((f32[32,2,256]{2,1,0:T(2,128)}), f32[32,2,256]{2,1,0:T(2,128)S(1)}, u32[]{:S(2)}, u32[]{:S(2)}) async-start(f32[32,2,256]{2,1,0:T(2,128)} %broadcast_in_dim.52), calls=%async_computation.1 | async-start | bytes 131072 | tf_op jit(solution)/shard_map/all_to_all | solution.py:32
  144.9 2.5 %copy-start.24 = (f32[4,256,256]{2,1,0:T(8,128)S(1)}, f32[4,256,256]{2,1,0:T(8,128)}, u32[]{:S(2)}) copy-start(f32[4,256,256]{2,1,0:T(8,128)} %get-tuple-element.49) | copy-start | bytes 3145732
  144.9 2.5 %copy-start.25 = (f32[4,256,256]{2,1,0:T(8,128)S(1)}, f32[4,256,256]{2,1,0:T(8,128)}, u32[]{:S(2)}) copy-start(f32[4,256,256]{2,1,0:T(8,128)} %get-tuple-element.50) | copy-start | bytes 3145732
  150.5 5.3 %collective-permute-start.12 = (f32[256,256]{1,0:T(8,128)}, f32[256,256]{1,0:T(8,128)}, u32[]{:S(2)}, u32[]{:S(2)}) collective-permute-start(f32[256,256]{1,0:T(8,128)} %get-tuple-element.25), channel_id=1, source_target_pairs={{4,8},{8,4},{12,16},{16,12},{20,24},{24,20},{5,9},{9,5},{13,17},{1... | collective-permute-start | bytes 786440 | tf_op jit(solution)/shard_map/ppermute | solution.py:25
  151.9 15.0 %collective-permute-start.13 = (f32[256,256]{1,0:T(8,128)}, f32[256,256]{1,0:T(8,128)}, u32[]{:S(2)}, u32[]{:S(2)}) collective-permute-start(f32[256,256]{1,0:T(8,128)} %get-tuple-element.26), channel_id=1, source_target_pairs={{0,4},{4,0},{8,12},{12,8},{16,20},{20,16},{24,28},{28,24},{1,5},{5... | collective-permute-start | bytes 786440 | tf_op jit(solution)/shard_map/ppermute | solution.py:24
  172.0 28.6 %copy-start.26 = (f32[5,256,256]{2,1,0:T(8,128)}, f32[5,256,256]{2,1,0:T(8,128)S(1)}, u32[]{:S(2)}) copy-start(f32[5,256,256]{2,1,0:T(8,128)S(1)} %get-tuple-element.12) | copy-start | bytes 3932164
  172.0 1.1 copy-start.17
  172.2 2.0 copy-start.3
  174.9 7.9 %copy-start.32 = (f32[128,512]{1,0:T(8,128)S(1)}, f32[128,512]{1,0:T(8,128)}, u32[]{:S(2)}) copy-start(f32[128,512]{1,0:T(8,128)} %copy-done.30) | copy-start | bytes 786436
  183.1 15.6 %copy-start.39 = (f32[1,256,256]{2,1,0:T(8,128)S(1)}, f32[1,256,256]{2,1,0:T(8,128)}, u32[]{:S(2)}) copy-start(f32[1,256,256]{2,1,0:T(8,128)} %copy-done.38) | copy-start | bytes 786436
  184.3 14.4 %copy-start.21 = (f32[4,256,256]{2,1,0:T(8,128)S(1)}, f32[4,256,256]{2,1,0:T(8,128)}, u32[]{:S(2)}) copy-start(f32[4,256,256]{2,1,0:T(8,128)} %copy-done.20) | copy-start | bytes 3145732
  184.4 14.2 %collective-permute-start.15 = (f32[256,256]{1,0:T(8,128)S(1)}, f32[256,256]{1,0:T(8,128)S(1)}, u32[]{:S(2)}, u32[]{:S(2)}) collective-permute-start(f32[256,256]{1,0:T(8,128)S(1)} %get-tuple-element.21), channel_id=1, source_target_pairs={{0,4},{4,0},{8,12},{12,8},{16,20},{20,16},{24,28},{28,24},{1,5},{5... | collective-permute-start | bytes 786440 | tf_op jit(solution)/shard_map/ppermute | solution.py:24
  186.9 11.8 %copy-start.8 = (f32[5,256,256]{2,1,0:T(8,128)S(1)}, f32[5,256,256]{2,1,0:T(8,128)}, u32[]{:S(2)}) copy-start(f32[5,256,256]{2,1,0:T(8,128)} %copy-done.6) | copy-start | bytes 3932164
  186.9 11.8 %copy-start.10 = (f32[5,256,256]{2,1,0:T(8,128)S(1)}, f32[5,256,256]{2,1,0:T(8,128)}, u32[]{:S(2)}) copy-start(f32[5,256,256]{2,1,0:T(8,128)} %copy-done.9) | copy-start | bytes 3932164
  186.9 11.8 %copy-start.13 = (f32[5,256,256]{2,1,0:T(8,128)S(1)}, f32[5,256,256]{2,1,0:T(8,128)}, u32[]{:S(2)}) copy-start(f32[5,256,256]{2,1,0:T(8,128)} %copy-done.12) | copy-start | bytes 3932164
  186.9 11.8 %copy-start.19 = (f32[4,256,256]{2,1,0:T(8,128)S(1)}, f32[4,256,256]{2,1,0:T(8,128)}, u32[]{:S(2)}) copy-start(f32[4,256,256]{2,1,0:T(8,128)} %copy-done.18) | copy-start | bytes 3145732
  186.9 11.8 %copy-start.37 = (f32[1,256,256]{2,1,0:T(8,128)S(1)}, f32[1,256,256]{2,1,0:T(8,128)}, u32[]{:S(2)}) copy-start(f32[1,256,256]{2,1,0:T(8,128)} %copy-done.36) | copy-start | bytes 786436
  186.9 11.7 %collective-permute-start.14 = (f32[256,256]{1,0:T(8,128)S(1)}, f32[256,256]{1,0:T(8,128)S(1)}, u32[]{:S(2)}, u32[]{:S(2)}) collective-permute-start(f32[256,256]{1,0:T(8,128)S(1)} %get-tuple-element.22), channel_id=1, source_target_pairs={{4,8},{8,4},{12,16},{16,12},{20,24},{24,20},{5,9},{9,5},{13,17},{1... | collective-permute-start | bytes 786440 | tf_op jit(solution)/shard_map/ppermute | solution.py:25
  200.6 1.1 copy-start.27
  200.6 1.5 copy-start.28

commit v2 on v1

v2 whole, which is shorter than its diff:
```python
import functools

import jax
import jax.numpy as jnp
from jax import lax
from jax.experimental import pallas as pl
from jax.experimental.pallas import tpu as pltpu
from jax.sharding import PartitionSpec as P

ITERS = 3


HIGH = lax.Precision.HIGH
VMEM_LIMIT = 32 * 1024 * 1024


def split(values):
    high = values.astype(jnp.bfloat16)
    return high, (values - high.astype(jnp.float32)).astype(jnp.bfloat16)


def split_outside(values):
    high = lax.reduce_precision(values, exponent_bits=8, mantissa_bits=7)
    return high.astype(jnp.bfloat16), (values - high).astype(jnp.bfloat16)


def mul(first, second):
    return jnp.dot(first, second, preferred_element_type=jnp.float32)


def mul_rows(first, second):
    dims = (((1,), (1,)), ((), ()))
    return lax.dot_general(first, second, dims, preferred_element_type=jnp.float32)


def call(kernel, out_shapes, *operands):
    scalars = 1
    return pl.pallas_call(
        kernel,
        out_shape=[jax.ShapeDtypeStruct(shape, jnp.float32) for shape in out_shapes],
        in_specs=[pl.BlockSpec(memory_space=pltpu.SMEM)] * scalars
        + [pl.BlockSpec(memory_space=pltpu.VMEM)] * (len(operands) - scalars),
        out_specs=[pl.BlockSpec(memory_space=pltpu.VMEM)] * len(out_shapes),
        compiler_params=pltpu.CompilerParams(vmem_limit_bytes=VMEM_LIMIT),
    )(*operands)


def jump_edges(even, result, near, far, live):
    subs, width = result.shape[0], result.shape[2] // 2
    for edge in range(subs + 1):
        if edge == 0:
            right = jnp.where(even, far[...], near[...])
        else:
            right = result[edge - 1, :, width:]
        if edge == subs:
            left = jnp.where(even, near[...], far[...])
        else:
            left = result[edge, :, :width]
        yield edge, live[edge] * (right - left)


def send_faces(even, result, near_out, far_out):
    subs, width = result.shape[0], result.shape[2] // 2
    to_next, to_prev = result[subs - 1, :, width:], result[0, :, :width]
    near_out[...] = jnp.where(even, to_next, to_prev)
    far_out[...] = jnp.where(even, to_prev, to_next)


def panel_products(edges, panel, result, extra=None):
    parts = [split(edges[edge]) for edge in range(edges.shape[0])]
    for sub in range(panel.shape[0]):
        high = jnp.concatenate([-parts[sub][0], parts[sub + 1][0]], axis=1)
        low = jnp.concatenate([-parts[sub][1], parts[sub + 1][1]], axis=1)
        total = mul(high, panel[sub]) + mul(low, panel[sub])
        if extra is not None:
            total = total + extra(sub)
        result[sub] = total


def column(row, width):
    lanes = jnp.broadcast_to(row, (128, row.shape[1])).T
    return jnp.concatenate([lanes] * (width // 128), axis=1)


def row_sums(values):
    ones = jnp.ones((8, values.shape[1]), jnp.bfloat16)
    high, rest = split(values)
    middle, low = split(values - high.astype(jnp.float32))
    return (mul_rows(ones, high) + mul_rows(ones, middle) + mul_rows(ones, low))[:1]


def step_scalars(step, sums, before):
    totals = jnp.sum(sums[...], axis=0)
    rz_now, curvature = totals[:1], totals[1:2]
    if step == 0:
        return rz_now, rz_now / curvature, None
    beta = rz_now / before[0:1]
    return rz_now, rz_now / (curvature - beta * rz_now / before[1:2]), beta


def first_kernel(even_ref, edges, panel, result, near_out, far_out):
    panel_products(edges, panel, result)
    send_faces(even_ref[0] == 1, result, near_out, far_out)


def corner_kernel(even_ref, result, near, far, live, coupling, edges, corners):
    even = even_ref[0] == 1
    width = result.shape[2] // 2
    subs, rows = coupling.shape[0], coupling.shape[1] // 2
    for edge, value in jump_edges(even, result, near, far, live):
        edges[edge] = value
    parts = [split(edges[edge]) for edge in range(subs + 1)]
    for sub in range(subs):
        high = jnp.concatenate([-parts[sub][0], parts[sub + 1][0]], axis=1)
        low = jnp.concatenate([-parts[sub][1], parts[sub + 1][1]], axis=1)
        both = mul_rows(coupling[sub], high)
        corners[sub * rows : (sub + 1) * rows, :] = (
            both[:rows] + both[rows:] + mul_rows(coupling[sub, :rows], low)
        )


def dual_kernel(
    even_ref, edges, residual, panel, everyone, block, lift, result, near_out, far_out, sums
):
    even = even_ref[0] == 1
    subs, width = panel.shape[0], edges.shape[2]
    rows = block.shape[0] // 2
    high, low = split(everyone[...])
    both = mul(block[...], high)
    back = (both[:rows] + both[rows:] + mul(block[:rows], low)).T
    back_high, back_low = split(back)
    lifted = jnp.concatenate([back_high, back_low, back_high], axis=1)
    panel_products(edges, panel, result, lambda sub: mul(lifted, lift[sub]))
    send_faces(even, result, near_out, far_out)
    product = residual[1] * edges[1]
    curvature = result[0, :, width:] * edges[1] - result[0, :, :width] * edges[0]
    for sub in range(1, subs):
        product = product + residual[sub + 1] * edges[sub + 1]
        curvature = curvature + (
            result[sub, :, width:] * edges[sub + 1] - result[sub, :, :width] * edges[sub]
        )
    sums[...] = jnp.concatenate([row_sums(product), row_sums(curvature)], axis=0)


def update_kernel(step, even_ref, result, near, far, live, sums, before, image_old, residual,
                  panel, image_new, residual_new, result_new, near_out, far_out, scalars):
    even = even_ref[0] == 1
    width = near.shape[1]
    rz_now, alpha, beta = step_scalars(step, sums, before)
    scalars[...] = jnp.concatenate([rz_now, alpha], axis=0)
    alpha_column = column(alpha, width)
    beta_column = None if beta is None else column(beta, width)
    for edge, value in jump_edges(even, result, near, far, live):
        if beta is not None:
            value = value + beta_column * image_old[edge]
        image_new[edge] = value
        residual_new[edge] = residual[edge] - alpha_column * value
    panel_products(residual_new, panel, result_new)
    send_faces(even, result_new, near_out, far_out)


def last_kernel(step, even_ref, result, near, far, live, sums, before, older, image_old, residual,
                first, second, third, multipliers, residual_new):
    even = even_ref[0] == 1
    width = near.shape[1]
    rz_now, alpha, beta = step_scalars(step, sums, before)
    beta_before = before[0:1] / older[0:1]
    on_second = before[1:2] + alpha * beta
    on_first = older[1:2] + on_second * beta_before
    alpha_column, beta_column = column(alpha, width), column(beta, width)
    second_column, first_column = column(on_second, width), column(on_first, width)
    for edge, value in jump_edges(even, result, near, far, live):
        if edge > 0:
            value = value + beta_column * image_old[edge]
            residual_new[edge - 1] = residual[edge] - alpha_column * value
            multipliers[edge - 1] = (
                first_column * first[edge]
                + second_column * second[edge]
                + alpha_column * third[edge]
            )


def neighbour_pairs(size, first):
    pairs = [(i, i + 1) for i in range(first, size - 1, 2)]
    return [route for a, b in pairs for route in ((a, b), (b, a))]


def swap(near, far):
    size = lax.axis_size("sub")
    return (
        lax.ppermute(near, "sub", neighbour_pairs(size, 0)),
        lax.ppermute(far, "sub", neighbour_pairs(size, 1)),
    )


def from_all(rows):
    size = lax.axis_size("sub") * lax.axis_size("grp")
    copies = jnp.broadcast_to(rows[None], (size,) + rows.shape)
    return lax.all_to_all(copies, ("sub", "grp"), 0, 0)


def coarse_block(corner_map, coarse_inverse):
    rows, size = coarse_inverse.shape
    own = corner_map.size
    grp, group = lax.axis_index("grp"), lax.axis_size("grp")
    everyone = lax.all_gather(corner_map.reshape(own), "grp", tiled=True)
    columns = (everyone[None, :] == jnp.arange(size, dtype=jnp.int32)[:, None]).astype(jnp.float32)
    picked = jnp.dot(coarse_inverse, columns, precision=HIGH)
    owned = jnp.arange(rows, dtype=jnp.int32) + grp * rows

    def rows_for(member):
        wanted = lax.dynamic_slice_in_dim(everyone, member * own, own)
        chosen = (wanted[:, None] == owned[None, :]).astype(jnp.float32)
        return jnp.dot(chosen, picked, precision=HIGH)

    block = rows_for(grp)
    for distance in range(1, group):
        routes = [(i, i ^ distance) for i in range(group)]
        block = block + lax.ppermute(rows_for(grp ^ distance), "grp", routes)
    return block


def local(rhs, counts, solve_panel, dirichlet_panel, coupling, corner_map, coarse_inverse):
    subs, loads, width = rhs.shape[1:]
    corners = coupling.shape[2]
    solve, dirichlet, couple = solve_panel[0], dirichlet_panel[0], coupling[0]
    place, size = lax.axis_index("sub"), lax.axis_size("sub")
    even = (1 - place % 2).astype(jnp.int32).reshape(1)
    slots = jnp.arange(subs, dtype=jnp.int32)
    positions = jnp.arange(width, dtype=jnp.int32)
    not_last = jnp.logical_not((place == size - 1) & (slots == subs - 1))
    live = ((positions[None, :] < counts[0][:, None]) & not_last[:, None]).astype(jnp.float32)
    residual = live[:, None, :] * rhs[0]

    tail = jnp.concatenate([residual[-1], jnp.broadcast_to(live[-1:], (8, width))], axis=0)
    head = lax.ppermute(tail, "sub", [(i, i + 1) for i in range(size - 1)])
    residual = jnp.concatenate([head[None, :loads], residual], axis=0)
    live = jnp.concatenate([head[loads : loads + 1], live], axis=0)[:, None, :]

    block = jnp.concatenate(split_outside(coarse_block(corner_map[0], coarse_inverse[0])), axis=0)
    high, low = split_outside(couple)
    stacked = jnp.concatenate([high, low], axis=1)
    own = (slots[:, None] == slots[None, :])[:, :, None, None]

    def placed(part):
        wide = jnp.where(own, part[:, None], jnp.zeros((), part.dtype))
        return wide.reshape(subs, subs * corners, 2 * width)

    lift = jnp.concatenate([placed(high), placed(high), placed(low)], axis=1)

    edges_shape = (subs + 1, loads, width)
    result_shape = (subs, loads, 2 * width)
    face_shape = (loads, width)
    faces = [result_shape, face_shape, face_shape]

    result, near, far = call(first_kernel, faces, even, residual, dirichlet)
    scalars, images, preconds, image = [jnp.zeros((2, loads), jnp.float32)], [], [], None
    for step in range(ITERS):
        near, far = swap(near, far)
        edges, values = call(
            corner_kernel,
            [edges_shape, (subs * corners, loads)],
            even, result, near, far, 0.25 * live, stacked,
        )
        preconds.append(edges)
        everyone = lax.all_gather(values, "grp", tiled=True)
        result, near, far, sums = call(
            dual_kernel,
            faces + [(2, loads)],
            even, edges, residual, solve, everyone, block, lift,
        )
        sums = from_all(sums)
        near, far = swap(near, far)
        if step + 1 < ITERS:
            old = residual if image is None else image
            image, residual, result, near, far, now = call(
                functools.partial(update_kernel, step),
                [edges_shape, edges_shape] + faces + [(2, loads)],
                even, result, near, far, live, sums, scalars[-1], old, residual, dirichlet,
            )
            scalars.append(now)
    multipliers, residual = call(
        functools.partial(last_kernel, ITERS - 1),
        [(subs, loads, width)] * 2,
        even, result, near, far, live, sums, scalars[-1], scalars[-2], image, residual, *preconds,
    )
    return (multipliers[None], residual[None])


def solution(mesh):
    return jax.shard_map(
        local,
        mesh=mesh,
        in_specs=(
            P("grp", "sub", None, None),
            P("grp", "sub"),
            P("grp", "sub", None, None),
            P("grp", "sub", None, None),
            P("grp", "sub", None, None),
            P("grp", "sub", None),
            P("sub", "grp", None),
        ),
        out_specs=(P("grp", "sub", None, None), P("grp", "sub", None, None)),
        check_vma=False,
    )
```

time: 220 us -> 160 us (0.73)
  waiting for transfers between devices: 69.6 us -> 45 us
  other arithmetic: 23.2 us -> 0.66 us
  matrix products: 26.7 us -> 5.43 us
  Pallas kernels: 0 us -> 16.6 us
  starting transfers between devices: 42.7 us -> 27.8 us
  blocking collectives: 40.1 us -> 53.3 us
  local copies, waits for them, and re-layouts: 15.3 us -> 9.63 us
    ppermute x12, waiting for transfers between devices: 64.1 us -> 32.4 us  [the longest x6 32.4 us: swap(): lax.ppermute(near, 'sub', neighbour_pairs(size, 0))]
    dot_general x21 -> x0, matrix products: 19.8 us -> none  [the longest x6 7.85 us: panel_apply(): lax.dot_general(low, panel, dims, preferred_element_type=jnp.float32)]
    pallas_call x0 -> x10, Pallas kernels: none -> 16.6 us  [call(): pl.pallas_call(kernel, out_shape=[jax.ShapeDtypeStruct(shape, jnp.float32...]
    all_to_all x1 -> x2, blocking collectives: 12.7 us -> 27.1 us  [from_all(): return lax.all_to_all(copies, ('sub', 'grp'), 0, 0)]
    ppermute x12, starting transfers between devices: 25.2 us -> 15 us  [the longest x6 11 us: swap(): lax.ppermute(near, 'sub', neighbour_pairs(size, 0))]
    sub x4 -> x0, other arithmetic: 8.14 us -> none  [the longest x2 5.87 us: local(): precond = precond - expand(alpha) * step_precond]
    all_to_all x2 -> x1, waiting for transfers between devices: 0.01 us -> 7.38 us  [from_all(): return lax.all_to_all(copies, ('sub', 'grp'), 0, 0)]
    broadcast_in_dim x7 -> x0, other arithmetic: 6.58 us -> none  [the longest x1 4.31 us: local(): return (multipliers[None], residual[1:][None])]
  transfers between devices with their start and end apart: 18 -> 17, of which waited for: 8 -> 6; matrix products, arithmetic and copies ran while one was open for 8% -> 4% of each run, Pallas kernels for 0% -> 0%
where the time goes in v2:
time: 160 us; the launch traced here: 159 us
  blocking collectives  53.3 us (33%)
  waiting for transfers between devices  45 us (28%)
  starting transfers between devices  27.8 us (17%)
  Pallas kernels  16.6 us (10%)
  local copies, waits for them, and re-layouts  9.63 us (6%)
  matrix products  5.43 us (3%)
    ppermute x6, waiting for transfers between devices, swap(): lax.ppermute(near, 'sub', neighbour_pairs(size, 0))  32.4 us
    all_to_all x2, blocking collectives, from_all(): return lax.all_to_all(copies, ('sub', 'grp'), 0, 0)  27.1 us
    all_gather x3, blocking collectives, local(): everyone = lax.all_gather(values, 'grp', tiled=True)  20.2 us
    pallas_call x10, Pallas kernels, call(): pl.pallas_call(kernel, out_shape=[jax.ShapeDtypeStruct(shape, jnp.float32...  16.6 us
    ppermute x6, starting transfers between devices, swap(): lax.ppermute(near, 'sub', neighbour_pairs(size, 0))  11 us
    all_to_all x1, waiting for transfers between devices, from_all(): return lax.all_to_all(copies, ('sub', 'grp'), 0, 0)  7.38 us
    unnamed x35, local copies, waits for them, and re-layouts  6.84 us
    all_to_all x1, starting transfers between devices, from_all(): return lax.all_to_all(copies, ('sub', 'grp'), 0, 0)  6.33 us
  transfers between devices with their start and end apart: 17, of which 6 were waited for; matrix products, arithmetic and copies ran while one was open for 4% of the time, Pallas kernels for 0%

profile of v2, /device:TPU:0, one launch (start us, length us, event | category | flops | bytes accessed | tf_op | source)
XLA Modules:
  0.0 159.4 jit_solution(9717539783249444063)
XLA Ops:
  0.6 0.0 copy-start
  0.7 0.8 reshape.152
  1.5 6.0 %all-gather = s32[4,1,128]{2,1,0:T(1,128)S(1)} all-gather(s32[1,1,128]{2,1,0:T(1,128)S(1)} %reshape.152), channel_id=1, replica_groups=mesh['sub'=8,'grp'=4] {'grp'}, dimensions={0}, use_global_device_ids=true | all-gather | bytes 2560 | tf_op jit(solution)/shard_map/all_gather | solution.py:206
  7.5 1.0 fusion.3
  8.5 0.1 fusion.28
  8.6 1.0 fusion.13
  9.6 0.3 collective-permute-start.3
  9.9 1.0 fusion.11
  10.9 2.0 %collective-permute-start.4 = (f32[128,512]{1,0:T(8,128)}, f32[128,512]{1,0:T(8,128)}, u32[]{:S(2)}, u32[]{:S(2)}) collective-permute-start(f32[128,512]{1,0:T(8,128)} %fusion.11), channel_id=1, source_target_pairs={{0,2},{1,3},{2,0},{3,1},{4,6},{5,7},{6,4},{7,5},{8,10},{9,11},{10,... | collective-permute-start | bytes 786440 | tf_op jit(solution)/shard_map/ppermute | solution.py:219
  13.0 1.0 fusion.9
  14.0 0.1 fusion.26
  14.1 0.1 bitcast_multiply_fusion
  14.2 1.0 copy-done.12
  15.3 4.1 %collective-permute-start = (f32[264,256]{1,0:T(8,128)S(1)}, f32[264,256]{1,0:T(8,128)}, u32[]{:S(2)}, u32[]{:S(2)}) collective-permute-start(f32[264,256]{1,0:T(8,128)S(1)} %pad_maximum_fusion.2), channel_id=1, source_target_pairs={{0,4},{4,8},{8,12},{12,16},{16,20},{20,24},{24,28},{1,5},{5,9},{9,... | collective-permute-start | bytes 811016 | tf_op jit(solution)/shard_map/ppermute | solution.py:236
  19.4 0.1 broadcast_in_dim.112
  19.5 0.1 broadcast_in_dim.113
  19.6 0.1 bitcast_select_fusion.1
  19.8 0.1 pad_maximum_fusion.lift
  19.9 0.0 copy-start.13
  19.9 0.4 collective-permute-done.4
  20.4 4.8 %collective-permute-done.5 = f32[128,512]{1,0:T(8,128)} collective-permute-done((f32[128,512]{1,0:T(8,128)}, f32[128,512]{1,0:T(8,128)}, u32[]{:S(2)}, u32[]{:S(2)}) %collective-permute-start.5) | collective-permute-done | bytes 262176 | tf_op jit(solution)/shard_map/ppermute | solution.py:219
  25.2 1.4 reduce-precision_convert_fusion
  26.6 0.0 copy-start.5
  26.6 1.1 slice_bitcast_fusion
  27.7 0.1 pad_maximum_fusion.1.edges.residual.image_old
  27.8 0.4 copy-done.5
  28.3 1.3 shard_map.86
  29.6 1.5 collective-permute-start.1
  31.0 0.7 collective-permute-start.2
  31.7 0.7 fusion.27
  32.4 10.8 %collective-permute-done.1.near = f32[256,256]{1,0:T(8,128)S(1)} collective-permute-done((f32[256,256]{1,0:T(8,128)S(1)}, f32[256,256]{1,0:T(8,128)S(1)}, u32[]{:S(2)}, u32[]{:S(2)}) %collective-permute-start.1) | collective-permute-done | bytes 262176 | tf_op jit(solution)/shard_map/ppermute | solution.py:191
  43.2 0.8 shard_map.87
  44.0 0.0 copy-start.8
  44.0 7.2 %all_gather.12.everyone = f32[512,256]{1,0:T(8,128)S(1)} all-gather(f32[128,256]{1,0:T(8,128)S(1)} %get-tuple-element.41), channel_id=1, replica_groups=mesh['sub'=8,'grp'=4] {'grp'}, dimensions={0}, use_global_device_ids=true | all-gather | bytes 655360 | tf_op jit(solution)/shard_map/all_gather | solution.py:266
  51.2 3.1 %shard_map.88 = (f32[4,256,512]{2,1,0:T(8,128)S(1)}, f32[256,256]{1,0:T(8,128)}, f32[256,256]{1,0:T(8,128)}, f32[2,256]{1,0:T(2,128)S(1)}) custom-call(s32[1]{0:T(128)} %bitcast.even_ref, f32[5,256,256]{2,1,0:T(8,128)S(1)} %get-tuple-element.40.edges.first, f32[5,256,256]{2,1,0:T(8,128)S(1)} %pad_maximum_fusion.1.edges.residual.image_old, ...), custom_call_target="tpu_custom_call" | custom-call | tf_op jit(solution)/shard_map/pallas_call | solution.py:38
  54.3 1.3 copy-done.10
  55.6 2.5 %collective-permute-start.6 = (f32[256,256]{1,0:T(8,128)}, f32[256,256]{1,0:T(8,128)S(1)}, u32[]{:S(2)}, u32[]{:S(2)}) collective-permute-start(f32[256,256]{1,0:T(8,128)} %get-tuple-element.43), channel_id=1, source_target_pairs={{0,4},{4,0},{8,12},{12,8},{16,20},{20,16},{24,28},{28,24},{1,5},{5... | collective-permute-start | bytes 786440 | tf_op jit(solution)/shard_map/ppermute | solution.py:191
  58.1 0.7 collective-permute-start.7
  58.8 0.6 broadcast_in_dim.121
  59.4 6.3 %all-to-all-start = ((f32[32,2,256]{2,1,0:T(2,128)}), f32[32,2,256]{2,1,0:T(2,128)S(1)}, u32[]{:S(2)}, u32[]{:S(2)}) async-start(f32[32,2,256]{2,1,0:T(2,128)} %broadcast_in_dim.121), calls=%async_computation | async-start | bytes 131072 | tf_op jit(solution)/shard_map/all_to_all | solution.py:199
  65.8 7.4 %all-to-all-done.sums = f32[32,2,256]{2,1,0:T(2,128)S(1)} async-done(((f32[32,2,256]{2,1,0:T(2,128)}), f32[32,2,256]{2,1,0:T(2,128)S(1)}, u32[]{:S(2)}, u32[]{:S(2)}) %all-to-all-start) | async-done | bytes 65568 | tf_op jit(solution)/shard_map/all_to_all | solution.py:199
  73.2 1.6 copy-done.6
  74.8 1.6 copy-done.11
  76.4 1.6 shard_map.89
  78.0 0.7 collective-permute-start.8
  78.7 0.7 collective-permute-start.9
  79.3 10.8 %collective-permute-done.8.near = f32[256,256]{1,0:T(8,128)S(1)} collective-permute-done((f32[256,256]{1,0:T(8,128)S(1)}, f32[256,256]{1,0:T(8,128)S(1)}, u32[]{:S(2)}, u32[]{:S(2)}) %collective-permute-start.8) | collective-permute-done | bytes 262176 | tf_op jit(solution)/shard_map/ppermute | solution.py:191
  90.1 0.8 shard_map.90
  90.9 6.5 %all_gather.14.everyone = f32[512,256]{1,0:T(8,128)S(1)} all-gather(f32[128,256]{1,0:T(8,128)S(1)} %get-tuple-element.51), channel_id=1, replica_groups=mesh['sub'=8,'grp'=4] {'grp'}, dimensions={0}, use_global_device_ids=true | all-gather | bytes 655360 | tf_op jit(solution)/shard_map/all_gather | solution.py:266
  97.4 2.5 %shard_map.91 = (f32[4,256,512]{2,1,0:T(8,128)S(1)}, f32[256,256]{1,0:T(8,128)S(1)}, f32[256,256]{1,0:T(8,128)S(1)}, f32[2,256]{1,0:T(2,128)S(1)}) custom-call(s32[1]{0:T(128)} %bitcast.even_ref, f32[5,256,256]{2,1,0:T(8,128)S(1)} %get-tuple-element.49.edges.second, f32[5,256,256]{2,1,0:T(8,128)S(1)} %get-tuple-element.50.residual, ...), custom_call_target="tpu_custom_call" | custom-call | tf_op jit(solution)/shard_map/pallas_call | solution.py:38
  99.9 2.5 %collective-permute-start.10 = (f32[256,256]{1,0:T(8,128)S(1)}, f32[256,256]{1,0:T(8,128)S(1)}, u32[]{:S(2)}, u32[]{:S(2)}) collective-permute-start(f32[256,256]{1,0:T(8,128)S(1)} %get-tuple-element.53), channel_id=1, source_target_pairs={{0,4},{4,0},{8,12},{12,8},{16,20},{20,16},{24,28},{28,24},{1,5},{5... | collective-permute-start | bytes 786440 | tf_op jit(solution)/shard_map/ppermute | solution.py:191
  102.4 0.7 collective-permute-start.11
  103.1 13.5 %all_to_all.15.sums = f32[32,2,256]{2,1,0:T(2,128)S(1)} all-to-all(f32[32,2,256]{2,1,0:T(2,128)S(1)} %broadcast_in_dim.123), channel_id=1, replica_groups=mesh['sub'=8,'grp'=4] {'sub','grp'}, dimensions={0} | all-to-all | bytes 131072 | tf_op jit(solution)/shard_map/all_to_all | solution.py:199
  116.6 1.7 %shard_map.92 = (f32[5,256,256]{2,1,0:T(8,128)S(1)}, f32[5,256,256]{2,1,0:T(8,128)S(1)}, f32[4,256,512]{2,1,0:T(8,128)S(1)}, f32[256,256]{1,0:T(8,128)S(1)}, f32...) custom-call(s32[1]{0:T(128)} %bitcast.even_ref, f32[4,256,512]{2,1,0:T(8,128)S(1)} %get-tuple-element.52.result, ...), custom_call_target="tpu_custom_call" | custom-call | tf_op jit(solution)/shard_map/pallas_call | solution.py:38
  118.3 1.3 collective-permute-start.12
  119.6 0.7 collective-permute-start.13
  120.3 10.8 %collective-permute-done.12.near = f32[256,256]{1,0:T(8,128)S(1)} collective-permute-done((f32[256,256]{1,0:T(8,128)S(1)}, f32[256,256]{1,0:T(8,128)S(1)}, u32[]{:S(2)}, u32[]{:S(2)}) %collective-permute-start.12) | collective-permute-done | bytes 262176 | tf_op jit(solution)/shard_map/ppermute | solution.py:191
  131.1 0.8 shard_map.93
  131.8 6.5 %all_gather.15.everyone = f32[512,256]{1,0:T(8,128)S(1)} all-gather(f32[128,256]{1,0:T(8,128)S(1)} %get-tuple-element.63), channel_id=1, replica_groups=mesh['sub'=8,'grp'=4] {'grp'}, dimensions={0}, use_global_device_ids=true | all-gather | bytes 655360 | tf_op jit(solution)/shard_map/all_gather | solution.py:266
  138.4 2.5 %shard_map.94 = (f32[4,256,512]{2,1,0:T(8,128)S(1)}, f32[256,256]{1,0:T(8,128)S(1)}, f32[256,256]{1,0:T(8,128)S(1)}, f32[2,256]{1,0:T(2,128)S(1)}) custom-call(s32[1]{0:T(128)} %bitcast.even_ref, f32[5,256,256]{2,1,0:T(8,128)S(1)} %get-tuple-element.61.edges.third, f32[5,256,256]{2,1,0:T(8,128)S(1)} %get-tuple-element.62.residual, ...), custom_call_target="tpu_custom_call" | custom-call | tf_op jit(solution)/shard_map/pallas_call | solution.py:38
  140.8 2.5 %collective-permute-start.14 = (f32[256,256]{1,0:T(8,128)S(1)}, f32[256,256]{1,0:T(8,128)S(1)}, u32[]{:S(2)}, u32[]{:S(2)}) collective-permute-start(f32[256,256]{1,0:T(8,128)S(1)} %get-tuple-element.65), channel_id=1, source_target_pairs={{0,4},{4,0},{8,12},{12,8},{16,20},{20,16},{24,28},{28,24},{1,5},{5... | collective-permute-start | bytes 786440 | tf_op jit(solution)/shard_map/ppermute | solution.py:191
  143.3 0.7 collective-permute-start.15
  144.0 13.5 %all_to_all.16.sums = f32[32,2,256]{2,1,0:T(2,128)S(1)} all-to-all(f32[32,2,256]{2,1,0:T(2,128)S(1)} %broadcast_in_dim.124), channel_id=1, replica_groups=mesh['sub'=8,'grp'=4] {'sub','grp'}, dimensions={0} | all-to-all | bytes 131072 | tf_op jit(solution)/shard_map/all_to_all | solution.py:199
  157.6 1.8 %shard_map.95 = (f32[4,256,256]{2,1,0:T(8,128)}, f32[4,256,256]{2,1,0:T(8,128)}) custom-call(s32[1]{0:T(128)} %bitcast.even_ref, f32[4,256,512]{2,1,0:T(8,128)S(1)} %get-tuple-element.64.result, f32[256,256]{1,0:T(8,128)S(1)} %collective-permute-done.14.near, f32[256,256]{1,0:T(8,128)S(1)} %collective-permute-done.15.far, ...), custom_call_target="tpu_custom_call" | custom-call | tf_op jit(solution)/shard_map/pallas_call | solution.py:38
  (54 shorter events, 0.3 us)
Async XLA Ops:
  0.6 6.9 %copy-start = (f32[1,256,1024]{2,1,0:T(8,128)S(1)}, f32[1,256,1024]{2,1,0:T(8,128)}, u32[]{:S(2)}) copy-start(f32[1,256,1024]{2,1,0:T(8,128)} %param.13) | copy-start | bytes 3145732
  8.5 5.5 %copy-start.16 = (s32[1,4]{1,0:T(1,128)S(1)}, s32[1,4]{1,0:T(1,128)}, u32[]{:S(2)}) copy-start(s32[1,4]{1,0:T(1,128)} %param.8) | copy-start | bytes 52
  8.5 5.6 %copy-start.14 = (f32[1,4,256,256]{3,2,1,0:T(8,128)S(1)}, f32[1,4,256,256]{3,2,1,0:T(8,128)}, u32[]{:S(2)}) copy-start(f32[1,4,256,256]{3,2,1,0:T(8,128)} %param.7) | copy-start | bytes 3145732
  9.6 10.3 %collective-permute-start.3 = (f32[128,512]{1,0:T(8,128)}, f32[128,512]{1,0:T(8,128)S(1)}, u32[]{:S(2)}, u32[]{:S(2)}) collective-permute-start(f32[128,512]{1,0:T(8,128)} %fusion.13), channel_id=1, source_target_pairs={{0,1},{1,0},{2,3},{3,2},{4,5},{5,4},{6,7},{7,6},{8,9},{9,8},{10,11... | collective-permute-start | bytes 786440 | tf_op jit(solution)/shard_map/ppermute | solution.py:219
  10.9 9.4 %collective-permute-start.4 = (f32[128,512]{1,0:T(8,128)}, f32[128,512]{1,0:T(8,128)}, u32[]{:S(2)}, u32[]{:S(2)}) collective-permute-start(f32[128,512]{1,0:T(8,128)} %fusion.11), channel_id=1, source_target_pairs={{0,2},{1,3},{2,0},{3,1},{4,6},{5,7},{6,4},{7,5},{8,10},{9,11},{10,... | collective-permute-start | bytes 786440 | tf_op jit(solution)/shard_map/ppermute | solution.py:219
  14.0 11.2 %collective-permute-start.5 = (f32[128,512]{1,0:T(8,128)}, f32[128,512]{1,0:T(8,128)}, u32[]{:S(2)}, u32[]{:S(2)}) collective-permute-start(f32[128,512]{1,0:T(8,128)} %fusion.9), channel_id=1, source_target_pairs={{0,3},{1,2},{2,1},{3,0},{4,7},{5,6},{6,5},{7,4},{8,11},{9,10},{10,... | collective-permute-start | bytes 786440 | tf_op jit(solution)/shard_map/ppermute | solution.py:219
  14.1 5.5 %copy-start.15 = (f32[1,4,32,512]{3,2,1,0:T(8,128)S(1)}, f32[1,4,32,512]{3,2,1,0:T(8,128)}, u32[]{:S(2)}) copy-start(f32[1,4,32,512]{3,2,1,0:T(8,128)} %param.11) | copy-start | bytes 786436
  14.2 1.0 copy-start.12
  15.3 11.3 %collective-permute-start = (f32[264,256]{1,0:T(8,128)S(1)}, f32[264,256]{1,0:T(8,128)}, u32[]{:S(2)}, u32[]{:S(2)}) collective-permute-start(f32[264,256]{1,0:T(8,128)S(1)} %pad_maximum_fusion.2), channel_id=1, source_target_pairs={{0,4},{4,8},{8,12},{12,16},{16,20},{20,24},{24,28},{1,5},{5,9},{9,... | collective-permute-start | bytes 811016 | tf_op jit(solution)/shard_map/ppermute | solution.py:236
  19.9 31.3 %copy-start.1 = (bf16[4,384,512]{2,1,0:T(8,128)(2,1)}, bf16[4,384,512]{2,1,0:T(8,128)(2,1)S(1)}, u32[]{:S(2)}) copy-start(bf16[4,384,512]{2,1,0:T(8,128)(2,1)S(1)} %pad_maximum_fusion.lift) | copy-start | bytes 4718596
  19.9 7.8 %copy-start.13 = (f32[4,256,256]{2,1,0:T(8,128)S(1)}, f32[4,256,256]{2,1,0:T(8,128)}, u32[]{:S(2)}) copy-start(f32[4,256,256]{2,1,0:T(8,128)} %copy-done.12) | copy-start | bytes 3145732
  26.6 1.7 %copy-start.5 = (bf16[1,4,512,512]{3,2,1,0:T(8,128)(2,1)S(1)}, bf16[1,4,512,512]{3,2,1,0:T(8,128)(2,1)}, u32[]{:S(2)}) copy-start(bf16[1,4,512,512]{3,2,1,0:T(8,128)(2,1)} %param.10) | copy-start | bytes 6291460
  29.6 13.7 %collective-permute-start.1 = (f32[256,256]{1,0:T(8,128)S(1)}, f32[256,256]{1,0:T(8,128)S(1)}, u32[]{:S(2)}, u32[]{:S(2)}) collective-permute-start(f32[256,256]{1,0:T(8,128)S(1)} %get-tuple-element.38), channel_id=1, source_target_pairs={{0,4},{4,0},{8,12},{12,8},{16,20},{20,16},{24,28},{28,24},{1,5},{5... | collective-permute-start | bytes 786440 | tf_op jit(solution)/shard_map/ppermute | solution.py:191
  31.0 12.2 %collective-permute-start.2 = (f32[256,256]{1,0:T(8,128)S(1)}, f32[256,256]{1,0:T(8,128)S(1)}, u32[]{:S(2)}, u32[]{:S(2)}) collective-permute-start(f32[256,256]{1,0:T(8,128)S(1)} %get-tuple-element.39), channel_id=1, source_target_pairs={{4,8},{8,4},{12,16},{16,12},{20,24},{24,20},{5,9},{9,5},{13,17},{1... | collective-permute-start | bytes 786440 | tf_op jit(solution)/shard_map/ppermute | solution.py:192
  43.2 8.0 %copy-start.3 = (bf16[1,4,512,512]{3,2,1,0:T(8,128)(2,1)S(1)}, bf16[1,4,512,512]{3,2,1,0:T(8,128)(2,1)}, u32[]{:S(2)}) copy-start(bf16[1,4,512,512]{3,2,1,0:T(8,128)(2,1)} %param.9) | copy-start | bytes 6291460
  44.0 10.3 %copy-start.8 = (f32[5,256,256]{2,1,0:T(8,128)}, f32[5,256,256]{2,1,0:T(8,128)S(1)}, u32[]{:S(2)}) copy-start(f32[5,256,256]{2,1,0:T(8,128)S(1)} %get-tuple-element.40.edges.first) | copy-start | bytes 3932164
  54.3 1.3 copy-start.10
  55.6 17.6 %collective-permute-start.6 = (f32[256,256]{1,0:T(8,128)}, f32[256,256]{1,0:T(8,128)S(1)}, u32[]{:S(2)}, u32[]{:S(2)}) collective-permute-start(f32[256,256]{1,0:T(8,128)} %get-tuple-element.43), channel_id=1, source_target_pairs={{0,4},{4,0},{8,12},{12,8},{16,20},{20,16},{24,28},{28,24},{1,5},{5... | collective-permute-start | bytes 786440 | tf_op jit(solution)/shard_map/ppermute | solution.py:191
  58.1 15.1 %collective-permute-start.7 = (f32[256,256]{1,0:T(8,128)}, f32[256,256]{1,0:T(8,128)S(1)}, u32[]{:S(2)}, u32[]{:S(2)}) collective-permute-start(f32[256,256]{1,0:T(8,128)} %get-tuple-element.44), channel_id=1, source_target_pairs={{4,8},{8,4},{12,16},{16,12},{20,24},{24,20},{5,9},{9,5},{13,17},{1... | collective-permute-start | bytes 786440 | tf_op jit(solution)/shard_map/ppermute | solution.py:192
  59.4 13.8 %all-to-all-start = ((f32[32,2,256]{2,1,0:T(2,128)}), f32[32,2,256]{2,1,0:T(2,128)S(1)}, u32[]{:S(2)}, u32[]{:S(2)}) async-start(f32[32,2,256]{2,1,0:T(2,128)} %broadcast_in_dim.121), calls=%async_computation | async-start | bytes 131072 | tf_op jit(solution)/shard_map/all_to_all | solution.py:199
  73.2 1.6 %copy-start.6 = (bf16[1,4,512,512]{3,2,1,0:T(8,128)(2,1)S(1)}, bf16[1,4,512,512]{3,2,1,0:T(8,128)(2,1)}, u32[]{:S(2)}) copy-start(bf16[1,4,512,512]{3,2,1,0:T(8,128)(2,1)} %param.10) | copy-start | bytes 6291460
  74.8 1.6 copy-start.11
  76.4 21.0 %copy-start.4 = (bf16[1,4,512,512]{3,2,1,0:T(8,128)(2,1)S(1)}, bf16[1,4,512,512]{3,2,1,0:T(8,128)(2,1)}, u32[]{:S(2)}) copy-start(bf16[1,4,512,512]{3,2,1,0:T(8,128)(2,1)} %param.9) | copy-start | bytes 6291460
  78.0 12.2 %collective-permute-start.8 = (f32[256,256]{1,0:T(8,128)S(1)}, f32[256,256]{1,0:T(8,128)S(1)}, u32[]{:S(2)}, u32[]{:S(2)}) collective-permute-start(f32[256,256]{1,0:T(8,128)S(1)} %get-tuple-element.47), channel_id=1, source_target_pairs={{0,4},{4,0},{8,12},{12,8},{16,20},{20,16},{24,28},{28,24},{1,5},{5... | collective-permute-start | bytes 786440 | tf_op jit(solution)/shard_map/ppermute | solution.py:191
  78.7 11.5 %collective-permute-start.9 = (f32[256,256]{1,0:T(8,128)S(1)}, f32[256,256]{1,0:T(8,128)S(1)}, u32[]{:S(2)}, u32[]{:S(2)}) collective-permute-start(f32[256,256]{1,0:T(8,128)S(1)} %get-tuple-element.48), channel_id=1, source_target_pairs={{4,8},{8,4},{12,16},{16,12},{20,24},{24,20},{5,9},{9,5},{13,17},{1... | collective-permute-start | bytes 786440 | tf_op jit(solution)/shard_map/ppermute | solution.py:192
  90.1 7.3 %copy-start.2 = (bf16[4,384,512]{2,1,0:T(8,128)(2,1)S(1)}, bf16[4,384,512]{2,1,0:T(8,128)(2,1)}, u32[]{:S(2)}) copy-start(bf16[4,384,512]{2,1,0:T(8,128)(2,1)} %copy-done.1) | copy-start | bytes 4718596
  97.4 19.2 %copy-start.7 = (bf16[1,4,512,512]{3,2,1,0:T(8,128)(2,1)S(1)}, bf16[1,4,512,512]{3,2,1,0:T(8,128)(2,1)}, u32[]{:S(2)}) copy-start(bf16[1,4,512,512]{3,2,1,0:T(8,128)(2,1)} %param.10) | copy-start | bytes 6291460
  99.9 16.8 %collective-permute-start.10 = (f32[256,256]{1,0:T(8,128)S(1)}, f32[256,256]{1,0:T(8,128)S(1)}, u32[]{:S(2)}, u32[]{:S(2)}) collective-permute-start(f32[256,256]{1,0:T(8,128)S(1)} %get-tuple-element.53), channel_id=1, source_target_pairs={{0,4},{4,0},{8,12},{12,8},{16,20},{20,16},{24,28},{28,24},{1,5},{5... | collective-permute-start | bytes 786440 | tf_op jit(solution)/shard_map/ppermute | solution.py:191
  102.4 14.2 %collective-permute-start.11 = (f32[256,256]{1,0:T(8,128)S(1)}, f32[256,256]{1,0:T(8,128)S(1)}, u32[]{:S(2)}, u32[]{:S(2)}) collective-permute-start(f32[256,256]{1,0:T(8,128)S(1)} %get-tuple-element.54), channel_id=1, source_target_pairs={{4,8},{8,4},{12,16},{16,12},{20,24},{24,20},{5,9},{9,5},{13,17},{1... | collective-permute-start | bytes 786440 | tf_op jit(solution)/shard_map/ppermute | solution.py:192
  118.3 12.7 %collective-permute-start.12 = (f32[256,256]{1,0:T(8,128)S(1)}, f32[256,256]{1,0:T(8,128)S(1)}, u32[]{:S(2)}, u32[]{:S(2)}) collective-permute-start(f32[256,256]{1,0:T(8,128)S(1)} %get-tuple-element.59), channel_id=1, source_target_pairs={{0,4},{4,0},{8,12},{12,8},{16,20},{20,16},{24,28},{28,24},{1,5},{5... | collective-permute-start | bytes 786440 | tf_op jit(solution)/shard_map/ppermute | solution.py:191
  119.6 11.5 %collective-permute-start.13 = (f32[256,256]{1,0:T(8,128)S(1)}, f32[256,256]{1,0:T(8,128)S(1)}, u32[]{:S(2)}, u32[]{:S(2)}) collective-permute-start(f32[256,256]{1,0:T(8,128)S(1)} %get-tuple-element.60), channel_id=1, source_target_pairs={{4,8},{8,4},{12,16},{16,12},{20,24},{24,20},{5,9},{9,5},{13,17},{1... | collective-permute-start | bytes 786440 | tf_op jit(solution)/shard_map/ppermute | solution.py:192
  138.4 19.2 %copy-start.9 = (f32[5,256,256]{2,1,0:T(8,128)S(1)}, f32[5,256,256]{2,1,0:T(8,128)}, u32[]{:S(2)}) copy-start(f32[5,256,256]{2,1,0:T(8,128)} %copy-done.8) | copy-start | bytes 3932164
  140.8 16.8 %collective-permute-start.14 = (f32[256,256]{1,0:T(8,128)S(1)}, f32[256,256]{1,0:T(8,128)S(1)}, u32[]{:S(2)}, u32[]{:S(2)}) collective-permute-start(f32[256,256]{1,0:T(8,128)S(1)} %get-tuple-element.65), channel_id=1, source_target_pairs={{0,4},{4,0},{8,12},{12,8},{16,20},{20,16},{24,28},{28,24},{1,5},{5... | collective-permute-start | bytes 786440 | tf_op jit(solution)/shard_map/ppermute | solution.py:191
  143.3 14.2 %collective-permute-start.15 = (f32[256,256]{1,0:T(8,128)S(1)}, f32[256,256]{1,0:T(8,128)S(1)}, u32[]{:S(2)}, u32[]{:S(2)}) collective-permute-start(f32[256,256]{1,0:T(8,128)S(1)} %get-tuple-element.66), channel_id=1, source_target_pairs={{4,8},{8,4},{12,16},{16,12},{20,24},{24,20},{5,9},{9,5},{13,17},{1... | collective-permute-start | bytes 786440 | tf_op jit(solution)/shard_map/ppermute | solution.py:192

commit v3 on v2

--- a/solution.py
+++ b/solution.py
@@ -11,7 +11,7 @@
 
 
 HIGH = lax.Precision.HIGH
-VMEM_LIMIT = 32 * 1024 * 1024
+VMEM_LIMIT = 8 * 1024 * 1024
 
 
 def split(values):
@@ -33,8 +33,7 @@
     return lax.dot_general(first, second, dims, preferred_element_type=jnp.float32)
 
 
-def call(kernel, out_shapes, *operands):
-    scalars = 1
+def call(kernel, out_shapes, *operands, scalars=1):
     return pl.pallas_call(
         kernel,
         out_shape=[jax.ShapeDtypeStruct(shape, jnp.float32) for shape in out_shapes],
@@ -98,9 +97,39 @@
     return rz_now, rz_now / (curvature - beta * rz_now / before[1:2]), beta
 
 
-def first_kernel(even_ref, edges, panel, result, near_out, far_out):
+def first_kernel(even_ref, counts, rhs, head, panel, edges, live, result, near_out, far_out):
+    subs, loads, width = rhs.shape
+    positions = lax.broadcasted_iota(jnp.int32, (1, width), 1)
+    live[0] = head[loads : loads + 1]
+    edges[0] = head[:loads]
+    for sub in range(subs):
+        mask = (positions < counts[sub]).astype(jnp.float32)
+        live[sub + 1] = mask
+        edges[sub + 1] = mask * rhs[sub]
     panel_products(edges, panel, result)
     send_faces(even_ref[0] == 1, result, near_out, far_out)
+
+
+def pick_kernel(grp_ref, everyone, coarse, picked):
+    group, own = everyone.shape[0], everyone.shape[2]
+    rows, size = coarse.shape
+    grp = grp_ref[0]
+    high, rest = split(coarse[...])
+    middle, low = split(coarse[...] - high.astype(jnp.float32))
+    unknowns = lax.broadcasted_iota(jnp.int32, (size, own), 0)
+    columns = []
+    for member in range(group):
+        chosen = (unknowns == everyone[member]).astype(jnp.bfloat16)
+        columns.append(mul(high, chosen) + mul(middle, chosen) + mul(low, chosen))
+    high, rest = split(jnp.concatenate(columns, axis=1))
+    low = rest
+    owned = lax.broadcasted_iota(jnp.int32, (rows, own), 0) + grp * rows
+    dims = (((0,), (0,)), ((), ()))
+    for distance in range(group):
+        chosen = (owned == everyone[grp ^ distance]).astype(jnp.bfloat16)
+        picked[distance] = lax.dot_general(
+            chosen, high, dims, preferred_element_type=jnp.float32
+        ) + lax.dot_general(chosen, low, dims, preferred_element_type=jnp.float32)
 
 
 def corner_kernel(even_ref, result, near, far, live, coupling, edges, corners):
@@ -108,7 +137,7 @@
     width = result.shape[2] // 2
     subs, rows = coupling.shape[0], coupling.shape[1] // 2
     for edge, value in jump_edges(even, result, near, far, live):
-        edges[edge] = value
+        edges[edge] = 0.25 * value
     parts = [split(edges[edge]) for edge in range(subs + 1)]
     for sub in range(subs):
         high = jnp.concatenate([-parts[sub][0], parts[sub + 1][0]], axis=1)
@@ -199,24 +228,14 @@
     return lax.all_to_all(copies, ("sub", "grp"), 0, 0)
 
 
-def coarse_block(corner_map, coarse_inverse):
-    rows, size = coarse_inverse.shape
-    own = corner_map.size
-    grp, group = lax.axis_index("grp"), lax.axis_size("grp")
-    everyone = lax.all_gather(corner_map.reshape(own), "grp", tiled=True)
-    columns = (everyone[None, :] == jnp.arange(size, dtype=jnp.int32)[:, None]).astype(jnp.float32)
-    picked = jnp.dot(coarse_inverse, columns, precision=HIGH)
-    owned = jnp.arange(rows, dtype=jnp.int32) + grp * rows
-
-    def rows_for(member):
-        wanted = lax.dynamic_slice_in_dim(everyone, member * own, own)
-        chosen = (wanted[:, None] == owned[None, :]).astype(jnp.float32)
-        return jnp.dot(chosen, picked, precision=HIGH)
-
-    block = rows_for(grp)
+def coarse_block(everyone, coarse_inverse):
+    group, own = everyone.shape[0], everyone.shape[2]
+    grp = lax.axis_index("grp").reshape(1)
+    (picked,) = call(pick_kernel, [(group, own, group * own)], grp, everyone, coarse_inverse)
+    block = picked[0]
     for distance in range(1, group):
         routes = [(i, i ^ distance) for i in range(group)]
-        block = block + lax.ppermute(rows_for(grp ^ distance), "grp", routes)
+        block = block + lax.ppermute(picked[distance], "grp", routes)
     return block
 
 
@@ -227,40 +246,45 @@
     place, size = lax.axis_index("sub"), lax.axis_size("sub")
     even = (1 - place % 2).astype(jnp.int32).reshape(1)
     slots = jnp.arange(subs, dtype=jnp.int32)
+    live_counts = jnp.where((place == size - 1) & (slots == subs - 1), 0, counts[0])
     positions = jnp.arange(width, dtype=jnp.int32)
-    not_last = jnp.logical_not((place == size - 1) & (slots == subs - 1))
-    live = ((positions[None, :] < counts[0][:, None]) & not_last[:, None]).astype(jnp.float32)
-    residual = live[:, None, :] * rhs[0]
-
-    tail = jnp.concatenate([residual[-1], jnp.broadcast_to(live[-1:], (8, width))], axis=0)
+    last_live = (positions < live_counts[-1]).astype(jnp.float32)
+    tail = jnp.concatenate(
+        [last_live * rhs[0, -1], jnp.broadcast_to(last_live, (8, width))], axis=0
+    )
+    tail, corner_map = lax.optimization_barrier((tail, corner_map))
     head = lax.ppermute(tail, "sub", [(i, i + 1) for i in range(size - 1)])
-    residual = jnp.concatenate([head[None, :loads], residual], axis=0)
-    live = jnp.concatenate([head[loads : loads + 1], live], axis=0)[:, None, :]
-
-    block = jnp.concatenate(split_outside(coarse_block(corner_map[0], coarse_inverse[0])), axis=0)
-    high, low = split_outside(couple)
-    stacked = jnp.concatenate([high, low], axis=1)
-    own = (slots[:, None] == slots[None, :])[:, :, None, None]
-
-    def placed(part):
-        wide = jnp.where(own, part[:, None], jnp.zeros((), part.dtype))
-        return wide.reshape(subs, subs * corners, 2 * width)
-
-    lift = jnp.concatenate([placed(high), placed(high), placed(low)], axis=1)
+    everyone = lax.all_gather(corner_map.reshape(1, subs * corners), "grp")
 
     edges_shape = (subs + 1, loads, width)
     result_shape = (subs, loads, 2 * width)
     face_shape = (loads, width)
     faces = [result_shape, face_shape, face_shape]
 
-    result, near, far = call(first_kernel, faces, even, residual, dirichlet)
-    scalars, images, preconds, image = [jnp.zeros((2, loads), jnp.float32)], [], [], None
+    residual, live, result, near, far = call(
+        first_kernel,
+        [edges_shape, (subs + 1, 1, width)] + faces,
+        even, live_counts, rhs[0], head, dirichlet, scalars=2,
+    )
+    result, everyone, couple = lax.optimization_barrier((result, everyone, couple))
+    block = jnp.concatenate(split_outside(coarse_block(everyone, coarse_inverse[0])), axis=0)
+    high, low = split_outside(couple)
+    stacked = jnp.concatenate([high, low], axis=1)
+    own = (slots[:, None] == slots[None, :])[:, :, None, None]
+
+    def placed(part):
+        wide = jnp.where(own, part[:, None], jnp.zeros((), part.dtype))
+        return wide.reshape(subs, subs * corners, 2 * width)
+
+    lift = jnp.concatenate([placed(high), placed(high), placed(low)], axis=1)
+
+    scalars, preconds, image = [jnp.zeros((2, loads), jnp.float32)], [], None
     for step in range(ITERS):
         near, far = swap(near, far)
         edges, values = call(
             corner_kernel,
             [edges_shape, (subs * corners, loads)],
-            even, result, near, far, 0.25 * live, stacked,
+            even, result, near, far, live, stacked,
         )
         preconds.append(edges)
         everyone = lax.all_gather(values, "grp", tiled=True)

time: 160 us -> 148 us (0.925)
  waiting for transfers between devices: 45 us -> 27 us
  blocking collectives: 53.3 us -> 68.2 us
  matrix products: 5.43 us -> 0 us
  local copies, waits for them, and re-layouts: 9.63 us -> 4.47 us
  starting transfers between devices: 27.8 us -> 25.3 us
  other arithmetic: 0.66 us -> 2.86 us
  Pallas kernels: 16.6 us -> 18.8 us
    all_to_all x2 -> x3, blocking collectives: 27.1 us -> 40.8 us  [from_all(): return lax.all_to_all(copies, ('sub', 'grp'), 0, 0)]
    all_to_all x1 -> x0, waiting for transfers between devices: 7.38 us -> none  [from_all(): return lax.all_to_all(copies, ('sub', 'grp'), 0, 0)]
    all_to_all x1 -> x0, starting transfers between devices: 6.33 us -> none  [from_all(): return lax.all_to_all(copies, ('sub', 'grp'), 0, 0)]
    dot_general x5 -> x0, matrix products: 5.43 us -> none  [the longest x4 4.47 us: rows_for(): return jnp.dot(chosen, picked, precision=HIGH)]
    ppermute x6, waiting for transfers between devices: 32.4 us -> 27 us  [swap(): lax.ppermute(near, 'sub', neighbour_pairs(size, 0))]
    ppermute x3, waiting for transfers between devices: 5.22 us -> 0.01 us  [coarse_block(): block = block + lax.ppermute(picked[distance], 'grp', routes)]
    unnamed x35 -> x12, local copies, waits for them, and re-layouts: 6.84 us -> 2.84 us
    ppermute x6, starting transfers between devices: 11 us -> 14.3 us  [swap(): lax.ppermute(near, 'sub', neighbour_pairs(size, 0))]
  transfers between devices with their start and end apart: 17 -> 16, of which waited for: 6 -> 3; matrix products, arithmetic and copies ran while one was open for 4% -> 1% of each run, Pallas kernels for 0% -> 2%
where the time goes in v3:
time: 148 us
  blocking collectives  68.2 us (46%)
  waiting for transfers between devices  27 us (18%)
  starting transfers between devices  25.3 us (17%)
  Pallas kernels  18.8 us (13%)
  local copies, waits for them, and re-layouts  4.47 us (3%)
  other arithmetic  2.86 us (2%)
    all_to_all x3, blocking collectives, from_all(): return lax.all_to_all(copies, ('sub', 'grp'), 0, 0)  40.8 us
    ppermute x6, waiting for transfers between devices, swap(): lax.ppermute(near, 'sub', neighbour_pairs(size, 0))  27 us
    all_gather x3, blocking collectives, local(): everyone = lax.all_gather(values, 'grp', tiled=True)  22.3 us
    pallas_call x11, Pallas kernels, call(): pl.pallas_call(kernel, out_shape=[jax.ShapeDtypeStruct(shape, jnp.float32...  18.8 us
    ppermute x6, starting transfers between devices, swap(): lax.ppermute(near, 'sub', neighbour_pairs(size, 0))  14.3 us
    all_gather x1, blocking collectives, local(): everyone = lax.all_gather(corner_map.reshape(1, subs * corners), 'grp')  5.03 us
    ppermute x1, starting transfers between devices, local(): head = lax.ppermute(tail, 'sub', [(i, i + 1) for i in range(size - 1)])  4.86 us
    ppermute x6, starting transfers between devices, swap(): lax.ppermute(far, 'sub', neighbour_pairs(size, 1))  3.99 us
  transfers between devices with their start and end apart: 16, of which 3 were waited for; matrix products, arithmetic and copies ran while one was open for 1% of the time, Pallas kernels for 2%

profile of v3, /device:TPU:0, one launch (start us, length us, event | category | flops | bytes accessed | tf_op | source)
XLA Modules:
  0.0 147.6 jit_solution(4648769506287376361)
XLA Ops:
  0.6 0.7 and_select_fusion.counts
  1.3 0.6 slice.18
  1.9 0.6 compare_convert_fusion
  2.5 0.0 copy-start.4
  2.6 1.1 bitcast_multiply_fusion
  3.7 4.9 %collective-permute-start = (f32[264,256]{1,0:T(8,128)S(1)}, f32[264,256]{1,0:T(8,128)S(1)}, u32[]{:S(2)}, u32[]{:S(2)}) collective-permute-start(f32[264,256]{1,0:T(8,128)S(1)} %pad_maximum_fusion.1), channel_id=1, source_target_pairs={{0,4},{4,8},{8,12},{12,16},{16,20},{20,24},{24,28},{1,5},{5,9},{9,... | collective-permute-start | bytes 811016 | tf_op jit(solution)/shard_map/ppermute | solution.py:256
  8.5 0.1 broadcast_in_dim.93
  8.6 0.1 broadcast_in_dim.94
  8.7 0.8 all_gather_reshape.3
  9.5 5.0 %all_gather.12.everyone = s32[4,1,128]{2,1,0:T(1,128)S(1)} all-gather(s32[1,1,128]{2,1,0:T(1,128)S(1)} %all_gather_reshape.3), channel_id=1, replica_groups=mesh['sub'=8,'grp'=4] {'grp'}, dimensions={0}, use_global_device_ids=true | all-gather | bytes 2560 | tf_op jit(solution)/shard_map/all_gather | solution.py:257
  14.5 0.0 collective-permute-done.head
  14.5 1.6 %copy-done.1 = bf16[1,4,512,512]{3,2,1,0:T(8,128)(2,1)S(1)} copy-done((bf16[1,4,512,512]{3,2,1,0:T(8,128)(2,1)S(1)}, bf16[1,4,512,512]{3,2,1,0:T(8,128)(2,1)}, u32[]{:S(2)}) %copy-start.1) | copy-done | bytes 2097176
  16.1 1.2 copy-done.3
  17.3 1.8 %shard_map.86 = (f32[5,256,256]{2,1,0:T(8,128)S(1)}, f32[5,1,256]{2,1,0:T(1,128)S(1)}, f32[4,256,512]{2,1,0:T(8,128)S(1)}, f32[256,256]{1,0:T(8,128)S(1)}, f32[256,256]{1,0:T(8,128)S(1)}) custom-call(s32[1]{0:T(128)} %bitcast.even_ref, s32[4]{0:T(128)S(1)} %and_select_fusion.counts, f32[4,256,256]{2,1,0:T(8,128)S(1)} %bitcast.39, ...), custom_call_target="tpu_custom_call" | custom-call | tf_op jit(solution)/shard_map/pallas_call | solution.py:37
  19.2 2.3 %collective-permute-start.1 = (f32[256,256]{1,0:T(8,128)S(1)}, f32[256,256]{1,0:T(8,128)S(1)}, u32[]{:S(2)}, u32[]{:S(2)}) collective-permute-start(f32[256,256]{1,0:T(8,128)S(1)} %get-tuple-element.48), channel_id=1, source_target_pairs={{0,4},{4,0},{8,12},{12,8},{16,20},{20,16},{24,28},{28,24},{1,5},{5... | collective-permute-start | bytes 786440 | tf_op jit(solution)/shard_map/ppermute | solution.py:220
  21.5 0.7 collective-permute-start.2
  22.1 2.3 %shard_map.88 = f32[4,128,512]{2,1,0:T(8,128)S(1)} custom-call(s32[1]{0:T(128)} %bitcast.8.grp_ref, s32[4,1,128]{2,1,0:T(1,128)S(1)} %all_gather.12.everyone, f32[256,1024]{1,0:T(8,128)S(1)} %bitcast.40), custom_call_target="tpu_custom_call" | custom-call | tf_op jit(solution)/shard_map/pallas_call | solution.py:37
  24.4 0.1 slice_bitcast_fusion.2
  24.5 0.1 collective-permute-start.3
  24.6 1.6 %collective-permute-start.5 = (f32[128,512]{1,0:T(8,128)S(1)}, f32[128,512]{1,0:T(8,128)S(1)}, u32[]{:S(2)}, u32[]{:S(2)}) collective-permute-start(f32[128,512]{1,0:T(8,128)S(1)} %get-tuple-element.89), channel_id=1, source_target_pairs={{0,3},{1,2},{2,1},{3,0},{4,7},{5,6},{6,5},{7,4},{8,11},{9,10},{10,... | collective-permute-start | bytes 786440 | tf_op jit(solution)/shard_map/ppermute | solution.py:238
  26.2 0.5 collective-permute-start.4
  26.7 0.1 bitcast_select_fusion.1
  26.9 0.1 pad_maximum_fusion.lift
  27.0 5.4 %collective-permute-done.1.near = f32[256,256]{1,0:T(8,128)S(1)} collective-permute-done((f32[256,256]{1,0:T(8,128)S(1)}, f32[256,256]{1,0:T(8,128)S(1)}, u32[]{:S(2)}, u32[]{:S(2)}) %collective-permute-start.1) | collective-permute-done | bytes 262176 | tf_op jit(solution)/shard_map/ppermute | solution.py:220
  32.4 0.0 collective-permute-done.2.far
  32.4 0.8 shard_map.87
  33.2 0.0 copy-start
  33.2 9.3 %all_gather.13.everyone = f32[512,256]{1,0:T(8,128)S(1)} all-gather(f32[128,256]{1,0:T(8,128)S(1)} %get-tuple-element.54), channel_id=1, replica_groups=mesh['sub'=8,'grp'=4] {'grp'}, dimensions={0}, use_global_device_ids=true | all-gather | bytes 655360 | tf_op jit(solution)/shard_map/all_gather | solution.py:290
  42.5 0.0 collective-permute-done.3
  42.5 0.0 collective-permute-done.5
  42.5 0.0 collective-permute-done.4
  42.6 0.1 reduce-precision_convert_fusion
  42.7 0.0 copy-start.2
  42.7 2.5 %shard_map.89 = (f32[4,256,512]{2,1,0:T(8,128)S(1)}, f32[256,256]{1,0:T(8,128)S(1)}, f32[256,256]{1,0:T(8,128)S(1)}, f32[2,256]{1,0:T(2,128)S(1)}) custom-call(s32[1]{0:T(128)} %bitcast.even_ref, f32[5,256,256]{2,1,0:T(8,128)S(1)} %get-tuple-element.52.edges.first, f32[5,256,256]{2,1,0:T(8,128)S(1)} %get-tuple-element.53.residual.image_old, ...), custom_call_target="tpu_custom_call" | custom-call | tf_op jit(solution)/shard_map/pallas_call | solution.py:37
  45.2 4.3 %collective-permute-start.6 = (f32[256,256]{1,0:T(8,128)S(1)}, f32[256,256]{1,0:T(8,128)S(1)}, u32[]{:S(2)}, u32[]{:S(2)}) collective-permute-start(f32[256,256]{1,0:T(8,128)S(1)} %get-tuple-element.57), channel_id=1, source_target_pairs={{0,4},{4,0},{8,12},{12,8},{16,20},{20,16},{24,28},{28,24},{1,5},{5... | collective-permute-start | bytes 786440 | tf_op jit(solution)/shard_map/ppermute | solution.py:220
  49.5 0.7 collective-permute-start.7
  50.2 13.8 %all_to_all.15.sums = f32[32,2,256]{2,1,0:T(2,128)S(1)} all-to-all(f32[32,2,256]{2,1,0:T(2,128)S(1)} %broadcast_in_dim.101), channel_id=1, replica_groups=mesh['sub'=8,'grp'=4] {'sub','grp'}, dimensions={0} | all-to-all | bytes 131072 | tf_op jit(solution)/shard_map/all_to_all | solution.py:228
  64.0 0.0 collective-permute-done.6.near
  64.0 0.0 collective-permute-done.7.far
  64.0 1.6 %shard_map.90 = (f32[5,256,256]{2,1,0:T(8,128)S(1)}, f32[5,256,256]{2,1,0:T(8,128)S(1)}, f32[4,256,512]{2,1,0:T(8,128)S(1)}, f32[256,256]{1,0:T(8,128)S(1)}, f32...) custom-call(s32[1]{0:T(128)} %bitcast.even_ref, f32[4,256,512]{2,1,0:T(8,128)S(1)} %get-tuple-element.56.result, ...), custom_call_target="tpu_custom_call" | custom-call | tf_op jit(solution)/shard_map/pallas_call | solution.py:37
  65.6 1.3 collective-permute-start.8
  67.0 0.7 collective-permute-start.9
  67.6 10.8 %collective-permute-done.8.near = f32[256,256]{1,0:T(8,128)S(1)} collective-permute-done((f32[256,256]{1,0:T(8,128)S(1)}, f32[256,256]{1,0:T(8,128)S(1)}, u32[]{:S(2)}, u32[]{:S(2)}) %collective-permute-start.8) | collective-permute-done | bytes 262176 | tf_op jit(solution)/shard_map/ppermute | solution.py:220
  78.4 0.0 collective-permute-done.9.far
  78.4 0.8 shard_map.91
  79.2 6.5 %all_gather.14.everyone = f32[512,256]{1,0:T(8,128)S(1)} all-gather(f32[128,256]{1,0:T(8,128)S(1)} %get-tuple-element.65), channel_id=1, replica_groups=mesh['sub'=8,'grp'=4] {'grp'}, dimensions={0}, use_global_device_ids=true | all-gather | bytes 655360 | tf_op jit(solution)/shard_map/all_gather | solution.py:290
  85.7 2.4 %shard_map.92 = (f32[4,256,512]{2,1,0:T(8,128)S(1)}, f32[256,256]{1,0:T(8,128)S(1)}, f32[256,256]{1,0:T(8,128)S(1)}, f32[2,256]{1,0:T(2,128)S(1)}) custom-call(s32[1]{0:T(128)} %bitcast.even_ref, f32[5,256,256]{2,1,0:T(8,128)S(1)} %get-tuple-element.63.edges.second, f32[5,256,256]{2,1,0:T(8,128)S(1)} %get-tuple-element.64.residual, ...), custom_call_target="tpu_custom_call" | custom-call | tf_op jit(solution)/shard_map/pallas_call | solution.py:37
  88.2 2.5 %collective-permute-start.10 = (f32[256,256]{1,0:T(8,128)S(1)}, f32[256,256]{1,0:T(8,128)S(1)}, u32[]{:S(2)}, u32[]{:S(2)}) collective-permute-start(f32[256,256]{1,0:T(8,128)S(1)} %get-tuple-element.67), channel_id=1, source_target_pairs={{0,4},{4,0},{8,12},{12,8},{16,20},{20,16},{24,28},{28,24},{1,5},{5... | collective-permute-start | bytes 786440 | tf_op jit(solution)/shard_map/ppermute | solution.py:220
  90.7 0.7 collective-permute-start.11
  91.4 13.5 %all_to_all.16.sums = f32[32,2,256]{2,1,0:T(2,128)S(1)} all-to-all(f32[32,2,256]{2,1,0:T(2,128)S(1)} %broadcast_in_dim.103), channel_id=1, replica_groups=mesh['sub'=8,'grp'=4] {'sub','grp'}, dimensions={0} | all-to-all | bytes 131072 | tf_op jit(solution)/shard_map/all_to_all | solution.py:228
  104.9 1.7 %shard_map.93 = (f32[5,256,256]{2,1,0:T(8,128)S(1)}, f32[5,256,256]{2,1,0:T(8,128)S(1)}, f32[4,256,512]{2,1,0:T(8,128)S(1)}, f32[256,256]{1,0:T(8,128)S(1)}, f32...) custom-call(s32[1]{0:T(128)} %bitcast.even_ref, f32[4,256,512]{2,1,0:T(8,128)S(1)} %get-tuple-element.66.result, ...), custom_call_target="tpu_custom_call" | custom-call | tf_op jit(solution)/shard_map/pallas_call | solution.py:37
  106.5 1.3 collective-permute-start.12
  107.9 0.7 collective-permute-start.13
  108.5 10.8 %collective-permute-done.12.near = f32[256,256]{1,0:T(8,128)S(1)} collective-permute-done((f32[256,256]{1,0:T(8,128)S(1)}, f32[256,256]{1,0:T(8,128)S(1)}, u32[]{:S(2)}, u32[]{:S(2)}) %collective-permute-start.12) | collective-permute-done | bytes 262176 | tf_op jit(solution)/shard_map/ppermute | solution.py:220
  119.3 0.0 collective-permute-done.13.far
  119.3 0.8 shard_map.94
  120.2 6.5 %all_gather.15.everyone = f32[512,256]{1,0:T(8,128)S(1)} all-gather(f32[128,256]{1,0:T(8,128)S(1)} %get-tuple-element.77), channel_id=1, replica_groups=mesh['sub'=8,'grp'=4] {'grp'}, dimensions={0}, use_global_device_ids=true | all-gather | bytes 655360 | tf_op jit(solution)/shard_map/all_gather | solution.py:290
  126.7 2.4 %shard_map.95 = (f32[4,256,512]{2,1,0:T(8,128)S(1)}, f32[256,256]{1,0:T(8,128)S(1)}, f32[256,256]{1,0:T(8,128)S(1)}, f32[2,256]{1,0:T(2,128)S(1)}) custom-call(s32[1]{0:T(128)} %bitcast.even_ref, f32[5,256,256]{2,1,0:T(8,128)S(1)} %get-tuple-element.75.edges.third, f32[5,256,256]{2,1,0:T(8,128)S(1)} %get-tuple-element.76.residual, ...), custom_call_target="tpu_custom_call" | custom-call | tf_op jit(solution)/shard_map/pallas_call | solution.py:37
  129.1 2.5 %collective-permute-start.14 = (f32[256,256]{1,0:T(8,128)S(1)}, f32[256,256]{1,0:T(8,128)S(1)}, u32[]{:S(2)}, u32[]{:S(2)}) collective-permute-start(f32[256,256]{1,0:T(8,128)S(1)} %get-tuple-element.79), channel_id=1, source_target_pairs={{0,4},{4,0},{8,12},{12,8},{16,20},{20,16},{24,28},{28,24},{1,5},{5... | collective-permute-start | bytes 786440 | tf_op jit(solution)/shard_map/ppermute | solution.py:220
  131.6 0.7 collective-permute-start.15
  132.3 13.5 %all_to_all.17.sums = f32[32,2,256]{2,1,0:T(2,128)S(1)} all-to-all(f32[32,2,256]{2,1,0:T(2,128)S(1)} %broadcast_in_dim.104), channel_id=1, replica_groups=mesh['sub'=8,'grp'=4] {'sub','grp'}, dimensions={0} | all-to-all | bytes 131072 | tf_op jit(solution)/shard_map/all_to_all | solution.py:228
  145.8 0.0 collective-permute-done.14.near
  145.8 0.0 collective-permute-done.15.far
  145.8 1.8 %shard_map.96 = (f32[4,256,256]{2,1,0:T(8,128)}, f32[4,256,256]{2,1,0:T(8,128)}) custom-call(s32[1]{0:T(128)} %bitcast.even_ref, f32[4,256,512]{2,1,0:T(8,128)S(1)} %get-tuple-element.78.result, f32[256,256]{1,0:T(8,128)S(1)} %collective-permute-done.14.near, f32[256,256]{1,0:T(8,128)S(1)} %collective-permute-done.15.far, ...), custom_call_target="tpu_custom_call" | custom-call | tf_op jit(solution)/shard_map/pallas_call | solution.py:37
  (20 shorter events, 0.2 us)
Async XLA Ops:
  2.5 19.6 %copy-start.4 = (f32[1,256,1024]{2,1,0:T(8,128)S(1)}, f32[1,256,1024]{2,1,0:T(8,128)}, u32[]{:S(2)}) copy-start(f32[1,256,1024]{2,1,0:T(8,128)} %param.13) | copy-start | bytes 3145732
  3.7 10.9 %collective-permute-start = (f32[264,256]{1,0:T(8,128)S(1)}, f32[264,256]{1,0:T(8,128)S(1)}, u32[]{:S(2)}, u32[]{:S(2)}) collective-permute-start(f32[264,256]{1,0:T(8,128)S(1)} %pad_maximum_fusion.1), channel_id=1, source_target_pairs={{0,4},{4,8},{8,12},{12,16},{16,20},{20,24},{24,28},{1,5},{5,9},{9,... | collective-permute-start | bytes 811016 | tf_op jit(solution)/shard_map/ppermute | solution.py:256
  14.5 1.6 %copy-start.1 = (bf16[1,4,512,512]{3,2,1,0:T(8,128)(2,1)S(1)}, bf16[1,4,512,512]{3,2,1,0:T(8,128)(2,1)}, u32[]{:S(2)}) copy-start(bf16[1,4,512,512]{3,2,1,0:T(8,128)(2,1)} %param.10) | copy-start | bytes 6291460
  16.1 1.2 copy-start.3
  17.3 1.8 %copy-start.5 = (f32[1,4,32,512]{3,2,1,0:T(8,128)S(1)}, f32[1,4,32,512]{3,2,1,0:T(8,128)}, u32[]{:S(2)}) copy-start(f32[1,4,32,512]{3,2,1,0:T(8,128)} %param.11) | copy-start | bytes 786436
  19.2 13.3 %collective-permute-start.1 = (f32[256,256]{1,0:T(8,128)S(1)}, f32[256,256]{1,0:T(8,128)S(1)}, u32[]{:S(2)}, u32[]{:S(2)}) collective-permute-start(f32[256,256]{1,0:T(8,128)S(1)} %get-tuple-element.48), channel_id=1, source_target_pairs={{0,4},{4,0},{8,12},{12,8},{16,20},{20,16},{24,28},{28,24},{1,5},{5... | collective-permute-start | bytes 786440 | tf_op jit(solution)/shard_map/ppermute | solution.py:220
  21.5 11.0 %collective-permute-start.2 = (f32[256,256]{1,0:T(8,128)S(1)}, f32[256,256]{1,0:T(8,128)S(1)}, u32[]{:S(2)}, u32[]{:S(2)}) collective-permute-start(f32[256,256]{1,0:T(8,128)S(1)} %get-tuple-element.49), channel_id=1, source_target_pairs={{4,8},{8,4},{12,16},{16,12},{20,24},{24,20},{5,9},{9,5},{13,17},{1... | collective-permute-start | bytes 786440 | tf_op jit(solution)/shard_map/ppermute | solution.py:221
  24.5 18.0 %collective-permute-start.3 = (f32[128,512]{1,0:T(8,128)S(1)}, f32[128,512]{1,0:T(8,128)S(1)}, u32[]{:S(2)}, u32[]{:S(2)}) collective-permute-start(f32[128,512]{1,0:T(8,128)S(1)} %get-tuple-element.88), channel_id=1, source_target_pairs={{0,1},{1,0},{2,3},{3,2},{4,5},{5,4},{6,7},{7,6},{8,9},{9,8},{10,11... | collective-permute-start | bytes 786440 | tf_op jit(solution)/shard_map/ppermute | solution.py:238
  24.6 18.0 %collective-permute-start.5 = (f32[128,512]{1,0:T(8,128)S(1)}, f32[128,512]{1,0:T(8,128)S(1)}, u32[]{:S(2)}, u32[]{:S(2)}) collective-permute-start(f32[128,512]{1,0:T(8,128)S(1)} %get-tuple-element.89), channel_id=1, source_target_pairs={{0,3},{1,2},{2,1},{3,0},{4,7},{5,6},{6,5},{7,4},{8,11},{9,10},{10,... | collective-permute-start | bytes 786440 | tf_op jit(solution)/shard_map/ppermute | solution.py:238
  26.2 16.3 %collective-permute-start.4 = (f32[128,512]{1,0:T(8,128)S(1)}, f32[128,512]{1,0:T(8,128)S(1)}, u32[]{:S(2)}, u32[]{:S(2)}) collective-permute-start(f32[128,512]{1,0:T(8,128)S(1)} %get-tuple-element.90), channel_id=1, source_target_pairs={{0,2},{1,3},{2,0},{3,1},{4,6},{5,7},{6,4},{7,5},{8,10},{9,11},{10,... | collective-permute-start | bytes 786440 | tf_op jit(solution)/shard_map/ppermute | solution.py:238
  33.2 9.5 %copy-start = (bf16[1,4,512,512]{3,2,1,0:T(8,128)(2,1)S(1)}, bf16[1,4,512,512]{3,2,1,0:T(8,128)(2,1)}, u32[]{:S(2)}) copy-start(bf16[1,4,512,512]{3,2,1,0:T(8,128)(2,1)} %param.9) | copy-start | bytes 6291460
  42.7 21.3 %copy-start.2 = (bf16[1,4,512,512]{3,2,1,0:T(8,128)(2,1)S(1)}, bf16[1,4,512,512]{3,2,1,0:T(8,128)(2,1)}, u32[]{:S(2)}) copy-start(bf16[1,4,512,512]{3,2,1,0:T(8,128)(2,1)} %param.10) | copy-start | bytes 6291460
  45.2 18.8 %collective-permute-start.6 = (f32[256,256]{1,0:T(8,128)S(1)}, f32[256,256]{1,0:T(8,128)S(1)}, u32[]{:S(2)}, u32[]{:S(2)}) collective-permute-start(f32[256,256]{1,0:T(8,128)S(1)} %get-tuple-element.57), channel_id=1, source_target_pairs={{0,4},{4,0},{8,12},{12,8},{16,20},{20,16},{24,28},{28,24},{1,5},{5... | collective-permute-start | bytes 786440 | tf_op jit(solution)/shard_map/ppermute | solution.py:220
  49.5 14.5 %collective-permute-start.7 = (f32[256,256]{1,0:T(8,128)S(1)}, f32[256,256]{1,0:T(8,128)S(1)}, u32[]{:S(2)}, u32[]{:S(2)}) collective-permute-start(f32[256,256]{1,0:T(8,128)S(1)} %get-tuple-element.58), channel_id=1, source_target_pairs={{4,8},{8,4},{12,16},{16,12},{20,24},{24,20},{5,9},{9,5},{13,17},{1... | collective-permute-start | bytes 786440 | tf_op jit(solution)/shard_map/ppermute | solution.py:221
  65.6 12.8 %collective-permute-start.8 = (f32[256,256]{1,0:T(8,128)S(1)}, f32[256,256]{1,0:T(8,128)S(1)}, u32[]{:S(2)}, u32[]{:S(2)}) collective-permute-start(f32[256,256]{1,0:T(8,128)S(1)} %get-tuple-element.61), channel_id=1, source_target_pairs={{0,4},{4,0},{8,12},{12,8},{16,20},{20,16},{24,28},{28,24},{1,5},{5... | collective-permute-start | bytes 786440 | tf_op jit(solution)/shard_map/ppermute | solution.py:220
  67.0 11.5 %collective-permute-start.9 = (f32[256,256]{1,0:T(8,128)S(1)}, f32[256,256]{1,0:T(8,128)S(1)}, u32[]{:S(2)}, u32[]{:S(2)}) collective-permute-start(f32[256,256]{1,0:T(8,128)S(1)} %get-tuple-element.62), channel_id=1, source_target_pairs={{4,8},{8,4},{12,16},{16,12},{20,24},{24,20},{5,9},{9,5},{13,17},{1... | collective-permute-start | bytes 786440 | tf_op jit(solution)/shard_map/ppermute | solution.py:221
  88.2 16.7 %collective-permute-start.10 = (f32[256,256]{1,0:T(8,128)S(1)}, f32[256,256]{1,0:T(8,128)S(1)}, u32[]{:S(2)}, u32[]{:S(2)}) collective-permute-start(f32[256,256]{1,0:T(8,128)S(1)} %get-tuple-element.67), channel_id=1, source_target_pairs={{0,4},{4,0},{8,12},{12,8},{16,20},{20,16},{24,28},{28,24},{1,5},{5... | collective-permute-start | bytes 786440 | tf_op jit(solution)/shard_map/ppermute | solution.py:220
  90.7 14.2 %collective-permute-start.11 = (f32[256,256]{1,0:T(8,128)S(1)}, f32[256,256]{1,0:T(8,128)S(1)}, u32[]{:S(2)}, u32[]{:S(2)}) collective-permute-start(f32[256,256]{1,0:T(8,128)S(1)} %get-tuple-element.68), channel_id=1, source_target_pairs={{4,8},{8,4},{12,16},{16,12},{20,24},{24,20},{5,9},{9,5},{13,17},{1... | collective-permute-start | bytes 786440 | tf_op jit(solution)/shard_map/ppermute | solution.py:221
  106.5 12.8 %collective-permute-start.12 = (f32[256,256]{1,0:T(8,128)S(1)}, f32[256,256]{1,0:T(8,128)S(1)}, u32[]{:S(2)}, u32[]{:S(2)}) collective-permute-start(f32[256,256]{1,0:T(8,128)S(1)} %get-tuple-element.73), channel_id=1, source_target_pairs={{0,4},{4,0},{8,12},{12,8},{16,20},{20,16},{24,28},{28,24},{1,5},{5... | collective-permute-start | bytes 786440 | tf_op jit(solution)/shard_map/ppermute | solution.py:220
  107.9 11.5 %collective-permute-start.13 = (f32[256,256]{1,0:T(8,128)S(1)}, f32[256,256]{1,0:T(8,128)S(1)}, u32[]{:S(2)}, u32[]{:S(2)}) collective-permute-start(f32[256,256]{1,0:T(8,128)S(1)} %get-tuple-element.74), channel_id=1, source_target_pairs={{4,8},{8,4},{12,16},{16,12},{20,24},{24,20},{5,9},{9,5},{13,17},{1... | collective-permute-start | bytes 786440 | tf_op jit(solution)/shard_map/ppermute | solution.py:221
  129.1 16.7 %collective-permute-start.14 = (f32[256,256]{1,0:T(8,128)S(1)}, f32[256,256]{1,0:T(8,128)S(1)}, u32[]{:S(2)}, u32[]{:S(2)}) collective-permute-start(f32[256,256]{1,0:T(8,128)S(1)} %get-tuple-element.79), channel_id=1, source_target_pairs={{0,4},{4,0},{8,12},{12,8},{16,20},{20,16},{24,28},{28,24},{1,5},{5... | collective-permute-start | bytes 786440 | tf_op jit(solution)/shard_map/ppermute | solution.py:220
  131.6 14.2 %collective-permute-start.15 = (f32[256,256]{1,0:T(8,128)S(1)}, f32[256,256]{1,0:T(8,128)S(1)}, u32[]{:S(2)}, u32[]{:S(2)}) collective-permute-start(f32[256,256]{1,0:T(8,128)S(1)} %get-tuple-element.80), channel_id=1, source_target_pairs={{4,8},{8,4},{12,16},{16,12},{20,24},{24,20},{5,9},{9,5},{13,17},{1... | collective-permute-start | bytes 786440 | tf_op jit(solution)/shard_map/ppermute | solution.py:221

commit v4 on v3

v4 whole, which is shorter than its diff:
```python
import functools

import jax
import jax.numpy as jnp
from jax import lax
from jax.experimental import pallas as pl
from jax.experimental.pallas import tpu as pltpu
from jax.sharding import PartitionSpec as P

ITERS = 3


VMEM_LIMIT = 8 * 1024 * 1024
TAIL_LIMIT = 62 * 1024 * 1024


def split(values):
    high = values.astype(jnp.bfloat16)
    return high, (values - high.astype(jnp.float32)).astype(jnp.bfloat16)


def split_outside(values):
    high = lax.reduce_precision(values, exponent_bits=8, mantissa_bits=7)
    return high.astype(jnp.bfloat16), (values - high).astype(jnp.bfloat16)


def mul(first, second):
    return jnp.dot(first, second, preferred_element_type=jnp.float32)


def mul_rows(first, second):
    dims = (((1,), (1,)), ((), ()))
    return lax.dot_general(first, second, dims, preferred_element_type=jnp.float32)


def call(kernel, out_shapes, *operands, scalars=1):
    return pl.pallas_call(
        kernel,
        out_shape=[jax.ShapeDtypeStruct(shape, jnp.float32) for shape in out_shapes],
        in_specs=[pl.BlockSpec(memory_space=pltpu.SMEM)] * scalars
        + [pl.BlockSpec(memory_space=pltpu.VMEM)] * (len(operands) - scalars),
        out_specs=[pl.BlockSpec(memory_space=pltpu.VMEM)] * len(out_shapes),
        compiler_params=pltpu.CompilerParams(vmem_limit_bytes=VMEM_LIMIT),
    )(*operands)


class Joined:
    def __init__(self, first, rest):
        self.first, self.rest = first, rest

    def __getitem__(self, place):
        return self.first[...] if place == 0 else self.rest[place - 1]

    def __setitem__(self, place, value):
        if place == 0:
            self.first[...] = value
        else:
            self.rest[place - 1] = value


def jump_edge(even, result, near, far, live, edge, subs):
    width = near.shape[1]
    if edge == 0:
        right = jnp.where(even, far[...], near[...])
    else:
        right = result[edge - 1][:, width:]
    if edge == subs:
        left = jnp.where(even, near[...], far[...])
    else:
        left = result[edge][:, :width]
    return live[edge] * (right - left)


def send_faces(even, first, last, near_out, far_out):
    width = first.shape[1] // 2
    to_next, to_prev = last[:, width:], first[:, :width]
    near_out[...] = jnp.where(even, to_next, to_prev)
    far_out[...] = jnp.where(even, to_prev, to_next)


def panel_products(parts, panel, result, extra=None):
    subs = panel.shape[0]
    for sub in range(subs):
        high = jnp.concatenate([-parts[sub][0], parts[sub + 1][0]], axis=1)
        low = jnp.concatenate([-parts[sub][1], parts[sub + 1][1]], axis=1)
        total = mul(high, panel[sub]) + mul(low, panel[sub])
        if extra is not None:
            total = total + extra(sub)
        result[sub] = total


def column(row, width):
    lanes = jnp.broadcast_to(row, (128, row.shape[1])).T
    return jnp.concatenate([lanes] * (width // 128), axis=1)


def row_sums(values):
    ones = jnp.ones((8, values.shape[1]), jnp.bfloat16)
    high, rest = split(values)
    middle, low = split(values - high.astype(jnp.float32))
    return (mul_rows(ones, high) + mul_rows(ones, middle) + mul_rows(ones, low))[:1]


def step_scalars(step, sums, before):
    totals = jnp.sum(sums[...], axis=0)
    rz_now, curvature = totals[:1], totals[1:2]
    if step == 0:
        return rz_now, rz_now / curvature, None
    beta = rz_now / before[0:1]
    return rz_now, rz_now / (curvature - beta * rz_now / before[1:2]), beta


def tail_kernel(places, counts, rhs, tail, face, done):
    loads, width = rhs.shape[2:]
    copy = pltpu.make_async_copy(rhs.at[0, rhs.shape[1] - 1], face, done)
    copy.start()
    last = jnp.where(places[2] == 1, 0, counts[0, counts.shape[1] - 1])
    mask = (lax.broadcasted_iota(jnp.int32, (8, width), 1) < last).astype(jnp.float32)
    tail[loads:] = mask
    copy.wait()
    tail[:loads] = mask[:1] * face[...]


def early_kernel(places, counts, rhs, panel, live, own, partial, rest):
    subs, loads, width = own.shape
    positions = lax.broadcasted_iota(jnp.int32, (1, width), 1)
    parts = [None]
    for sub in range(subs):
        count = counts[0, sub]
        if sub == subs - 1:
            count = jnp.where(places[2] == 1, 0, count)
        mask = (positions < count).astype(jnp.float32)
        live[sub] = mask
        own[sub] = mask * rhs[0, sub]
        parts.append(split(own[sub]))
    partial[...] = mul(parts[1][0], panel[0, width:]) + mul(parts[1][1], panel[0, width:])
    for sub in range(1, subs):
        high = jnp.concatenate([-parts[sub][0], parts[sub + 1][0]], axis=1)
        low = jnp.concatenate([-parts[sub][1], parts[sub + 1][1]], axis=1)
        rest[sub - 1] = mul(high, panel[sub]) + mul(low, panel[sub])


def head_kernel(places, head, partial, rest, panel, live, edge, first, near_out, far_out):
    loads, width = edge.shape
    live[...] = head[loads : loads + 1]
    edge[...] = head[:loads]
    high, low = split(head[:loads])
    first[...] = partial[...] - mul(high, panel[0, :width]) - mul(low, panel[0, :width])
    last = rest[rest.shape[0] - 1]
    send_faces(places[0] == 1, first[...], last, near_out, far_out)


def pick_kernel(places, everyone, coarse, picked):
    group, own = everyone.shape[0], everyone.shape[2]
    rows, size = coarse.shape
    grp = places[1]
    high, low = split(coarse[...])
    unknowns = lax.broadcasted_iota(jnp.int32, (size, own), 0)
    columns = []
    for member in range(group):
        chosen = (unknowns == everyone[grp ^ member]).astype(jnp.bfloat16)
        columns.append(mul(high, chosen) + mul(low, chosen))
    high, low = split(jnp.concatenate(columns, axis=1))
    owned = lax.broadcasted_iota(jnp.int32, (rows, own), 0) + grp * rows
    dims = (((0,), (0,)), ((), ()))
    for distance in range(group):
        chosen = (owned == everyone[distance]).astype(jnp.bfloat16)
        picked[distance] = lax.dot_general(
            chosen, high, dims, preferred_element_type=jnp.float32
        ) + lax.dot_general(chosen, low, dims, preferred_element_type=jnp.float32)


def corner_kernel(places, first, rest, near, far, live_first, live_rest, coupling,
                  edge, own, corners):
    even = places[0] == 1
    subs, rows = coupling.shape[0], coupling.shape[1] // 2
    result, live, edges = Joined(first, rest), Joined(live_first, live_rest), Joined(edge, own)
    parts = []
    for place in range(subs + 1):
        edges[place] = 0.25 * jump_edge(even, result, near, far, live, place, subs)
        parts.append(split(edges[place]))
    for sub in range(subs):
        high = jnp.concatenate([-parts[sub][0], parts[sub + 1][0]], axis=1)
        low = jnp.concatenate([-parts[sub][1], parts[sub + 1][1]], axis=1)
        both = mul_rows(coupling[sub], high)
        corners[sub * rows : (sub + 1) * rows, :] = (
            both[:rows] + both[rows:] + mul_rows(coupling[sub, :rows], low)
        )


def dual_kernel(places, edge, own, residual, panel, everyone, block, lift,
                first, rest, near_out, far_out, sums):
    even = places[0] == 1
    subs, width = panel.shape[0], edge.shape[1]
    edges, result = Joined(edge, own), Joined(first, rest)
    rows = block.shape[0] // 2
    high, low = split(everyone[...])
    both = mul(block[...], high)
    back = (both[:rows] + both[rows:] + mul(block[:rows], low)).T
    back_high, back_low = split(back)
    lifted = jnp.concatenate([back_high, back_low, back_high], axis=1)
    parts = [split(edges[place]) for place in range(subs + 1)]
    panel_products(parts, panel, result, lambda sub: mul(lifted, lift[sub]))
    send_faces(even, result[0], result[subs - 1], near_out, far_out)
    product = curvature = 0.0
    for sub in range(subs):
        product = product + residual[sub] * edges[sub + 1]
        curvature = curvature + (
            result[sub][:, width:] * edges[sub + 1] - result[sub][:, :width] * edges[sub]
        )
    sums[...] = jnp.concatenate([row_sums(product), row_sums(curvature)], axis=0)


def update_kernel(step, places, first, rest, near, far, live_first, live_rest, sums, before,
                  old_edge, old_own, residual_edge, residual_own, panel,
                  image_edge, image_own, new_edge, new_own,
                  first_new, rest_new, near_out, far_out, scalars):
    even = places[0] == 1
    subs, width = panel.shape[0], near.shape[1]
    result, live = Joined(first, rest), Joined(live_first, live_rest)
    image_old, residual = Joined(old_edge, old_own), Joined(residual_edge, residual_own)
    image, residual_new = Joined(image_edge, image_own), Joined(new_edge, new_own)
    result_new = Joined(first_new, rest_new)
    rz_now, alpha, beta = step_scalars(step, sums, before)
    scalars[...] = jnp.concatenate([rz_now, alpha], axis=0)
    alpha_column = column(alpha, width)
    beta_column = None if beta is None else column(beta, width)
    parts = []
    for place in range(subs + 1):
        value = jump_edge(even, result, near, far, live, place, subs)
        if beta is not None:
            value = value + beta_column * image_old[place]
        image[place] = value
        residual_new[place] = residual[place] - alpha_column * value
        parts.append(split(residual_new[place]))
    panel_products(parts, panel, result_new)
    send_faces(even, result_new[0], result_new[subs - 1], near_out, far_out)


def last_kernel(step, places, first, rest, following, live, sums, before, older, image_old,
                residual, first_z, second_z, third_z, multipliers, residual_new):
    subs, width = residual.shape[0], following.shape[1]
    result = Joined(first, rest)
    rz_now, alpha, beta = step_scalars(step, sums, before)
    beta_before = before[0:1] / older[0:1]
    on_second = before[1:2] + alpha * beta
    on_first = older[1:2] + on_second * beta_before
    alpha_column, beta_column = column(alpha, width), column(beta, width)
    second_column, first_column = column(on_second, width), column(on_first, width)
    for sub in range(subs):
        left = following[...] if sub == subs - 1 else result[sub + 1][:, :width]
        image = live[sub] * (result[sub][:, width:] - left) + beta_column * image_old[sub]
        residual_new[sub] = residual[sub] - alpha_column * image
        multipliers[sub] = (
            first_column * first_z[sub]
            + second_column * second_z[sub]
            + alpha_column * third_z[sub]
        )


def neighbour_pairs(size, first):
    pairs = [(i, i + 1) for i in range(first, size - 1, 2)]
    return [route for a, b in pairs for route in ((a, b), (b, a))]


def swap(near, far):
    size = lax.axis_size("sub")
    return (
        lax.ppermute(near, "sub", neighbour_pairs(size, 0)),
        lax.ppermute(far, "sub", neighbour_pairs(size, 1)),
    )


def from_all(rows):
    size = lax.axis_size("sub") * lax.axis_size("grp")
    copies = jnp.broadcast_to(rows[None], (size,) + rows.shape)
    return lax.all_to_all(copies, ("sub", "grp"), 0, 0)


def from_group(values):
    group = lax.axis_size("grp")
    received = [values]
    for distance in range(1, group):
        routes = [(i, i ^ distance) for i in range(group)]
        received.append(lax.ppermute(values, "grp", routes))
    return jnp.stack(received)


def swap_blocks(picked):
    group = lax.axis_size("grp")
    block = picked[0]
    for distance in range(1, group):
        routes = [(i, i ^ distance) for i in range(group)]
        block = block + lax.ppermute(picked[distance], "grp", routes)
    return block


def make_tail(places, counts, rhs):
    loads, width = rhs.shape[2:]
    return pl.pallas_call(
        tail_kernel,
        out_shape=jax.ShapeDtypeStruct((loads + 8, width), jnp.float32),
        in_specs=[
            pl.BlockSpec(memory_space=pltpu.SMEM),
            pl.BlockSpec(memory_space=pltpu.SMEM),
            pl.BlockSpec(memory_space=pltpu.HBM),
        ],
        out_specs=pl.BlockSpec(memory_space=pltpu.VMEM),
        scratch_shapes=[pltpu.VMEM((loads, width), jnp.float32), pltpu.SemaphoreType.DMA],
        compiler_params=pltpu.CompilerParams(vmem_limit_bytes=TAIL_LIMIT),
    )(places, counts, rhs)


def local(rhs, counts, solve_panel, dirichlet_panel, coupling, corner_map, coarse_inverse):
    subs, loads, width = rhs.shape[1:]
    corners = coupling.shape[2]
    solve, dirichlet, couple = solve_panel[0], dirichlet_panel[0], coupling[0]
    place, size = lax.axis_index("sub"), lax.axis_size("sub")
    places = jnp.stack([1 - place % 2, lax.axis_index("grp"), place == size - 1]).astype(jnp.int32)

    face_shape, own_shape = (loads, width), (subs, loads, width)
    first_shape, rest_shape = (loads, 2 * width), (subs - 1, loads, 2 * width)
    edges_shapes = [face_shape, own_shape]
    result_shapes = [first_shape, rest_shape, face_shape, face_shape]

    tail = make_tail(places, counts, rhs)
    tail, places, corner_map = lax.optimization_barrier((tail, places, corner_map))
    head = lax.ppermute(tail, "sub", [(i, i + 1) for i in range(size - 1)])
    everyone = from_group(corner_map.reshape(1, subs * corners))
    live_own, residual_own, partial, rest = call(
        early_kernel,
        [(subs, 1, width), own_shape, first_shape, rest_shape],
        places, counts, rhs, dirichlet, scalars=2,
    )
    group = everyone.shape[0]
    (picked,) = call(
        pick_kernel, [(group, subs * corners, group * subs * corners)],
        places, everyone, coarse_inverse[0],
    )
    head, picked, rest = lax.optimization_barrier((head, picked, rest))
    live_edge, residual_edge, first, near, far = call(
        head_kernel,
        [(1, width), face_shape, first_shape, face_shape, face_shape],
        places, head, partial, rest, dirichlet,
    )
    first, couple = lax.optimization_barrier((first, couple))
    block = jnp.concatenate(split_outside(swap_blocks(picked)), axis=0)
    high, low = split_outside(couple)
    stacked = jnp.concatenate([high, low], axis=1)
    slots = jnp.arange(subs, dtype=jnp.int32)
    own = (slots[:, None] == slots[None, :])[:, :, None, None]

    def placed(part):
        wide = jnp.where(own, part[:, None], jnp.zeros((), part.dtype))
        return wide.reshape(subs, subs * corners, 2 * width)

    lift = jnp.concatenate([placed(high), placed(high), placed(low)], axis=1)

    scalars, preconds = [jnp.zeros((2, loads), jnp.float32)], []
    image = residual = (residual_edge, residual_own)
    live = (live_edge, live_own)
    for step in range(ITERS):
        near, far = swap(near, far)
        edge, own, values = call(
            corner_kernel,
            edges_shapes + [(subs * corners, loads)],
            places, first, rest, near, far, *live, stacked,
        )
        preconds.append(own)
        everyone = lax.all_gather(values, "grp", tiled=True)
        first, rest, near, far, sums = call(
            dual_kernel,
            result_shapes + [(2, loads)],
            places, edge, own, residual[1], solve, everyone, block, lift,
        )
        sums = from_all(sums)
        if step + 1 < ITERS:
            near, far = swap(near, far)
            *new, first, rest, near, far, now = call(
                functools.partial(update_kernel, step),
                edges_shapes + edges_shapes + result_shapes + [(2, loads)],
                places, first, rest, near, far, *live, sums, scalars[-1],
                *image, *residual, dirichlet,
            )
            image, residual = new[:2], new[2:]
            scalars.append(now)
    following = lax.ppermute(first[:, :width], "sub", [(i + 1, i) for i in range(size - 1)])
    multipliers, residual = call(
        functools.partial(last_kernel, ITERS - 1),
        [own_shape] * 2,
        places, first, rest, following, live[1], sums, scalars[-1], scalars[-2],
        image[1], residual[1], *preconds,
    )
    return (multipliers[None], residual[None])


def solution(mesh):
    return jax.shard_map(
        local,
        mesh=mesh,
        in_specs=(
            P("grp", "sub", None, None),
            P("grp", "sub"),
            P("grp", "sub", None, None),
            P("grp", "sub", None, None),
            P("grp", "sub", None, None),
            P("grp", "sub", None),
            P("sub", "grp", None),
        ),
        out_specs=(P("grp", "sub", None, None), P("grp", "sub", None, None)),
        check_vma=False,
    )
```

time: 148 us -> 150 us (1.014)
  Pallas kernels: 18.8 us -> 28 us
  blocking collectives: 68.2 us -> 59.5 us
  waiting for transfers between devices: 27 us -> 29.9 us
  other arithmetic: 2.86 us -> 1.06 us
    pallas_call x11 -> x12, Pallas kernels: 18.8 us -> 25.7 us  [call(): pl.pallas_call(kernel, out_shape=[jax.ShapeDtypeStruct(shape, jnp.float32...]
    all_gather x1 -> x0, blocking collectives: 5.03 us -> none  [local(): everyone = lax.all_gather(corner_map.reshape(1, subs * corners), 'grp')]
    ppermute x3 -> x7, starting transfers between devices: 2.21 us -> 5.37 us  [the longest x3 2.21 us: swap_blocks(): block = block + lax.ppermute(picked[distance], 'grp', routes)]
    ppermute x6 -> x5, waiting for transfers between devices: 27 us -> 29.9 us  [swap(): lax.ppermute(near, 'sub', neighbour_pairs(size, 0))]
    ppermute x6 -> x5, starting transfers between devices: 14.3 us -> 11.8 us  [swap(): lax.ppermute(near, 'sub', neighbour_pairs(size, 0))]
    pallas_call x0 -> x1, Pallas kernels: none -> 2.35 us  [make_tail(): pl.pallas_call(tail_kernel, out_shape=jax.ShapeDtypeStruct((loads + 8, wi...]
    all_gather x3, blocking collectives: 22.3 us -> 20.2 us  [local(): everyone = lax.all_gather(values, 'grp', tiled=True)]
    all_to_all x3, blocking collectives: 40.8 us -> 39.3 us  [from_all(): return lax.all_to_all(copies, ('sub', 'grp'), 0, 0)]
  transfers between devices with their start and end apart: 16 -> 18, of which waited for: 3 -> 3; matrix products, arithmetic and copies ran while one was open for 1% -> 1% of each run, Pallas kernels for 2% -> 4%
where the time goes in v4:
time: 150 us
  blocking collectives  59.5 us (40%)
  waiting for transfers between devices  29.9 us (20%)
  Pallas kernels  28 us (19%)
  starting transfers between devices  25.4 us (17%)
  local copies, waits for them, and re-layouts  4.75 us (3%)
    all_to_all x3, blocking collectives, from_all(): return lax.all_to_all(copies, ('sub', 'grp'), 0, 0)  39.3 us
    ppermute x5, waiting for transfers between devices, swap(): lax.ppermute(near, 'sub', neighbour_pairs(size, 0))  29.9 us
    pallas_call x12, Pallas kernels, call(): pl.pallas_call(kernel, out_shape=[jax.ShapeDtypeStruct(shape, jnp.float32...  25.7 us
    all_gather x3, blocking collectives, local(): everyone = lax.all_gather(values, 'grp', tiled=True)  20.2 us
    ppermute x5, starting transfers between devices, swap(): lax.ppermute(near, 'sub', neighbour_pairs(size, 0))  11.8 us
    ppermute x1, starting transfers between devices, local(): head = lax.ppermute(tail, 'sub', [(i, i + 1) for i in range(size - 1)])  4.86 us
    ppermute x5, starting transfers between devices, swap(): lax.ppermute(far, 'sub', neighbour_pairs(size, 1))  3.33 us
  transfers between devices with their start and end apart: 18, of which 3 were waited for; matrix products, arithmetic and copies ran while one was open for 1% of the time, Pallas kernels for 4%

profile of v4, /device:TPU:0, one launch (start us, length us, event | category | flops | bytes accessed | tf_op | source)
XLA Modules:
  0.0 149.5 jit_solution(13259681752854329324)
XLA Ops:
  0.6 0.0 copy-start.3
  0.7 0.6 pad_add_fusion.1.places
  1.2 2.4 %shard_map.86 = f32[264,256]{1,0:T(8,128)} custom-call(s32[3]{0:T(128)} %pad_add_fusion.1.places, s32[1,4]{1,0:T(1,128)} %counts.3, f32[1,4,256,256]{3,2,1,0:T(8,128)} %rhs.3), custom_call_target="tpu_custom_call" | custom-call | tf_op jit(solution)/shard_map/pallas_call | solution.py:300
  3.6 4.9 %collective-permute-start = (f32[264,256]{1,0:T(8,128)}, f32[264,256]{1,0:T(8,128)S(1)}, u32[]{:S(2)}, u32[]{:S(2)}) collective-permute-start(f32[264,256]{1,0:T(8,128)} %shard_map.86), channel_id=1, source_target_pairs={{0,4},{4,8},{8,12},{12,16},{16,20},{20,24},{24,28},{1,5},{5,9},{9,... | collective-permute-start | bytes 811016 | tf_op jit(solution)/shard_map/ppermute | solution.py:328
  8.5 0.8 reshape.31
  9.2 0.7 collective-permute-start.3
  9.9 0.9 collective-permute-start.2
  10.8 0.3 collective-permute-start.1
  11.1 0.8 stack_reshape.3
  11.9 0.1 broadcast_in_dim.83
  12.0 0.1 broadcast_in_dim.84
  12.0 1.6 %copy-done = bf16[1,4,512,512]{3,2,1,0:T(8,128)(2,1)S(1)} copy-done((bf16[1,4,512,512]{3,2,1,0:T(8,128)(2,1)S(1)}, bf16[1,4,512,512]{3,2,1,0:T(8,128)(2,1)}, u32[]{:S(2)}) %copy-start) | copy-done | bytes 2097176
  13.6 0.6 copy-done.5
  14.3 0.7 copy-done.7
  14.9 1.6 %shard_map.88 = (f32[4,1,256]{2,1,0:T(1,128)S(1)}, f32[4,256,256]{2,1,0:T(8,128)S(1)}, f32[256,512]{1,0:T(8,128)S(1)}, f32[3,256,512]{2,1,0:T(8,128)S(1)}) custom-call(s32[3]{0:T(128)S(1)} %copy-done.5, s32[1,4]{1,0:T(1,128)S(1)} %copy-done.7, f32[1,4,256,256]{3,2,1,0:T(8,128)S(1)} %copy-done.3, bf16[4,512,512]{2,1,0:T(8,128)(2,1)S(1)} %bitcast.29), custom_call_target="tpu_custom_call" | custom-call | tf_op jit(solution)/shard_map/pallas_call | solution.py:37
  16.6 0.0 copy-start.1
  16.6 0.0 collective-permute-done.2
  16.6 2.3 %shard_map.87 = f32[4,128,512]{2,1,0:T(8,128)S(1)} custom-call(s32[3]{0:T(128)S(1)} %copy-done.6, s32[4,1,128]{2,1,0:T(1,128)S(1)} %pad_add_fusion.everyone, f32[256,1024]{1,0:T(8,128)S(1)} %bitcast.36), custom_call_target="tpu_custom_call" | custom-call | tf_op jit(solution)/shard_map/pallas_call | solution.py:37
  19.0 0.0 collective-permute-done.head
  19.0 0.0 copy-start.8
  19.0 0.9 shard_map.89
  19.9 0.0 copy-done.8
  20.0 1.6 %collective-permute-start.4 = (f32[256,256]{1,0:T(8,128)S(1)}, f32[256,256]{1,0:T(8,128)S(1)}, u32[]{:S(2)}, u32[]{:S(2)}) collective-permute-start(f32[256,256]{1,0:T(8,128)S(1)} %get-tuple-element.68), channel_id=1, source_target_pairs={{0,4},{4,0},{8,12},{12,8},{16,20},{20,16},{24,28},{28,24},{1,5},{5... | collective-permute-start | bytes 786440 | tf_op jit(solution)/shard_map/ppermute | solution.py:269
  21.6 0.7 collective-permute-start.5
  22.3 0.1 slice_bitcast_fusion.2
  22.3 0.1 collective-permute-start.6
  22.4 1.6 %collective-permute-start.8 = (f32[128,512]{1,0:T(8,128)S(1)}, f32[128,512]{1,0:T(8,128)S(1)}, u32[]{:S(2)}, u32[]{:S(2)}) collective-permute-start(f32[128,512]{1,0:T(8,128)S(1)} %get-tuple-element.119), channel_id=1, source_target_pairs={{0,3},{1,2},{2,1},{3,0},{4,7},{5,6},{6,5},{7,4},{8,11},{9,10},{10,... | collective-permute-start | bytes 786440 | tf_op jit(solution)/shard_map/ppermute | solution.py:294
  24.0 0.5 collective-permute-start.7
  24.5 0.1 bitcast_select_fusion.1
  24.7 0.1 pad_maximum_fusion.lift
  24.9 8.3 %collective-permute-done.4.near = f32[256,256]{1,0:T(8,128)S(1)} collective-permute-done((f32[256,256]{1,0:T(8,128)S(1)}, f32[256,256]{1,0:T(8,128)S(1)}, u32[]{:S(2)}, u32[]{:S(2)}) %collective-permute-start.4) | collective-permute-done | bytes 262176 | tf_op jit(solution)/shard_map/ppermute | solution.py:269
  33.1 1.3 shard_map.90
  34.4 0.0 copy-start.2
  34.5 7.1 %all_gather.9.everyone = f32[512,256]{1,0:T(8,128)S(1)} all-gather(f32[128,256]{1,0:T(8,128)S(1)} %get-tuple-element.76), channel_id=1, replica_groups=mesh['sub'=8,'grp'=4] {'grp'}, dimensions={0}, use_global_device_ids=true | all-gather | bytes 655360 | tf_op jit(solution)/shard_map/all_gather | solution.py:370
  41.6 0.0 collective-permute-done.6
  41.6 0.0 collective-permute-done.8
  41.6 0.0 collective-permute-done.7
  41.6 0.1 reduce-precision_convert_fusion
  41.8 3.0 %shard_map.91 = (f32[256,512]{1,0:T(8,128)S(1)}, f32[3,256,512]{2,1,0:T(8,128)S(1)}, f32[256,256]{1,0:T(8,128)S(1)}, f32[256,256]{1,0:T(8,128)S(1)}, f32[2,256]{1,0:T(2,128)S(1)}) custom-call(s32[3]{0:T(128)S(1)} %copy-done.6, f32[256,256]{1,0:T(8,128)S(1)} %get-tuple-element.73.edge, f32[4,256,256]{2,1,0:T(8,128)S(1)} %get-tuple-element.74.own.first_z, ...), custom_call_target="tpu_custom_call" | custom-call | tf_op jit(solution)/shard_map/pallas_call | solution.py:37
  44.8 3.1 %collective-permute-start.9 = (f32[256,256]{1,0:T(8,128)S(1)}, f32[256,256]{1,0:T(8,128)S(1)}, u32[]{:S(2)}, u32[]{:S(2)}) collective-permute-start(f32[256,256]{1,0:T(8,128)S(1)} %get-tuple-element.80), channel_id=1, source_target_pairs={{0,4},{4,0},{8,12},{12,8},{16,20},{20,16},{24,28},{28,24},{1,5},{5... | collective-permute-start | bytes 786440 | tf_op jit(solution)/shard_map/ppermute | solution.py:269
  47.8 0.7 collective-permute-start.10
  48.5 12.8 %all_to_all.15.sums = f32[32,2,256]{2,1,0:T(2,128)S(1)} all-to-all(f32[32,2,256]{2,1,0:T(2,128)S(1)} %broadcast_in_dim.91), channel_id=1, replica_groups=mesh['sub'=8,'grp'=4] {'sub','grp'}, dimensions={0} | all-to-all | bytes 131072 | tf_op jit(solution)/shard_map/all_to_all | solution.py:277
  61.4 2.1 %shard_map.92 = (f32[256,256]{1,0:T(8,128)S(1)}, f32[4,256,256]{2,1,0:T(8,128)S(1)}, f32[256,256]{1,0:T(8,128)S(1)}, f32[4,256,256]{2,1,0:T(8,128)S(1)}, f32[256...) custom-call(s32[3]{0:T(128)S(1)} %copy-done.6, ...), custom_call_target="tpu_custom_call" | custom-call | tf_op jit(solution)/shard_map/pallas_call | solution.py:37
  63.5 2.3 %collective-permute-start.11 = (f32[256,256]{1,0:T(8,128)S(1)}, f32[256,256]{1,0:T(8,128)S(1)}, u32[]{:S(2)}, u32[]{:S(2)}) collective-permute-start(f32[256,256]{1,0:T(8,128)S(1)} %get-tuple-element.86), channel_id=1, source_target_pairs={{0,4},{4,0},{8,12},{12,8},{16,20},{20,16},{24,28},{28,24},{1,5},{5... | collective-permute-start | bytes 786440 | tf_op jit(solution)/shard_map/ppermute | solution.py:269
  65.9 0.7 collective-permute-start.12
  66.5 10.8 %collective-permute-done.11.near = f32[256,256]{1,0:T(8,128)S(1)} collective-permute-done((f32[256,256]{1,0:T(8,128)S(1)}, f32[256,256]{1,0:T(8,128)S(1)}, u32[]{:S(2)}, u32[]{:S(2)}) %collective-permute-start.11) | collective-permute-done | bytes 262176 | tf_op jit(solution)/shard_map/ppermute | solution.py:269
  77.3 0.0 collective-permute-done.12.far
  77.3 1.3 shard_map.93
  78.7 6.5 %all_gather.10.everyone = f32[512,256]{1,0:T(8,128)S(1)} all-gather(f32[128,256]{1,0:T(8,128)S(1)} %get-tuple-element.91), channel_id=1, replica_groups=mesh['sub'=8,'grp'=4] {'grp'}, dimensions={0}, use_global_device_ids=true | all-gather | bytes 655360 | tf_op jit(solution)/shard_map/all_gather | solution.py:370
  85.2 3.1 %shard_map.94 = (f32[256,512]{1,0:T(8,128)S(1)}, f32[3,256,512]{2,1,0:T(8,128)S(1)}, f32[256,256]{1,0:T(8,128)S(1)}, f32[256,256]{1,0:T(8,128)S(1)}, f32[2,256]{1,0:T(2,128)S(1)}) custom-call(s32[3]{0:T(128)S(1)} %copy-done.6, f32[256,256]{1,0:T(8,128)S(1)} %get-tuple-element.88.edge, f32[4,256,256]{2,1,0:T(8,128)S(1)} %get-tuple-element.89.own.second_z, ...), custom_call_target="tpu_custom_call" | custom-call | tf_op jit(solution)/shard_map/pallas_call | solution.py:37
  88.3 2.5 %collective-permute-start.13 = (f32[256,256]{1,0:T(8,128)S(1)}, f32[256,256]{1,0:T(8,128)S(1)}, u32[]{:S(2)}, u32[]{:S(2)}) collective-permute-start(f32[256,256]{1,0:T(8,128)S(1)} %get-tuple-element.94), channel_id=1, source_target_pairs={{0,4},{4,0},{8,12},{12,8},{16,20},{20,16},{24,28},{28,24},{1,5},{5... | collective-permute-start | bytes 786440 | tf_op jit(solution)/shard_map/ppermute | solution.py:269
  90.8 0.7 collective-permute-start.14
  91.5 12.5 %all_to_all.16.sums = f32[32,2,256]{2,1,0:T(2,128)S(1)} all-to-all(f32[32,2,256]{2,1,0:T(2,128)S(1)} %broadcast_in_dim.93), channel_id=1, replica_groups=mesh['sub'=8,'grp'=4] {'sub','grp'}, dimensions={0} | all-to-all | bytes 131072 | tf_op jit(solution)/shard_map/all_to_all | solution.py:277
  104.0 2.8 %shard_map.95 = (f32[256,256]{1,0:T(8,128)}, f32[4,256,256]{2,1,0:T(8,128)S(1)}, f32[256,256]{1,0:T(8,128)}, f32[4,256,256]{2,1,0:T(8,128)S(1)}, f32[256,512]{1,...) custom-call(s32[3]{0:T(128)S(1)} %copy-done.6, ...), custom_call_target="tpu_custom_call" | custom-call | tf_op jit(solution)/shard_map/pallas_call | solution.py:37
  106.7 2.3 %collective-permute-start.15 = (f32[256,256]{1,0:T(8,128)S(1)}, f32[256,256]{1,0:T(8,128)S(1)}, u32[]{:S(2)}, u32[]{:S(2)}) collective-permute-start(f32[256,256]{1,0:T(8,128)S(1)} %get-tuple-element.103), channel_id=1, source_target_pairs={{0,4},{4,0},{8,12},{12,8},{16,20},{20,16},{24,28},{28,24},{1,5},{5... | collective-permute-start | bytes 786440 | tf_op jit(solution)/shard_map/ppermute | solution.py:269
  109.0 0.7 collective-permute-start.16
  109.7 10.8 %collective-permute-done.15.near = f32[256,256]{1,0:T(8,128)S(1)} collective-permute-done((f32[256,256]{1,0:T(8,128)S(1)}, f32[256,256]{1,0:T(8,128)S(1)}, u32[]{:S(2)}, u32[]{:S(2)}) %collective-permute-start.15) | collective-permute-done | bytes 262176 | tf_op jit(solution)/shard_map/ppermute | solution.py:269
  120.5 1.3 shard_map.96
  121.8 6.5 %all_gather.11.everyone = f32[512,256]{1,0:T(8,128)S(1)} all-gather(f32[128,256]{1,0:T(8,128)S(1)} %get-tuple-element.108), channel_id=1, replica_groups=mesh['sub'=8,'grp'=4] {'grp'}, dimensions={0}, use_global_device_ids=true | all-gather | bytes 655360 | tf_op jit(solution)/shard_map/all_gather | solution.py:370
  128.3 3.5 %shard_map.97 = (f32[256,512]{1,0:T(8,128)S(1)}, f32[3,256,512]{2,1,0:T(8,128)S(1)}, f32[256,256]{1,0:T(8,128)}, f32[256,256]{1,0:T(8,128)}, f32[2,256]{1,0:T(2,128)S(1)}) custom-call(s32[3]{0:T(128)S(1)} %copy-done.6, f32[256,256]{1,0:T(8,128)S(1)} %get-tuple-element.105.edge, f32[4,256,256]{2,1,0:T(8,128)S(1)} %get-tuple-element.106.own.third_z, ...), custom_call_target="tpu_custom_call" | custom-call | tf_op jit(solution)/shard_map/pallas_call | solution.py:37
  131.9 1.3 collective-permute-start.17
  133.2 14.0 %all_to_all.17.sums = f32[32,2,256]{2,1,0:T(2,128)S(1)} all-to-all(f32[32,2,256]{2,1,0:T(2,128)S(1)} %broadcast_in_dim.94), channel_id=1, replica_groups=mesh['sub'=8,'grp'=4] {'sub','grp'}, dimensions={0} | all-to-all | bytes 131072 | tf_op jit(solution)/shard_map/all_to_all | solution.py:277
  147.2 0.0 collective-permute-done.17.following
  147.2 2.3 %shard_map.98 = (f32[4,256,256]{2,1,0:T(8,128)}, f32[4,256,256]{2,1,0:T(8,128)}) custom-call(s32[3]{0:T(128)S(1)} %copy-done.6, f32[256,512]{1,0:T(8,128)S(1)} %get-tuple-element.109.first, f32[3,256,512]{2,1,0:T(8,128)S(1)} %get-tuple-element.110.rest, f32[256,256]{1,0:T(8,128)S(1)} %collective-permute-done.17.following, ...), custom_call_target="tpu_custom_call" | custom-call | tf_op jit(solution)/shard_map/pallas_call | solution.py:37
  (29 shorter events, 0.2 us)
Async XLA Ops:
  0.6 11.4 %copy-start.3 = (f32[1,4,256,256]{3,2,1,0:T(8,128)S(1)}, f32[1,4,256,256]{3,2,1,0:T(8,128)}, u32[]{:S(2)}) copy-start(f32[1,4,256,256]{3,2,1,0:T(8,128)} %rhs.3) | copy-start | bytes 3145732
  3.6 15.4 %collective-permute-start = (f32[264,256]{1,0:T(8,128)}, f32[264,256]{1,0:T(8,128)S(1)}, u32[]{:S(2)}, u32[]{:S(2)}) collective-permute-start(f32[264,256]{1,0:T(8,128)} %shard_map.86), channel_id=1, source_target_pairs={{0,4},{4,8},{8,12},{12,16},{16,20},{20,24},{24,28},{1,5},{5,9},{9,... | collective-permute-start | bytes 811016 | tf_op jit(solution)/shard_map/ppermute | solution.py:328
  9.2 7.3 %collective-permute-start.3 = (s32[1,128]{1,0:T(1,128)S(1)}, s32[1,128]{1,0:T(1,128)S(1)}, u32[]{:S(2)}, u32[]{:S(2)}) collective-permute-start(s32[1,128]{1,0:T(1,128)S(1)} %reshape.31), channel_id=1, source_target_pairs={{0,3},{1,2},{2,1},{3,0},{4,7},{5,6},{6,5},{7,4},{8,11},{9,10},{10,... | collective-permute-start | bytes 1544 | tf_op jit(solution)/shard_map/ppermute | solution.py:285
  9.9 6.7 %collective-permute-start.2 = (s32[1,128]{1,0:T(1,128)S(1)}, s32[1,128]{1,0:T(1,128)S(1)}, u32[]{:S(2)}, u32[]{:S(2)}) collective-permute-start(s32[1,128]{1,0:T(1,128)S(1)} %reshape.31), channel_id=1, source_target_pairs={{0,2},{1,3},{2,0},{3,1},{4,6},{5,7},{6,4},{7,5},{8,10},{9,11},{10,... | collective-permute-start | bytes 1544 | tf_op jit(solution)/shard_map/ppermute | solution.py:285
  10.8 5.8 %collective-permute-start.1 = (s32[1,128]{1,0:T(1,128)S(1)}, s32[1,128]{1,0:T(1,128)S(1)}, u32[]{:S(2)}, u32[]{:S(2)}) collective-permute-start(s32[1,128]{1,0:T(1,128)S(1)} %reshape.31), channel_id=1, source_target_pairs={{0,1},{1,0},{2,3},{3,2},{4,5},{5,4},{6,7},{7,6},{8,9},{9,8},{10,11... | collective-permute-start | bytes 1544 | tf_op jit(solution)/shard_map/ppermute | solution.py:285
  12.0 1.6 %copy-start = (bf16[1,4,512,512]{3,2,1,0:T(8,128)(2,1)S(1)}, bf16[1,4,512,512]{3,2,1,0:T(8,128)(2,1)}, u32[]{:S(2)}) copy-start(bf16[1,4,512,512]{3,2,1,0:T(8,128)(2,1)} %param.10) | copy-start | bytes 6291460
  13.6 0.6 copy-start.5
  14.2 0.7 copy-start.7
  14.9 1.7 %copy-start.4 = (f32[1,256,1024]{2,1,0:T(8,128)S(1)}, f32[1,256,1024]{2,1,0:T(8,128)}, u32[]{:S(2)}) copy-start(f32[1,256,1024]{2,1,0:T(8,128)} %param.13) | copy-start | bytes 3145732
  14.9 1.7 %copy-start.6 = (s32[3]{0:T(128)S(1)}, s32[3]{0:T(128)}, u32[]{:S(2)}) copy-start(s32[3]{0:T(128)} %pad_add_fusion.1.places) | copy-start | bytes 40
  16.6 2.4 %copy-start.1 = (bf16[1,4,512,512]{3,2,1,0:T(8,128)(2,1)S(1)}, bf16[1,4,512,512]{3,2,1,0:T(8,128)(2,1)}, u32[]{:S(2)}) copy-start(bf16[1,4,512,512]{3,2,1,0:T(8,128)(2,1)} %param.10) | copy-start | bytes 6291460
  19.0 1.0 copy-start.8
  20.0 13.2 %collective-permute-start.4 = (f32[256,256]{1,0:T(8,128)S(1)}, f32[256,256]{1,0:T(8,128)S(1)}, u32[]{:S(2)}, u32[]{:S(2)}) collective-permute-start(f32[256,256]{1,0:T(8,128)S(1)} %get-tuple-element.68), channel_id=1, source_target_pairs={{0,4},{4,0},{8,12},{12,8},{16,20},{20,16},{24,28},{28,24},{1,5},{5... | collective-permute-start | bytes 786440 | tf_op jit(solution)/shard_map/ppermute | solution.py:269
  21.6 11.6 %collective-permute-start.5 = (f32[256,256]{1,0:T(8,128)S(1)}, f32[256,256]{1,0:T(8,128)S(1)}, u32[]{:S(2)}, u32[]{:S(2)}) collective-permute-start(f32[256,256]{1,0:T(8,128)S(1)} %get-tuple-element.69), channel_id=1, source_target_pairs={{4,8},{8,4},{12,16},{16,12},{20,24},{24,20},{5,9},{9,5},{13,17},{1... | collective-permute-start | bytes 786440 | tf_op jit(solution)/shard_map/ppermute | solution.py:270
  22.3 19.3 %collective-permute-start.6 = (f32[128,512]{1,0:T(8,128)S(1)}, f32[128,512]{1,0:T(8,128)S(1)}, u32[]{:S(2)}, u32[]{:S(2)}) collective-permute-start(f32[128,512]{1,0:T(8,128)S(1)} %get-tuple-element.118), channel_id=1, source_target_pairs={{0,1},{1,0},{2,3},{3,2},{4,5},{5,4},{6,7},{7,6},{8,9},{9,8},{10,11... | collective-permute-start | bytes 786440 | tf_op jit(solution)/shard_map/ppermute | solution.py:294
  22.4 19.2 %collective-permute-start.8 = (f32[128,512]{1,0:T(8,128)S(1)}, f32[128,512]{1,0:T(8,128)S(1)}, u32[]{:S(2)}, u32[]{:S(2)}) collective-permute-start(f32[128,512]{1,0:T(8,128)S(1)} %get-tuple-element.119), channel_id=1, source_target_pairs={{0,3},{1,2},{2,1},{3,0},{4,7},{5,6},{6,5},{7,4},{8,11},{9,10},{10,... | collective-permute-start | bytes 786440 | tf_op jit(solution)/shard_map/ppermute | solution.py:294
  24.0 17.6 %collective-permute-start.7 = (f32[128,512]{1,0:T(8,128)S(1)}, f32[128,512]{1,0:T(8,128)S(1)}, u32[]{:S(2)}, u32[]{:S(2)}) collective-permute-start(f32[128,512]{1,0:T(8,128)S(1)} %get-tuple-element.120), channel_id=1, source_target_pairs={{0,2},{1,3},{2,0},{3,1},{4,6},{5,7},{6,4},{7,5},{8,10},{9,11},{10,... | collective-permute-start | bytes 786440 | tf_op jit(solution)/shard_map/ppermute | solution.py:294
  34.4 7.3 %copy-start.2 = (bf16[1,4,512,512]{3,2,1,0:T(8,128)(2,1)S(1)}, bf16[1,4,512,512]{3,2,1,0:T(8,128)(2,1)}, u32[]{:S(2)}) copy-start(bf16[1,4,512,512]{3,2,1,0:T(8,128)(2,1)} %param.9) | copy-start | bytes 6291460
  44.8 16.6 %collective-permute-start.9 = (f32[256,256]{1,0:T(8,128)S(1)}, f32[256,256]{1,0:T(8,128)S(1)}, u32[]{:S(2)}, u32[]{:S(2)}) collective-permute-start(f32[256,256]{1,0:T(8,128)S(1)} %get-tuple-element.80), channel_id=1, source_target_pairs={{0,4},{4,0},{8,12},{12,8},{16,20},{20,16},{24,28},{28,24},{1,5},{5... | collective-permute-start | bytes 786440 | tf_op jit(solution)/shard_map/ppermute | solution.py:269
  47.8 13.5 %collective-permute-start.10 = (f32[256,256]{1,0:T(8,128)S(1)}, f32[256,256]{1,0:T(8,128)S(1)}, u32[]{:S(2)}, u32[]{:S(2)}) collective-permute-start(f32[256,256]{1,0:T(8,128)S(1)} %get-tuple-element.81), channel_id=1, source_target_pairs={{4,8},{8,4},{12,16},{16,12},{20,24},{24,20},{5,9},{9,5},{13,17},{1... | collective-permute-start | bytes 786440 | tf_op jit(solution)/shard_map/ppermute | solution.py:270
  63.5 13.8 %collective-permute-start.11 = (f32[256,256]{1,0:T(8,128)S(1)}, f32[256,256]{1,0:T(8,128)S(1)}, u32[]{:S(2)}, u32[]{:S(2)}) collective-permute-start(f32[256,256]{1,0:T(8,128)S(1)} %get-tuple-element.86), channel_id=1, source_target_pairs={{0,4},{4,0},{8,12},{12,8},{16,20},{20,16},{24,28},{28,24},{1,5},{5... | collective-permute-start | bytes 786440 | tf_op jit(solution)/shard_map/ppermute | solution.py:269
  65.9 11.5 %collective-permute-start.12 = (f32[256,256]{1,0:T(8,128)S(1)}, f32[256,256]{1,0:T(8,128)S(1)}, u32[]{:S(2)}, u32[]{:S(2)}) collective-permute-start(f32[256,256]{1,0:T(8,128)S(1)} %get-tuple-element.87), channel_id=1, source_target_pairs={{4,8},{8,4},{12,16},{16,12},{20,24},{24,20},{5,9},{9,5},{13,17},{1... | collective-permute-start | bytes 786440 | tf_op jit(solution)/shard_map/ppermute | solution.py:270
  88.3 15.7 %collective-permute-start.13 = (f32[256,256]{1,0:T(8,128)S(1)}, f32[256,256]{1,0:T(8,128)S(1)}, u32[]{:S(2)}, u32[]{:S(2)}) collective-permute-start(f32[256,256]{1,0:T(8,128)S(1)} %get-tuple-element.94), channel_id=1, source_target_pairs={{0,4},{4,0},{8,12},{12,8},{16,20},{20,16},{24,28},{28,24},{1,5},{5... | collective-permute-start | bytes 786440 | tf_op jit(solution)/shard_map/ppermute | solution.py:269
  90.8 13.2 %collective-permute-start.14 = (f32[256,256]{1,0:T(8,128)S(1)}, f32[256,256]{1,0:T(8,128)S(1)}, u32[]{:S(2)}, u32[]{:S(2)}) collective-permute-start(f32[256,256]{1,0:T(8,128)S(1)} %get-tuple-element.95), channel_id=1, source_target_pairs={{4,8},{8,4},{12,16},{16,12},{20,24},{24,20},{5,9},{9,5},{13,17},{1... | collective-permute-start | bytes 786440 | tf_op jit(solution)/shard_map/ppermute | solution.py:270
  106.7 13.7 %collective-permute-start.15 = (f32[256,256]{1,0:T(8,128)S(1)}, f32[256,256]{1,0:T(8,128)S(1)}, u32[]{:S(2)}, u32[]{:S(2)}) collective-permute-start(f32[256,256]{1,0:T(8,128)S(1)} %get-tuple-element.103), channel_id=1, source_target_pairs={{0,4},{4,0},{8,12},{12,8},{16,20},{20,16},{24,28},{28,24},{1,5},{5... | collective-permute-start | bytes 786440 | tf_op jit(solution)/shard_map/ppermute | solution.py:269
  109.0 11.5 %collective-permute-start.16 = (f32[256,256]{1,0:T(8,128)S(1)}, f32[256,256]{1,0:T(8,128)S(1)}, u32[]{:S(2)}, u32[]{:S(2)}) collective-permute-start(f32[256,256]{1,0:T(8,128)S(1)} %get-tuple-element.104), channel_id=1, source_target_pairs={{4,8},{8,4},{12,16},{16,12},{20,24},{24,20},{5,9},{9,5},{13,17},{1... | collective-permute-start | bytes 786440 | tf_op jit(solution)/shard_map/ppermute | solution.py:270
  131.9 15.3 %collective-permute-start.17 = (f32[256,256]{1,0:T(8,128)S(1)}, f32[256,256]{1,0:T(8,128)S(1)}, u32[]{:S(2)}, u32[]{:S(2)}) collective-permute-start(f32[256,256]{1,0:T(8,128)S(1)} %slice.19), channel_id=1, source_target_pairs={{4,0},{8,4},{12,8},{16,12},{20,16},{24,20},{28,24},{5,1},{9,5},{13... | collective-permute-start | bytes 786440 | tf_op jit(solution)/shard_map/ppermute | solution.py:387

commit v5 on v4

--- a/solution.py
+++ b/solution.py
@@ -33,12 +33,11 @@
     return lax.dot_general(first, second, dims, preferred_element_type=jnp.float32)
 
 
-def call(kernel, out_shapes, *operands, scalars=1):
+def call(kernel, out_shapes, *operands):
     return pl.pallas_call(
         kernel,
         out_shape=[jax.ShapeDtypeStruct(shape, jnp.float32) for shape in out_shapes],
-        in_specs=[pl.BlockSpec(memory_space=pltpu.SMEM)] * scalars
-        + [pl.BlockSpec(memory_space=pltpu.VMEM)] * (len(operands) - scalars),
+        in_specs=[pl.BlockSpec(memory_space=pltpu.VMEM)] * len(operands),
         out_specs=[pl.BlockSpec(memory_space=pltpu.VMEM)] * len(out_shapes),
         compiler_params=pltpu.CompilerParams(vmem_limit_bytes=VMEM_LIMIT),
     )(*operands)
@@ -110,28 +109,38 @@
     return rz_now, rz_now / (curvature - beta * rz_now / before[1:2]), beta
 
 
-def tail_kernel(places, counts, rhs, tail, face, done):
+def even_place():
+    return lax.rem(lax.axis_index("sub"), 2) == 0
+
+
+def live_rows(counts, sub, rows, width):
+    last = lax.axis_index("sub") == lax.axis_size("sub") - 1
+    count = jnp.broadcast_to(counts[:, sub : sub + 1], (rows, width))
+    if sub == counts.shape[1] - 1:
+        count = jnp.where(last, 0, count)
+    return (lax.broadcasted_iota(jnp.int32, (rows, width), 1) < count).astype(jnp.float32)
+
+
+def tail_kernel(counts_ref, rhs, tail, counts, face, counts_done, face_done):
     loads, width = rhs.shape[2:]
-    copy = pltpu.make_async_copy(rhs.at[0, rhs.shape[1] - 1], face, done)
-    copy.start()
-    last = jnp.where(places[2] == 1, 0, counts[0, counts.shape[1] - 1])
-    mask = (lax.broadcasted_iota(jnp.int32, (8, width), 1) < last).astype(jnp.float32)
+    counts_copy = pltpu.make_async_copy(counts_ref, counts, counts_done)
+    face_copy = pltpu.make_async_copy(rhs.at[0, rhs.shape[1] - 1], face, face_done)
+    counts_copy.start()
+    face_copy.start()
+    counts_copy.wait()
+    mask = live_rows(counts, counts.shape[1] - 1, 8, width)
     tail[loads:] = mask
-    copy.wait()
+    face_copy.wait()
     tail[:loads] = mask[:1] * face[...]
 
 
-def early_kernel(places, counts, rhs, panel, live, own, partial, rest):
+def early_kernel(counts, rhs, panel, live, own, partial, rest):
     subs, loads, width = own.shape
-    positions = lax.broadcasted_iota(jnp.int32, (1, width), 1)
     parts = [None]
     for sub in range(subs):
-        count = counts[0, sub]
-        if sub == subs - 1:
-            count = jnp.where(places[2] == 1, 0, count)
-        mask = (positions < count).astype(jnp.float32)
+        mask = live_rows(counts, sub, 1, width)
         live[sub] = mask
-        own[sub] = mask * rhs[0, sub]
+        own[sub] = mask * rhs[sub]
         parts.append(split(own[sub]))
     partial[...] = mul(parts[1][0], panel[0, width:]) + mul(parts[1][1], panel[0, width:])
     for sub in range(1, subs):
@@ -140,20 +149,20 @@
         rest[sub - 1] = mul(high, panel[sub]) + mul(low, panel[sub])
 
 
-def head_kernel(places, head, partial, rest, panel, live, edge, first, near_out, far_out):
+def head_kernel(head, partial, rest, panel, live, edge, first, near_out, far_out):
     loads, width = edge.shape
     live[...] = head[loads : loads + 1]
     edge[...] = head[:loads]
     high, low = split(head[:loads])
     first[...] = partial[...] - mul(high, panel[0, :width]) - mul(low, panel[0, :width])
     last = rest[rest.shape[0] - 1]
-    send_faces(places[0] == 1, first[...], last, near_out, far_out)
-
-
-def pick_kernel(places, everyone, coarse, picked):
+    send_faces(even_place(), first[...], last, near_out, far_out)
+
+
+def pick_kernel(everyone, coarse, picked):
     group, own = everyone.shape[0], everyone.shape[2]
     rows, size = coarse.shape
-    grp = places[1]
+    grp = lax.axis_index("grp")
     high, low = split(coarse[...])
     unknowns = lax.broadcasted_iota(jnp.int32, (size, own), 0)
     columns = []
@@ -170,9 +179,9 @@
         ) + lax.dot_general(chosen, low, dims, preferred_element_type=jnp.float32)
 
 
-def corner_kernel(places, first, rest, near, far, live_first, live_rest, coupling,
+def corner_kernel(first, rest, near, far, live_first, live_rest, coupling,
                   edge, own, corners):
-    even = places[0] == 1
+    even = even_place()
     subs, rows = coupling.shape[0], coupling.shape[1] // 2
     result, live, edges = Joined(first, rest), Joined(live_first, live_rest), Joined(edge, own)
     parts = []
@@ -188,9 +197,9 @@
         )
 
 
-def dual_kernel(places, edge, own, residual, panel, everyone, block, lift,
+def dual_kernel(edge, own, residual, panel, everyone, block, lift,
                 first, rest, near_out, far_out, sums):
-    even = places[0] == 1
+    even = even_place()
     subs, width = panel.shape[0], edge.shape[1]
     edges, result = Joined(edge, own), Joined(first, rest)
     rows = block.shape[0] // 2
@@ -211,11 +220,11 @@
     sums[...] = jnp.concatenate([row_sums(product), row_sums(curvature)], axis=0)
 
 
-def update_kernel(step, places, first, rest, near, far, live_first, live_rest, sums, before,
+def update_kernel(step, first, rest, near, far, live_first, live_rest, sums, before,
                   old_edge, old_own, residual_edge, residual_own, panel,
                   image_edge, image_own, new_edge, new_own,
                   first_new, rest_new, near_out, far_out, scalars):
-    even = places[0] == 1
+    even = even_place()
     subs, width = panel.shape[0], near.shape[1]
     result, live = Joined(first, rest), Joined(live_first, live_rest)
     image_old, residual = Joined(old_edge, old_own), Joined(residual_edge, residual_own)
@@ -237,7 +246,7 @@
     send_faces(even, result_new[0], result_new[subs - 1], near_out, far_out)
 
 
-def last_kernel(step, places, first, rest, following, live, sums, before, older, image_old,
+def last_kernel(step, first, rest, following, live, sums, before, older, image_old,
                 residual, first_z, second_z, third_z, multipliers, residual_new):
     subs, width = residual.shape[0], following.shape[1]
     result = Joined(first, rest)
@@ -295,53 +304,56 @@
     return block
 
 
-def make_tail(places, counts, rhs):
+def make_tail(counts, rhs):
     loads, width = rhs.shape[2:]
     return pl.pallas_call(
         tail_kernel,
         out_shape=jax.ShapeDtypeStruct((loads + 8, width), jnp.float32),
         in_specs=[
-            pl.BlockSpec(memory_space=pltpu.SMEM),
-            pl.BlockSpec(memory_space=pltpu.SMEM),
+            pl.BlockSpec(memory_space=pltpu.HBM),
             pl.BlockSpec(memory_space=pltpu.HBM),
         ],
         out_specs=pl.BlockSpec(memory_space=pltpu.VMEM),
-        scratch_shapes=[pltpu.VMEM((loads, width), jnp.float32), pltpu.SemaphoreType.DMA],
+        scratch_shapes=[
+            pltpu.VMEM(counts.shape, counts.dtype),
+            pltpu.VMEM((loads, width), jnp.float32),
+            pltpu.SemaphoreType.DMA,
+            pltpu.SemaphoreType.DMA,
+        ],
         compiler_params=pltpu.CompilerParams(vmem_limit_bytes=TAIL_LIMIT),
-    )(places, counts, rhs)
+    )(counts, rhs)
 
 
 def local(rhs, counts, solve_panel, dirichlet_panel, coupling, corner_map, coarse_inverse):
     subs, loads, width = rhs.shape[1:]
     corners = coupling.shape[2]
     solve, dirichlet, couple = solve_panel[0], dirichlet_panel[0], coupling[0]
-    place, size = lax.axis_index("sub"), lax.axis_size("sub")
-    places = jnp.stack([1 - place % 2, lax.axis_index("grp"), place == size - 1]).astype(jnp.int32)
+    size = lax.axis_size("sub")
 
     face_shape, own_shape = (loads, width), (subs, loads, width)
     first_shape, rest_shape = (loads, 2 * width), (subs - 1, loads, 2 * width)
     edges_shapes = [face_shape, own_shape]
     result_shapes = [first_shape, rest_shape, face_shape, face_shape]
 
-    tail = make_tail(places, counts, rhs)
-    tail, places, corner_map = lax.optimization_barrier((tail, places, corner_map))
+    tail = make_tail(counts, rhs)
+    tail, counts, corner_map = lax.optimization_barrier((tail, counts, corner_map))
     head = lax.ppermute(tail, "sub", [(i, i + 1) for i in range(size - 1)])
     everyone = from_group(corner_map.reshape(1, subs * corners))
     live_own, residual_own, partial, rest = call(
         early_kernel,
         [(subs, 1, width), own_shape, first_shape, rest_shape],
-        places, counts, rhs, dirichlet, scalars=2,
+        counts, rhs[0], dirichlet,
     )
     group = everyone.shape[0]
     (picked,) = call(
         pick_kernel, [(group, subs * corners, group * subs * corners)],
-        places, everyone, coarse_inverse[0],
+        everyone, coarse_inverse[0],
     )
     head, picked, rest = lax.optimization_barrier((head, picked, rest))
     live_edge, residual_edge, first, near, far = call(
         head_kernel,
         [(1, width), face_shape, first_shape, face_shape, face_shape],
-        places, head, partial, rest, dirichlet,
+        head, partial, rest, dirichlet,
     )
     first, couple = lax.optimization_barrier((first, couple))
     block = jnp.concatenate(split_outside(swap_blocks(picked)), axis=0)
@@ -364,14 +376,14 @@
         edge, own, values = call(
             corner_kernel,
             edges_shapes + [(subs * corners, loads)],
-            places, first, rest, near, far, *live, stacked,
+            first, rest, near, far, *live, stacked,
         )
         preconds.append(own)
         everyone = lax.all_gather(values, "grp", tiled=True)
         first, rest, near, far, sums = call(
             dual_kernel,
             result_shapes + [(2, loads)],
-            places, edge, own, residual[1], solve, everyone, block, lift,
+            edge, own, residual[1], solve, everyone, block, lift,
         )
         sums = from_all(sums)
         if step + 1 < ITERS:
@@ -379,7 +391,7 @@
             *new, first, rest, near, far, now = call(
                 functools.partial(update_kernel, step),
                 edges_shapes + edges_shapes + result_shapes + [(2, loads)],
-                places, first, rest, near, far, *live, sums, scalars[-1],
+                first, rest, near, far, *live, sums, scalars[-1],
                 *image, *residual, dirichlet,
             )
             image, residual = new[:2], new[2:]
@@ -388,7 +400,7 @@
     multipliers, residual = call(
         functools.partial(last_kernel, ITERS - 1),
         [own_shape] * 2,
-        places, first, rest, following, live[1], sums, scalars[-1], scalars[-2],
+        first, rest, following, live[1], sums, scalars[-1], scalars[-2],
         image[1], residual[1], *preconds,
     )
     return (multipliers[None], residual[None])

time: 150 us -> 143 us (0.953)
  Pallas kernels: 28 us -> 20.7 us
    pallas_call x12, Pallas kernels: 25.7 us -> 18.9 us  [call(): pl.pallas_call(kernel, out_shape=[jax.ShapeDtypeStruct(shape, jnp.float32...]
  transfers between devices with their start and end apart: 18 -> 18, of which waited for: 3 -> 3; matrix products, arithmetic and copies ran while one was open for 1% -> 1% of each run, Pallas kernels for 4% -> 3%
where the time goes in v5:
time: 143 us; the launch traced here: 142 us
  blocking collectives  59.5 us (42%)
  waiting for transfers between devices  29.9 us (21%)
  starting transfers between devices  25.9 us (18%)
  Pallas kernels  20.7 us (14%)
  local copies, waits for them, and re-layouts  4.72 us (3%)
    all_to_all x3, blocking collectives, from_all(): return lax.all_to_all(copies, ('sub', 'grp'), 0, 0)  39.3 us
    ppermute x5, waiting for transfers between devices, swap(): lax.ppermute(near, 'sub', neighbour_pairs(size, 0))  29.9 us
    all_gather x3, blocking collectives, local(): everyone = lax.all_gather(values, 'grp', tiled=True)  20.1 us
    pallas_call x12, Pallas kernels, call(): pl.pallas_call(kernel, out_shape=[jax.ShapeDtypeStruct(shape, jnp.float32...  18.9 us
    ppermute x5, starting transfers between devices, swap(): lax.ppermute(near, 'sub', neighbour_pairs(size, 0))  12.4 us
    ppermute x1, starting transfers between devices, local(): head = lax.ppermute(tail, 'sub', [(i, i + 1) for i in range(size - 1)])  4.86 us
    ppermute x5, starting transfers between devices, swap(): lax.ppermute(far, 'sub', neighbour_pairs(size, 1))  3.33 us
    unnamed x14, local copies, waits for them, and re-layouts  2.9 us
  transfers between devices with their start and end apart: 18, of which 3 were waited for; matrix products, arithmetic and copies ran while one was open for 1% of the time, Pallas kernels for 3%

profile of v5, /device:TPU:0, one launch (start us, length us, event | category | flops | bytes accessed | tf_op | source)
XLA Modules:
  0.0 142.2 jit_solution(14838956065329420681)
XLA Ops:
  0.6 1.8 %shard_map.86 = f32[264,256]{1,0:T(8,128)} custom-call(s32[1,4]{1,0:T(1,128)} %counts, f32[1,4,256,256]{3,2,1,0:T(8,128)} %rhs.1), custom_call_target="tpu_custom_call" | custom-call | tf_op jit(solution)/shard_map/pallas_call | solution.py:309
  2.4 4.9 %collective-permute-start = (f32[264,256]{1,0:T(8,128)}, f32[264,256]{1,0:T(8,128)S(1)}, u32[]{:S(2)}, u32[]{:S(2)}) collective-permute-start(f32[264,256]{1,0:T(8,128)} %shard_map.86), channel_id=1, source_target_pairs={{0,4},{4,8},{8,12},{12,16},{16,20},{20,24},{24,28},{1,5},{5,9},{9,... | collective-permute-start | bytes 811016 | tf_op jit(solution)/shard_map/ppermute | solution.py:340
  7.3 0.8 reshape.31
  8.1 0.7 collective-permute-start.3
  8.8 0.9 collective-permute-start.2
  9.6 0.3 collective-permute-start.1
  9.9 0.8 stack_reshape.3
  10.7 0.1 broadcast_in_dim.83
  10.8 0.1 broadcast_in_dim.84
  10.9 1.6 %copy-done = bf16[1,4,512,512]{3,2,1,0:T(8,128)(2,1)S(1)} copy-done((bf16[1,4,512,512]{3,2,1,0:T(8,128)(2,1)S(1)}, bf16[1,4,512,512]{3,2,1,0:T(8,128)(2,1)}, u32[]{:S(2)}) %copy-start) | copy-done | bytes 2097176
  12.5 0.7 copy-done.5
  13.1 1.2 shard_map.88
  14.3 0.0 copy-start.1
  14.3 0.0 collective-permute-done.3
  14.3 0.0 collective-permute-done.2
  14.4 0.0 collective-permute-done.1
  14.4 1.8 %shard_map.87 = f32[4,128,512]{2,1,0:T(8,128)S(1)} custom-call(s32[4,1,128]{2,1,0:T(1,128)S(1)} %pad_add_fusion.everyone, f32[256,1024]{1,0:T(8,128)S(1)} %bitcast.35), custom_call_target="tpu_custom_call" | custom-call | tf_op jit(solution)/shard_map/pallas_call | solution.py:37
  16.2 0.0 collective-permute-done.head
  16.2 0.0 copy-start.6
  16.2 0.3 shard_map.89
  16.5 0.6 copy-done.6
  17.2 1.6 %collective-permute-start.4 = (f32[256,256]{1,0:T(8,128)S(1)}, f32[256,256]{1,0:T(8,128)S(1)}, u32[]{:S(2)}, u32[]{:S(2)}) collective-permute-start(f32[256,256]{1,0:T(8,128)S(1)} %get-tuple-element.68), channel_id=1, source_target_pairs={{0,4},{4,0},{8,12},{12,8},{16,20},{20,16},{24,28},{28,24},{1,5},{5... | collective-permute-start | bytes 786440 | tf_op jit(solution)/shard_map/ppermute | solution.py:278
  18.8 0.7 collective-permute-start.5
  19.5 0.1 slice_bitcast_fusion.2
  19.5 0.1 collective-permute-start.6
  19.6 1.6 %collective-permute-start.8 = (f32[128,512]{1,0:T(8,128)S(1)}, f32[128,512]{1,0:T(8,128)S(1)}, u32[]{:S(2)}, u32[]{:S(2)}) collective-permute-start(f32[128,512]{1,0:T(8,128)S(1)} %get-tuple-element.119), channel_id=1, source_target_pairs={{0,3},{1,2},{2,1},{3,0},{4,7},{5,6},{6,5},{7,4},{8,11},{9,10},{10,... | collective-permute-start | bytes 786440 | tf_op jit(solution)/shard_map/ppermute | solution.py:303
  21.3 0.5 collective-permute-start.7
  21.8 0.1 bitcast_select_fusion.1
  21.9 0.1 pad_maximum_fusion.lift
  22.1 8.3 %collective-permute-done.4.near = f32[256,256]{1,0:T(8,128)S(1)} collective-permute-done((f32[256,256]{1,0:T(8,128)S(1)}, f32[256,256]{1,0:T(8,128)S(1)}, u32[]{:S(2)}, u32[]{:S(2)}) %collective-permute-start.4) | collective-permute-done | bytes 262176 | tf_op jit(solution)/shard_map/ppermute | solution.py:278
  30.4 0.0 collective-permute-done.5.far
  30.4 0.7 shard_map.90
  31.1 0.0 copy-start.2
  31.1 7.1 %all_gather.9.everyone = f32[512,256]{1,0:T(8,128)S(1)} all-gather(f32[128,256]{1,0:T(8,128)S(1)} %get-tuple-element.76), channel_id=1, replica_groups=mesh['sub'=8,'grp'=4] {'grp'}, dimensions={0}, use_global_device_ids=true | all-gather | bytes 655360 | tf_op jit(solution)/shard_map/all_gather | solution.py:382
  38.2 0.0 collective-permute-done.6
  38.2 0.0 collective-permute-done.8
  38.2 0.0 collective-permute-done.7
  38.2 0.1 reduce-precision_convert_fusion
  38.4 2.5 %shard_map.91 = (f32[256,512]{1,0:T(8,128)S(1)}, f32[3,256,512]{2,1,0:T(8,128)S(1)}, f32[256,256]{1,0:T(8,128)S(1)}, f32[256,256]{1,0:T(8,128)S(1)}, f32[2,256]{1,0:T(2,128)S(1)}) custom-call(f32[256,256]{1,0:T(8,128)S(1)} %get-tuple-element.73.edge, f32[4,256,256]{2,1,0:T(8,128)S(1)} %get-tuple-element.74.own.first_z, ...), custom_call_target="tpu_custom_call" | custom-call | tf_op jit(solution)/shard_map/pallas_call | solution.py:37
  40.9 3.6 %collective-permute-start.9 = (f32[256,256]{1,0:T(8,128)S(1)}, f32[256,256]{1,0:T(8,128)S(1)}, u32[]{:S(2)}, u32[]{:S(2)}) collective-permute-start(f32[256,256]{1,0:T(8,128)S(1)} %get-tuple-element.80), channel_id=1, source_target_pairs={{0,4},{4,0},{8,12},{12,8},{16,20},{20,16},{24,28},{28,24},{1,5},{5... | collective-permute-start | bytes 786440 | tf_op jit(solution)/shard_map/ppermute | solution.py:278
  44.5 0.7 collective-permute-start.10
  45.2 12.8 %all_to_all.15.sums = f32[32,2,256]{2,1,0:T(2,128)S(1)} all-to-all(f32[32,2,256]{2,1,0:T(2,128)S(1)} %broadcast_in_dim.91), channel_id=1, replica_groups=mesh['sub'=8,'grp'=4] {'sub','grp'}, dimensions={0} | all-to-all | bytes 131072 | tf_op jit(solution)/shard_map/all_to_all | solution.py:286
  58.0 1.5 %shard_map.92 = (f32[256,256]{1,0:T(8,128)S(1)}, f32[4,256,256]{2,1,0:T(8,128)S(1)}, f32[256,256]{1,0:T(8,128)S(1)}, f32[4,256,256]{2,1,0:T(8,128)S(1)}, f32[256...) custom-call(f32[256,512]{1,0:T(8,128)S(1)} %get-tuple-element.78.fir, ...), custom_call_target="tpu_custom_call" | custom-call | tf_op jit(solution)/shard_map/pallas_call | solution.py:37
  59.6 2.3 %collective-permute-start.11 = (f32[256,256]{1,0:T(8,128)S(1)}, f32[256,256]{1,0:T(8,128)S(1)}, u32[]{:S(2)}, u32[]{:S(2)}) collective-permute-start(f32[256,256]{1,0:T(8,128)S(1)} %get-tuple-element.86), channel_id=1, source_target_pairs={{0,4},{4,0},{8,12},{12,8},{16,20},{20,16},{24,28},{28,24},{1,5},{5... | collective-permute-start | bytes 786440 | tf_op jit(solution)/shard_map/ppermute | solution.py:278
  61.9 0.7 collective-permute-start.12
  62.6 10.8 %collective-permute-done.11.near = f32[256,256]{1,0:T(8,128)S(1)} collective-permute-done((f32[256,256]{1,0:T(8,128)S(1)}, f32[256,256]{1,0:T(8,128)S(1)}, u32[]{:S(2)}, u32[]{:S(2)}) %collective-permute-start.11) | collective-permute-done | bytes 262176 | tf_op jit(solution)/shard_map/ppermute | solution.py:278
  73.4 0.7 shard_map.93
  74.1 6.5 %all_gather.10.everyone = f32[512,256]{1,0:T(8,128)S(1)} all-gather(f32[128,256]{1,0:T(8,128)S(1)} %get-tuple-element.91), channel_id=1, replica_groups=mesh['sub'=8,'grp'=4] {'grp'}, dimensions={0}, use_global_device_ids=true | all-gather | bytes 655360 | tf_op jit(solution)/shard_map/all_gather | solution.py:382
  80.6 2.4 %shard_map.94 = (f32[256,512]{1,0:T(8,128)S(1)}, f32[3,256,512]{2,1,0:T(8,128)S(1)}, f32[256,256]{1,0:T(8,128)S(1)}, f32[256,256]{1,0:T(8,128)S(1)}, f32[2,256]{1,0:T(2,128)S(1)}) custom-call(f32[256,256]{1,0:T(8,128)S(1)} %get-tuple-element.88.edge, f32[4,256,256]{2,1,0:T(8,128)S(1)} %get-tuple-element.89.own.second_z, ...), custom_call_target="tpu_custom_call" | custom-call | tf_op jit(solution)/shard_map/pallas_call | solution.py:37
  83.1 2.5 %collective-permute-start.13 = (f32[256,256]{1,0:T(8,128)S(1)}, f32[256,256]{1,0:T(8,128)S(1)}, u32[]{:S(2)}, u32[]{:S(2)}) collective-permute-start(f32[256,256]{1,0:T(8,128)S(1)} %get-tuple-element.94), channel_id=1, source_target_pairs={{0,4},{4,0},{8,12},{12,8},{16,20},{20,16},{24,28},{28,24},{1,5},{5... | collective-permute-start | bytes 786440 | tf_op jit(solution)/shard_map/ppermute | solution.py:278
  85.6 0.7 collective-permute-start.14
  86.3 12.5 %all_to_all.16.sums = f32[32,2,256]{2,1,0:T(2,128)S(1)} all-to-all(f32[32,2,256]{2,1,0:T(2,128)S(1)} %broadcast_in_dim.93), channel_id=1, replica_groups=mesh['sub'=8,'grp'=4] {'sub','grp'}, dimensions={0} | all-to-all | bytes 131072 | tf_op jit(solution)/shard_map/all_to_all | solution.py:286
  98.8 0.0 collective-permute-done.13.near
  98.8 2.2 %shard_map.95 = (f32[256,256]{1,0:T(8,128)}, f32[4,256,256]{2,1,0:T(8,128)S(1)}, f32[256,256]{1,0:T(8,128)}, f32[4,256,256]{2,1,0:T(8,128)S(1)}, f32[256,512]{1,...) custom-call(f32[256,512]{1,0:T(8,128)S(1)} %get-tuple-element.92.fir, ...), custom_call_target="tpu_custom_call" | custom-call | tf_op jit(solution)/shard_map/pallas_call | solution.py:37
  101.0 2.3 %collective-permute-start.15 = (f32[256,256]{1,0:T(8,128)S(1)}, f32[256,256]{1,0:T(8,128)S(1)}, u32[]{:S(2)}, u32[]{:S(2)}) collective-permute-start(f32[256,256]{1,0:T(8,128)S(1)} %get-tuple-element.103), channel_id=1, source_target_pairs={{0,4},{4,0},{8,12},{12,8},{16,20},{20,16},{24,28},{28,24},{1,5},{5... | collective-permute-start | bytes 786440 | tf_op jit(solution)/shard_map/ppermute | solution.py:278
  103.3 0.7 collective-permute-start.16
  104.0 10.8 %collective-permute-done.15.near = f32[256,256]{1,0:T(8,128)S(1)} collective-permute-done((f32[256,256]{1,0:T(8,128)S(1)}, f32[256,256]{1,0:T(8,128)S(1)}, u32[]{:S(2)}, u32[]{:S(2)}) %collective-permute-start.15) | collective-permute-done | bytes 262176 | tf_op jit(solution)/shard_map/ppermute | solution.py:278
  114.7 0.0 collective-permute-done.16.far
  114.8 0.8 shard_map.96
  115.5 6.5 %all_gather.11.everyone = f32[512,256]{1,0:T(8,128)S(1)} all-gather(f32[128,256]{1,0:T(8,128)S(1)} %get-tuple-element.108), channel_id=1, replica_groups=mesh['sub'=8,'grp'=4] {'grp'}, dimensions={0}, use_global_device_ids=true | all-gather | bytes 655360 | tf_op jit(solution)/shard_map/all_gather | solution.py:382
  122.0 3.0 %shard_map.97 = (f32[256,512]{1,0:T(8,128)S(1)}, f32[3,256,512]{2,1,0:T(8,128)S(1)}, f32[256,256]{1,0:T(8,128)}, f32[256,256]{1,0:T(8,128)}, f32[2,256]{1,0:T(2,128)S(1)}) custom-call(f32[256,256]{1,0:T(8,128)S(1)} %get-tuple-element.105.edge, f32[4,256,256]{2,1,0:T(8,128)S(1)} %get-tuple-element.106.own.third_z, ...), custom_call_target="tpu_custom_call" | custom-call | tf_op jit(solution)/shard_map/pallas_call | solution.py:37
  125.0 1.3 collective-permute-start.17
  126.3 14.0 %all_to_all.17.sums = f32[32,2,256]{2,1,0:T(2,128)S(1)} all-to-all(f32[32,2,256]{2,1,0:T(2,128)S(1)} %broadcast_in_dim.94), channel_id=1, replica_groups=mesh['sub'=8,'grp'=4] {'sub','grp'}, dimensions={0} | all-to-all | bytes 131072 | tf_op jit(solution)/shard_map/all_to_all | solution.py:286
  140.4 1.8 %shard_map.98 = (f32[4,256,256]{2,1,0:T(8,128)}, f32[4,256,256]{2,1,0:T(8,128)}) custom-call(f32[256,512]{1,0:T(8,128)S(1)} %get-tuple-element.109.first, f32[3,256,512]{2,1,0:T(8,128)S(1)} %get-tuple-element.110.rest, f32[256,256]{1,0:T(8,128)S(1)} %collective-permute-done.17.following, f32[4,1,256]{2,1,0:T(1,128)S(1)} %get-tuple-element.71.live_rest.live, ...), custom_call_target="tpu_custom_call" | custom-call | tf_op jit(solution)/shard_map/pallas_call | solution.py:37
  (24 shorter events, 0.2 us)
Async XLA Ops:
  0.6 10.2 %copy-start.3 = (f32[1,4,256,256]{3,2,1,0:T(8,128)S(1)}, f32[1,4,256,256]{3,2,1,0:T(8,128)}, u32[]{:S(2)}) copy-start(f32[1,4,256,256]{3,2,1,0:T(8,128)} %rhs.1) | copy-start | bytes 3145732
  2.4 13.8 %collective-permute-start = (f32[264,256]{1,0:T(8,128)}, f32[264,256]{1,0:T(8,128)S(1)}, u32[]{:S(2)}, u32[]{:S(2)}) collective-permute-start(f32[264,256]{1,0:T(8,128)} %shard_map.86), channel_id=1, source_target_pairs={{0,4},{4,8},{8,12},{12,16},{16,20},{20,24},{24,28},{1,5},{5,9},{9,... | collective-permute-start | bytes 811016 | tf_op jit(solution)/shard_map/ppermute | solution.py:340
  8.1 6.3 %collective-permute-start.3 = (s32[1,128]{1,0:T(1,128)S(1)}, s32[1,128]{1,0:T(1,128)S(1)}, u32[]{:S(2)}, u32[]{:S(2)}) collective-permute-start(s32[1,128]{1,0:T(1,128)S(1)} %reshape.31), channel_id=1, source_target_pairs={{0,3},{1,2},{2,1},{3,0},{4,7},{5,6},{6,5},{7,4},{8,11},{9,10},{10,... | collective-permute-start | bytes 1544 | tf_op jit(solution)/shard_map/ppermute | solution.py:294
  8.8 5.6 %collective-permute-start.2 = (s32[1,128]{1,0:T(1,128)S(1)}, s32[1,128]{1,0:T(1,128)S(1)}, u32[]{:S(2)}, u32[]{:S(2)}) collective-permute-start(s32[1,128]{1,0:T(1,128)S(1)} %reshape.31), channel_id=1, source_target_pairs={{0,2},{1,3},{2,0},{3,1},{4,6},{5,7},{6,4},{7,5},{8,10},{9,11},{10,... | collective-permute-start | bytes 1544 | tf_op jit(solution)/shard_map/ppermute | solution.py:294
  9.6 4.7 %collective-permute-start.1 = (s32[1,128]{1,0:T(1,128)S(1)}, s32[1,128]{1,0:T(1,128)S(1)}, u32[]{:S(2)}, u32[]{:S(2)}) collective-permute-start(s32[1,128]{1,0:T(1,128)S(1)} %reshape.31), channel_id=1, source_target_pairs={{0,1},{1,0},{2,3},{3,2},{4,5},{5,4},{6,7},{7,6},{8,9},{9,8},{10,11... | collective-permute-start | bytes 1544 | tf_op jit(solution)/shard_map/ppermute | solution.py:294
  10.9 1.6 %copy-start = (bf16[1,4,512,512]{3,2,1,0:T(8,128)(2,1)S(1)}, bf16[1,4,512,512]{3,2,1,0:T(8,128)(2,1)}, u32[]{:S(2)}) copy-start(bf16[1,4,512,512]{3,2,1,0:T(8,128)(2,1)} %param.10) | copy-start | bytes 6291460
  12.5 0.7 copy-start.5
  13.1 1.3 copy-start.4
  14.3 1.9 %copy-start.1 = (bf16[1,4,512,512]{3,2,1,0:T(8,128)(2,1)S(1)}, bf16[1,4,512,512]{3,2,1,0:T(8,128)(2,1)}, u32[]{:S(2)}) copy-start(bf16[1,4,512,512]{3,2,1,0:T(8,128)(2,1)} %param.10) | copy-start | bytes 6291460
  16.2 1.0 copy-start.6
  17.2 13.2 %collective-permute-start.4 = (f32[256,256]{1,0:T(8,128)S(1)}, f32[256,256]{1,0:T(8,128)S(1)}, u32[]{:S(2)}, u32[]{:S(2)}) collective-permute-start(f32[256,256]{1,0:T(8,128)S(1)} %get-tuple-element.68), channel_id=1, source_target_pairs={{0,4},{4,0},{8,12},{12,8},{16,20},{20,16},{24,28},{28,24},{1,5},{5... | collective-permute-start | bytes 786440 | tf_op jit(solution)/shard_map/ppermute | solution.py:278
  18.8 11.6 %collective-permute-start.5 = (f32[256,256]{1,0:T(8,128)S(1)}, f32[256,256]{1,0:T(8,128)S(1)}, u32[]{:S(2)}, u32[]{:S(2)}) collective-permute-start(f32[256,256]{1,0:T(8,128)S(1)} %get-tuple-element.69), channel_id=1, source_target_pairs={{4,8},{8,4},{12,16},{16,12},{20,24},{24,20},{5,9},{9,5},{13,17},{1... | collective-permute-start | bytes 786440 | tf_op jit(solution)/shard_map/ppermute | solution.py:279
  19.5 18.7 %collective-permute-start.6 = (f32[128,512]{1,0:T(8,128)S(1)}, f32[128,512]{1,0:T(8,128)S(1)}, u32[]{:S(2)}, u32[]{:S(2)}) collective-permute-start(f32[128,512]{1,0:T(8,128)S(1)} %get-tuple-element.118), channel_id=1, source_target_pairs={{0,1},{1,0},{2,3},{3,2},{4,5},{5,4},{6,7},{7,6},{8,9},{9,8},{10,11... | collective-permute-start | bytes 786440 | tf_op jit(solution)/shard_map/ppermute | solution.py:303
  19.6 18.6 %collective-permute-start.8 = (f32[128,512]{1,0:T(8,128)S(1)}, f32[128,512]{1,0:T(8,128)S(1)}, u32[]{:S(2)}, u32[]{:S(2)}) collective-permute-start(f32[128,512]{1,0:T(8,128)S(1)} %get-tuple-element.119), channel_id=1, source_target_pairs={{0,3},{1,2},{2,1},{3,0},{4,7},{5,6},{6,5},{7,4},{8,11},{9,10},{10,... | collective-permute-start | bytes 786440 | tf_op jit(solution)/shard_map/ppermute | solution.py:303
  21.3 17.0 %collective-permute-start.7 = (f32[128,512]{1,0:T(8,128)S(1)}, f32[128,512]{1,0:T(8,128)S(1)}, u32[]{:S(2)}, u32[]{:S(2)}) collective-permute-start(f32[128,512]{1,0:T(8,128)S(1)} %get-tuple-element.120), channel_id=1, source_target_pairs={{0,2},{1,3},{2,0},{3,1},{4,6},{5,7},{6,4},{7,5},{8,10},{9,11},{10,... | collective-permute-start | bytes 786440 | tf_op jit(solution)/shard_map/ppermute | solution.py:303
  31.1 7.3 %copy-start.2 = (bf16[1,4,512,512]{3,2,1,0:T(8,128)(2,1)S(1)}, bf16[1,4,512,512]{3,2,1,0:T(8,128)(2,1)}, u32[]{:S(2)}) copy-start(bf16[1,4,512,512]{3,2,1,0:T(8,128)(2,1)} %param.9) | copy-start | bytes 6291460
  40.9 17.2 %collective-permute-start.9 = (f32[256,256]{1,0:T(8,128)S(1)}, f32[256,256]{1,0:T(8,128)S(1)}, u32[]{:S(2)}, u32[]{:S(2)}) collective-permute-start(f32[256,256]{1,0:T(8,128)S(1)} %get-tuple-element.80), channel_id=1, source_target_pairs={{0,4},{4,0},{8,12},{12,8},{16,20},{20,16},{24,28},{28,24},{1,5},{5... | collective-permute-start | bytes 786440 | tf_op jit(solution)/shard_map/ppermute | solution.py:278
  44.5 13.5 %collective-permute-start.10 = (f32[256,256]{1,0:T(8,128)S(1)}, f32[256,256]{1,0:T(8,128)S(1)}, u32[]{:S(2)}, u32[]{:S(2)}) collective-permute-start(f32[256,256]{1,0:T(8,128)S(1)} %get-tuple-element.81), channel_id=1, source_target_pairs={{4,8},{8,4},{12,16},{16,12},{20,24},{24,20},{5,9},{9,5},{13,17},{1... | collective-permute-start | bytes 786440 | tf_op jit(solution)/shard_map/ppermute | solution.py:279
  59.6 13.8 %collective-permute-start.11 = (f32[256,256]{1,0:T(8,128)S(1)}, f32[256,256]{1,0:T(8,128)S(1)}, u32[]{:S(2)}, u32[]{:S(2)}) collective-permute-start(f32[256,256]{1,0:T(8,128)S(1)} %get-tuple-element.86), channel_id=1, source_target_pairs={{0,4},{4,0},{8,12},{12,8},{16,20},{20,16},{24,28},{28,24},{1,5},{5... | collective-permute-start | bytes 786440 | tf_op jit(solution)/shard_map/ppermute | solution.py:278
  61.9 11.5 %collective-permute-start.12 = (f32[256,256]{1,0:T(8,128)S(1)}, f32[256,256]{1,0:T(8,128)S(1)}, u32[]{:S(2)}, u32[]{:S(2)}) collective-permute-start(f32[256,256]{1,0:T(8,128)S(1)} %get-tuple-element.87), channel_id=1, source_target_pairs={{4,8},{8,4},{12,16},{16,12},{20,24},{24,20},{5,9},{9,5},{13,17},{1... | collective-permute-start | bytes 786440 | tf_op jit(solution)/shard_map/ppermute | solution.py:279
  83.1 15.7 %collective-permute-start.13 = (f32[256,256]{1,0:T(8,128)S(1)}, f32[256,256]{1,0:T(8,128)S(1)}, u32[]{:S(2)}, u32[]{:S(2)}) collective-permute-start(f32[256,256]{1,0:T(8,128)S(1)} %get-tuple-element.94), channel_id=1, source_target_pairs={{0,4},{4,0},{8,12},{12,8},{16,20},{20,16},{24,28},{28,24},{1,5},{5... | collective-permute-start | bytes 786440 | tf_op jit(solution)/shard_map/ppermute | solution.py:278
  85.6 13.2 %collective-permute-start.14 = (f32[256,256]{1,0:T(8,128)S(1)}, f32[256,256]{1,0:T(8,128)S(1)}, u32[]{:S(2)}, u32[]{:S(2)}) collective-permute-start(f32[256,256]{1,0:T(8,128)S(1)} %get-tuple-element.95), channel_id=1, source_target_pairs={{4,8},{8,4},{12,16},{16,12},{20,24},{24,20},{5,9},{9,5},{13,17},{1... | collective-permute-start | bytes 786440 | tf_op jit(solution)/shard_map/ppermute | solution.py:279
  101.0 13.7 %collective-permute-start.15 = (f32[256,256]{1,0:T(8,128)S(1)}, f32[256,256]{1,0:T(8,128)S(1)}, u32[]{:S(2)}, u32[]{:S(2)}) collective-permute-start(f32[256,256]{1,0:T(8,128)S(1)} %get-tuple-element.103), channel_id=1, source_target_pairs={{0,4},{4,0},{8,12},{12,8},{16,20},{20,16},{24,28},{28,24},{1,5},{5... | collective-permute-start | bytes 786440 | tf_op jit(solution)/shard_map/ppermute | solution.py:278
  103.3 11.5 %collective-permute-start.16 = (f32[256,256]{1,0:T(8,128)S(1)}, f32[256,256]{1,0:T(8,128)S(1)}, u32[]{:S(2)}, u32[]{:S(2)}) collective-permute-start(f32[256,256]{1,0:T(8,128)S(1)} %get-tuple-element.104), channel_id=1, source_target_pairs={{4,8},{8,4},{12,16},{16,12},{20,24},{24,20},{5,9},{9,5},{13,17},{1... | collective-permute-start | bytes 786440 | tf_op jit(solution)/shard_map/ppermute | solution.py:279
  125.0 15.4 %collective-permute-start.17 = (f32[256,256]{1,0:T(8,128)S(1)}, f32[256,256]{1,0:T(8,128)S(1)}, u32[]{:S(2)}, u32[]{:S(2)}) collective-permute-start(f32[256,256]{1,0:T(8,128)S(1)} %slice.19), channel_id=1, source_target_pairs={{4,0},{8,4},{12,8},{16,12},{20,16},{24,20},{28,24},{5,1},{9,5},{13... | collective-permute-start | bytes 786440 | tf_op jit(solution)/shard_map/ppermute | solution.py:399

commit v6 on v5

--- a/solution.py
+++ b/solution.py
@@ -33,12 +33,14 @@
     return lax.dot_general(first, second, dims, preferred_element_type=jnp.float32)
 
 
-def call(kernel, out_shapes, *operands):
+def call(kernel, out_shapes, *operands, kinds=None, scratch=()):
+    kinds = kinds or [jnp.float32] * len(out_shapes)
     return pl.pallas_call(
         kernel,
-        out_shape=[jax.ShapeDtypeStruct(shape, jnp.float32) for shape in out_shapes],
+        out_shape=[jax.ShapeDtypeStruct(*shape) for shape in zip(out_shapes, kinds)],
         in_specs=[pl.BlockSpec(memory_space=pltpu.VMEM)] * len(operands),
         out_specs=[pl.BlockSpec(memory_space=pltpu.VMEM)] * len(out_shapes),
+        scratch_shapes=list(scratch),
         compiler_params=pltpu.CompilerParams(vmem_limit_bytes=VMEM_LIMIT),
     )(*operands)
 
@@ -94,10 +96,8 @@
 
 
 def row_sums(values):
-    ones = jnp.ones((8, values.shape[1]), jnp.bfloat16)
-    high, rest = split(values)
-    middle, low = split(values - high.astype(jnp.float32))
-    return (mul_rows(ones, high) + mul_rows(ones, middle) + mul_rows(ones, low))[:1]
+    half = values.shape[1] // 2
+    return jnp.sum((values[:, :half] + values[:, half:]).T, axis=0, keepdims=True)
 
 
 def step_scalars(step, sums, before):
@@ -159,10 +159,22 @@
     send_faces(even_place(), first[...], last, near_out, far_out)
 
 
-def pick_kernel(everyone, coarse, picked):
-    group, own = everyone.shape[0], everyone.shape[2]
+def setup_kernel(*refs):
+    group = (len(refs) - 5) // 2
+    maps, (coarse, coupling) = refs[:group], refs[group : group + 2]
+    picked, (stacked, lift, everyone) = refs[group + 2 : -3], refs[-3:]
+    subs, corners = maps[0].shape
     rows, size = coarse.shape
+    own = subs * corners
     grp = lax.axis_index("grp")
+    for sub in range(subs):
+        high, low = split(coupling[sub])
+        spare = jnp.zeros((lift.shape[1] - 3 * corners, high.shape[1]), jnp.bfloat16)
+        stacked[sub] = jnp.concatenate([high, low], axis=0)
+        lift[sub] = jnp.concatenate([high, high, low, spare], axis=0)
+    for distance in range(group):
+        unknowns = [maps[distance][sub : sub + 1, :] for sub in range(subs)]
+        everyone[distance] = jnp.concatenate(unknowns, axis=1)
     high, low = split(coarse[...])
     unknowns = lax.broadcasted_iota(jnp.int32, (size, own), 0)
     columns = []
@@ -174,7 +186,7 @@
     dims = (((0,), (0,)), ((), ()))
     for distance in range(group):
         chosen = (owned == everyone[distance]).astype(jnp.bfloat16)
-        picked[distance] = lax.dot_general(
+        picked[distance][...] = lax.dot_general(
             chosen, high, dims, preferred_element_type=jnp.float32
         ) + lax.dot_general(chosen, low, dims, preferred_element_type=jnp.float32)
 
@@ -205,11 +217,18 @@
     rows = block.shape[0] // 2
     high, low = split(everyone[...])
     both = mul(block[...], high)
-    back = (both[:rows] + both[rows:] + mul(block[:rows], low)).T
-    back_high, back_low = split(back)
-    lifted = jnp.concatenate([back_high, back_low, back_high], axis=1)
+    back = both[:rows] + both[rows:] + mul(block[:rows], low)
+    corners = rows // subs
+
+    def lifted(sub):
+        own = back[sub * corners : (sub + 1) * corners]
+        own_high = own.astype(jnp.bfloat16).astype(jnp.float32)
+        terms = [own_high, own - own_high, own_high]
+        spare = jnp.zeros((lift.shape[1] - 3 * corners, own.shape[1]), jnp.float32)
+        return mul(jnp.concatenate(terms + [spare], axis=0).T.astype(jnp.bfloat16), lift[sub])
+
     parts = [split(edges[place]) for place in range(subs + 1)]
-    panel_products(parts, panel, result, lambda sub: mul(lifted, lift[sub]))
+    panel_products(parts, panel, result, lifted)
     send_faces(even, result[0], result[subs - 1], near_out, far_out)
     product = curvature = 0.0
     for sub in range(subs):
@@ -292,7 +311,7 @@
     for distance in range(1, group):
         routes = [(i, i ^ distance) for i in range(group)]
         received.append(lax.ppermute(values, "grp", routes))
-    return jnp.stack(received)
+    return received
 
 
 def swap_blocks(picked):
@@ -327,7 +346,7 @@
 def local(rhs, counts, solve_panel, dirichlet_panel, coupling, corner_map, coarse_inverse):
     subs, loads, width = rhs.shape[1:]
     corners = coupling.shape[2]
-    solve, dirichlet, couple = solve_panel[0], dirichlet_panel[0], coupling[0]
+    solve, dirichlet = solve_panel[0], dirichlet_panel[0]
     size = lax.axis_size("sub")
 
     face_shape, own_shape = (loads, width), (subs, loads, width)
@@ -338,16 +357,20 @@
     tail = make_tail(counts, rhs)
     tail, counts, corner_map = lax.optimization_barrier((tail, counts, corner_map))
     head = lax.ppermute(tail, "sub", [(i, i + 1) for i in range(size - 1)])
-    everyone = from_group(corner_map.reshape(1, subs * corners))
+    maps = from_group(corner_map[0])
     live_own, residual_own, partial, rest = call(
         early_kernel,
         [(subs, 1, width), own_shape, first_shape, rest_shape],
         counts, rhs[0], dirichlet,
     )
-    group = everyone.shape[0]
-    (picked,) = call(
-        pick_kernel, [(group, subs * corners, group * subs * corners)],
-        everyone, coarse_inverse[0],
+    group, own = len(maps), subs * corners
+    *picked, stacked, lift = call(
+        setup_kernel,
+        [(own, group * own)] * group
+        + [(subs, 2 * corners, 2 * width), (subs, 3 * corners + -3 * corners % 128, 2 * width)],
+        *maps, coarse_inverse[0], coupling[0],
+        kinds=[jnp.float32] * group + [jnp.bfloat16] * 2,
+        scratch=[pltpu.VMEM((group, 1, own), jnp.int32)],
     )
     head, picked, rest = lax.optimization_barrier((head, picked, rest))
     live_edge, residual_edge, first, near, far = call(
@@ -355,18 +378,7 @@
         [(1, width), face_shape, first_shape, face_shape, face_shape],
         head, partial, rest, dirichlet,
     )
-    first, couple = lax.optimization_barrier((first, couple))
     block = jnp.concatenate(split_outside(swap_blocks(picked)), axis=0)
-    high, low = split_outside(couple)
-    stacked = jnp.concatenate([high, low], axis=1)
-    slots = jnp.arange(subs, dtype=jnp.int32)
-    own = (slots[:, None] == slots[None, :])[:, :, None, None]
-
-    def placed(part):
-        wide = jnp.where(own, part[:, None], jnp.zeros((), part.dtype))
-        return wide.reshape(subs, subs * corners, 2 * width)
-
-    lift = jnp.concatenate([placed(high), placed(high), placed(low)], axis=1)
 
     scalars, preconds = [jnp.zeros((2, loads), jnp.float32)], []
     image = residual = (residual_edge, residual_own)

time: 143 us -> 140 us (0.979)
  starting transfers between devices: 25.9 us -> 22.2 us
  waiting for transfers between devices: 29.9 us -> 32.7 us
  blocking collectives: 59.5 us -> 62.3 us
  local copies, waits for them, and re-layouts: 4.72 us -> 2.35 us
    ppermute x3, waiting for transfers between devices: 0.01 us -> 9.21 us  [swap_blocks(): block = block + lax.ppermute(picked[distance], 'grp', routes)]
    ppermute x5, waiting for transfers between devices: 29.9 us -> 23.4 us  [swap(): lax.ppermute(near, 'sub', neighbour_pairs(size, 0))]
    ppermute x5, starting transfers between devices: 12.4 us -> 8.88 us  [swap(): lax.ppermute(near, 'sub', neighbour_pairs(size, 0))]
    all_to_all x3, blocking collectives: 39.3 us -> 41.7 us  [from_all(): return lax.all_to_all(copies, ('sub', 'grp'), 0, 0)]
    unnamed x14 -> x16, local copies, waits for them, and re-layouts: 2.9 us -> 2.27 us
  transfers between devices with their start and end apart: 18 -> 18, of which waited for: 3 -> 5; matrix products, arithmetic and copies ran while one was open for 1% -> 0% of each run, Pallas kernels for 3% -> 2%
where the time goes in v6:
time: 140 us
  blocking collectives  62.3 us (44%)
  waiting for transfers between devices  32.7 us (23%)
  starting transfers between devices  22.2 us (16%)
  Pallas kernels  19.5 us (14%)
  local copies, waits for them, and re-layouts  2.35 us (2%)
    all_to_all x3, blocking collectives, from_all(): return lax.all_to_all(copies, ('sub', 'grp'), 0, 0)  41.7 us
    ppermute x5, waiting for transfers between devices, swap(): lax.ppermute(near, 'sub', neighbour_pairs(size, 0))  23.4 us
    all_gather x3, blocking collectives, local(): everyone = lax.all_gather(values, 'grp', tiled=True)  20.5 us
    pallas_call x12, Pallas kernels, call(): pl.pallas_call(kernel, out_shape=[jax.ShapeDtypeStruct(*shape) for shape...  17.7 us
    ppermute x3, waiting for transfers between devices, swap_blocks(): block = block + lax.ppermute(picked[distance], 'grp', routes)  9.21 us
    ppermute x5, starting transfers between devices, swap(): lax.ppermute(near, 'sub', neighbour_pairs(size, 0))  8.88 us
    ppermute x1, starting transfers between devices, local(): head = lax.ppermute(tail, 'sub', [(i, i + 1) for i in range(size - 1)])  4.86 us
    ppermute x5, starting transfers between devices, swap(): lax.ppermute(far, 'sub', neighbour_pairs(size, 1))  3.33 us
  transfers between devices with their start and end apart: 18, of which 5 were waited for; matrix products, arithmetic and copies ran while one was open for 0% of the time, Pallas kernels for 2%

profile of v6, /device:TPU:0, one launch (start us, length us, event | category | flops | bytes accessed | tf_op | source)
XLA Modules:
  0.0 140.1 jit_solution(2349409813868602081)
XLA Ops:
  0.6 0.0 copy-start.3
  0.6 0.0 copy-start.5
  0.6 1.8 %shard_map.86 = f32[264,256]{1,0:T(8,128)} custom-call(s32[1,4]{1,0:T(1,128)} %counts, f32[1,4,256,256]{3,2,1,0:T(8,128)} %rhs.1), custom_call_target="tpu_custom_call" | custom-call | tf_op jit(solution)/shard_map/pallas_call | solution.py:328
  2.5 4.9 %collective-permute-start = (f32[264,256]{1,0:T(8,128)}, f32[264,256]{1,0:T(8,128)S(1)}, u32[]{:S(2)}, u32[]{:S(2)}) collective-permute-start(f32[264,256]{1,0:T(8,128)} %shard_map.86), channel_id=1, source_target_pairs={{0,4},{4,8},{8,12},{12,16},{16,20},{20,24},{24,28},{1,5},{5,9},{9,... | collective-permute-start | bytes 811016 | tf_op jit(solution)/shard_map/ppermute | solution.py:359
  7.3 0.7 collective-permute-start.3
  8.1 0.9 collective-permute-start.2
  9.0 0.3 collective-permute-start.1
  9.3 0.0 copy-done.3
  9.3 1.6 %copy-done = bf16[1,4,512,512]{3,2,1,0:T(8,128)(2,1)S(1)} copy-done((bf16[1,4,512,512]{3,2,1,0:T(8,128)(2,1)S(1)}, bf16[1,4,512,512]{3,2,1,0:T(8,128)(2,1)}, u32[]{:S(2)}) %copy-start) | copy-done | bytes 2097176
  10.9 0.7 copy-done.7
  11.5 1.2 shard_map.88
  12.7 0.0 collective-permute-done.3.refs_3_
  12.7 0.0 collective-permute-done.2.refs_2_
  12.7 0.0 collective-permute-done.1.refs_1_
  12.7 0.0 copy-done.5
  12.8 0.0 copy-done.4
  12.8 0.0 copy-done.6
  12.8 1.9 %shard_map.87 = (f32[128,512]{1,0:T(8,128)S(1)}, f32[128,512]{1,0:T(8,128)S(1)}, f32[128,512]{1,0:T(8,128)S(1)}, f32[128,512]{1,0:T(8,128)S(1)}, bf16[4,64,512]{...) custom-call(s32[4,32]{1,0:T(4,128)S(1)} %bitcast.21, s32[4,32]{1,0:T(4,128)S(1)} %collective-permute-done.1.refs_1_, ...), custom_call_target="tpu_custom_call" | custom-call | tf_op jit(solution)/shard_map/pallas_call | solution.py:38
  14.7 0.0 collective-permute-done.head
  14.7 0.3 collective-permute-start.6
  15.0 1.4 collective-permute-start.7
  16.4 0.3 collective-permute-start.8
  16.6 0.3 shard_map.89
  17.0 1.6 %collective-permute-start.4 = (f32[256,256]{1,0:T(8,128)S(1)}, f32[256,256]{1,0:T(8,128)S(1)}, u32[]{:S(2)}, u32[]{:S(2)}) collective-permute-start(f32[256,256]{1,0:T(8,128)S(1)} %get-tuple-element.78), channel_id=1, source_target_pairs={{0,4},{4,0},{8,12},{12,8},{16,20},{20,16},{24,28},{28,24},{1,5},{5... | collective-permute-start | bytes 786440 | tf_op jit(solution)/shard_map/ppermute | solution.py:297
  18.6 0.7 collective-permute-start.5
  19.2 0.0 collective-permute-done.6
  19.2 4.9 %collective-permute-done.7 = f32[128,512]{1,0:T(8,128)S(1)} collective-permute-done((f32[128,512]{1,0:T(8,128)S(1)}, f32[128,512]{1,0:T(8,128)S(1)}, u32[]{:S(2)}, u32[]{:S(2)}) %collective-permute-start.7) | collective-permute-done | bytes 262176 | tf_op jit(solution)/shard_map/ppermute | solution.py:322
  24.2 4.3 %collective-permute-done.8 = f32[128,512]{1,0:T(8,128)S(1)} collective-permute-done((f32[128,512]{1,0:T(8,128)S(1)}, f32[128,512]{1,0:T(8,128)S(1)}, u32[]{:S(2)}, u32[]{:S(2)}) %collective-permute-start.8) | collective-permute-done | bytes 262176 | tf_op jit(solution)/shard_map/ppermute | solution.py:322
  28.4 0.1 reduce-precision_convert_fusion
  28.6 1.9 %collective-permute-done.4.near = f32[256,256]{1,0:T(8,128)S(1)} collective-permute-done((f32[256,256]{1,0:T(8,128)S(1)}, f32[256,256]{1,0:T(8,128)S(1)}, u32[]{:S(2)}, u32[]{:S(2)}) %collective-permute-start.4) | collective-permute-done | bytes 262176 | tf_op jit(solution)/shard_map/ppermute | solution.py:297
  30.4 0.0 collective-permute-done.5.far
  30.4 0.7 shard_map.90
  31.2 7.0 %all_gather.9.everyone = f32[512,256]{1,0:T(8,128)S(1)} all-gather(f32[128,256]{1,0:T(8,128)S(1)} %get-tuple-element.86), channel_id=1, replica_groups=mesh['sub'=8,'grp'=4] {'grp'}, dimensions={0}, use_global_device_ids=true | all-gather | bytes 655360 | tf_op jit(solution)/shard_map/all_gather | solution.py:394
  38.2 1.9 %shard_map.91 = (f32[256,512]{1,0:T(8,128)S(1)}, f32[3,256,512]{2,1,0:T(8,128)S(1)}, f32[256,256]{1,0:T(8,128)S(1)}, f32[256,256]{1,0:T(8,128)S(1)}, f32[2,256]{1,0:T(2,128)S(1)}) custom-call(f32[256,256]{1,0:T(8,128)S(1)} %get-tuple-element.83.edge, f32[4,256,256]{2,1,0:T(8,128)S(1)} %get-tuple-element.84.own.first_z, ...), custom_call_target="tpu_custom_call" | custom-call | tf_op jit(solution)/shard_map/pallas_call | solution.py:38
  40.2 2.6 %collective-permute-start.9 = (f32[256,256]{1,0:T(8,128)S(1)}, f32[256,256]{1,0:T(8,128)S(1)}, u32[]{:S(2)}, u32[]{:S(2)}) collective-permute-start(f32[256,256]{1,0:T(8,128)S(1)} %get-tuple-element.94), channel_id=1, source_target_pairs={{0,4},{4,0},{8,12},{12,8},{16,20},{20,16},{24,28},{28,24},{1,5},{5... | collective-permute-start | bytes 786440 | tf_op jit(solution)/shard_map/ppermute | solution.py:297
  42.7 0.7 collective-permute-start.10
  43.4 13.3 %all_to_all.15.sums = f32[32,2,256]{2,1,0:T(2,128)S(1)} all-to-all(f32[32,2,256]{2,1,0:T(2,128)S(1)} %broadcast_in_dim.12), channel_id=1, replica_groups=mesh['sub'=8,'grp'=4] {'sub','grp'}, dimensions={0} | all-to-all | bytes 131072 | tf_op jit(solution)/shard_map/all_to_all | solution.py:305
  56.8 0.0 collective-permute-done.9.near
  56.8 0.0 collective-permute-done.10.far
  56.8 1.6 %shard_map.92 = (f32[256,256]{1,0:T(8,128)S(1)}, f32[4,256,256]{2,1,0:T(8,128)S(1)}, f32[256,256]{1,0:T(8,128)S(1)}, f32[4,256,256]{2,1,0:T(8,128)S(1)}, f32[256...) custom-call(f32[256,512]{1,0:T(8,128)S(1)} %get-tuple-element.92.fir, ...), custom_call_target="tpu_custom_call" | custom-call | tf_op jit(solution)/shard_map/pallas_call | solution.py:38
  58.3 1.1 collective-permute-start.11
  59.4 0.7 collective-permute-start.12
  60.1 10.8 %collective-permute-done.11.near = f32[256,256]{1,0:T(8,128)S(1)} collective-permute-done((f32[256,256]{1,0:T(8,128)S(1)}, f32[256,256]{1,0:T(8,128)S(1)}, u32[]{:S(2)}, u32[]{:S(2)}) %collective-permute-start.11) | collective-permute-done | bytes 262176 | tf_op jit(solution)/shard_map/ppermute | solution.py:297
  70.9 0.0 collective-permute-done.12.far
  70.9 0.7 shard_map.93
  71.7 6.8 %all_gather.10.everyone = f32[512,256]{1,0:T(8,128)S(1)} all-gather(f32[128,256]{1,0:T(8,128)S(1)} %get-tuple-element.105), channel_id=1, replica_groups=mesh['sub'=8,'grp'=4] {'grp'}, dimensions={0}, use_global_device_ids=true | all-gather | bytes 655360 | tf_op jit(solution)/shard_map/all_gather | solution.py:394
  78.5 1.9 %shard_map.94 = (f32[256,512]{1,0:T(8,128)S(1)}, f32[3,256,512]{2,1,0:T(8,128)S(1)}, f32[256,256]{1,0:T(8,128)S(1)}, f32[256,256]{1,0:T(8,128)S(1)}, f32[2,256]{1,0:T(2,128)S(1)}) custom-call(f32[256,256]{1,0:T(8,128)S(1)} %get-tuple-element.102.edge, f32[4,256,256]{2,1,0:T(8,128)S(1)} %get-tuple-element.103.own.second_z, ...), custom_call_target="tpu_custom_call" | custom-call | tf_op jit(solution)/shard_map/pallas_call | solution.py:38
  80.4 2.6 %collective-permute-start.13 = (f32[256,256]{1,0:T(8,128)S(1)}, f32[256,256]{1,0:T(8,128)S(1)}, u32[]{:S(2)}, u32[]{:S(2)}) collective-permute-start(f32[256,256]{1,0:T(8,128)S(1)} %get-tuple-element.108), channel_id=1, source_target_pairs={{0,4},{4,0},{8,12},{12,8},{16,20},{20,16},{24,28},{28,24},{1,5},{5... | collective-permute-start | bytes 786440 | tf_op jit(solution)/shard_map/ppermute | solution.py:297
  82.9 0.7 collective-permute-start.14
  83.6 13.4 %all_to_all.16.sums = f32[32,2,256]{2,1,0:T(2,128)S(1)} all-to-all(f32[32,2,256]{2,1,0:T(2,128)S(1)} %broadcast_in_dim.14), channel_id=1, replica_groups=mesh['sub'=8,'grp'=4] {'sub','grp'}, dimensions={0} | all-to-all | bytes 131072 | tf_op jit(solution)/shard_map/all_to_all | solution.py:305
  97.1 0.0 collective-permute-done.13.near
  97.1 0.0 collective-permute-done.14.far
  97.1 2.2 %shard_map.95 = (f32[256,256]{1,0:T(8,128)}, f32[4,256,256]{2,1,0:T(8,128)S(1)}, f32[256,256]{1,0:T(8,128)}, f32[4,256,256]{2,1,0:T(8,128)S(1)}, f32[256,512]{1,...) custom-call(f32[256,512]{1,0:T(8,128)S(1)} %get-tuple-element.106.fi, ...), custom_call_target="tpu_custom_call" | custom-call | tf_op jit(solution)/shard_map/pallas_call | solution.py:38
  99.3 1.0 collective-permute-start.15
  100.4 0.7 collective-permute-start.16
  101.0 10.8 %collective-permute-done.15.near = f32[256,256]{1,0:T(8,128)S(1)} collective-permute-done((f32[256,256]{1,0:T(8,128)S(1)}, f32[256,256]{1,0:T(8,128)S(1)}, u32[]{:S(2)}, u32[]{:S(2)}) %collective-permute-start.15) | collective-permute-done | bytes 262176 | tf_op jit(solution)/shard_map/ppermute | solution.py:297
  111.8 0.0 collective-permute-done.16.far
  111.8 0.7 shard_map.96
  112.6 6.7 %all_gather.11.everyone = f32[512,256]{1,0:T(8,128)S(1)} all-gather(f32[128,256]{1,0:T(8,128)S(1)} %get-tuple-element.122), channel_id=1, replica_groups=mesh['sub'=8,'grp'=4] {'grp'}, dimensions={0}, use_global_device_ids=true | all-gather | bytes 655360 | tf_op jit(solution)/shard_map/all_gather | solution.py:394
  119.3 2.7 %shard_map.97 = (f32[256,512]{1,0:T(8,128)S(1)}, f32[3,256,512]{2,1,0:T(8,128)S(1)}, f32[256,256]{1,0:T(8,128)}, f32[256,256]{1,0:T(8,128)}, f32[2,256]{1,0:T(2,128)S(1)}) custom-call(f32[256,256]{1,0:T(8,128)S(1)} %get-tuple-element.119.edge, f32[4,256,256]{2,1,0:T(8,128)S(1)} %get-tuple-element.120.own.third_z, ...), custom_call_target="tpu_custom_call" | custom-call | tf_op jit(solution)/shard_map/pallas_call | solution.py:38
  122.0 1.3 collective-permute-start.17
  123.3 15.0 %all_to_all.17.sums = f32[32,2,256]{2,1,0:T(2,128)S(1)} all-to-all(f32[32,2,256]{2,1,0:T(2,128)S(1)} %broadcast_in_dim.30), channel_id=1, replica_groups=mesh['sub'=8,'grp'=4] {'sub','grp'}, dimensions={0} | all-to-all | bytes 131072 | tf_op jit(solution)/shard_map/all_to_all | solution.py:305
  138.3 0.0 collective-permute-done.17.following
  138.3 1.8 %shard_map.98 = (f32[4,256,256]{2,1,0:T(8,128)}, f32[4,256,256]{2,1,0:T(8,128)}) custom-call(f32[256,512]{1,0:T(8,128)S(1)} %get-tuple-element.123.first, f32[3,256,512]{2,1,0:T(8,128)S(1)} %get-tuple-element.124.rest, f32[256,256]{1,0:T(8,128)S(1)} %collective-permute-done.17.following, f32[4,1,256]{2,1,0:T(1,128)S(1)} %get-tuple-element.81.live_rest.live, ...), custom_call_target="tpu_custom_call" | custom-call | tf_op jit(solution)/shard_map/pallas_call | solution.py:38
  (15 shorter events, 0.1 us)
Async XLA Ops:
  0.6 8.6 %copy-start.3 = (f32[1,4,256,256]{3,2,1,0:T(8,128)S(1)}, f32[1,4,256,256]{3,2,1,0:T(8,128)}, u32[]{:S(2)}) copy-start(f32[1,4,256,256]{3,2,1,0:T(8,128)} %rhs.1) | copy-start | bytes 3145732
  0.6 12.1 %copy-start.5 = (f32[1,4,32,512]{3,2,1,0:T(8,128)S(1)}, f32[1,4,32,512]{3,2,1,0:T(8,128)}, u32[]{:S(2)}) copy-start(f32[1,4,32,512]{3,2,1,0:T(8,128)} %param.11) | copy-start | bytes 786436
  2.5 12.2 %collective-permute-start = (f32[264,256]{1,0:T(8,128)}, f32[264,256]{1,0:T(8,128)S(1)}, u32[]{:S(2)}, u32[]{:S(2)}) collective-permute-start(f32[264,256]{1,0:T(8,128)} %shard_map.86), channel_id=1, source_target_pairs={{0,4},{4,8},{8,12},{12,16},{16,20},{20,24},{24,28},{1,5},{5,9},{9,... | collective-permute-start | bytes 811016 | tf_op jit(solution)/shard_map/ppermute | solution.py:359
  7.3 5.4 %collective-permute-start.3 = (s32[4,32]{1,0:T(4,128)}, s32[4,32]{1,0:T(4,128)S(1)}, u32[]{:S(2)}, u32[]{:S(2)}) collective-permute-start(s32[4,32]{1,0:T(4,128)} %bitcast.18), channel_id=1, source_target_pairs={{0,3},{1,2},{2,1},{3,0},{4,7},{5,6},{6,5},{7,4},{8,11},{9,10},{10,... | collective-permute-start | bytes 1544 | tf_op jit(solution)/shard_map/ppermute | solution.py:313
  8.1 4.7 %collective-permute-start.2 = (s32[4,32]{1,0:T(4,128)}, s32[4,32]{1,0:T(4,128)S(1)}, u32[]{:S(2)}, u32[]{:S(2)}) collective-permute-start(s32[4,32]{1,0:T(4,128)} %bitcast.19), channel_id=1, source_target_pairs={{0,2},{1,3},{2,0},{3,1},{4,6},{5,7},{6,4},{7,5},{8,10},{9,11},{10,... | collective-permute-start | bytes 1544 | tf_op jit(solution)/shard_map/ppermute | solution.py:313
  9.0 3.7 %collective-permute-start.1 = (s32[4,32]{1,0:T(4,128)}, s32[4,32]{1,0:T(4,128)S(1)}, u32[]{:S(2)}, u32[]{:S(2)}) collective-permute-start(s32[4,32]{1,0:T(4,128)} %bitcast.20), channel_id=1, source_target_pairs={{0,1},{1,0},{2,3},{3,2},{4,5},{5,4},{6,7},{7,6},{8,9},{9,8},{10,11... | collective-permute-start | bytes 1544 | tf_op jit(solution)/shard_map/ppermute | solution.py:313
  9.3 1.6 %copy-start = (bf16[1,4,512,512]{3,2,1,0:T(8,128)(2,1)S(1)}, bf16[1,4,512,512]{3,2,1,0:T(8,128)(2,1)}, u32[]{:S(2)}) copy-start(bf16[1,4,512,512]{3,2,1,0:T(8,128)(2,1)} %param.10) | copy-start | bytes 6291460
  10.9 0.7 copy-start.7
  11.5 1.2 copy-start.4
  11.5 1.3 copy-start.6
  11.5 5.1 %copy-start.1 = (bf16[1,4,512,512]{3,2,1,0:T(8,128)(2,1)S(1)}, bf16[1,4,512,512]{3,2,1,0:T(8,128)(2,1)}, u32[]{:S(2)}) copy-start(bf16[1,4,512,512]{3,2,1,0:T(8,128)(2,1)} %param.10) | copy-start | bytes 6291460
  14.7 4.5 %collective-permute-start.6 = (f32[128,512]{1,0:T(8,128)S(1)}, f32[128,512]{1,0:T(8,128)S(1)}, u32[]{:S(2)}, u32[]{:S(2)}) collective-permute-start(f32[128,512]{1,0:T(8,128)S(1)} %get-tuple-element.88), channel_id=1, source_target_pairs={{0,1},{1,0},{2,3},{3,2},{4,5},{5,4},{6,7},{7,6},{8,9},{9,8},{10,11... | collective-permute-start | bytes 786440 | tf_op jit(solution)/shard_map/ppermute | solution.py:322
  15.0 9.1 %collective-permute-start.7 = (f32[128,512]{1,0:T(8,128)S(1)}, f32[128,512]{1,0:T(8,128)S(1)}, u32[]{:S(2)}, u32[]{:S(2)}) collective-permute-start(f32[128,512]{1,0:T(8,128)S(1)} %get-tuple-element.89), channel_id=1, source_target_pairs={{0,2},{1,3},{2,0},{3,1},{4,6},{5,7},{6,4},{7,5},{8,10},{9,11},{10,... | collective-permute-start | bytes 786440 | tf_op jit(solution)/shard_map/ppermute | solution.py:322
  16.4 12.1 %collective-permute-start.8 = (f32[128,512]{1,0:T(8,128)S(1)}, f32[128,512]{1,0:T(8,128)S(1)}, u32[]{:S(2)}, u32[]{:S(2)}) collective-permute-start(f32[128,512]{1,0:T(8,128)S(1)} %get-tuple-element.90), channel_id=1, source_target_pairs={{0,3},{1,2},{2,1},{3,0},{4,7},{5,6},{6,5},{7,4},{8,11},{9,10},{10,... | collective-permute-start | bytes 786440 | tf_op jit(solution)/shard_map/ppermute | solution.py:322
  17.0 13.5 %collective-permute-start.4 = (f32[256,256]{1,0:T(8,128)S(1)}, f32[256,256]{1,0:T(8,128)S(1)}, u32[]{:S(2)}, u32[]{:S(2)}) collective-permute-start(f32[256,256]{1,0:T(8,128)S(1)} %get-tuple-element.78), channel_id=1, source_target_pairs={{0,4},{4,0},{8,12},{12,8},{16,20},{20,16},{24,28},{28,24},{1,5},{5... | collective-permute-start | bytes 786440 | tf_op jit(solution)/shard_map/ppermute | solution.py:297
  18.6 11.9 %collective-permute-start.5 = (f32[256,256]{1,0:T(8,128)S(1)}, f32[256,256]{1,0:T(8,128)S(1)}, u32[]{:S(2)}, u32[]{:S(2)}) collective-permute-start(f32[256,256]{1,0:T(8,128)S(1)} %get-tuple-element.79), channel_id=1, source_target_pairs={{4,8},{8,4},{12,16},{16,12},{20,24},{24,20},{5,9},{9,5},{13,17},{1... | collective-permute-start | bytes 786440 | tf_op jit(solution)/shard_map/ppermute | solution.py:298
  30.4 7.8 %copy-start.2 = (bf16[1,4,512,512]{3,2,1,0:T(8,128)(2,1)S(1)}, bf16[1,4,512,512]{3,2,1,0:T(8,128)(2,1)}, u32[]{:S(2)}) copy-start(bf16[1,4,512,512]{3,2,1,0:T(8,128)(2,1)} %param.9) | copy-start | bytes 6291460
  40.2 16.6 %collective-permute-start.9 = (f32[256,256]{1,0:T(8,128)S(1)}, f32[256,256]{1,0:T(8,128)S(1)}, u32[]{:S(2)}, u32[]{:S(2)}) collective-permute-start(f32[256,256]{1,0:T(8,128)S(1)} %get-tuple-element.94), channel_id=1, source_target_pairs={{0,4},{4,0},{8,12},{12,8},{16,20},{20,16},{24,28},{28,24},{1,5},{5... | collective-permute-start | bytes 786440 | tf_op jit(solution)/shard_map/ppermute | solution.py:297
  42.7 14.0 %collective-permute-start.10 = (f32[256,256]{1,0:T(8,128)S(1)}, f32[256,256]{1,0:T(8,128)S(1)}, u32[]{:S(2)}, u32[]{:S(2)}) collective-permute-start(f32[256,256]{1,0:T(8,128)S(1)} %get-tuple-element.95), channel_id=1, source_target_pairs={{4,8},{8,4},{12,16},{16,12},{20,24},{24,20},{5,9},{9,5},{13,17},{1... | collective-permute-start | bytes 786440 | tf_op jit(solution)/shard_map/ppermute | solution.py:298
  58.3 12.6 %collective-permute-start.11 = (f32[256,256]{1,0:T(8,128)S(1)}, f32[256,256]{1,0:T(8,128)S(1)}, u32[]{:S(2)}, u32[]{:S(2)}) collective-permute-start(f32[256,256]{1,0:T(8,128)S(1)} %get-tuple-element.100), channel_id=1, source_target_pairs={{0,4},{4,0},{8,12},{12,8},{16,20},{20,16},{24,28},{28,24},{1,5},{5... | collective-permute-start | bytes 786440 | tf_op jit(solution)/shard_map/ppermute | solution.py:297
  59.4 11.5 %collective-permute-start.12 = (f32[256,256]{1,0:T(8,128)S(1)}, f32[256,256]{1,0:T(8,128)S(1)}, u32[]{:S(2)}, u32[]{:S(2)}) collective-permute-start(f32[256,256]{1,0:T(8,128)S(1)} %get-tuple-element.101), channel_id=1, source_target_pairs={{4,8},{8,4},{12,16},{16,12},{20,24},{24,20},{5,9},{9,5},{13,17},{1... | collective-permute-start | bytes 786440 | tf_op jit(solution)/shard_map/ppermute | solution.py:298
  80.4 16.7 %collective-permute-start.13 = (f32[256,256]{1,0:T(8,128)S(1)}, f32[256,256]{1,0:T(8,128)S(1)}, u32[]{:S(2)}, u32[]{:S(2)}) collective-permute-start(f32[256,256]{1,0:T(8,128)S(1)} %get-tuple-element.108), channel_id=1, source_target_pairs={{0,4},{4,0},{8,12},{12,8},{16,20},{20,16},{24,28},{28,24},{1,5},{5... | collective-permute-start | bytes 786440 | tf_op jit(solution)/shard_map/ppermute | solution.py:297
  82.9 14.1 %collective-permute-start.14 = (f32[256,256]{1,0:T(8,128)S(1)}, f32[256,256]{1,0:T(8,128)S(1)}, u32[]{:S(2)}, u32[]{:S(2)}) collective-permute-start(f32[256,256]{1,0:T(8,128)S(1)} %get-tuple-element.109), channel_id=1, source_target_pairs={{4,8},{8,4},{12,16},{16,12},{20,24},{24,20},{5,9},{9,5},{13,17},{1... | collective-permute-start | bytes 786440 | tf_op jit(solution)/shard_map/ppermute | solution.py:298
  99.3 12.5 %collective-permute-start.15 = (f32[256,256]{1,0:T(8,128)S(1)}, f32[256,256]{1,0:T(8,128)S(1)}, u32[]{:S(2)}, u32[]{:S(2)}) collective-permute-start(f32[256,256]{1,0:T(8,128)S(1)} %get-tuple-element.117), channel_id=1, source_target_pairs={{0,4},{4,0},{8,12},{12,8},{16,20},{20,16},{24,28},{28,24},{1,5},{5... | collective-permute-start | bytes 786440 | tf_op jit(solution)/shard_map/ppermute | solution.py:297
  100.4 11.5 %collective-permute-start.16 = (f32[256,256]{1,0:T(8,128)S(1)}, f32[256,256]{1,0:T(8,128)S(1)}, u32[]{:S(2)}, u32[]{:S(2)}) collective-permute-start(f32[256,256]{1,0:T(8,128)S(1)} %get-tuple-element.118), channel_id=1, source_target_pairs={{4,8},{8,4},{12,16},{16,12},{20,24},{24,20},{5,9},{9,5},{13,17},{1... | collective-permute-start | bytes 786440 | tf_op jit(solution)/shard_map/ppermute | solution.py:298
  122.0 16.3 %collective-permute-start.17 = (f32[256,256]{1,0:T(8,128)S(1)}, f32[256,256]{1,0:T(8,128)S(1)}, u32[]{:S(2)}, u32[]{:S(2)}) collective-permute-start(f32[256,256]{1,0:T(8,128)S(1)} %slice.3), channel_id=1, source_target_pairs={{4,0},{8,4},{12,8},{16,12},{20,16},{24,20},{28,24},{5,1},{9,5},{13... | collective-permute-start | bytes 786440 | tf_op jit(solution)/shard_map/ppermute | solution.py:411

commit v7 on v6

--- a/solution.py
+++ b/solution.py
@@ -6,9 +6,6 @@
 from jax.experimental import pallas as pl
 from jax.experimental.pallas import tpu as pltpu
 from jax.sharding import PartitionSpec as P
-
-ITERS = 3
-
 
 VMEM_LIMIT = 8 * 1024 * 1024
 TAIL_LIMIT = 62 * 1024 * 1024
@@ -60,23 +57,33 @@
 
 
 def jump_edge(even, result, near, far, live, edge, subs):
-    width = near.shape[1]
+    loads, width = result[0].shape[0], near.shape[1]
     if edge == 0:
-        right = jnp.where(even, far[...], near[...])
+        right = jnp.where(even, far[:loads], near[:loads])
     else:
         right = result[edge - 1][:, width:]
     if edge == subs:
-        left = jnp.where(even, near[...], far[...])
+        left = jnp.where(even, near[:loads], far[:loads])
     else:
         left = result[edge][:, :width]
     return live[edge] * (right - left)
 
 
+def outer_rows(operator, edge):
+    rows = operator.shape[0] // 2
+    high, low = split(edge)
+    both = mul_rows(operator[...], high)
+    return both[:rows] + both[rows:] + mul_rows(operator[:rows], low)
+
+
+def send(even, to_next, to_prev, near_out, far_out):
+    near_out[...] = jnp.where(even, to_next, to_prev)
+    far_out[...] = jnp.where(even, to_prev, to_next)
+
+
 def send_faces(even, first, last, near_out, far_out):
     width = first.shape[1] // 2
-    to_next, to_prev = last[:, width:], first[:, :width]
-    near_out[...] = jnp.where(even, to_next, to_prev)
-    far_out[...] = jnp.where(even, to_prev, to_next)
+    send(even, last[:, width:], first[:, :width], near_out, far_out)
 
 
 def panel_products(parts, panel, result, extra=None):
@@ -160,9 +167,9 @@
 
 
 def setup_kernel(*refs):
-    group = (len(refs) - 5) // 2
+    group = (len(refs) - 7) // 2
     maps, (coarse, coupling) = refs[:group], refs[group : group + 2]
-    picked, (stacked, lift, everyone) = refs[group + 2 : -3], refs[-3:]
+    picked, (stacked, lift, near_out, far_out, everyone) = refs[group + 2 : -5], refs[-5:]
     subs, corners = maps[0].shape
     rows, size = coarse.shape
     own = subs * corners
@@ -172,6 +179,8 @@
         spare = jnp.zeros((lift.shape[1] - 3 * corners, high.shape[1]), jnp.bfloat16)
         stacked[sub] = jnp.concatenate([high, low], axis=0)
         lift[sub] = jnp.concatenate([high, high, low, spare], axis=0)
+    width = coupling.shape[2] // 2
+    send(even_place(), coupling[subs - 1, :, width:], coupling[0, :, :width], near_out, far_out)
     for distance in range(group):
         unknowns = [maps[distance][sub : sub + 1, :] for sub in range(subs)]
         everyone[distance] = jnp.concatenate(unknowns, axis=1)
@@ -209,11 +218,82 @@
         )
 
 
-def dual_kernel(edge, own, residual, panel, everyone, block, lift,
-                first, rest, near_out, far_out, sums):
+def operators_kernel(coupling, live_edge, live_own, near, far, panel,
+                     taken, ends, for_next, for_prev, given):
     even = even_place()
-    subs, width = panel.shape[0], edge.shape[1]
-    edges, result = Joined(edge, own), Joined(first, rest)
+    subs, rows = coupling.shape[0], coupling.shape[1]
+    width = coupling.shape[2] // 2
+    live = Joined(live_edge, live_own)
+    before = jnp.where(even, far[...], near[...])
+    after = jnp.where(even, near[...], far[...])
+    left = [coupling[sub, :, :width] * (0.25 * live[sub]) for sub in range(subs)]
+    left.append(after * (0.25 * live[subs]))
+    right = [before * (0.25 * live[0])]
+    right += [coupling[sub, :, width:] * (0.25 * live[sub + 1]) for sub in range(subs)]
+    none = jnp.zeros((rows, width), jnp.float32)
+    inner, ahead, behind = [], [], []
+    for sub in range(subs):
+        factors = jnp.concatenate(
+            [
+                jnp.concatenate([left[sub], right[sub + 1]], axis=1),
+                jnp.concatenate([none, left[sub + 1]], axis=1),
+                jnp.concatenate([right[sub], none], axis=1),
+            ],
+            axis=0,
+        )
+        both = mul(jnp.concatenate(split(factors), axis=0), panel[sub])
+        product = both[: 3 * rows] + both[3 * rows :]
+        inner.append(product[:rows])
+        ahead.append(product[rows : 2 * rows])
+        behind.append(product[2 * rows :])
+    total = subs * rows
+    for sub in range(subs):
+        blocks = [none] * (subs + 1)
+        blocks[sub] = -inner[sub][:, :width]
+        blocks[sub + 1] = inner[sub][:, width:]
+        if sub > 0:
+            blocks[sub - 1] = ahead[sub - 1][:, :width]
+            blocks[sub] = blocks[sub] - ahead[sub - 1][:, width:]
+        if sub + 1 < subs:
+            blocks[sub + 1] = blocks[sub + 1] + behind[sub + 1][:, :width]
+            blocks[sub + 2] = -behind[sub + 1][:, width:]
+        if sub == 0:
+            ends[0] = blocks[0]
+            blocks[0] = none
+        if sub == subs - 1:
+            ends[1] = blocks[subs]
+            blocks[subs] = none
+        high, low = split(jnp.concatenate(blocks, axis=1))
+        taken[sub * rows : (sub + 1) * rows, :] = high
+        taken[total + sub * rows : total + (sub + 1) * rows, :] = low
+    for_next[...] = jnp.concatenate(split(ahead[subs - 1][:, :width]), axis=0)
+    for_prev[...] = jnp.concatenate(split(-behind[0][:, width:]), axis=0)
+    given[0] = -ahead[subs - 1][:, width:]
+    given[1] = behind[0][:, :width]
+
+
+def early_corner_kernel(taken, ends, outside, edge, own, corners):
+    subs, rows = own.shape[0], ends.shape[1]
+    total = subs * rows
+    edges = Joined(edge, own)
+    parts = [split(edges[place]) for place in range(subs + 1)]
+    high = jnp.concatenate([part[0] for part in parts], axis=1)
+    low = jnp.concatenate([part[1] for part in parts], axis=1)
+    both = mul_rows(taken[...], high)
+    values = both[:total] + both[total:] + mul_rows(taken[:total], low)
+    corners[...] = values
+    for end, place in ((0, 0), (1, subs)):
+        operator = jnp.concatenate(split(ends[end]), axis=0)
+        row = end * (total - rows)
+        corners[row : row + rows, :] = (
+            values[row : row + rows]
+            + outer_rows(operator, edges[place])
+            + outside[end * rows : (end + 1) * rows, :]
+        )
+
+
+def dual_products(edges, residual, panel, everyone, block, lift, result, sums):
+    subs, width = panel.shape[0], panel.shape[1] // 2
     rows = block.shape[0] // 2
     high, low = split(everyone[...])
     both = mul(block[...], high)
@@ -229,7 +309,6 @@
 
     parts = [split(edges[place]) for place in range(subs + 1)]
     panel_products(parts, panel, result, lifted)
-    send_faces(even, result[0], result[subs - 1], near_out, far_out)
     product = curvature = 0.0
     for sub in range(subs):
         product = product + residual[sub] * edges[sub + 1]
@@ -239,25 +318,85 @@
     sums[...] = jnp.concatenate([row_sums(product), row_sums(curvature)], axis=0)
 
 
-def update_kernel(step, first, rest, near, far, live_first, live_rest, sums, before,
-                  old_edge, old_own, residual_edge, residual_own, panel,
-                  image_edge, image_own, new_edge, new_own,
-                  first_new, rest_new, near_out, far_out, scalars):
+def send_dual(result, live_own, subs, for_next, for_prev, near_out, far_out, residual=None,
+              given=None):
     even = even_place()
-    subs, width = panel.shape[0], near.shape[1]
+    width = near_out.shape[1]
+    to_next, to_prev = [result[subs - 1][:, width:]], [result[0][:, :width]]
+    if given is not None:
+        to_next += [given[0], outer_rows(for_next, residual[subs - 2])]
+        to_prev += [given[1], outer_rows(for_prev, residual[0])]
+    upper = live_own[subs - 2] * (result[subs - 2][:, width:] - result[subs - 1][:, :width])
+    lower = live_own[0] * (result[0][:, width:] - result[1][:, :width])
+    to_next.append(outer_rows(for_next, upper))
+    to_prev.append(outer_rows(for_prev, lower))
+    row = 0
+    for ahead, behind in zip(to_next, to_prev):
+        rows = slice(row, row + ahead.shape[0])
+        near_out[rows, :] = jnp.where(even, ahead, behind)
+        far_out[rows, :] = jnp.where(even, behind, ahead)
+        row += ahead.shape[0]
+
+
+def first_dual_kernel(edge, own, residual, panel, everyone, block, lift, live_own,
+                      for_next, for_prev, given, first, rest, near_out, far_out, sums):
+    result = Joined(first, rest)
+    dual_products(Joined(edge, own), residual, panel, everyone, block, lift, result, sums)
+    send_dual(result, live_own, panel.shape[0], for_next, for_prev, near_out, far_out,
+              residual, given)
+
+
+def dual_kernel(last, *refs):
+    first, rest, near, far, live_edge, live_own = refs[:6]
+    residual, panel, everyone, block, lift = refs[6:11]
+    even, subs = even_place(), panel.shape[0]
+    before, live = Joined(first, rest), Joined(live_edge, live_own)
+    edges = [
+        0.25 * jump_edge(even, before, near, far, live, place, subs) for place in range(subs + 1)
+    ]
+    if last:
+        own, first_new, rest_new, face, sums = refs[11:]
+    else:
+        for_next, for_prev, own, first_new, rest_new, near_out, far_out, sums = refs[11:]
+    for sub in range(subs):
+        own[sub] = edges[sub + 1]
+    result = Joined(first_new, rest_new)
+    dual_products(edges, residual, panel, everyone, block, lift, result, sums)
+    if last:
+        face[...] = result[0][:, : face.shape[1]]
+    else:
+        send_dual(result, live_own, subs, for_next, for_prev, near_out, far_out)
+
+
+def received(even, near, far, start, rows):
+    part = slice(start, start + rows)
+    return jnp.concatenate(
+        [jnp.where(even, far[part], near[part]), jnp.where(even, near[part], far[part])], axis=0
+    )
+
+
+def first_update_kernel(first, rest, near, far, live_first, live_rest, sums,
+                        residual_edge, residual_own, panel, ends,
+                        image_own, image_edge, new_edge, new_own, first_new, rest_new,
+                        near_out, far_out, scalars, full_ends, outside_image, outside):
+    even = even_place()
+    loads, width = residual_edge.shape
+    subs, rows = panel.shape[0], ends.shape[1]
     result, live = Joined(first, rest), Joined(live_first, live_rest)
-    image_old, residual = Joined(old_edge, old_own), Joined(residual_edge, residual_own)
-    image, residual_new = Joined(image_edge, image_own), Joined(new_edge, new_own)
-    result_new = Joined(first_new, rest_new)
-    rz_now, alpha, beta = step_scalars(step, sums, before)
+    residual, image = Joined(residual_edge, residual_own), Joined(image_edge, image_own)
+    residual_new, result_new = Joined(new_edge, new_own), Joined(first_new, rest_new)
+    rz_now, alpha, _ = step_scalars(0, sums, None)
     scalars[...] = jnp.concatenate([rz_now, alpha], axis=0)
+    operators = received(even, near, far, loads, rows)
+    full_ends[0] = ends[0] + operators[:rows]
+    full_ends[1] = ends[1] + operators[rows:]
+    values = received(even, near, far, loads + 2 * rows, rows)
+    outside_image[...] = values
+    outside[...] = received(even, near, far, loads + rows, rows) - alpha * values
     alpha_column = column(alpha, width)
-    beta_column = None if beta is None else column(beta, width)
     parts = []
     for place in range(subs + 1):
         value = jump_edge(even, result, near, far, live, place, subs)
-        if beta is not None:
-            value = value + beta_column * image_old[place]
         image[place] = value
         residual_new[place] = residual[place] - alpha_column * value
         parts.append(split(residual_new[place]))
@@ -265,11 +404,39 @@
     send_faces(even, result_new[0], result_new[subs - 1], near_out, far_out)
 
 
-def last_kernel(step, first, rest, following, live, sums, before, older, image_old,
+def update_kernel(first, rest, near, far, live_first, live_rest, sums, before,
+                  old_edge, old_own, residual_edge, residual_own, panel,
+                  outside_image_old, outside_old,
+                  image_own, new_edge, new_own, first_new, rest_new,
+                  near_out, far_out, scalars, outside):
+    even = even_place()
+    loads, width = residual_edge.shape
+    subs, rows = panel.shape[0], outside.shape[0] // 2
+    result, live = Joined(first, rest), Joined(live_first, live_rest)
+    image_old, residual = Joined(old_edge, old_own), Joined(residual_edge, residual_own)
+    residual_new, result_new = Joined(new_edge, new_own), Joined(first_new, rest_new)
+    rz_now, alpha, beta = step_scalars(1, sums, before)
+    scalars[...] = jnp.concatenate([rz_now, alpha], axis=0)
+    values = received(even, near, far, loads, rows) + beta * outside_image_old[...]
+    outside[...] = outside_old[...] - alpha * values
+    alpha_column, beta_column = column(alpha, width), column(beta, width)
+    parts = []
+    for place in range(subs + 1):
+        value = jump_edge(even, result, near, far, live, place, subs)
+        value = value + beta_column * image_old[place]
+        if place > 0:
+            image_own[place - 1] = value
+        residual_new[place] = residual[place] - alpha_column * value
+        parts.append(split(residual_new[place]))
+    panel_products(parts, panel, result_new)
+    send_faces(even, result_new[0], result_new[subs - 1], near_out, far_out)
+
+
+def last_kernel(first, rest, following, live, sums, before, older, image_old,
                 residual, first_z, second_z, third_z, multipliers, residual_new):
     subs, width = residual.shape[0], following.shape[1]
     result = Joined(first, rest)
-    rz_now, alpha, beta = step_scalars(step, sums, before)
+    rz_now, alpha, beta = step_scalars(2, sums, before)
     beta_before = before[0:1] / older[0:1]
     on_second = before[1:2] + alpha * beta
     on_first = older[1:2] + on_second * beta_before
@@ -364,12 +531,14 @@
         counts, rhs[0], dirichlet,
     )
     group, own = len(maps), subs * corners
-    *picked, stacked, lift = call(
+    pair = [(corners, width)] * 2
+    *picked, stacked, lift, near_side, far_side = call(
         setup_kernel,
         [(own, group * own)] * group
-        + [(subs, 2 * corners, 2 * width), (subs, 3 * corners + -3 * corners % 128, 2 * width)],
+        + [(subs, 2 * corners, 2 * width), (subs, 3 * corners + -3 * corners % 128, 2 * width)]
+        + pair,
         *maps, coarse_inverse[0], coupling[0],
-        kinds=[jnp.float32] * group + [jnp.bfloat16] * 2,
+        kinds=[jnp.float32] * group + [jnp.bfloat16] * 2 + [jnp.float32] * 2,
         scratch=[pltpu.VMEM((group, 1, own), jnp.int32)],
     )
     head, picked, rest = lax.optimization_barrier((head, picked, rest))
@@ -378,42 +547,76 @@
         [(1, width), face_shape, first_shape, face_shape, face_shape],
         head, partial, rest, dirichlet,
     )
+    near, far, near_side, far_side = lax.optimization_barrier((near, far, near_side, far_side))
+    near, far = swap(near, far)
+    near_side, far_side = swap(near_side, far_side)
     block = jnp.concatenate(split_outside(swap_blocks(picked)), axis=0)
-
-    scalars, preconds = [jnp.zeros((2, loads), jnp.float32)], []
-    image = residual = (residual_edge, residual_own)
-    live = (live_edge, live_own)
-    for step in range(ITERS):
-        near, far = swap(near, far)
-        edge, own, values = call(
-            corner_kernel,
-            edges_shapes + [(subs * corners, loads)],
-            first, rest, near, far, *live, stacked,
-        )
-        preconds.append(own)
-        everyone = lax.all_gather(values, "grp", tiled=True)
-        first, rest, near, far, sums = call(
-            dual_kernel,
-            result_shapes + [(2, loads)],
-            edge, own, residual[1], solve, everyone, block, lift,
-        )
-        sums = from_all(sums)
-        if step + 1 < ITERS:
-            near, far = swap(near, far)
-            *new, first, rest, near, far, now = call(
-                functools.partial(update_kernel, step),
-                edges_shapes + edges_shapes + result_shapes + [(2, loads)],
-                first, rest, near, far, *live, sums, scalars[-1],
-                *image, *residual, dirichlet,
-            )
-            image, residual = new[:2], new[2:]
-            scalars.append(now)
-    following = lax.ppermute(first[:, :width], "sub", [(i + 1, i) for i in range(size - 1)])
+    live, residual = (live_edge, live_own), (residual_edge, residual_own)
+    taken, ends, for_next, for_prev, given = call(
+        operators_kernel,
+        [(2 * own, (subs + 1) * width), (2,) + pair[0], (2 * corners, width),
+         (2 * corners, width), (2,) + pair[0]],
+        coupling[0], *live, near_side, far_side, dirichlet,
+        kinds=[jnp.bfloat16, jnp.float32, jnp.bfloat16, jnp.bfloat16, jnp.float32],
+    )
+
+    scalars_shape, outside_shape = (2, loads), (2 * corners, loads)
+    long_shape, longer_shape = (loads + corners, width), (loads + 3 * corners, width)
+    edge, first_z, values = call(
+        corner_kernel,
+        edges_shapes + [(own, loads)],
+        first, rest, near, far, *live, stacked,
+    )
+    everyone = lax.all_gather(values, "grp", tiled=True)
+    first, rest, near, far, sums = call(
+        first_dual_kernel,
+        [first_shape, rest_shape, longer_shape, longer_shape, scalars_shape],
+        edge, first_z, residual[1], solve, everyone, block, lift, live[1],
+        for_next, for_prev, given,
+    )
+    sums = from_all(sums)
+    near, far = swap(near, far)
+    (image_own, image_edge, *residual, first, rest, near, far, scalars_first, ends, outside_image,
+     outside) = call(
+        first_update_kernel,
+        [own_shape, face_shape] + edges_shapes + result_shapes
+        + [scalars_shape, (2,) + pair[0], outside_shape, outside_shape],
+        first, rest, near, far, *live, sums, *residual, dirichlet, ends,
+    )
+
+    near, far = swap(near, far)
+    (values,) = call(early_corner_kernel, [(own, loads)], taken, ends, outside, *residual)
+    everyone = lax.all_gather(values, "grp", tiled=True)
+    second_z, first, rest, near, far, sums = call(
+        functools.partial(dual_kernel, False),
+        [own_shape, first_shape, rest_shape, long_shape, long_shape, scalars_shape],
+        first, rest, near, far, *live, residual[1], solve, everyone, block, lift,
+        for_next, for_prev,
+    )
+    sums = from_all(sums)
+    near, far = swap(near, far)
+    image_own, *residual, first, rest, near, far, scalars_second, outside = call(
+        update_kernel,
+        [own_shape] + edges_shapes + result_shapes + [scalars_shape, outside_shape],
+        first, rest, near, far, *live, sums, scalars_first, image_edge, image_own, *residual,
+        dirichlet, outside_image, outside,
+    )
+
+    near, far = swap(near, far)
+    (values,) = call(early_corner_kernel, [(own, loads)], taken, ends, outside, *residual)
+    everyone = lax.all_gather(values, "grp", tiled=True)
+    third_z, first, rest, face, sums = call(
+        functools.partial(dual_kernel, True),
+        [own_shape, first_shape, rest_shape, face_shape, scalars_shape],
+        first, rest, near, far, *live, residual[1], solve, everyone, block, lift,
+    )
+    sums = from_all(sums)
+    following = lax.ppermute(face, "sub", [(i + 1, i) for i in range(size - 1)])
     multipliers, residual = call(
-        functools.partial(last_kernel, ITERS - 1),
+        last_kernel,
         [own_shape] * 2,
-        first, rest, following, live[1], sums, scalars[-1], scalars[-2],
-        image[1], residual[1], *preconds,
+        first, rest, following, live[1], sums, scalars_second, scalars_first,
+        image_own, residual[1], first_z, second_z, third_z,
     )
     return (multipliers[None], residual[None])
 

time: 140 us -> 134 us (0.957)
  waiting for transfers between devices: 32.7 us -> 18.2 us
  starting transfers between devices: 22.2 us -> 28.1 us
    ppermute x5 -> x6, waiting for transfers between devices: 23.4 us -> 14.6 us  [swap(): lax.ppermute(near, 'sub', neighbour_pairs(size, 0))]
    ppermute x3, waiting for transfers between devices: 9.21 us -> 3.58 us  [swap_blocks(): block = block + lax.ppermute(picked[distance], 'grp', routes)]
    ppermute x5 -> x6, starting transfers between devices: 8.88 us -> 14.1 us  [swap(): lax.ppermute(near, 'sub', neighbour_pairs(size, 0))]
    ppermute x5 -> x6, starting transfers between devices: 3.33 us -> 3.99 us  [swap(): lax.ppermute(far, 'sub', neighbour_pairs(size, 1))]
    pallas_call x12 -> x13, Pallas kernels: 17.7 us -> 17.7 us  [call(): pl.pallas_call(kernel, out_shape=[jax.ShapeDtypeStruct(*shape) for shape...]
  transfers between devices with their start and end apart: 18 -> 20, of which waited for: 5 -> 5; matrix products, arithmetic and copies ran while one was open for 0% -> 0% of each run, Pallas kernels for 2% -> 4%
where the time goes in v7:
time: 134 us
  blocking collectives  63.2 us (47%)
  starting transfers between devices  28.1 us (21%)
  Pallas kernels  19.5 us (15%)
  waiting for transfers between devices  18.2 us (14%)
  local copies, waits for them, and re-layouts  3.54 us (3%)
    all_to_all x3, blocking collectives, from_all(): return lax.all_to_all(copies, ('sub', 'grp'), 0, 0)  42.6 us
    all_gather x3, blocking collectives, local(): everyone = lax.all_gather(values, 'grp', tiled=True)  20.7 us
    pallas_call x13, Pallas kernels, call(): pl.pallas_call(kernel, out_shape=[jax.ShapeDtypeStruct(*shape) for shape...  17.7 us
    ppermute x6, waiting for transfers between devices, swap(): lax.ppermute(near, 'sub', neighbour_pairs(size, 0))  14.6 us
    ppermute x6, starting transfers between devices, swap(): lax.ppermute(near, 'sub', neighbour_pairs(size, 0))  14.1 us
    ppermute x1, starting transfers between devices, local(): head = lax.ppermute(tail, 'sub', [(i, i + 1) for i in range(size - 1)])  4.86 us
    ppermute x6, starting transfers between devices, swap(): lax.ppermute(far, 'sub', neighbour_pairs(size, 1))  3.99 us
    ppermute x3, waiting for transfers between devices, swap_blocks(): block = block + lax.ppermute(picked[distance], 'grp', routes)  3.58 us
  transfers between devices with their start and end apart: 20, of which 5 were waited for; matrix products, arithmetic and copies ran while one was open for 0% of the time, Pallas kernels for 4%

profile of v7, /device:TPU:0, one launch (start us, length us, event | category | flops | bytes accessed | tf_op | source)
XLA Modules:
  0.0 133.7 jit_solution(5451492486703792237)
XLA Ops:
  0.6 1.8 %shard_map.86 = f32[264,256]{1,0:T(8,128)} custom-call(s32[1,4]{1,0:T(1,128)} %counts, f32[1,4,256,256]{3,2,1,0:T(8,128)} %rhs.1), custom_call_target="tpu_custom_call" | custom-call | tf_op jit(solution)/shard_map/pallas_call | solution.py:495
  2.4 4.9 %collective-permute-start = (f32[264,256]{1,0:T(8,128)}, f32[264,256]{1,0:T(8,128)S(1)}, u32[]{:S(2)}, u32[]{:S(2)}) collective-permute-start(f32[264,256]{1,0:T(8,128)} %shard_map.86), channel_id=1, source_target_pairs={{0,4},{4,8},{8,12},{12,16},{16,20},{20,24},{24,28},{1,5},{5,9},{9,... | collective-permute-start | bytes 811016 | tf_op jit(solution)/shard_map/ppermute | solution.py:526
  7.3 0.7 collective-permute-start.3
  8.1 0.9 collective-permute-start.2
  9.0 0.3 collective-permute-start.1
  9.2 1.6 %copy-done = bf16[1,4,512,512]{3,2,1,0:T(8,128)(2,1)S(1)} copy-done((bf16[1,4,512,512]{3,2,1,0:T(8,128)(2,1)S(1)}, bf16[1,4,512,512]{3,2,1,0:T(8,128)(2,1)}, u32[]{:S(2)}) %copy-start) | copy-done | bytes 2097176
  10.8 0.7 copy-done.7
  11.5 1.2 shard_map.88
  12.7 0.0 collective-permute-done.3.refs_3_
  12.7 0.0 collective-permute-done.2.refs_2_
  12.7 0.0 collective-permute-done.1.refs_1_
  12.7 0.0 copy-start.5
  12.7 1.2 copy-done.5
  14.0 1.9 %shard_map.87 = (f32[128,512]{1,0:T(8,128)S(1)}, f32[128,512]{1,0:T(8,128)S(1)}, f32[128,512]{1,0:T(8,128)S(1)}, f32[128,512]{1,0:T(8,128)S(1)}, bf16[4,64,512]{...) custom-call(s32[4,32]{1,0:T(4,128)S(1)} %bitcast.23, ...), custom_call_target="tpu_custom_call" | custom-call | tf_op jit(solution)/shard_map/pallas_call | solution.py:35
  15.9 0.0 collective-permute-done.head
  15.9 0.3 collective-permute-start.6
  16.2 1.3 %collective-permute-start.7 = (f32[128,512]{1,0:T(8,128)S(1)}, f32[128,512]{1,0:T(8,128)S(1)}, u32[]{:S(2)}, u32[]{:S(2)}) collective-permute-start(f32[128,512]{1,0:T(8,128)S(1)} %get-tuple-element.106), channel_id=1, source_target_pairs={{0,2},{1,3},{2,0},{3,1},{4,6},{5,7},{6,4},{7,5},{8,10},{9,11},{10,... | collective-permute-start | bytes 786440 | tf_op jit(solution)/shard_map/ppermute | solution.py:489
  17.5 0.3 collective-permute-start.8
  17.8 0.3 shard_map.89
  18.1 1.6 %collective-permute-start.9 = (f32[32,256]{1,0:T(8,128)S(1)}, f32[32,256]{1,0:T(8,128)S(1)}, u32[]{:S(2)}, u32[]{:S(2)}) collective-permute-start(f32[32,256]{1,0:T(8,128)S(1)} %get-tuple-element.109), channel_id=1, source_target_pairs={{0,4},{4,0},{8,12},{12,8},{16,20},{20,16},{24,28},{28,24},{1,5},{5... | collective-permute-start | bytes 98312 | tf_op jit(solution)/shard_map/ppermute | solution.py:464
  19.7 0.7 collective-permute-start.10
  20.4 1.7 %collective-permute-done.9.near = f32[32,256]{1,0:T(8,128)S(1)} collective-permute-done((f32[32,256]{1,0:T(8,128)S(1)}, f32[32,256]{1,0:T(8,128)S(1)}, u32[]{:S(2)}, u32[]{:S(2)}) %collective-permute-start.9) | collective-permute-done | bytes 32800 | tf_op jit(solution)/shard_map/ppermute | solution.py:464
  22.1 2.6 %collective-permute-start.4 = (f32[256,256]{1,0:T(8,128)S(1)}, f32[256,256]{1,0:T(8,128)S(1)}, u32[]{:S(2)}, u32[]{:S(2)}) collective-permute-start(f32[256,256]{1,0:T(8,128)S(1)} %get-tuple-element.95), channel_id=1, source_target_pairs={{0,4},{4,0},{8,12},{12,8},{16,20},{20,16},{24,28},{28,24},{1,5},{5... | collective-permute-start | bytes 786440 | tf_op jit(solution)/shard_map/ppermute | solution.py:464
  24.8 0.0 collective-permute-done.10.far
  24.8 0.7 collective-permute-start.5
  25.4 0.6 shard_map.91
  26.0 0.0 collective-permute-done.6
  26.0 0.0 collective-permute-done.7
  26.0 3.6 %collective-permute-done.8 = f32[128,512]{1,0:T(8,128)S(1)} collective-permute-done((f32[128,512]{1,0:T(8,128)S(1)}, f32[128,512]{1,0:T(8,128)S(1)}, u32[]{:S(2)}, u32[]{:S(2)}) %collective-permute-start.8) | collective-permute-done | bytes 262176 | tf_op jit(solution)/shard_map/ppermute | solution.py:489
  29.6 0.1 reduce-precision_convert_fusion
  29.7 6.3 %collective-permute-done.4.near = f32[256,256]{1,0:T(8,128)S(1)} collective-permute-done((f32[256,256]{1,0:T(8,128)S(1)}, f32[256,256]{1,0:T(8,128)S(1)}, u32[]{:S(2)}, u32[]{:S(2)}) %collective-permute-start.4) | collective-permute-done | bytes 262176 | tf_op jit(solution)/shard_map/ppermute | solution.py:464
  36.1 0.0 collective-permute-done.5.far
  36.1 0.7 shard_map.90
  36.8 7.0 %all_gather.9.everyone = f32[512,256]{1,0:T(8,128)S(1)} all-gather(f32[128,256]{1,0:T(8,128)S(1)} %get-tuple-element.103), channel_id=1, replica_groups=mesh['sub'=8,'grp'=4] {'grp'}, dimensions={0}, use_global_device_ids=true | all-gather | bytes 655360 | tf_op jit(solution)/shard_map/all_gather | solution.py:570
  43.8 2.3 %shard_map.92 = (f32[256,512]{1,0:T(8,128)S(1)}, f32[3,256,512]{2,1,0:T(8,128)S(1)}, f32[352,256]{1,0:T(8,128)S(1)}, f32[352,256]{1,0:T(8,128)S(1)}, f32[2,256]{1,0:T(2,128)S(1)}) custom-call(f32[256,256]{1,0:T(8,128)S(1)} %get-tuple-element.100.edge, f32[4,256,256]{2,1,0:T(8,128)S(1)} %get-tuple-element.101.own.first_z, ...), custom_call_target="tpu_custom_call" | custom-call | tf_op jit(solution)/shard_map/pallas_call | solution.py:35
  46.1 2.5 %collective-permute-start.11 = (f32[352,256]{1,0:T(8,128)S(1)}, f32[352,256]{1,0:T(8,128)S(1)}, u32[]{:S(2)}, u32[]{:S(2)}) collective-permute-start(f32[352,256]{1,0:T(8,128)S(1)} %get-tuple-element.116), channel_id=1, source_target_pairs={{0,4},{4,0},{8,12},{12,8},{16,20},{20,16},{24,28},{28,24},{1,5},{5... | collective-permute-start | bytes 1081352 | tf_op jit(solution)/shard_map/ppermute | solution.py:464
  48.6 0.7 collective-permute-start.12
  49.3 15.9 %all_to_all.15.sums = f32[32,2,256]{2,1,0:T(2,128)S(1)} all-to-all(f32[32,2,256]{2,1,0:T(2,128)S(1)} %broadcast_in_dim.10), channel_id=1, replica_groups=mesh['sub'=8,'grp'=4] {'sub','grp'}, dimensions={0} | all-to-all | bytes 131072 | tf_op jit(solution)/shard_map/all_to_all | solution.py:472
  65.2 0.0 collective-permute-done.11.near
  65.2 0.0 collective-permute-done.12.far
  65.2 1.6 %shard_map.93 = (f32[4,256,256]{2,1,0:T(8,128)S(1)}, f32[256,256]{1,0:T(8,128)S(1)}, f32[256,256]{1,0:T(8,128)S(1)}, f32[4,256,256]{2,1,0:T(8,128)S(1)}, f32[256...) custom-call(f32[256,512]{1,0:T(8,128)S(1)} %get-tuple-element.114.fi, ...), custom_call_target="tpu_custom_call" | custom-call | tf_op jit(solution)/shard_map/pallas_call | solution.py:35
  66.8 2.8 %collective-permute-start.13 = (f32[256,256]{1,0:T(8,128)S(1)}, f32[256,256]{1,0:T(8,128)S(1)}, u32[]{:S(2)}, u32[]{:S(2)}) collective-permute-start(f32[256,256]{1,0:T(8,128)S(1)} %get-tuple-element.123), channel_id=1, source_target_pairs={{0,4},{4,0},{8,12},{12,8},{16,20},{20,16},{24,28},{28,24},{1,5},{5... | collective-permute-start | bytes 786440 | tf_op jit(solution)/shard_map/ppermute | solution.py:464
  69.6 0.7 collective-permute-start.14
  70.3 0.7 shard_map.94
  71.0 6.8 %all_gather.10.refs_8_ = f32[512,256]{1,0:T(8,128)S(1)} all-gather(f32[128,256]{1,0:T(8,128)S(1)} %shard_map.94), channel_id=1, replica_groups=mesh['sub'=8,'grp'=4] {'grp'}, dimensions={0}, use_global_device_ids=true | all-gather | bytes 655360 | tf_op jit(solution)/shard_map/all_gather | solution.py:589
  77.8 3.2 %collective-permute-done.13.refs_2_ = f32[256,256]{1,0:T(8,128)S(1)} collective-permute-done((f32[256,256]{1,0:T(8,128)S(1)}, f32[256,256]{1,0:T(8,128)S(1)}, u32[]{:S(2)}, u32[]{:S(2)}) %collective-permute-start.13) | collective-permute-done | bytes 262176 | tf_op jit(solution)/shard_map/ppermute | solution.py:464
  81.0 0.0 collective-permute-done.14.refs_3_
  81.1 2.3 %shard_map.95 = (f32[4,256,256]{2,1,0:T(8,128)S(1)}, f32[256,512]{1,0:T(8,128)S(1)}, f32[3,256,512]{2,1,0:T(8,128)S(1)}, f32[288,256]{1,0:T(8,128)S(1)}, f32[288,256]{1,0:T(8,128)S(1)}, /*index=5*/f32[2,256]{1,0:T(2,128)S(1)}) custom-call(f32[256,512]{1,0:T(8,128)S(1)} %get-tuple-element.121.refs_0_, f32[3,256,512]{2,1,0:T(8,128)S(1)} %get-tuple-element.122.refs_1_, ...), custom_call_target="tpu_custom_call" | custom-call | tf_op jit(solution)/shard_map/pallas_call | solution.py:35
  83.4 2.5 %collective-permute-start.15 = (f32[288,256]{1,0:T(8,128)S(1)}, f32[288,256]{1,0:T(8,128)S(1)}, u32[]{:S(2)}, u32[]{:S(2)}) collective-permute-start(f32[288,256]{1,0:T(8,128)S(1)} %get-tuple-element.132), channel_id=1, source_target_pairs={{0,4},{4,0},{8,12},{12,8},{16,20},{20,16},{24,28},{28,24},{1,5},{5... | collective-permute-start | bytes 884744 | tf_op jit(solution)/shard_map/ppermute | solution.py:464
  85.9 0.7 collective-permute-start.16
  86.6 13.0 %all_to_all.16.sums = f32[32,2,256]{2,1,0:T(2,128)S(1)} all-to-all(f32[32,2,256]{2,1,0:T(2,128)S(1)} %broadcast_in_dim.11), channel_id=1, replica_groups=mesh['sub'=8,'grp'=4] {'sub','grp'}, dimensions={0} | all-to-all | bytes 131072 | tf_op jit(solution)/shard_map/all_to_all | solution.py:472
  99.6 0.0 collective-permute-done.15.near
  99.6 0.0 collective-permute-done.16.far
  99.6 1.7 %shard_map.96 = (f32[4,256,256]{2,1,0:T(8,128)S(1)}, f32[256,256]{1,0:T(8,128)S(1)}, f32[4,256,256]{2,1,0:T(8,128)S(1)}, f32[256,512]{1,0:T(8,128)S(1)}, f32[3,2...) custom-call(f32[256,512]{1,0:T(8,128)S(1)} %get-tuple-element.130.fi, ...), custom_call_target="tpu_custom_call" | custom-call | tf_op jit(solution)/shard_map/pallas_call | solution.py:35
  101.3 2.1 %collective-permute-start.17 = (f32[256,256]{1,0:T(8,128)S(1)}, f32[256,256]{1,0:T(8,128)S(1)}, u32[]{:S(2)}, u32[]{:S(2)}) collective-permute-start(f32[256,256]{1,0:T(8,128)S(1)} %get-tuple-element.141), channel_id=1, source_target_pairs={{0,4},{4,0},{8,12},{12,8},{16,20},{20,16},{24,28},{28,24},{1,5},{5... | collective-permute-start | bytes 786440 | tf_op jit(solution)/shard_map/ppermute | solution.py:464
  103.4 0.7 collective-permute-start.18
  104.1 0.7 shard_map.97
  104.8 6.8 %all_gather.11.refs_8_ = f32[512,256]{1,0:T(8,128)S(1)} all-gather(f32[128,256]{1,0:T(8,128)S(1)} %shard_map.97), channel_id=1, replica_groups=mesh['sub'=8,'grp'=4] {'grp'}, dimensions={0}, use_global_device_ids=true | all-gather | bytes 655360 | tf_op jit(solution)/shard_map/all_gather | solution.py:607
  111.6 3.3 %collective-permute-done.17.refs_2_ = f32[256,256]{1,0:T(8,128)S(1)} collective-permute-done((f32[256,256]{1,0:T(8,128)S(1)}, f32[256,256]{1,0:T(8,128)S(1)}, u32[]{:S(2)}, u32[]{:S(2)}) %collective-permute-start.17) | collective-permute-done | bytes 262176 | tf_op jit(solution)/shard_map/ppermute | solution.py:464
  114.9 0.0 collective-permute-done.18.refs_3_
  114.9 2.1 %shard_map.98 = (f32[4,256,256]{2,1,0:T(8,128)S(1)}, f32[256,512]{1,0:T(8,128)S(1)}, f32[3,256,512]{2,1,0:T(8,128)S(1)}, f32[256,256]{1,0:T(8,128)S(1)}, f32[2,256]{1,0:T(2,128)S(1)}) custom-call(f32[256,512]{1,0:T(8,128)S(1)} %get-tuple-element.139.refs_0_, f32[3,256,512]{2,1,0:T(8,128)S(1)} %get-tuple-element.140.refs_1_, ...), custom_call_target="tpu_custom_call" | custom-call | tf_op jit(solution)/shard_map/pallas_call | solution.py:35
  116.9 1.3 collective-permute-start.19
  118.2 13.7 %all_to_all.17.sums = f32[32,2,256]{2,1,0:T(2,128)S(1)} all-to-all(f32[32,2,256]{2,1,0:T(2,128)S(1)} %broadcast_in_dim.12), channel_id=1, replica_groups=mesh['sub'=8,'grp'=4] {'sub','grp'}, dimensions={0} | all-to-all | bytes 131072 | tf_op jit(solution)/shard_map/all_to_all | solution.py:472
  131.9 1.8 %shard_map.99 = (f32[4,256,256]{2,1,0:T(8,128)}, f32[4,256,256]{2,1,0:T(8,128)}) custom-call(f32[256,512]{1,0:T(8,128)S(1)} %get-tuple-element.146.first, f32[3,256,512]{2,1,0:T(8,128)S(1)} %get-tuple-element.147.rest, f32[256,256]{1,0:T(8,128)S(1)} %collective-permute-done.19.following, f32[4,1,256]{2,1,0:T(1,128)S(1)} %get-tuple-element.98.live_rest.live_own.refs_5_.live, ...), custom_call_target="tpu_custom_call" | custom-call | tf_op jit(solution)/shard_map/pallas_call | solution.py:35
  (18 shorter events, 0.1 us)
Async XLA Ops:
  0.6 8.6 %copy-start.3 = (f32[1,4,256,256]{3,2,1,0:T(8,128)S(1)}, f32[1,4,256,256]{3,2,1,0:T(8,128)}, u32[]{:S(2)}) copy-start(f32[1,4,256,256]{3,2,1,0:T(8,128)} %rhs.1) | copy-start | bytes 3145732
  2.4 13.4 %collective-permute-start = (f32[264,256]{1,0:T(8,128)}, f32[264,256]{1,0:T(8,128)S(1)}, u32[]{:S(2)}, u32[]{:S(2)}) collective-permute-start(f32[264,256]{1,0:T(8,128)} %shard_map.86), channel_id=1, source_target_pairs={{0,4},{4,8},{8,12},{12,16},{16,20},{20,24},{24,28},{1,5},{5,9},{9,... | collective-permute-start | bytes 811016 | tf_op jit(solution)/shard_map/ppermute | solution.py:526
  7.3 5.4 %collective-permute-start.3 = (s32[4,32]{1,0:T(4,128)}, s32[4,32]{1,0:T(4,128)S(1)}, u32[]{:S(2)}, u32[]{:S(2)}) collective-permute-start(s32[4,32]{1,0:T(4,128)} %bitcast.20), channel_id=1, source_target_pairs={{0,3},{1,2},{2,1},{3,0},{4,7},{5,6},{6,5},{7,4},{8,11},{9,10},{10,... | collective-permute-start | bytes 1544 | tf_op jit(solution)/shard_map/ppermute | solution.py:480
  8.1 4.6 %collective-permute-start.2 = (s32[4,32]{1,0:T(4,128)}, s32[4,32]{1,0:T(4,128)S(1)}, u32[]{:S(2)}, u32[]{:S(2)}) collective-permute-start(s32[4,32]{1,0:T(4,128)} %bitcast.21), channel_id=1, source_target_pairs={{0,2},{1,3},{2,0},{3,1},{4,6},{5,7},{6,4},{7,5},{8,10},{9,11},{10,... | collective-permute-start | bytes 1544 | tf_op jit(solution)/shard_map/ppermute | solution.py:480
  9.0 3.7 %collective-permute-start.1 = (s32[4,32]{1,0:T(4,128)}, s32[4,32]{1,0:T(4,128)S(1)}, u32[]{:S(2)}, u32[]{:S(2)}) collective-permute-start(s32[4,32]{1,0:T(4,128)} %bitcast.22), channel_id=1, source_target_pairs={{0,1},{1,0},{2,3},{3,2},{4,5},{5,4},{6,7},{7,6},{8,9},{9,8},{10,11... | collective-permute-start | bytes 1544 | tf_op jit(solution)/shard_map/ppermute | solution.py:480
  9.2 1.6 %copy-start = (bf16[1,4,512,512]{3,2,1,0:T(8,128)(2,1)S(1)}, bf16[1,4,512,512]{3,2,1,0:T(8,128)(2,1)}, u32[]{:S(2)}) copy-start(bf16[1,4,512,512]{3,2,1,0:T(8,128)(2,1)} %param.10) | copy-start | bytes 6291460
  10.8 0.7 copy-start.7
  11.5 1.2 copy-start.4
  11.5 1.2 copy-start.6
  11.5 6.3 %copy-start.1 = (bf16[1,4,512,512]{3,2,1,0:T(8,128)(2,1)S(1)}, bf16[1,4,512,512]{3,2,1,0:T(8,128)(2,1)}, u32[]{:S(2)}) copy-start(bf16[1,4,512,512]{3,2,1,0:T(8,128)(2,1)} %param.10) | copy-start | bytes 6291460
  12.7 1.2 copy-start.5
  15.9 10.1 %collective-permute-start.6 = (f32[128,512]{1,0:T(8,128)S(1)}, f32[128,512]{1,0:T(8,128)S(1)}, u32[]{:S(2)}, u32[]{:S(2)}) collective-permute-start(f32[128,512]{1,0:T(8,128)S(1)} %get-tuple-element.105), channel_id=1, source_target_pairs={{0,1},{1,0},{2,3},{3,2},{4,5},{5,4},{6,7},{7,6},{8,9},{9,8},{10,11... | collective-permute-start | bytes 786440 | tf_op jit(solution)/shard_map/ppermute | solution.py:489
  16.2 9.8 %collective-permute-start.7 = (f32[128,512]{1,0:T(8,128)S(1)}, f32[128,512]{1,0:T(8,128)S(1)}, u32[]{:S(2)}, u32[]{:S(2)}) collective-permute-start(f32[128,512]{1,0:T(8,128)S(1)} %get-tuple-element.106), channel_id=1, source_target_pairs={{0,2},{1,3},{2,0},{3,1},{4,6},{5,7},{6,4},{7,5},{8,10},{9,11},{10,... | collective-permute-start | bytes 786440 | tf_op jit(solution)/shard_map/ppermute | solution.py:489
  17.5 12.1 %collective-permute-start.8 = (f32[128,512]{1,0:T(8,128)S(1)}, f32[128,512]{1,0:T(8,128)S(1)}, u32[]{:S(2)}, u32[]{:S(2)}) collective-permute-start(f32[128,512]{1,0:T(8,128)S(1)} %get-tuple-element.107), channel_id=1, source_target_pairs={{0,3},{1,2},{2,1},{3,0},{4,7},{5,6},{6,5},{7,4},{8,11},{9,10},{10,... | collective-permute-start | bytes 786440 | tf_op jit(solution)/shard_map/ppermute | solution.py:489
  18.1 4.0 %collective-permute-start.9 = (f32[32,256]{1,0:T(8,128)S(1)}, f32[32,256]{1,0:T(8,128)S(1)}, u32[]{:S(2)}, u32[]{:S(2)}) collective-permute-start(f32[32,256]{1,0:T(8,128)S(1)} %get-tuple-element.109), channel_id=1, source_target_pairs={{0,4},{4,0},{8,12},{12,8},{16,20},{20,16},{24,28},{28,24},{1,5},{5... | collective-permute-start | bytes 98312 | tf_op jit(solution)/shard_map/ppermute | solution.py:464
  19.7 5.0 %collective-permute-start.10 = (f32[32,256]{1,0:T(8,128)S(1)}, f32[32,256]{1,0:T(8,128)S(1)}, u32[]{:S(2)}, u32[]{:S(2)}) collective-permute-start(f32[32,256]{1,0:T(8,128)S(1)} %get-tuple-element.110), channel_id=1, source_target_pairs={{4,8},{8,4},{12,16},{16,12},{20,24},{24,20},{5,9},{9,5},{13,17},{1... | collective-permute-start | bytes 98312 | tf_op jit(solution)/shard_map/ppermute | solution.py:465
  22.1 14.0 %collective-permute-start.4 = (f32[256,256]{1,0:T(8,128)S(1)}, f32[256,256]{1,0:T(8,128)S(1)}, u32[]{:S(2)}, u32[]{:S(2)}) collective-permute-start(f32[256,256]{1,0:T(8,128)S(1)} %get-tuple-element.95), channel_id=1, source_target_pairs={{0,4},{4,0},{8,12},{12,8},{16,20},{20,16},{24,28},{28,24},{1,5},{5... | collective-permute-start | bytes 786440 | tf_op jit(solution)/shard_map/ppermute | solution.py:464
  24.8 11.3 %collective-permute-start.5 = (f32[256,256]{1,0:T(8,128)S(1)}, f32[256,256]{1,0:T(8,128)S(1)}, u32[]{:S(2)}, u32[]{:S(2)}) collective-permute-start(f32[256,256]{1,0:T(8,128)S(1)} %get-tuple-element.96), channel_id=1, source_target_pairs={{4,8},{8,4},{12,16},{16,12},{20,24},{24,20},{5,9},{9,5},{13,17},{1... | collective-permute-start | bytes 786440 | tf_op jit(solution)/shard_map/ppermute | solution.py:465
  36.1 7.8 %copy-start.2 = (bf16[1,4,512,512]{3,2,1,0:T(8,128)(2,1)S(1)}, bf16[1,4,512,512]{3,2,1,0:T(8,128)(2,1)}, u32[]{:S(2)}) copy-start(bf16[1,4,512,512]{3,2,1,0:T(8,128)(2,1)} %param.9) | copy-start | bytes 6291460
  46.1 19.1 %collective-permute-start.11 = (f32[352,256]{1,0:T(8,128)S(1)}, f32[352,256]{1,0:T(8,128)S(1)}, u32[]{:S(2)}, u32[]{:S(2)}) collective-permute-start(f32[352,256]{1,0:T(8,128)S(1)} %get-tuple-element.116), channel_id=1, source_target_pairs={{0,4},{4,0},{8,12},{12,8},{16,20},{20,16},{24,28},{28,24},{1,5},{5... | collective-permute-start | bytes 1081352 | tf_op jit(solution)/shard_map/ppermute | solution.py:464
  48.6 16.6 %collective-permute-start.12 = (f32[352,256]{1,0:T(8,128)S(1)}, f32[352,256]{1,0:T(8,128)S(1)}, u32[]{:S(2)}, u32[]{:S(2)}) collective-permute-start(f32[352,256]{1,0:T(8,128)S(1)} %get-tuple-element.117), channel_id=1, source_target_pairs={{4,8},{8,4},{12,16},{16,12},{20,24},{24,20},{5,9},{9,5},{13,17},{1... | collective-permute-start | bytes 1081352 | tf_op jit(solution)/shard_map/ppermute | solution.py:465
  66.8 14.2 %collective-permute-start.13 = (f32[256,256]{1,0:T(8,128)S(1)}, f32[256,256]{1,0:T(8,128)S(1)}, u32[]{:S(2)}, u32[]{:S(2)}) collective-permute-start(f32[256,256]{1,0:T(8,128)S(1)} %get-tuple-element.123), channel_id=1, source_target_pairs={{0,4},{4,0},{8,12},{12,8},{16,20},{20,16},{24,28},{28,24},{1,5},{5... | collective-permute-start | bytes 786440 | tf_op jit(solution)/shard_map/ppermute | solution.py:464
  69.6 11.5 %collective-permute-start.14 = (f32[256,256]{1,0:T(8,128)S(1)}, f32[256,256]{1,0:T(8,128)S(1)}, u32[]{:S(2)}, u32[]{:S(2)}) collective-permute-start(f32[256,256]{1,0:T(8,128)S(1)} %get-tuple-element.124), channel_id=1, source_target_pairs={{4,8},{8,4},{12,16},{16,12},{20,24},{24,20},{5,9},{9,5},{13,17},{1... | collective-permute-start | bytes 786440 | tf_op jit(solution)/shard_map/ppermute | solution.py:465
  83.4 16.2 %collective-permute-start.15 = (f32[288,256]{1,0:T(8,128)S(1)}, f32[288,256]{1,0:T(8,128)S(1)}, u32[]{:S(2)}, u32[]{:S(2)}) collective-permute-start(f32[288,256]{1,0:T(8,128)S(1)} %get-tuple-element.132), channel_id=1, source_target_pairs={{0,4},{4,0},{8,12},{12,8},{16,20},{20,16},{24,28},{28,24},{1,5},{5... | collective-permute-start | bytes 884744 | tf_op jit(solution)/shard_map/ppermute | solution.py:464
  85.9 13.7 %collective-permute-start.16 = (f32[288,256]{1,0:T(8,128)S(1)}, f32[288,256]{1,0:T(8,128)S(1)}, u32[]{:S(2)}, u32[]{:S(2)}) collective-permute-start(f32[288,256]{1,0:T(8,128)S(1)} %get-tuple-element.133), channel_id=1, source_target_pairs={{4,8},{8,4},{12,16},{16,12},{20,24},{24,20},{5,9},{9,5},{13,17},{1... | collective-permute-start | bytes 884744 | tf_op jit(solution)/shard_map/ppermute | solution.py:465
  101.3 13.6 %collective-permute-start.17 = (f32[256,256]{1,0:T(8,128)S(1)}, f32[256,256]{1,0:T(8,128)S(1)}, u32[]{:S(2)}, u32[]{:S(2)}) collective-permute-start(f32[256,256]{1,0:T(8,128)S(1)} %get-tuple-element.141), channel_id=1, source_target_pairs={{0,4},{4,0},{8,12},{12,8},{16,20},{20,16},{24,28},{28,24},{1,5},{5... | collective-permute-start | bytes 786440 | tf_op jit(solution)/shard_map/ppermute | solution.py:464
  103.4 11.5 %collective-permute-start.18 = (f32[256,256]{1,0:T(8,128)S(1)}, f32[256,256]{1,0:T(8,128)S(1)}, u32[]{:S(2)}, u32[]{:S(2)}) collective-permute-start(f32[256,256]{1,0:T(8,128)S(1)} %get-tuple-element.142), channel_id=1, source_target_pairs={{4,8},{8,4},{12,16},{16,12},{20,24},{24,20},{5,9},{9,5},{13,17},{1... | collective-permute-start | bytes 786440 | tf_op jit(solution)/shard_map/ppermute | solution.py:465
  116.9 15.0 %collective-permute-start.19 = (f32[256,256]{1,0:T(8,128)S(1)}, f32[256,256]{1,0:T(8,128)S(1)}, u32[]{:S(2)}, u32[]{:S(2)}) collective-permute-start(f32[256,256]{1,0:T(8,128)S(1)} %get-tuple-element.148), channel_id=1, source_target_pairs={{4,0},{8,4},{12,8},{16,12},{20,16},{24,20},{28,24},{5,1},{9,5},{13... | collective-permute-start | bytes 786440 | tf_op jit(solution)/shard_map/ppermute | solution.py:614

commit v8 on v7

--- a/solution.py
+++ b/solution.py
@@ -77,13 +77,17 @@
 
 
 def send(even, to_next, to_prev, near_out, far_out):
-    near_out[...] = jnp.where(even, to_next, to_prev)
-    far_out[...] = jnp.where(even, to_prev, to_next)
+    row = 0
+    for ahead, behind in zip(to_next, to_prev):
+        rows = slice(row, row + ahead.shape[0])
+        near_out[rows, :] = jnp.where(even, ahead, behind)
+        far_out[rows, :] = jnp.where(even, behind, ahead)
+        row += ahead.shape[0]
 
 
 def send_faces(even, first, last, near_out, far_out):
     width = first.shape[1] // 2
-    send(even, last[:, width:], first[:, :width], near_out, far_out)
+    send(even, [last[:, width:]], [first[:, :width]], near_out, far_out)
 
 
 def panel_products(parts, panel, result, extra=None):
@@ -156,20 +160,21 @@
         rest[sub - 1] = mul(high, panel[sub]) + mul(low, panel[sub])
 
 
-def head_kernel(head, partial, rest, panel, live, edge, first, near_out, far_out):
+def head_kernel(head, partial, rest, panel, coupling, live, edge, first, near_out, far_out):
     loads, width = edge.shape
     live[...] = head[loads : loads + 1]
     edge[...] = head[:loads]
     high, low = split(head[:loads])
     first[...] = partial[...] - mul(high, panel[0, :width]) - mul(low, panel[0, :width])
     last = rest[rest.shape[0] - 1]
-    send_faces(even_place(), first[...], last, near_out, far_out)
+    to_next = [last[:, width:], coupling[coupling.shape[0] - 1, :, width:]]
+    send(even_place(), to_next, [first[:, :width], coupling[0, :, :width]], near_out, far_out)
 
 
 def setup_kernel(*refs):
-    group = (len(refs) - 7) // 2
+    group = (len(refs) - 5) // 2
     maps, (coarse, coupling) = refs[:group], refs[group : group + 2]
-    picked, (stacked, lift, near_out, far_out, everyone) = refs[group + 2 : -5], refs[-5:]
+    picked, (stacked, lift, everyone) = refs[group + 2 : -3], refs[-3:]
     subs, corners = maps[0].shape
     rows, size = coarse.shape
     own = subs * corners
@@ -179,8 +184,6 @@
         spare = jnp.zeros((lift.shape[1] - 3 * corners, high.shape[1]), jnp.bfloat16)
         stacked[sub] = jnp.concatenate([high, low], axis=0)
         lift[sub] = jnp.concatenate([high, high, low, spare], axis=0)
-    width = coupling.shape[2] // 2
-    send(even_place(), coupling[subs - 1, :, width:], coupling[0, :, :width], near_out, far_out)
     for distance in range(group):
         unknowns = [maps[distance][sub : sub + 1, :] for sub in range(subs)]
         everyone[distance] = jnp.concatenate(unknowns, axis=1)
@@ -224,8 +227,8 @@
     subs, rows = coupling.shape[0], coupling.shape[1]
     width = coupling.shape[2] // 2
     live = Joined(live_edge, live_own)
-    before = jnp.where(even, far[...], near[...])
-    after = jnp.where(even, near[...], far[...])
+    sides = received(even, near, far, near.shape[0] - rows, rows)
+    before, after = sides[:rows], sides[rows:]
     left = [coupling[sub, :, :width] * (0.25 * live[sub]) for sub in range(subs)]
     left.append(after * (0.25 * live[subs]))
     right = [before * (0.25 * live[0])]
@@ -330,12 +333,7 @@
     lower = live_own[0] * (result[0][:, width:] - result[1][:, :width])
     to_next.append(outer_rows(for_next, upper))
     to_prev.append(outer_rows(for_prev, lower))
-    row = 0
-    for ahead, behind in zip(to_next, to_prev):
-        rows = slice(row, row + ahead.shape[0])
-        near_out[rows, :] = jnp.where(even, ahead, behind)
-        far_out[rows, :] = jnp.where(even, behind, ahead)
-        row += ahead.shape[0]
+    send(even, to_next, to_prev, near_out, far_out)
 
 
 def first_dual_kernel(edge, own, residual, panel, everyone, block, lift, live_own,
@@ -518,6 +516,8 @@
 
     face_shape, own_shape = (loads, width), (subs, loads, width)
     first_shape, rest_shape = (loads, 2 * width), (subs - 1, loads, 2 * width)
+    scalars_shape, outside_shape, side_shape = (2, loads), (2 * corners, loads), (corners, width)
+    long_shape, longer_shape = (loads + corners, width), (loads + 3 * corners, width)
     edges_shapes = [face_shape, own_shape]
     result_shapes = [first_shape, rest_shape, face_shape, face_shape]
 
@@ -532,36 +532,31 @@
     )
     group, own = len(maps), subs * corners
     pair = [(corners, width)] * 2
-    *picked, stacked, lift, near_side, far_side = call(
+    *picked, stacked, lift = call(
         setup_kernel,
         [(own, group * own)] * group
-        + [(subs, 2 * corners, 2 * width), (subs, 3 * corners + -3 * corners % 128, 2 * width)]
-        + pair,
+        + [(subs, 2 * corners, 2 * width), (subs, 3 * corners + -3 * corners % 128, 2 * width)],
         *maps, coarse_inverse[0], coupling[0],
-        kinds=[jnp.float32] * group + [jnp.bfloat16] * 2 + [jnp.float32] * 2,
+        kinds=[jnp.float32] * group + [jnp.bfloat16] * 2,
         scratch=[pltpu.VMEM((group, 1, own), jnp.int32)],
     )
     head, picked, rest = lax.optimization_barrier((head, picked, rest))
     live_edge, residual_edge, first, near, far = call(
         head_kernel,
-        [(1, width), face_shape, first_shape, face_shape, face_shape],
-        head, partial, rest, dirichlet,
-    )
-    near, far, near_side, far_side = lax.optimization_barrier((near, far, near_side, far_side))
+        [(1, width), face_shape, first_shape, long_shape, long_shape],
+        head, partial, rest, dirichlet, coupling[0],
+    )
     near, far = swap(near, far)
-    near_side, far_side = swap(near_side, far_side)
     block = jnp.concatenate(split_outside(swap_blocks(picked)), axis=0)
     live, residual = (live_edge, live_own), (residual_edge, residual_own)
     taken, ends, for_next, for_prev, given = call(
         operators_kernel,
-        [(2 * own, (subs + 1) * width), (2,) + pair[0], (2 * corners, width),
-         (2 * corners, width), (2,) + pair[0]],
-        coupling[0], *live, near_side, far_side, dirichlet,
+        [(2 * own, (subs + 1) * width), (2,) + side_shape, (2 * corners, width),
+         (2 * corners, width), (2,) + side_shape],
+        coupling[0], *live, near, far, dirichlet,
         kinds=[jnp.bfloat16, jnp.float32, jnp.bfloat16, jnp.bfloat16, jnp.float32],
     )
 
-    scalars_shape, outside_shape = (2, loads), (2 * corners, loads)
-    long_shape, longer_shape = (loads + corners, width), (loads + 3 * corners, width)
     edge, first_z, values = call(
         corner_kernel,
         edges_shapes + [(own, loads)],
@@ -580,7 +575,7 @@
      outside) = call(
         first_update_kernel,
         [own_shape, face_shape] + edges_shapes + result_shapes
-        + [scalars_shape, (2,) + pair[0], outside_shape, outside_shape],
+        + [scalars_shape, (2,) + side_shape, outside_shape, outside_shape],
         first, rest, near, far, *live, sums, *residual, dirichlet, ends,
     )
 

time: 134 us -> 133 us (level)
  starting transfers between devices: 28.1 us -> 24.4 us
    ppermute x3, waiting for transfers between devices: 3.58 us -> 9.2 us  [swap_blocks(): block = block + lax.ppermute(picked[distance], 'grp', routes)]
    ppermute x6 -> x5, waiting for transfers between devices: 14.6 us -> 9.74 us  [swap(): lax.ppermute(near, 'sub', neighbour_pairs(size, 0))]
    ppermute x6 -> x5, starting transfers between devices: 14.1 us -> 11.1 us  [swap(): lax.ppermute(near, 'sub', neighbour_pairs(size, 0))]
    ppermute x6 -> x5, starting transfers between devices: 3.99 us -> 3.34 us  [swap(): lax.ppermute(far, 'sub', neighbour_pairs(size, 1))]
  transfers between devices with their start and end apart: 20 -> 18, of which waited for: 5 -> 5; matrix products, arithmetic and copies ran while one was open for 0% -> 0% of each run, Pallas kernels for 4% -> 4%
where the time goes in v8:
time: 133 us
  blocking collectives  64.5 us (48%)
  starting transfers between devices  24.4 us (18%)
  Pallas kernels  19.4 us (15%)
  waiting for transfers between devices  19 us (14%)
  local copies, waits for them, and re-layouts  4.54 us (3%)
    all_to_all x3, blocking collectives, from_all(): return lax.all_to_all(copies, ('sub', 'grp'), 0, 0)  43.8 us
    all_gather x3, blocking collectives, local(): everyone = lax.all_gather(values, 'grp', tiled=True)  20.7 us
    pallas_call x13, Pallas kernels, call(): pl.pallas_call(kernel, out_shape=[jax.ShapeDtypeStruct(*shape) for shape...  17.6 us
    ppermute x5, starting transfers between devices, swap(): lax.ppermute(near, 'sub', neighbour_pairs(size, 0))  11.1 us
    ppermute x5, waiting for transfers between devices, swap(): lax.ppermute(near, 'sub', neighbour_pairs(size, 0))  9.74 us
    ppermute x3, waiting for transfers between devices, swap_blocks(): block = block + lax.ppermute(picked[distance], 'grp', routes)  9.2 us
    ppermute x1, starting transfers between devices, local(): head = lax.ppermute(tail, 'sub', [(i, i + 1) for i in range(size - 1)])  4.86 us
    unnamed x16, local copies, waits for them, and re-layouts  4.48 us
  transfers between devices with their start and end apart: 18, of which 5 were waited for; matrix products, arithmetic and copies ran while one was open for 0% of the time, Pallas kernels for 4%

profile of v8, /device:TPU:0, one launch (start us, length us, event | category | flops | bytes accessed | tf_op | source)
XLA Modules:
  0.0 132.8 jit_solution(5191630489609463938)
XLA Ops:
  0.6 0.0 copy-start.3
  0.6 1.8 %shard_map.86 = f32[264,256]{1,0:T(8,128)} custom-call(s32[1,4]{1,0:T(1,128)} %counts, f32[1,4,256,256]{3,2,1,0:T(8,128)} %rhs.1), custom_call_target="tpu_custom_call" | custom-call | tf_op jit(solution)/shard_map/pallas_call | solution.py:493
  2.4 4.9 %collective-permute-start = (f32[264,256]{1,0:T(8,128)}, f32[264,256]{1,0:T(8,128)S(1)}, u32[]{:S(2)}, u32[]{:S(2)}) collective-permute-start(f32[264,256]{1,0:T(8,128)} %shard_map.86), channel_id=1, source_target_pairs={{0,4},{4,8},{8,12},{12,16},{16,20},{20,24},{24,28},{1,5},{5,9},{9,... | collective-permute-start | bytes 811016 | tf_op jit(solution)/shard_map/ppermute | solution.py:526
  7.3 0.7 collective-permute-start.3
  8.1 0.9 collective-permute-start.2
  9.0 0.3 collective-permute-start.1
  9.2 1.6 %copy-done = bf16[1,4,512,512]{3,2,1,0:T(8,128)(2,1)S(1)} copy-done((bf16[1,4,512,512]{3,2,1,0:T(8,128)(2,1)S(1)}, bf16[1,4,512,512]{3,2,1,0:T(8,128)(2,1)}, u32[]{:S(2)}) %copy-start) | copy-done | bytes 2097176
  10.8 0.7 copy-done.7
  11.5 1.2 shard_map.88
  12.7 0.0 collective-permute-done.3.refs_3_
  12.7 0.0 collective-permute-done.2.refs_2_
  12.7 0.0 collective-permute-done.1.refs_1_
  12.7 0.0 copy-start.5
  12.8 1.2 copy-done.5
  14.0 1.9 %shard_map.87 = (f32[128,512]{1,0:T(8,128)S(1)}, f32[128,512]{1,0:T(8,128)S(1)}, f32[128,512]{1,0:T(8,128)S(1)}, f32[128,512]{1,0:T(8,128)S(1)}, bf16[4,64,512]{...) custom-call(s32[4,32]{1,0:T(4,128)S(1)} %bitcast.24, s32[4,32]{1,0:T(4,128)S(1)} %collective-permute-done.1.refs_1_, ...), custom_call_target="tpu_custom_call" | custom-call | tf_op jit(solution)/shard_map/pallas_call | solution.py:35
  15.9 0.0 collective-permute-done.head
  15.9 0.3 collective-permute-start.6
  16.2 1.3 %collective-permute-start.7 = (f32[128,512]{1,0:T(8,128)S(1)}, f32[128,512]{1,0:T(8,128)S(1)}, u32[]{:S(2)}, u32[]{:S(2)}) collective-permute-start(f32[128,512]{1,0:T(8,128)S(1)} %get-tuple-element.96), channel_id=1, source_target_pairs={{0,2},{1,3},{2,0},{3,1},{4,6},{5,7},{6,4},{7,5},{8,10},{9,11},{10,... | collective-permute-start | bytes 786440 | tf_op jit(solution)/shard_map/ppermute | solution.py:487
  17.6 0.3 collective-permute-start.8
  17.8 0.0 copy-done.1
  17.8 0.3 shard_map.89
  18.2 1.6 %collective-permute-start.4 = (f32[288,256]{1,0:T(8,128)S(1)}, f32[288,256]{1,0:T(8,128)S(1)}, u32[]{:S(2)}, u32[]{:S(2)}) collective-permute-start(f32[288,256]{1,0:T(8,128)S(1)} %get-tuple-element.85), channel_id=1, source_target_pairs={{0,4},{4,0},{8,12},{12,8},{16,20},{20,16},{24,28},{28,24},{1,5},{5... | collective-permute-start | bytes 884744 | tf_op jit(solution)/shard_map/ppermute | solution.py:462
  19.8 0.7 collective-permute-start.5
  20.4 0.0 collective-permute-done.6
  20.4 4.9 %collective-permute-done.7 = f32[128,512]{1,0:T(8,128)S(1)} collective-permute-done((f32[128,512]{1,0:T(8,128)S(1)}, f32[128,512]{1,0:T(8,128)S(1)}, u32[]{:S(2)}, u32[]{:S(2)}) %collective-permute-start.7) | collective-permute-done | bytes 262176 | tf_op jit(solution)/shard_map/ppermute | solution.py:487
  25.4 4.3 %collective-permute-done.8 = f32[128,512]{1,0:T(8,128)S(1)} collective-permute-done((f32[128,512]{1,0:T(8,128)S(1)}, f32[128,512]{1,0:T(8,128)S(1)}, u32[]{:S(2)}, u32[]{:S(2)}) %collective-permute-start.8) | collective-permute-done | bytes 262176 | tf_op jit(solution)/shard_map/ppermute | solution.py:487
  29.6 0.1 reduce-precision_convert_fusion
  29.8 3.2 %collective-permute-done.4.near = f32[288,256]{1,0:T(8,128)S(1)} collective-permute-done((f32[288,256]{1,0:T(8,128)S(1)}, f32[288,256]{1,0:T(8,128)S(1)}, u32[]{:S(2)}, u32[]{:S(2)}) %collective-permute-start.4) | collective-permute-done | bytes 294944 | tf_op jit(solution)/shard_map/ppermute | solution.py:462
  33.0 0.0 collective-permute-done.5.far
  33.0 0.7 shard_map.90
  33.8 7.0 %all_gather.9.everyone = f32[512,256]{1,0:T(8,128)S(1)} all-gather(f32[128,256]{1,0:T(8,128)S(1)} %get-tuple-element.93), channel_id=1, replica_groups=mesh['sub'=8,'grp'=4] {'grp'}, dimensions={0}, use_global_device_ids=true | all-gather | bytes 655360 | tf_op jit(solution)/shard_map/all_gather | solution.py:565
  40.8 0.6 shard_map.91
  41.4 1.0 copy-done.2
  42.4 2.2 %shard_map.92 = (f32[256,512]{1,0:T(8,128)S(1)}, f32[3,256,512]{2,1,0:T(8,128)S(1)}, f32[352,256]{1,0:T(8,128)S(1)}, f32[352,256]{1,0:T(8,128)S(1)}, f32[2,256]{1,0:T(2,128)S(1)}) custom-call(f32[256,256]{1,0:T(8,128)S(1)} %get-tuple-element.90.edge, f32[4,256,256]{2,1,0:T(8,128)S(1)} %get-tuple-element.91.own.first_z, ...), custom_call_target="tpu_custom_call" | custom-call | tf_op jit(solution)/shard_map/pallas_call | solution.py:35
  44.6 2.5 %collective-permute-start.9 = (f32[352,256]{1,0:T(8,128)S(1)}, f32[352,256]{1,0:T(8,128)S(1)}, u32[]{:S(2)}, u32[]{:S(2)}) collective-permute-start(f32[352,256]{1,0:T(8,128)S(1)} %get-tuple-element.104), channel_id=1, source_target_pairs={{0,4},{4,0},{8,12},{12,8},{16,20},{20,16},{24,28},{28,24},{1,5},{5... | collective-permute-start | bytes 1081352 | tf_op jit(solution)/shard_map/ppermute | solution.py:462
  47.2 0.7 collective-permute-start.10
  47.9 15.9 %all_to_all.15.sums = f32[32,2,256]{2,1,0:T(2,128)S(1)} all-to-all(f32[32,2,256]{2,1,0:T(2,128)S(1)} %broadcast_in_dim.10), channel_id=1, replica_groups=mesh['sub'=8,'grp'=4] {'sub','grp'}, dimensions={0} | all-to-all | bytes 131072 | tf_op jit(solution)/shard_map/all_to_all | solution.py:470
  63.8 0.0 collective-permute-done.9.near
  63.8 0.0 collective-permute-done.10.far
  63.8 1.6 %shard_map.93 = (f32[4,256,256]{2,1,0:T(8,128)S(1)}, f32[256,256]{1,0:T(8,128)S(1)}, f32[256,256]{1,0:T(8,128)S(1)}, f32[4,256,256]{2,1,0:T(8,128)S(1)}, f32[256...) custom-call(f32[256,512]{1,0:T(8,128)S(1)} %get-tuple-element.102.fi, ...), custom_call_target="tpu_custom_call" | custom-call | tf_op jit(solution)/shard_map/pallas_call | solution.py:35
  65.4 2.8 %collective-permute-start.11 = (f32[256,256]{1,0:T(8,128)S(1)}, f32[256,256]{1,0:T(8,128)S(1)}, u32[]{:S(2)}, u32[]{:S(2)}) collective-permute-start(f32[256,256]{1,0:T(8,128)S(1)} %get-tuple-element.111), channel_id=1, source_target_pairs={{0,4},{4,0},{8,12},{12,8},{16,20},{20,16},{24,28},{28,24},{1,5},{5... | collective-permute-start | bytes 786440 | tf_op jit(solution)/shard_map/ppermute | solution.py:462
  68.1 0.7 collective-permute-start.12
  68.8 0.7 shard_map.94
  69.5 6.8 %all_gather.10.refs_8_ = f32[512,256]{1,0:T(8,128)S(1)} all-gather(f32[128,256]{1,0:T(8,128)S(1)} %shard_map.94), channel_id=1, replica_groups=mesh['sub'=8,'grp'=4] {'grp'}, dimensions={0}, use_global_device_ids=true | all-gather | bytes 655360 | tf_op jit(solution)/shard_map/all_gather | solution.py:584
  76.4 3.2 %collective-permute-done.11.refs_2_ = f32[256,256]{1,0:T(8,128)S(1)} collective-permute-done((f32[256,256]{1,0:T(8,128)S(1)}, f32[256,256]{1,0:T(8,128)S(1)}, u32[]{:S(2)}, u32[]{:S(2)}) %collective-permute-start.11) | collective-permute-done | bytes 262176 | tf_op jit(solution)/shard_map/ppermute | solution.py:462
  79.6 0.0 collective-permute-done.12.refs_3_
  79.6 2.2 %shard_map.95 = (f32[4,256,256]{2,1,0:T(8,128)S(1)}, f32[256,512]{1,0:T(8,128)S(1)}, f32[3,256,512]{2,1,0:T(8,128)S(1)}, f32[288,256]{1,0:T(8,128)S(1)}, f32[288,256]{1,0:T(8,128)S(1)}, /*index=5*/f32[2,256]{1,0:T(2,128)S(1)}) custom-call(f32[256,512]{1,0:T(8,128)S(1)} %get-tuple-element.109.refs_0_, f32[3,256,512]{2,1,0:T(8,128)S(1)} %get-tuple-element.110.refs_1_, ...), custom_call_target="tpu_custom_call" | custom-call | tf_op jit(solution)/shard_map/pallas_call | solution.py:35
  81.8 2.5 %collective-permute-start.13 = (f32[288,256]{1,0:T(8,128)S(1)}, f32[288,256]{1,0:T(8,128)S(1)}, u32[]{:S(2)}, u32[]{:S(2)}) collective-permute-start(f32[288,256]{1,0:T(8,128)S(1)} %get-tuple-element.120), channel_id=1, source_target_pairs={{0,4},{4,0},{8,12},{12,8},{16,20},{20,16},{24,28},{28,24},{1,5},{5... | collective-permute-start | bytes 884744 | tf_op jit(solution)/shard_map/ppermute | solution.py:462
  84.3 0.7 collective-permute-start.14
  85.0 13.5 %all_to_all.16.sums = f32[32,2,256]{2,1,0:T(2,128)S(1)} all-to-all(f32[32,2,256]{2,1,0:T(2,128)S(1)} %broadcast_in_dim.11), channel_id=1, replica_groups=mesh['sub'=8,'grp'=4] {'sub','grp'}, dimensions={0} | all-to-all | bytes 131072 | tf_op jit(solution)/shard_map/all_to_all | solution.py:470
  98.5 0.0 collective-permute-done.13.near
  98.5 0.0 collective-permute-done.14.far
  98.5 1.7 %shard_map.96 = (f32[4,256,256]{2,1,0:T(8,128)S(1)}, f32[256,256]{1,0:T(8,128)S(1)}, f32[4,256,256]{2,1,0:T(8,128)S(1)}, f32[256,512]{1,0:T(8,128)S(1)}, f32[3,2...) custom-call(f32[256,512]{1,0:T(8,128)S(1)} %get-tuple-element.118.fi, ...), custom_call_target="tpu_custom_call" | custom-call | tf_op jit(solution)/shard_map/pallas_call | solution.py:35
  100.2 1.7 %collective-permute-start.15 = (f32[256,256]{1,0:T(8,128)S(1)}, f32[256,256]{1,0:T(8,128)S(1)}, u32[]{:S(2)}, u32[]{:S(2)}) collective-permute-start(f32[256,256]{1,0:T(8,128)S(1)} %get-tuple-element.129), channel_id=1, source_target_pairs={{0,4},{4,0},{8,12},{12,8},{16,20},{20,16},{24,28},{28,24},{1,5},{5... | collective-permute-start | bytes 786440 | tf_op jit(solution)/shard_map/ppermute | solution.py:462
  101.9 0.7 collective-permute-start.16
  102.5 0.7 shard_map.97
  103.2 6.8 %all_gather.11.refs_8_ = f32[512,256]{1,0:T(8,128)S(1)} all-gather(f32[128,256]{1,0:T(8,128)S(1)} %shard_map.97), channel_id=1, replica_groups=mesh['sub'=8,'grp'=4] {'grp'}, dimensions={0}, use_global_device_ids=true | all-gather | bytes 655360 | tf_op jit(solution)/shard_map/all_gather | solution.py:602
  110.0 3.3 %collective-permute-done.15.refs_2_ = f32[256,256]{1,0:T(8,128)S(1)} collective-permute-done((f32[256,256]{1,0:T(8,128)S(1)}, f32[256,256]{1,0:T(8,128)S(1)}, u32[]{:S(2)}, u32[]{:S(2)}) %collective-permute-start.15) | collective-permute-done | bytes 262176 | tf_op jit(solution)/shard_map/ppermute | solution.py:462
  113.3 0.0 collective-permute-done.16.refs_3_
  113.3 2.0 %shard_map.98 = (f32[4,256,256]{2,1,0:T(8,128)S(1)}, f32[256,512]{1,0:T(8,128)S(1)}, f32[3,256,512]{2,1,0:T(8,128)S(1)}, f32[256,256]{1,0:T(8,128)S(1)}, f32[2,256]{1,0:T(2,128)S(1)}) custom-call(f32[256,512]{1,0:T(8,128)S(1)} %get-tuple-element.127.refs_0_, f32[3,256,512]{2,1,0:T(8,128)S(1)} %get-tuple-element.128.refs_1_, ...), custom_call_target="tpu_custom_call" | custom-call | tf_op jit(solution)/shard_map/pallas_call | solution.py:35
  115.3 1.3 collective-permute-start.17
  116.7 14.4 %all_to_all.17.sums = f32[32,2,256]{2,1,0:T(2,128)S(1)} all-to-all(f32[32,2,256]{2,1,0:T(2,128)S(1)} %broadcast_in_dim.12), channel_id=1, replica_groups=mesh['sub'=8,'grp'=4] {'sub','grp'}, dimensions={0} | all-to-all | bytes 131072 | tf_op jit(solution)/shard_map/all_to_all | solution.py:470
  131.1 0.0 collective-permute-done.17.following
  131.1 1.8 %shard_map.99 = (f32[4,256,256]{2,1,0:T(8,128)}, f32[4,256,256]{2,1,0:T(8,128)}) custom-call(f32[256,512]{1,0:T(8,128)S(1)} %get-tuple-element.134.first, f32[3,256,512]{2,1,0:T(8,128)S(1)} %get-tuple-element.135.rest, f32[256,256]{1,0:T(8,128)S(1)} %collective-permute-done.17.following, f32[4,1,256]{2,1,0:T(1,128)S(1)} %get-tuple-element.88.live_rest.live_own.refs_5_.live, ...), custom_call_target="tpu_custom_call" | custom-call | tf_op jit(solution)/shard_map/pallas_call | solution.py:35
  (14 shorter events, 0.1 us)
Async XLA Ops:
  0.6 8.6 %copy-start.3 = (f32[1,4,256,256]{3,2,1,0:T(8,128)S(1)}, f32[1,4,256,256]{3,2,1,0:T(8,128)}, u32[]{:S(2)}) copy-start(f32[1,4,256,256]{3,2,1,0:T(8,128)} %rhs.1) | copy-start | bytes 3145732
  2.4 13.5 %collective-permute-start = (f32[264,256]{1,0:T(8,128)}, f32[264,256]{1,0:T(8,128)S(1)}, u32[]{:S(2)}, u32[]{:S(2)}) collective-permute-start(f32[264,256]{1,0:T(8,128)} %shard_map.86), channel_id=1, source_target_pairs={{0,4},{4,8},{8,12},{12,16},{16,20},{20,24},{24,28},{1,5},{5,9},{9,... | collective-permute-start | bytes 811016 | tf_op jit(solution)/shard_map/ppermute | solution.py:526
  7.3 5.4 %collective-permute-start.3 = (s32[4,32]{1,0:T(4,128)}, s32[4,32]{1,0:T(4,128)S(1)}, u32[]{:S(2)}, u32[]{:S(2)}) collective-permute-start(s32[4,32]{1,0:T(4,128)} %bitcast.21), channel_id=1, source_target_pairs={{0,3},{1,2},{2,1},{3,0},{4,7},{5,6},{6,5},{7,4},{8,11},{9,10},{10,... | collective-permute-start | bytes 1544 | tf_op jit(solution)/shard_map/ppermute | solution.py:478
  8.1 4.7 %collective-permute-start.2 = (s32[4,32]{1,0:T(4,128)}, s32[4,32]{1,0:T(4,128)S(1)}, u32[]{:S(2)}, u32[]{:S(2)}) collective-permute-start(s32[4,32]{1,0:T(4,128)} %bitcast.22), channel_id=1, source_target_pairs={{0,2},{1,3},{2,0},{3,1},{4,6},{5,7},{6,4},{7,5},{8,10},{9,11},{10,... | collective-permute-start | bytes 1544 | tf_op jit(solution)/shard_map/ppermute | solution.py:478
  9.0 3.7 %collective-permute-start.1 = (s32[4,32]{1,0:T(4,128)}, s32[4,32]{1,0:T(4,128)S(1)}, u32[]{:S(2)}, u32[]{:S(2)}) collective-permute-start(s32[4,32]{1,0:T(4,128)} %bitcast.23), channel_id=1, source_target_pairs={{0,1},{1,0},{2,3},{3,2},{4,5},{5,4},{6,7},{7,6},{8,9},{9,8},{10,11... | collective-permute-start | bytes 1544 | tf_op jit(solution)/shard_map/ppermute | solution.py:478
  9.2 1.6 %copy-start = (bf16[1,4,512,512]{3,2,1,0:T(8,128)(2,1)S(1)}, bf16[1,4,512,512]{3,2,1,0:T(8,128)(2,1)}, u32[]{:S(2)}) copy-start(bf16[1,4,512,512]{3,2,1,0:T(8,128)(2,1)} %param.10) | copy-start | bytes 6291460
  10.8 0.7 copy-start.7
  11.5 1.2 copy-start.4
  11.5 1.2 copy-start.6
  11.5 6.3 %copy-start.1 = (bf16[1,4,512,512]{3,2,1,0:T(8,128)(2,1)S(1)}, bf16[1,4,512,512]{3,2,1,0:T(8,128)(2,1)}, u32[]{:S(2)}) copy-start(bf16[1,4,512,512]{3,2,1,0:T(8,128)(2,1)} %param.10) | copy-start | bytes 6291460
  12.7 1.2 copy-start.5
  15.9 4.5 %collective-permute-start.6 = (f32[128,512]{1,0:T(8,128)S(1)}, f32[128,512]{1,0:T(8,128)S(1)}, u32[]{:S(2)}, u32[]{:S(2)}) collective-permute-start(f32[128,512]{1,0:T(8,128)S(1)} %get-tuple-element.95), channel_id=1, source_target_pairs={{0,1},{1,0},{2,3},{3,2},{4,5},{5,4},{6,7},{7,6},{8,9},{9,8},{10,11... | collective-permute-start | bytes 786440 | tf_op jit(solution)/shard_map/ppermute | solution.py:487
  16.2 9.1 %collective-permute-start.7 = (f32[128,512]{1,0:T(8,128)S(1)}, f32[128,512]{1,0:T(8,128)S(1)}, u32[]{:S(2)}, u32[]{:S(2)}) collective-permute-start(f32[128,512]{1,0:T(8,128)S(1)} %get-tuple-element.96), channel_id=1, source_target_pairs={{0,2},{1,3},{2,0},{3,1},{4,6},{5,7},{6,4},{7,5},{8,10},{9,11},{10,... | collective-permute-start | bytes 786440 | tf_op jit(solution)/shard_map/ppermute | solution.py:487
  17.6 12.1 %collective-permute-start.8 = (f32[128,512]{1,0:T(8,128)S(1)}, f32[128,512]{1,0:T(8,128)S(1)}, u32[]{:S(2)}, u32[]{:S(2)}) collective-permute-start(f32[128,512]{1,0:T(8,128)S(1)} %get-tuple-element.97), channel_id=1, source_target_pairs={{0,3},{1,2},{2,1},{3,0},{4,7},{5,6},{6,5},{7,4},{8,11},{9,10},{10,... | collective-permute-start | bytes 786440 | tf_op jit(solution)/shard_map/ppermute | solution.py:487
  18.2 14.9 %collective-permute-start.4 = (f32[288,256]{1,0:T(8,128)S(1)}, f32[288,256]{1,0:T(8,128)S(1)}, u32[]{:S(2)}, u32[]{:S(2)}) collective-permute-start(f32[288,256]{1,0:T(8,128)S(1)} %get-tuple-element.85), channel_id=1, source_target_pairs={{0,4},{4,0},{8,12},{12,8},{16,20},{20,16},{24,28},{28,24},{1,5},{5... | collective-permute-start | bytes 884744 | tf_op jit(solution)/shard_map/ppermute | solution.py:462
  19.8 13.3 %collective-permute-start.5 = (f32[288,256]{1,0:T(8,128)S(1)}, f32[288,256]{1,0:T(8,128)S(1)}, u32[]{:S(2)}, u32[]{:S(2)}) collective-permute-start(f32[288,256]{1,0:T(8,128)S(1)} %get-tuple-element.86), channel_id=1, source_target_pairs={{4,8},{8,4},{12,16},{16,12},{20,24},{24,20},{5,9},{9,5},{13,17},{1... | collective-permute-start | bytes 884744 | tf_op jit(solution)/shard_map/ppermute | solution.py:463
  40.8 1.6 %copy-start.2 = (bf16[1,4,512,512]{3,2,1,0:T(8,128)(2,1)S(1)}, bf16[1,4,512,512]{3,2,1,0:T(8,128)(2,1)}, u32[]{:S(2)}) copy-start(bf16[1,4,512,512]{3,2,1,0:T(8,128)(2,1)} %param.9) | copy-start | bytes 6291460
  44.6 19.1 %collective-permute-start.9 = (f32[352,256]{1,0:T(8,128)S(1)}, f32[352,256]{1,0:T(8,128)S(1)}, u32[]{:S(2)}, u32[]{:S(2)}) collective-permute-start(f32[352,256]{1,0:T(8,128)S(1)} %get-tuple-element.104), channel_id=1, source_target_pairs={{0,4},{4,0},{8,12},{12,8},{16,20},{20,16},{24,28},{28,24},{1,5},{5... | collective-permute-start | bytes 1081352 | tf_op jit(solution)/shard_map/ppermute | solution.py:462
  47.2 16.6 %collective-permute-start.10 = (f32[352,256]{1,0:T(8,128)S(1)}, f32[352,256]{1,0:T(8,128)S(1)}, u32[]{:S(2)}, u32[]{:S(2)}) collective-permute-start(f32[352,256]{1,0:T(8,128)S(1)} %get-tuple-element.105), channel_id=1, source_target_pairs={{4,8},{8,4},{12,16},{16,12},{20,24},{24,20},{5,9},{9,5},{13,17},{1... | collective-permute-start | bytes 1081352 | tf_op jit(solution)/shard_map/ppermute | solution.py:463
  65.4 14.2 %collective-permute-start.11 = (f32[256,256]{1,0:T(8,128)S(1)}, f32[256,256]{1,0:T(8,128)S(1)}, u32[]{:S(2)}, u32[]{:S(2)}) collective-permute-start(f32[256,256]{1,0:T(8,128)S(1)} %get-tuple-element.111), channel_id=1, source_target_pairs={{0,4},{4,0},{8,12},{12,8},{16,20},{20,16},{24,28},{28,24},{1,5},{5... | collective-permute-start | bytes 786440 | tf_op jit(solution)/shard_map/ppermute | solution.py:462
  68.1 11.5 %collective-permute-start.12 = (f32[256,256]{1,0:T(8,128)S(1)}, f32[256,256]{1,0:T(8,128)S(1)}, u32[]{:S(2)}, u32[]{:S(2)}) collective-permute-start(f32[256,256]{1,0:T(8,128)S(1)} %get-tuple-element.112), channel_id=1, source_target_pairs={{4,8},{8,4},{12,16},{16,12},{20,24},{24,20},{5,9},{9,5},{13,17},{1... | collective-permute-start | bytes 786440 | tf_op jit(solution)/shard_map/ppermute | solution.py:463
  81.8 16.7 %collective-permute-start.13 = (f32[288,256]{1,0:T(8,128)S(1)}, f32[288,256]{1,0:T(8,128)S(1)}, u32[]{:S(2)}, u32[]{:S(2)}) collective-permute-start(f32[288,256]{1,0:T(8,128)S(1)} %get-tuple-element.120), channel_id=1, source_target_pairs={{0,4},{4,0},{8,12},{12,8},{16,20},{20,16},{24,28},{28,24},{1,5},{5... | collective-permute-start | bytes 884744 | tf_op jit(solution)/shard_map/ppermute | solution.py:462
  84.3 14.2 %collective-permute-start.14 = (f32[288,256]{1,0:T(8,128)S(1)}, f32[288,256]{1,0:T(8,128)S(1)}, u32[]{:S(2)}, u32[]{:S(2)}) collective-permute-start(f32[288,256]{1,0:T(8,128)S(1)} %get-tuple-element.121), channel_id=1, source_target_pairs={{4,8},{8,4},{12,16},{16,12},{20,24},{24,20},{5,9},{9,5},{13,17},{1... | collective-permute-start | bytes 884744 | tf_op jit(solution)/shard_map/ppermute | solution.py:463
  100.2 13.1 %collective-permute-start.15 = (f32[256,256]{1,0:T(8,128)S(1)}, f32[256,256]{1,0:T(8,128)S(1)}, u32[]{:S(2)}, u32[]{:S(2)}) collective-permute-start(f32[256,256]{1,0:T(8,128)S(1)} %get-tuple-element.129), channel_id=1, source_target_pairs={{0,4},{4,0},{8,12},{12,8},{16,20},{20,16},{24,28},{28,24},{1,5},{5... | collective-permute-start | bytes 786440 | tf_op jit(solution)/shard_map/ppermute | solution.py:462
  101.9 11.5 %collective-permute-start.16 = (f32[256,256]{1,0:T(8,128)S(1)}, f32[256,256]{1,0:T(8,128)S(1)}, u32[]{:S(2)}, u32[]{:S(2)}) collective-permute-start(f32[256,256]{1,0:T(8,128)S(1)} %get-tuple-element.130), channel_id=1, source_target_pairs={{4,8},{8,4},{12,16},{16,12},{20,24},{24,20},{5,9},{9,5},{13,17},{1... | collective-permute-start | bytes 786440 | tf_op jit(solution)/shard_map/ppermute | solution.py:463
  115.3 15.8 %collective-permute-start.17 = (f32[256,256]{1,0:T(8,128)S(1)}, f32[256,256]{1,0:T(8,128)S(1)}, u32[]{:S(2)}, u32[]{:S(2)}) collective-permute-start(f32[256,256]{1,0:T(8,128)S(1)} %get-tuple-element.136), channel_id=1, source_target_pairs={{4,0},{8,4},{12,8},{16,12},{20,16},{24,20},{28,24},{5,1},{9,5},{13... | collective-permute-start | bytes 786440 | tf_op jit(solution)/shard_map/ppermute | solution.py:609

commit v9 on v8

--- a/solution.py
+++ b/solution.py
@@ -8,7 +8,6 @@
 from jax.sharding import PartitionSpec as P
 
 VMEM_LIMIT = 8 * 1024 * 1024
-TAIL_LIMIT = 62 * 1024 * 1024
 
 
 def split(values):
@@ -132,20 +131,7 @@
     return (lax.broadcasted_iota(jnp.int32, (rows, width), 1) < count).astype(jnp.float32)
 
 
-def tail_kernel(counts_ref, rhs, tail, counts, face, counts_done, face_done):
-    loads, width = rhs.shape[2:]
-    counts_copy = pltpu.make_async_copy(counts_ref, counts, counts_done)
-    face_copy = pltpu.make_async_copy(rhs.at[0, rhs.shape[1] - 1], face, face_done)
-    counts_copy.start()
-    face_copy.start()
-    counts_copy.wait()
-    mask = live_rows(counts, counts.shape[1] - 1, 8, width)
-    tail[loads:] = mask
-    face_copy.wait()
-    tail[:loads] = mask[:1] * face[...]
-
-
-def early_kernel(counts, rhs, panel, live, own, partial, rest):
+def early_kernel(counts, rhs, panel, coupling, live, own, partial, rest, near_out, far_out):
     subs, loads, width = own.shape
     parts = [None]
     for sub in range(subs):
@@ -158,17 +144,11 @@
         high = jnp.concatenate([-parts[sub][0], parts[sub + 1][0]], axis=1)
         low = jnp.concatenate([-parts[sub][1], parts[sub + 1][1]], axis=1)
         rest[sub - 1] = mul(high, panel[sub]) + mul(low, panel[sub])
-
-
-def head_kernel(head, partial, rest, panel, coupling, live, edge, first, near_out, far_out):
-    loads, width = edge.shape
-    live[...] = head[loads : loads + 1]
-    edge[...] = head[:loads]
-    high, low = split(head[:loads])
-    first[...] = partial[...] - mul(high, panel[0, :width]) - mul(low, panel[0, :width])
-    last = rest[rest.shape[0] - 1]
-    to_next = [last[:, width:], coupling[coupling.shape[0] - 1, :, width:]]
-    send(even_place(), to_next, [first[:, :width], coupling[0, :, :width]], near_out, far_out)
+    to_next = [rest[subs - 2][:, width:], coupling[subs - 1, :, width:], own[subs - 1],
+               jnp.broadcast_to(live[subs - 1], (8, width))]
+    to_prev = [partial[:, :width], coupling[0, :, :width],
+               panel[0, :width, :width].astype(jnp.float32), jnp.zeros((8, width), jnp.float32)]
+    send(even_place(), to_next, to_prev, near_out, far_out)
 
 
 def setup_kernel(*refs):
@@ -203,14 +183,28 @@
         ) + lax.dot_general(chosen, low, dims, preferred_element_type=jnp.float32)
 
 
-def corner_kernel(first, rest, near, far, live_first, live_rest, coupling,
-                  edge, own, corners):
+def corner_kernel(partial, rest, near, far, live_own, residual_own, panel, coupling,
+                  live_edge, residual_edge, edge, own, corners):
     even = even_place()
     subs, rows = coupling.shape[0], coupling.shape[1] // 2
-    result, live, edges = Joined(first, rest), Joined(live_first, live_rest), Joined(edge, own)
+    loads, width = residual_edge.shape
+    start = loads + rows
+    completing = received(even, near, far, start, loads + 8)
+    halo, block = completing[:loads], completing[loads + 8 : 2 * loads + 8].astype(jnp.bfloat16)
+    live_edge[...] = completing[loads : loads + 1]
+    residual_edge[...] = halo
+    live, edges = Joined(live_edge, live_own), Joined(edge, own)
+    faces = received(even, near, far, 0, loads)
+    high, low = split(halo)
+    first = partial[...] - mul(high, panel[0, :width]) - mul(low, panel[0, :width])
+    high, low = split(residual_own[subs - 1])
+    following = faces[loads:] - mul(high, block) - mul(low, block)
+    results = [first] + [rest[sub] for sub in range(subs - 1)]
+    right = [faces[:loads]] + [result[:, width:] for result in results]
+    left = [result[:, :width] for result in results] + [following]
     parts = []
     for place in range(subs + 1):
-        edges[place] = 0.25 * jump_edge(even, result, near, far, live, place, subs)
+        edges[place] = 0.25 * live[place] * (right[place] - left[place])
         parts.append(split(edges[place]))
     for sub in range(subs):
         high = jnp.concatenate([-parts[sub][0], parts[sub + 1][0]], axis=1)
@@ -227,7 +221,7 @@
     subs, rows = coupling.shape[0], coupling.shape[1]
     width = coupling.shape[2] // 2
     live = Joined(live_edge, live_own)
-    sides = received(even, near, far, near.shape[0] - rows, rows)
+    sides = received(even, near, far, panel.shape[1] // 2, rows)
     before, after = sides[:rows], sides[rows:]
     left = [coupling[sub, :, :width] * (0.25 * live[sub]) for sub in range(subs)]
     left.append(after * (0.25 * live[subs]))
@@ -488,26 +482,6 @@
     return block
 
 
-def make_tail(counts, rhs):
-    loads, width = rhs.shape[2:]
-    return pl.pallas_call(
-        tail_kernel,
-        out_shape=jax.ShapeDtypeStruct((loads + 8, width), jnp.float32),
-        in_specs=[
-            pl.BlockSpec(memory_space=pltpu.HBM),
-            pl.BlockSpec(memory_space=pltpu.HBM),
-        ],
-        out_specs=pl.BlockSpec(memory_space=pltpu.VMEM),
-        scratch_shapes=[
-            pltpu.VMEM(counts.shape, counts.dtype),
-            pltpu.VMEM((loads, width), jnp.float32),
-            pltpu.SemaphoreType.DMA,
-            pltpu.SemaphoreType.DMA,
-        ],
-        compiler_params=pltpu.CompilerParams(vmem_limit_bytes=TAIL_LIMIT),
-    )(counts, rhs)
-
-
 def local(rhs, counts, solve_panel, dirichlet_panel, coupling, corner_map, coarse_inverse):
     subs, loads, width = rhs.shape[1:]
     corners = coupling.shape[2]
@@ -518,36 +492,36 @@
     first_shape, rest_shape = (loads, 2 * width), (subs - 1, loads, 2 * width)
     scalars_shape, outside_shape, side_shape = (2, loads), (2 * corners, loads), (corners, width)
     long_shape, longer_shape = (loads + corners, width), (loads + 3 * corners, width)
+    begin_shape = (2 * loads + corners + 8, width)
     edges_shapes = [face_shape, own_shape]
     result_shapes = [first_shape, rest_shape, face_shape, face_shape]
 
-    tail = make_tail(counts, rhs)
-    tail, counts, corner_map = lax.optimization_barrier((tail, counts, corner_map))
-    head = lax.ppermute(tail, "sub", [(i, i + 1) for i in range(size - 1)])
+    live_own, residual_own, partial, rest, near, far = call(
+        early_kernel,
+        [(subs, 1, width), own_shape, first_shape, rest_shape, begin_shape, begin_shape],
+        counts, rhs[0], dirichlet, coupling[0],
+    )
+    near, far, corner_map, coarse = lax.optimization_barrier(
+        (near, far, corner_map, coarse_inverse[0])
+    )
+    near, far = swap(near, far)
     maps = from_group(corner_map[0])
-    live_own, residual_own, partial, rest = call(
-        early_kernel,
-        [(subs, 1, width), own_shape, first_shape, rest_shape],
-        counts, rhs[0], dirichlet,
-    )
     group, own = len(maps), subs * corners
     pair = [(corners, width)] * 2
     *picked, stacked, lift = call(
         setup_kernel,
         [(own, group * own)] * group
         + [(subs, 2 * corners, 2 * width), (subs, 3 * corners + -3 * corners % 128, 2 * width)],
-        *maps, coarse_inverse[0], coupling[0],
+        *maps, coarse, coupling[0],
         kinds=[jnp.float32] * group + [jnp.bfloat16] * 2,
         scratch=[pltpu.VMEM((group, 1, own), jnp.int32)],
     )
-    head, picked, rest = lax.optimization_barrier((head, picked, rest))
-    live_edge, residual_edge, first, near, far = call(
-        head_kernel,
-        [(1, width), face_shape, first_shape, long_shape, long_shape],
-        head, partial, rest, dirichlet, coupling[0],
-    )
-    near, far = swap(near, far)
     block = jnp.concatenate(split_outside(swap_blocks(picked)), axis=0)
+    live_edge, residual_edge, edge, first_z, values = call(
+        corner_kernel,
+        [(1, width), face_shape] + edges_shapes + [(own, loads)],
+        partial, rest, near, far, live_own, residual_own, dirichlet, stacked,
+    )
     live, residual = (live_edge, live_own), (residual_edge, residual_own)
     taken, ends, for_next, for_prev, given = call(
         operators_kernel,
@@ -555,12 +529,6 @@
          (2 * corners, width), (2,) + side_shape],
         coupling[0], *live, near, far, dirichlet,
         kinds=[jnp.bfloat16, jnp.float32, jnp.bfloat16, jnp.bfloat16, jnp.float32],
-    )
-
-    edge, first_z, values = call(
-        corner_kernel,
-        edges_shapes + [(own, loads)],
-        first, rest, near, far, *live, stacked,
     )
     everyone = lax.all_gather(values, "grp", tiled=True)
     first, rest, near, far, sums = call(

time: 133 us -> 143 us (1.075)
  waiting for transfers between devices: 19 us -> 33.3 us
  starting transfers between devices: 24.4 us -> 21.1 us
  Pallas kernels: 19.4 us -> 17.7 us
    ppermute x5, waiting for transfers between devices: 9.74 us -> 20.5 us  [swap(): lax.ppermute(near, 'sub', neighbour_pairs(size, 0))]
    ppermute x1 -> x0, starting transfers between devices: 4.86 us -> none  [local(): head = lax.ppermute(tail, 'sub', [(i, i + 1) for i in range(size - 1)])]
    ppermute x3, waiting for transfers between devices: 0.01 us -> 2.91 us  [from_group(): received.append(lax.ppermute(values, 'grp', routes))]
    pallas_call x1 -> x0, Pallas kernels: 1.79 us -> none  [make_tail(): pl.pallas_call(tail_kernel, out_shape=jax.ShapeDtypeStruct((loads + 8, wi...]
    unnamed x16 -> x18, local copies, waits for them, and re-layouts: 4.48 us -> 5.43 us
    pallas_call x13 -> x12, Pallas kernels: 17.6 us -> 17.7 us  [call(): pl.pallas_call(kernel, out_shape=[jax.ShapeDtypeStruct(*shape) for shape...]
  transfers between devices with their start and end apart: 18 -> 17, of which waited for: 5 -> 7; matrix products, arithmetic and copies ran while one was open for 0% -> 0% of each run, Pallas kernels for 4% -> 1%
where the time goes in v9:
time: 143 us; the launch traced here: 142 us
  blocking collectives  64 us (45%)
  waiting for transfers between devices  33.3 us (23%)
  starting transfers between devices  21.1 us (15%)
  Pallas kernels  17.7 us (12%)
  local copies, waits for them, and re-layouts  5.48 us (4%)
    all_to_all x3, blocking collectives, from_all(): return lax.all_to_all(copies, ('sub', 'grp'), 0, 0)  43.8 us
    ppermute x5, waiting for transfers between devices, swap(): lax.ppermute(near, 'sub', neighbour_pairs(size, 0))  20.5 us
    all_gather x3, blocking collectives, local(): everyone = lax.all_gather(values, 'grp', tiled=True)  20.2 us
    pallas_call x12, Pallas kernels, call(): pl.pallas_call(kernel, out_shape=[jax.ShapeDtypeStruct(*shape) for shape...  17.7 us
    ppermute x5, starting transfers between devices, swap(): lax.ppermute(near, 'sub', neighbour_pairs(size, 0))  11.3 us
    ppermute x3, waiting for transfers between devices, swap_blocks(): block = block + lax.ppermute(picked[distance], 'grp', routes)  9.83 us
    unnamed x18, local copies, waits for them, and re-layouts  5.43 us
    ppermute x5, starting transfers between devices, swap(): lax.ppermute(far, 'sub', neighbour_pairs(size, 1))  3.35 us
  transfers between devices with their start and end apart: 17, of which 7 were waited for; matrix products, arithmetic and copies ran while one was open for 0% of the time, Pallas kernels for 1%

profile of v9, /device:TPU:0, one launch (start us, length us, event | category | flops | bytes accessed | tf_op | source)
XLA Modules:
  0.0 142.4 jit_solution(16308408883807523388)
XLA Ops:
  0.6 0.0 copy-start
  0.6 1.6 %copy-done = bf16[1,4,512,512]{3,2,1,0:T(8,128)(2,1)S(1)} copy-done((bf16[1,4,512,512]{3,2,1,0:T(8,128)(2,1)S(1)}, bf16[1,4,512,512]{3,2,1,0:T(8,128)(2,1)}, u32[]{:S(2)}) %copy-start) | copy-done | bytes 2097176
  2.2 0.9 copy-done.3
  3.2 1.2 copy-done.6
  4.4 0.7 copy-done.8
  5.1 1.2 shard_map.86
  6.3 0.0 copy-done.7
  6.3 0.0 copy-start.1
  6.3 2.5 %collective-permute-start.4 = (s32[4,32]{1,0:T(4,128)S(1)}, s32[4,32]{1,0:T(4,128)S(1)}, u32[]{:S(2)}, u32[]{:S(2)}) collective-permute-start(s32[4,32]{1,0:T(4,128)S(1)} %bitcast.21), channel_id=1, source_target_pairs={{0,3},{1,2},{2,1},{3,0},{4,7},{5,6},{6,5},{7,4},{8,11},{9,10},{10,... | collective-permute-start | bytes 1544 | tf_op jit(solution)/shard_map/ppermute | solution.py:472
  8.8 0.6 collective-permute-start.3
  9.4 0.0 collective-permute-start.2
  9.4 0.6 collective-permute-done.4.refs_3_
  10.1 2.3 %collective-permute-done.3.refs_2_ = s32[4,32]{1,0:T(4,128)S(1)} collective-permute-done((s32[4,32]{1,0:T(4,128)S(1)}, s32[4,32]{1,0:T(4,128)S(1)}, u32[]{:S(2)}, u32[]{:S(2)}) %collective-permute-start.3) | collective-permute-done | bytes 544 | tf_op jit(solution)/shard_map/ppermute | solution.py:472
  12.3 0.0 collective-permute-done.2.refs_1_
  12.4 0.0 copy-done.5
  12.4 1.9 %shard_map.87 = (f32[128,512]{1,0:T(8,128)S(1)}, f32[128,512]{1,0:T(8,128)S(1)}, f32[128,512]{1,0:T(8,128)S(1)}, f32[128,512]{1,0:T(8,128)S(1)}, bf16[4,64,512]{...) custom-call(s32[4,32]{1,0:T(4,128)S(1)} %bitcast.24, s32[4,32]{1,0:T(4,128)S(1)} %collective-permute-done.2.refs_1_, ...), custom_call_target="tpu_custom_call" | custom-call | tf_op jit(solution)/shard_map/pallas_call | solution.py:34
  14.3 0.1 collective-permute-start.5
  14.4 0.7 collective-permute-start.6
  15.1 1.2 collective-permute-start.7
  16.2 1.5 %collective-permute-start = (f32[552,256]{1,0:T(8,128)S(1)}, f32[552,256]{1,0:T(8,128)S(1)}, u32[]{:S(2)}, u32[]{:S(2)}) collective-permute-start(f32[552,256]{1,0:T(8,128)S(1)} %get-tuple-element.71), channel_id=1, source_target_pairs={{0,4},{4,0},{8,12},{12,8},{16,20},{20,16},{24,28},{28,24},{1,5},{5... | collective-permute-start | bytes 1695752 | tf_op jit(solution)/shard_map/ppermute | solution.py:456
  17.7 0.7 collective-permute-start.1
  18.4 0.0 collective-permute-done.5
  18.4 5.1 %collective-permute-done.6 = f32[128,512]{1,0:T(8,128)S(1)} collective-permute-done((f32[128,512]{1,0:T(8,128)S(1)}, f32[128,512]{1,0:T(8,128)S(1)}, u32[]{:S(2)}, u32[]{:S(2)}) %collective-permute-start.6) | collective-permute-done | bytes 262176 | tf_op jit(solution)/shard_map/ppermute | solution.py:481
  23.5 4.7 %collective-permute-done.7 = f32[128,512]{1,0:T(8,128)S(1)} collective-permute-done((f32[128,512]{1,0:T(8,128)S(1)}, f32[128,512]{1,0:T(8,128)S(1)}, u32[]{:S(2)}, u32[]{:S(2)}) %collective-permute-start.7) | collective-permute-done | bytes 262176 | tf_op jit(solution)/shard_map/ppermute | solution.py:481
  28.2 0.1 reduce-precision_convert_fusion
  28.4 14.0 %collective-permute-done.near = f32[552,256]{1,0:T(8,128)S(1)} collective-permute-done((f32[552,256]{1,0:T(8,128)S(1)}, f32[552,256]{1,0:T(8,128)S(1)}, u32[]{:S(2)}, u32[]{:S(2)}) %collective-permute-start) | collective-permute-done | bytes 565280 | tf_op jit(solution)/shard_map/ppermute | solution.py:456
  42.4 0.0 collective-permute-done.1.far
  42.4 0.0 copy-done.1
  42.4 1.1 shard_map.88
  43.5 6.5 %all_gather.9.everyone = f32[512,256]{1,0:T(8,128)S(1)} all-gather(f32[128,256]{1,0:T(8,128)S(1)} %get-tuple-element.80), channel_id=1, replica_groups=mesh['sub'=8,'grp'=4] {'grp'}, dimensions={0}, use_global_device_ids=true | all-gather | bytes 655360 | tf_op jit(solution)/shard_map/all_gather | solution.py:533
  50.0 0.0 copy-done.4
  50.0 0.6 shard_map.89
  50.6 1.0 copy-done.2
  51.6 2.2 %shard_map.90 = (f32[256,512]{1,0:T(8,128)S(1)}, f32[3,256,512]{2,1,0:T(8,128)S(1)}, f32[352,256]{1,0:T(8,128)S(1)}, f32[352,256]{1,0:T(8,128)S(1)}, f32[2,256]{1,0:T(2,128)S(1)}) custom-call(f32[256,256]{1,0:T(8,128)S(1)} %get-tuple-element.78.edge, f32[4,256,256]{2,1,0:T(8,128)S(1)} %get-tuple-element.79.own.first_z, ...), custom_call_target="tpu_custom_call" | custom-call | tf_op jit(solution)/shard_map/pallas_call | solution.py:34
  53.9 2.5 %collective-permute-start.8 = (f32[352,256]{1,0:T(8,128)S(1)}, f32[352,256]{1,0:T(8,128)S(1)}, u32[]{:S(2)}, u32[]{:S(2)}) collective-permute-start(f32[352,256]{1,0:T(8,128)S(1)} %get-tuple-element.92), channel_id=1, source_target_pairs={{0,4},{4,0},{8,12},{12,8},{16,20},{20,16},{24,28},{28,24},{1,5},{5... | collective-permute-start | bytes 1081352 | tf_op jit(solution)/shard_map/ppermute | solution.py:456
  56.4 0.7 collective-permute-start.9
  57.1 15.9 %all_to_all.15.sums = f32[32,2,256]{2,1,0:T(2,128)S(1)} all-to-all(f32[32,2,256]{2,1,0:T(2,128)S(1)} %broadcast_in_dim.10), channel_id=1, replica_groups=mesh['sub'=8,'grp'=4] {'sub','grp'}, dimensions={0} | all-to-all | bytes 131072 | tf_op jit(solution)/shard_map/all_to_all | solution.py:464
  73.0 0.0 collective-permute-done.8.near
  73.0 0.0 collective-permute-done.9.far
  73.0 1.6 %shard_map.91 = (f32[4,256,256]{2,1,0:T(8,128)S(1)}, f32[256,256]{1,0:T(8,128)S(1)}, f32[256,256]{1,0:T(8,128)S(1)}, f32[4,256,256]{2,1,0:T(8,128)S(1)}, f32[256...) custom-call(f32[256,512]{1,0:T(8,128)S(1)} %get-tuple-element.90.fir, ...), custom_call_target="tpu_custom_call" | custom-call | tf_op jit(solution)/shard_map/pallas_call | solution.py:34
  74.6 3.1 %collective-permute-start.10 = (f32[256,256]{1,0:T(8,128)S(1)}, f32[256,256]{1,0:T(8,128)S(1)}, u32[]{:S(2)}, u32[]{:S(2)}) collective-permute-start(f32[256,256]{1,0:T(8,128)S(1)} %get-tuple-element.99), channel_id=1, source_target_pairs={{0,4},{4,0},{8,12},{12,8},{16,20},{20,16},{24,28},{28,24},{1,5},{5... | collective-permute-start | bytes 786440 | tf_op jit(solution)/shard_map/ppermute | solution.py:456
  77.7 0.7 collective-permute-start.11
  78.4 0.7 shard_map.92
  79.1 6.8 %all_gather.10.refs_8_ = f32[512,256]{1,0:T(8,128)S(1)} all-gather(f32[128,256]{1,0:T(8,128)S(1)} %shard_map.92), channel_id=1, replica_groups=mesh['sub'=8,'grp'=4] {'grp'}, dimensions={0}, use_global_device_ids=true | all-gather | bytes 655360 | tf_op jit(solution)/shard_map/all_gather | solution.py:552
  85.9 3.3 %collective-permute-done.10.refs_2_ = f32[256,256]{1,0:T(8,128)S(1)} collective-permute-done((f32[256,256]{1,0:T(8,128)S(1)}, f32[256,256]{1,0:T(8,128)S(1)}, u32[]{:S(2)}, u32[]{:S(2)}) %collective-permute-start.10) | collective-permute-done | bytes 262176 | tf_op jit(solution)/shard_map/ppermute | solution.py:456
  89.2 0.0 collective-permute-done.11.refs_3_
  89.2 2.2 %shard_map.93 = (f32[4,256,256]{2,1,0:T(8,128)S(1)}, f32[256,512]{1,0:T(8,128)S(1)}, f32[3,256,512]{2,1,0:T(8,128)S(1)}, f32[288,256]{1,0:T(8,128)S(1)}, f32[288,256]{1,0:T(8,128)S(1)}, /*index=5*/f32[2,256]{1,0:T(2,128)S(1)}) custom-call(f32[256,512]{1,0:T(8,128)S(1)} %get-tuple-element.97.refs_0_, f32[3,256,512]{2,1,0:T(8,128)S(1)} %get-tuple-element.98.refs_1_, ...), custom_call_target="tpu_custom_call" | custom-call | tf_op jit(solution)/shard_map/pallas_call | solution.py:34
  91.4 2.5 %collective-permute-start.12 = (f32[288,256]{1,0:T(8,128)S(1)}, f32[288,256]{1,0:T(8,128)S(1)}, u32[]{:S(2)}, u32[]{:S(2)}) collective-permute-start(f32[288,256]{1,0:T(8,128)S(1)} %get-tuple-element.108), channel_id=1, source_target_pairs={{0,4},{4,0},{8,12},{12,8},{16,20},{20,16},{24,28},{28,24},{1,5},{5... | collective-permute-start | bytes 884744 | tf_op jit(solution)/shard_map/ppermute | solution.py:456
  93.9 0.7 collective-permute-start.13
  94.6 13.1 %all_to_all.16.sums = f32[32,2,256]{2,1,0:T(2,128)S(1)} all-to-all(f32[32,2,256]{2,1,0:T(2,128)S(1)} %broadcast_in_dim.11), channel_id=1, replica_groups=mesh['sub'=8,'grp'=4] {'sub','grp'}, dimensions={0} | all-to-all | bytes 131072 | tf_op jit(solution)/shard_map/all_to_all | solution.py:464
  107.7 0.0 collective-permute-done.12.near
  107.7 0.0 collective-permute-done.13.far
  107.7 1.7 %shard_map.94 = (f32[4,256,256]{2,1,0:T(8,128)S(1)}, f32[256,256]{1,0:T(8,128)S(1)}, f32[4,256,256]{2,1,0:T(8,128)S(1)}, f32[256,512]{1,0:T(8,128)S(1)}, f32[3,2...) custom-call(f32[256,512]{1,0:T(8,128)S(1)} %get-tuple-element.106.fi, ...), custom_call_target="tpu_custom_call" | custom-call | tf_op jit(solution)/shard_map/pallas_call | solution.py:34
  109.4 1.7 %collective-permute-start.14 = (f32[256,256]{1,0:T(8,128)S(1)}, f32[256,256]{1,0:T(8,128)S(1)}, u32[]{:S(2)}, u32[]{:S(2)}) collective-permute-start(f32[256,256]{1,0:T(8,128)S(1)} %get-tuple-element.117), channel_id=1, source_target_pairs={{0,4},{4,0},{8,12},{12,8},{16,20},{20,16},{24,28},{28,24},{1,5},{5... | collective-permute-start | bytes 786440 | tf_op jit(solution)/shard_map/ppermute | solution.py:456
  111.1 0.7 collective-permute-start.15
  111.8 0.7 shard_map.95
  112.4 6.9 %all_gather.11.refs_8_ = f32[512,256]{1,0:T(8,128)S(1)} all-gather(f32[128,256]{1,0:T(8,128)S(1)} %shard_map.95), channel_id=1, replica_groups=mesh['sub'=8,'grp'=4] {'grp'}, dimensions={0}, use_global_device_ids=true | all-gather | bytes 655360 | tf_op jit(solution)/shard_map/all_gather | solution.py:570
  119.3 3.2 %collective-permute-done.14.refs_2_ = f32[256,256]{1,0:T(8,128)S(1)} collective-permute-done((f32[256,256]{1,0:T(8,128)S(1)}, f32[256,256]{1,0:T(8,128)S(1)}, u32[]{:S(2)}, u32[]{:S(2)}) %collective-permute-start.14) | collective-permute-done | bytes 262176 | tf_op jit(solution)/shard_map/ppermute | solution.py:456
  122.5 0.0 collective-permute-done.15.refs_3_
  122.5 2.0 %shard_map.96 = (f32[4,256,256]{2,1,0:T(8,128)S(1)}, f32[256,512]{1,0:T(8,128)S(1)}, f32[3,256,512]{2,1,0:T(8,128)S(1)}, f32[256,256]{1,0:T(8,128)S(1)}, f32[2,256]{1,0:T(2,128)S(1)}) custom-call(f32[256,512]{1,0:T(8,128)S(1)} %get-tuple-element.115.refs_0_, f32[3,256,512]{2,1,0:T(8,128)S(1)} %get-tuple-element.116.refs_1_, ...), custom_call_target="tpu_custom_call" | custom-call | tf_op jit(solution)/shard_map/pallas_call | solution.py:34
  124.5 1.3 collective-permute-start.16
  125.9 14.8 %all_to_all.17.sums = f32[32,2,256]{2,1,0:T(2,128)S(1)} all-to-all(f32[32,2,256]{2,1,0:T(2,128)S(1)} %broadcast_in_dim.12), channel_id=1, replica_groups=mesh['sub'=8,'grp'=4] {'sub','grp'}, dimensions={0} | all-to-all | bytes 131072 | tf_op jit(solution)/shard_map/all_to_all | solution.py:464
  140.7 0.0 collective-permute-done.16.following
  140.7 1.8 %shard_map.97 = (f32[4,256,256]{2,1,0:T(8,128)}, f32[4,256,256]{2,1,0:T(8,128)}) custom-call(f32[256,512]{1,0:T(8,128)S(1)} %get-tuple-element.122.first, f32[3,256,512]{2,1,0:T(8,128)S(1)} %get-tuple-element.123.rest, f32[256,256]{1,0:T(8,128)S(1)} %collective-permute-done.16.following, f32[4,1,256]{2,1,0:T(1,128)S(1)} %get-tuple-element.73.live_own.live_rest.refs_5_.live, ...), custom_call_target="tpu_custom_call" | custom-call | tf_op jit(solution)/shard_map/pallas_call | solution.py:34
  (12 shorter events, 0.1 us)
Async XLA Ops:
  0.6 1.6 %copy-start = (bf16[1,4,512,512]{3,2,1,0:T(8,128)(2,1)S(1)}, bf16[1,4,512,512]{3,2,1,0:T(8,128)(2,1)}, u32[]{:S(2)}) copy-start(bf16[1,4,512,512]{3,2,1,0:T(8,128)(2,1)} %param.10) | copy-start | bytes 6291460
  2.2 0.9 copy-start.3
  3.2 1.2 copy-start.6
  4.4 0.7 copy-start.8
  5.1 1.2 copy-start.7
  5.1 7.3 %copy-start.5 = (f32[1,256,1024]{2,1,0:T(8,128)S(1)}, f32[1,256,1024]{2,1,0:T(8,128)}, u32[]{:S(2)}) copy-start(f32[1,256,1024]{2,1,0:T(8,128)} %param.13) | copy-start | bytes 3145732
  6.3 36.1 %copy-start.1 = (bf16[1,4,512,512]{3,2,1,0:T(8,128)(2,1)S(1)}, bf16[1,4,512,512]{3,2,1,0:T(8,128)(2,1)}, u32[]{:S(2)}) copy-start(bf16[1,4,512,512]{3,2,1,0:T(8,128)(2,1)} %param.10) | copy-start | bytes 6291460
  6.3 3.8 %collective-permute-start.4 = (s32[4,32]{1,0:T(4,128)S(1)}, s32[4,32]{1,0:T(4,128)S(1)}, u32[]{:S(2)}, u32[]{:S(2)}) collective-permute-start(s32[4,32]{1,0:T(4,128)S(1)} %bitcast.21), channel_id=1, source_target_pairs={{0,3},{1,2},{2,1},{3,0},{4,7},{5,6},{6,5},{7,4},{8,11},{9,10},{10,... | collective-permute-start | bytes 1544 | tf_op jit(solution)/shard_map/ppermute | solution.py:472
  8.8 3.6 %collective-permute-start.3 = (s32[4,32]{1,0:T(4,128)S(1)}, s32[4,32]{1,0:T(4,128)S(1)}, u32[]{:S(2)}, u32[]{:S(2)}) collective-permute-start(s32[4,32]{1,0:T(4,128)S(1)} %bitcast.22), channel_id=1, source_target_pairs={{0,2},{1,3},{2,0},{3,1},{4,6},{5,7},{6,4},{7,5},{8,10},{9,11},{10,... | collective-permute-start | bytes 1544 | tf_op jit(solution)/shard_map/ppermute | solution.py:472
  9.4 2.9 %collective-permute-start.2 = (s32[4,32]{1,0:T(4,128)S(1)}, s32[4,32]{1,0:T(4,128)S(1)}, u32[]{:S(2)}, u32[]{:S(2)}) collective-permute-start(s32[4,32]{1,0:T(4,128)S(1)} %bitcast.23), channel_id=1, source_target_pairs={{0,1},{1,0},{2,3},{3,2},{4,5},{5,4},{6,7},{7,6},{8,9},{9,8},{10,11... | collective-permute-start | bytes 1544 | tf_op jit(solution)/shard_map/ppermute | solution.py:472
  14.3 4.1 %collective-permute-start.5 = (f32[128,512]{1,0:T(8,128)S(1)}, f32[128,512]{1,0:T(8,128)S(1)}, u32[]{:S(2)}, u32[]{:S(2)}) collective-permute-start(f32[128,512]{1,0:T(8,128)S(1)} %get-tuple-element.82), channel_id=1, source_target_pairs={{0,1},{1,0},{2,3},{3,2},{4,5},{5,4},{6,7},{7,6},{8,9},{9,8},{10,11... | collective-permute-start | bytes 786440 | tf_op jit(solution)/shard_map/ppermute | solution.py:481
  14.4 9.2 %collective-permute-start.6 = (f32[128,512]{1,0:T(8,128)S(1)}, f32[128,512]{1,0:T(8,128)S(1)}, u32[]{:S(2)}, u32[]{:S(2)}) collective-permute-start(f32[128,512]{1,0:T(8,128)S(1)} %get-tuple-element.83), channel_id=1, source_target_pairs={{0,2},{1,3},{2,0},{3,1},{4,6},{5,7},{6,4},{7,5},{8,10},{9,11},{10,... | collective-permute-start | bytes 786440 | tf_op jit(solution)/shard_map/ppermute | solution.py:481
  15.1 13.2 %collective-permute-start.7 = (f32[128,512]{1,0:T(8,128)S(1)}, f32[128,512]{1,0:T(8,128)S(1)}, u32[]{:S(2)}, u32[]{:S(2)}) collective-permute-start(f32[128,512]{1,0:T(8,128)S(1)} %get-tuple-element.84), channel_id=1, source_target_pairs={{0,3},{1,2},{2,1},{3,0},{4,7},{5,6},{6,5},{7,4},{8,11},{9,10},{10,... | collective-permute-start | bytes 786440 | tf_op jit(solution)/shard_map/ppermute | solution.py:481
  16.2 26.2 %collective-permute-start = (f32[552,256]{1,0:T(8,128)S(1)}, f32[552,256]{1,0:T(8,128)S(1)}, u32[]{:S(2)}, u32[]{:S(2)}) collective-permute-start(f32[552,256]{1,0:T(8,128)S(1)} %get-tuple-element.71), channel_id=1, source_target_pairs={{0,4},{4,0},{8,12},{12,8},{16,20},{20,16},{24,28},{28,24},{1,5},{5... | collective-permute-start | bytes 1695752 | tf_op jit(solution)/shard_map/ppermute | solution.py:456
  17.7 24.7 %collective-permute-start.1 = (f32[552,256]{1,0:T(8,128)S(1)}, f32[552,256]{1,0:T(8,128)S(1)}, u32[]{:S(2)}, u32[]{:S(2)}) collective-permute-start(f32[552,256]{1,0:T(8,128)S(1)} %get-tuple-element.72), channel_id=1, source_target_pairs={{4,8},{8,4},{12,16},{16,12},{20,24},{24,20},{5,9},{9,5},{13,17},{1... | collective-permute-start | bytes 1695752 | tf_op jit(solution)/shard_map/ppermute | solution.py:457
  42.4 7.6 %copy-start.4 = (f32[1,4,32,512]{3,2,1,0:T(8,128)S(1)}, f32[1,4,32,512]{3,2,1,0:T(8,128)}, u32[]{:S(2)}) copy-start(f32[1,4,32,512]{3,2,1,0:T(8,128)} %param.11) | copy-start | bytes 786436
  50.0 1.6 %copy-start.2 = (bf16[1,4,512,512]{3,2,1,0:T(8,128)(2,1)S(1)}, bf16[1,4,512,512]{3,2,1,0:T(8,128)(2,1)}, u32[]{:S(2)}) copy-start(bf16[1,4,512,512]{3,2,1,0:T(8,128)(2,1)} %param.9) | copy-start | bytes 6291460
  53.9 19.1 %collective-permute-start.8 = (f32[352,256]{1,0:T(8,128)S(1)}, f32[352,256]{1,0:T(8,128)S(1)}, u32[]{:S(2)}, u32[]{:S(2)}) collective-permute-start(f32[352,256]{1,0:T(8,128)S(1)} %get-tuple-element.92), channel_id=1, source_target_pairs={{0,4},{4,0},{8,12},{12,8},{16,20},{20,16},{24,28},{28,24},{1,5},{5... | collective-permute-start | bytes 1081352 | tf_op jit(solution)/shard_map/ppermute | solution.py:456
  56.4 16.6 %collective-permute-start.9 = (f32[352,256]{1,0:T(8,128)S(1)}, f32[352,256]{1,0:T(8,128)S(1)}, u32[]{:S(2)}, u32[]{:S(2)}) collective-permute-start(f32[352,256]{1,0:T(8,128)S(1)} %get-tuple-element.93), channel_id=1, source_target_pairs={{4,8},{8,4},{12,16},{16,12},{20,24},{24,20},{5,9},{9,5},{13,17},{1... | collective-permute-start | bytes 1081352 | tf_op jit(solution)/shard_map/ppermute | solution.py:457
  74.6 14.6 %collective-permute-start.10 = (f32[256,256]{1,0:T(8,128)S(1)}, f32[256,256]{1,0:T(8,128)S(1)}, u32[]{:S(2)}, u32[]{:S(2)}) collective-permute-start(f32[256,256]{1,0:T(8,128)S(1)} %get-tuple-element.99), channel_id=1, source_target_pairs={{0,4},{4,0},{8,12},{12,8},{16,20},{20,16},{24,28},{28,24},{1,5},{5... | collective-permute-start | bytes 786440 | tf_op jit(solution)/shard_map/ppermute | solution.py:456
  77.7 11.5 %collective-permute-start.11 = (f32[256,256]{1,0:T(8,128)S(1)}, f32[256,256]{1,0:T(8,128)S(1)}, u32[]{:S(2)}, u32[]{:S(2)}) collective-permute-start(f32[256,256]{1,0:T(8,128)S(1)} %get-tuple-element.100), channel_id=1, source_target_pairs={{4,8},{8,4},{12,16},{16,12},{20,24},{24,20},{5,9},{9,5},{13,17},{1... | collective-permute-start | bytes 786440 | tf_op jit(solution)/shard_map/ppermute | solution.py:457
  91.4 16.3 %collective-permute-start.12 = (f32[288,256]{1,0:T(8,128)S(1)}, f32[288,256]{1,0:T(8,128)S(1)}, u32[]{:S(2)}, u32[]{:S(2)}) collective-permute-start(f32[288,256]{1,0:T(8,128)S(1)} %get-tuple-element.108), channel_id=1, source_target_pairs={{0,4},{4,0},{8,12},{12,8},{16,20},{20,16},{24,28},{28,24},{1,5},{5... | collective-permute-start | bytes 884744 | tf_op jit(solution)/shard_map/ppermute | solution.py:456
  93.9 13.8 %collective-permute-start.13 = (f32[288,256]{1,0:T(8,128)S(1)}, f32[288,256]{1,0:T(8,128)S(1)}, u32[]{:S(2)}, u32[]{:S(2)}) collective-permute-start(f32[288,256]{1,0:T(8,128)S(1)} %get-tuple-element.109), channel_id=1, source_target_pairs={{4,8},{8,4},{12,16},{16,12},{20,24},{24,20},{5,9},{9,5},{13,17},{1... | collective-permute-start | bytes 884744 | tf_op jit(solution)/shard_map/ppermute | solution.py:457
  109.4 13.1 %collective-permute-start.14 = (f32[256,256]{1,0:T(8,128)S(1)}, f32[256,256]{1,0:T(8,128)S(1)}, u32[]{:S(2)}, u32[]{:S(2)}) collective-permute-start(f32[256,256]{1,0:T(8,128)S(1)} %get-tuple-element.117), channel_id=1, source_target_pairs={{0,4},{4,0},{8,12},{12,8},{16,20},{20,16},{24,28},{28,24},{1,5},{5... | collective-permute-start | bytes 786440 | tf_op jit(solution)/shard_map/ppermute | solution.py:456
  111.1 11.5 %collective-permute-start.15 = (f32[256,256]{1,0:T(8,128)S(1)}, f32[256,256]{1,0:T(8,128)S(1)}, u32[]{:S(2)}, u32[]{:S(2)}) collective-permute-start(f32[256,256]{1,0:T(8,128)S(1)} %get-tuple-element.118), channel_id=1, source_target_pairs={{4,8},{8,4},{12,16},{16,12},{20,24},{24,20},{5,9},{9,5},{13,17},{1... | collective-permute-start | bytes 786440 | tf_op jit(solution)/shard_map/ppermute | solution.py:457
  124.5 16.1 %collective-permute-start.16 = (f32[256,256]{1,0:T(8,128)S(1)}, f32[256,256]{1,0:T(8,128)S(1)}, u32[]{:S(2)}, u32[]{:S(2)}) collective-permute-start(f32[256,256]{1,0:T(8,128)S(1)} %get-tuple-element.124), channel_id=1, source_target_pairs={{4,0},{8,4},{12,8},{16,12},{20,16},{24,20},{28,24},{5,1},{9,5},{13... | collective-permute-start | bytes 786440 | tf_op jit(solution)/shard_map/ppermute | solution.py:577

commit v10 on v8

--- a/solution.py
+++ b/solution.py
@@ -30,13 +30,13 @@
     return lax.dot_general(first, second, dims, preferred_element_type=jnp.float32)
 
 
-def call(kernel, out_shapes, *operands, kinds=None, scratch=()):
+def call(kernel, out_shapes, *operands, kinds=None, scratch=(), place=pltpu.VMEM):
     kinds = kinds or [jnp.float32] * len(out_shapes)
     return pl.pallas_call(
         kernel,
         out_shape=[jax.ShapeDtypeStruct(*shape) for shape in zip(out_shapes, kinds)],
         in_specs=[pl.BlockSpec(memory_space=pltpu.VMEM)] * len(operands),
-        out_specs=[pl.BlockSpec(memory_space=pltpu.VMEM)] * len(out_shapes),
+        out_specs=[pl.BlockSpec(memory_space=place)] * len(out_shapes),
         scratch_shapes=list(scratch),
         compiler_params=pltpu.CompilerParams(vmem_limit_bytes=VMEM_LIMIT),
     )(*operands)
@@ -203,7 +203,7 @@
         ) + lax.dot_general(chosen, low, dims, preferred_element_type=jnp.float32)
 
 
-def corner_kernel(first, rest, near, far, live_first, live_rest, coupling,
+def corner_kernel(first, rest, near, far, live_first, live_rest, coupling, _solve,
                   edge, own, corners):
     even = even_place()
     subs, rows = coupling.shape[0], coupling.shape[1] // 2
@@ -431,7 +431,8 @@
 
 
 def last_kernel(first, rest, following, live, sums, before, older, image_old,
-                residual, first_z, second_z, third_z, multipliers, residual_new):
+                residual, first_z, second_z, third_z, multipliers, residual_new,
+                solution_slots, residual_slots, done):
     subs, width = residual.shape[0], following.shape[1]
     result = Joined(first, rest)
     rz_now, alpha, beta = step_scalars(2, sums, before)
@@ -440,15 +441,26 @@
     on_first = older[1:2] + on_second * beta_before
     alpha_column, beta_column = column(alpha, width), column(beta, width)
     second_column, first_column = column(on_second, width), column(on_first, width)
+    copies = []
     for sub in range(subs):
         left = following[...] if sub == subs - 1 else result[sub + 1][:, :width]
         image = live[sub] * (result[sub][:, width:] - left) + beta_column * image_old[sub]
-        residual_new[sub] = residual[sub] - alpha_column * image
-        multipliers[sub] = (
+        residual_slots[sub] = residual[sub] - alpha_column * image
+        copies.append(
+            pltpu.make_async_copy(residual_slots.at[sub], residual_new.at[sub], done.at[0, sub])
+        )
+        copies[-1].start()
+        solution_slots[sub] = (
             first_column * first_z[sub]
             + second_column * second_z[sub]
             + alpha_column * third_z[sub]
         )
+        copies.append(
+            pltpu.make_async_copy(solution_slots.at[sub], multipliers.at[sub], done.at[1, sub])
+        )
+        copies[-1].start()
+    for copy in copies:
+        copy.wait()
 
 
 def neighbour_pairs(size, first):
@@ -530,23 +542,23 @@
         [(subs, 1, width), own_shape, first_shape, rest_shape],
         counts, rhs[0], dirichlet,
     )
+    live_edge, residual_edge, first, near, far = call(
+        head_kernel,
+        [(1, width), face_shape, first_shape, long_shape, long_shape],
+        head, partial, rest, dirichlet, coupling[0],
+    )
+    near, far, maps, coarse = lax.optimization_barrier((near, far, maps, coarse_inverse[0]))
+    near, far = swap(near, far)
     group, own = len(maps), subs * corners
     pair = [(corners, width)] * 2
     *picked, stacked, lift = call(
         setup_kernel,
         [(own, group * own)] * group
         + [(subs, 2 * corners, 2 * width), (subs, 3 * corners + -3 * corners % 128, 2 * width)],
-        *maps, coarse_inverse[0], coupling[0],
+        *maps, coarse, coupling[0],
         kinds=[jnp.float32] * group + [jnp.bfloat16] * 2,
         scratch=[pltpu.VMEM((group, 1, own), jnp.int32)],
     )
-    head, picked, rest = lax.optimization_barrier((head, picked, rest))
-    live_edge, residual_edge, first, near, far = call(
-        head_kernel,
-        [(1, width), face_shape, first_shape, long_shape, long_shape],
-        head, partial, rest, dirichlet, coupling[0],
-    )
-    near, far = swap(near, far)
     block = jnp.concatenate(split_outside(swap_blocks(picked)), axis=0)
     live, residual = (live_edge, live_own), (residual_edge, residual_own)
     taken, ends, for_next, for_prev, given = call(
@@ -560,7 +572,7 @@
     edge, first_z, values = call(
         corner_kernel,
         edges_shapes + [(own, loads)],
-        first, rest, near, far, *live, stacked,
+        first, rest, near, far, *live, stacked, solve,
     )
     everyone = lax.all_gather(values, "grp", tiled=True)
     first, rest, near, far, sums = call(
@@ -612,6 +624,8 @@
         [own_shape] * 2,
         first, rest, following, live[1], sums, scalars_second, scalars_first,
         image_own, residual[1], first_z, second_z, third_z,
+        scratch=[pltpu.VMEM(own_shape, jnp.float32)] * 2 + [pltpu.SemaphoreType.DMA((2, subs))],
+        place=pltpu.HBM,
     )
     return (multipliers[None], residual[None])
 

time: 133 us -> 134 us (level)
  blocking collectives: 64.5 us -> 66.3 us
  local copies, waits for them, and re-layouts: 4.54 us -> 3.18 us
    all_to_all x3, blocking collectives: 43.8 us -> 45.4 us  [from_all(): return lax.all_to_all(copies, ('sub', 'grp'), 0, 0)]
    unnamed x16, local copies, waits for them, and re-layouts: 4.48 us -> 3.13 us
  transfers between devices with their start and end apart: 18 -> 18, of which waited for: 5 -> 6; matrix products, arithmetic and copies ran while one was open for 0% -> 0% of each run, Pallas kernels for 4% -> 2%
where the time goes in v10:
time: 134 us
  blocking collectives  66.3 us (49%)
  starting transfers between devices  24.3 us (18%)
  Pallas kernels  19.5 us (15%)
  waiting for transfers between devices  19.5 us (15%)
  local copies, waits for them, and re-layouts  3.18 us (2%)
    all_to_all x3, blocking collectives, from_all(): return lax.all_to_all(copies, ('sub', 'grp'), 0, 0)  45.4 us
    all_gather x3, blocking collectives, local(): everyone = lax.all_gather(values, 'grp', tiled=True)  20.8 us
    pallas_call x13, Pallas kernels, call(): pl.pallas_call(kernel, out_shape=[jax.ShapeDtypeStruct(*shape) for shape...  17.7 us
    ppermute x5, starting transfers between devices, swap(): lax.ppermute(near, 'sub', neighbour_pairs(size, 0))  10.9 us
    ppermute x5, waiting for transfers between devices, swap(): lax.ppermute(near, 'sub', neighbour_pairs(size, 0))  9.86 us
    ppermute x3, waiting for transfers between devices, swap_blocks(): block = block + lax.ppermute(picked[distance], 'grp', routes)  8.96 us
    ppermute x1, starting transfers between devices, local(): head = lax.ppermute(tail, 'sub', [(i, i + 1) for i in range(size - 1)])  4.86 us
    ppermute x5, starting transfers between devices, swap(): lax.ppermute(far, 'sub', neighbour_pairs(size, 1))  3.34 us
  transfers between devices with their start and end apart: 18, of which 6 were waited for; matrix products, arithmetic and copies ran while one was open for 0% of the time, Pallas kernels for 2%

profile of v10, /device:TPU:0, one launch (start us, length us, event | category | flops | bytes accessed | tf_op | source)
XLA Modules:
  0.0 133.9 jit_solution(11080902582488301638)
XLA Ops:
  0.6 0.0 copy-start.3
  0.6 1.8 %shard_map.86 = f32[264,256]{1,0:T(8,128)} custom-call(s32[1,4]{1,0:T(1,128)} %counts, f32[1,4,256,256]{3,2,1,0:T(8,128)} %rhs.1), custom_call_target="tpu_custom_call" | custom-call | tf_op jit(solution)/shard_map/pallas_call | solution.py:505
  2.4 4.9 %collective-permute-start = (f32[264,256]{1,0:T(8,128)}, f32[264,256]{1,0:T(8,128)S(1)}, u32[]{:S(2)}, u32[]{:S(2)}) collective-permute-start(f32[264,256]{1,0:T(8,128)} %shard_map.86), channel_id=1, source_target_pairs={{0,4},{4,8},{8,12},{12,16},{16,20},{20,24},{24,28},{1,5},{5,9},{9,... | collective-permute-start | bytes 811016 | tf_op jit(solution)/shard_map/ppermute | solution.py:538
  7.3 0.7 collective-permute-start.3
  8.1 0.9 collective-permute-start.2
  9.0 0.3 collective-permute-start.1
  9.2 0.0 copy-done.3
  9.2 1.6 %copy-done = bf16[1,4,512,512]{3,2,1,0:T(8,128)(2,1)S(1)} copy-done((bf16[1,4,512,512]{3,2,1,0:T(8,128)(2,1)S(1)}, bf16[1,4,512,512]{3,2,1,0:T(8,128)(2,1)}, u32[]{:S(2)}) %copy-start) | copy-done | bytes 2097176
  10.8 0.7 copy-done.7
  11.5 1.2 shard_map.87
  12.7 0.6 collective-permute-done.head
  13.3 0.0 copy-done.1
  13.3 0.3 shard_map.88
  13.7 0.0 collective-permute-done.3.refs_3_
  13.7 0.0 collective-permute-done.2.refs_2_
  13.7 0.0 collective-permute-done.1.refs_1_
  13.7 0.9 copy-done.5
  14.6 0.0 copy-done.6
  14.6 1.9 %shard_map.89 = (f32[128,512]{1,0:T(8,128)S(1)}, f32[128,512]{1,0:T(8,128)S(1)}, f32[128,512]{1,0:T(8,128)S(1)}, f32[128,512]{1,0:T(8,128)S(1)}, bf16[4,64,512]{...) custom-call(s32[4,32]{1,0:T(4,128)S(1)} %bitcast.25, s32[4,32]{1,0:T(4,128)S(1)} %collective-permute-done.1.refs_1_, ...), custom_call_target="tpu_custom_call" | custom-call | tf_op jit(solution)/shard_map/pallas_call | solution.py:35
  16.5 0.1 collective-permute-start.6
  16.6 1.6 %collective-permute-start.7 = (f32[128,512]{1,0:T(8,128)S(1)}, f32[128,512]{1,0:T(8,128)S(1)}, u32[]{:S(2)}, u32[]{:S(2)}) collective-permute-start(f32[128,512]{1,0:T(8,128)S(1)} %get-tuple-element.98), channel_id=1, source_target_pairs={{0,2},{1,3},{2,0},{3,1},{4,6},{5,7},{6,4},{7,5},{8,10},{9,11},{10,... | collective-permute-start | bytes 786440 | tf_op jit(solution)/shard_map/ppermute | solution.py:499
  18.1 0.3 collective-permute-start.8
  18.4 2.4 %collective-permute-start.4 = (f32[288,256]{1,0:T(8,128)S(1)}, f32[288,256]{1,0:T(8,128)S(1)}, u32[]{:S(2)}, u32[]{:S(2)}) collective-permute-start(f32[288,256]{1,0:T(8,128)S(1)} %get-tuple-element.82), channel_id=1, source_target_pairs={{0,4},{4,0},{8,12},{12,8},{16,20},{20,16},{24,28},{28,24},{1,5},{5... | collective-permute-start | bytes 884744 | tf_op jit(solution)/shard_map/ppermute | solution.py:474
  20.8 0.7 collective-permute-start.5
  21.5 0.0 collective-permute-done.6
  21.5 4.2 %collective-permute-done.7 = f32[128,512]{1,0:T(8,128)S(1)} collective-permute-done((f32[128,512]{1,0:T(8,128)S(1)}, f32[128,512]{1,0:T(8,128)S(1)}, u32[]{:S(2)}, u32[]{:S(2)}) %collective-permute-start.7) | collective-permute-done | bytes 262176 | tf_op jit(solution)/shard_map/ppermute | solution.py:499
  25.7 4.7 %collective-permute-done.8 = f32[128,512]{1,0:T(8,128)S(1)} collective-permute-done((f32[128,512]{1,0:T(8,128)S(1)}, f32[128,512]{1,0:T(8,128)S(1)}, u32[]{:S(2)}, u32[]{:S(2)}) %collective-permute-start.8) | collective-permute-done | bytes 262176 | tf_op jit(solution)/shard_map/ppermute | solution.py:499
  30.4 0.1 reduce-precision_convert_fusion
  30.6 3.3 %collective-permute-done.4.near = f32[288,256]{1,0:T(8,128)S(1)} collective-permute-done((f32[288,256]{1,0:T(8,128)S(1)}, f32[288,256]{1,0:T(8,128)S(1)}, u32[]{:S(2)}, u32[]{:S(2)}) %collective-permute-start.4) | collective-permute-done | bytes 294944 | tf_op jit(solution)/shard_map/ppermute | solution.py:474
  33.9 0.0 collective-permute-done.5.far
  33.9 0.7 shard_map.90
  34.7 7.2 %all_gather.9.everyone = f32[512,256]{1,0:T(8,128)S(1)} all-gather(f32[128,256]{1,0:T(8,128)S(1)} %get-tuple-element.95), channel_id=1, replica_groups=mesh['sub'=8,'grp'=4] {'grp'}, dimensions={0}, use_global_device_ids=true | all-gather | bytes 655360 | tf_op jit(solution)/shard_map/all_gather | solution.py:577
  41.9 0.6 shard_map.91
  42.5 2.2 %shard_map.92 = (f32[256,512]{1,0:T(8,128)S(1)}, f32[3,256,512]{2,1,0:T(8,128)S(1)}, f32[352,256]{1,0:T(8,128)S(1)}, f32[352,256]{1,0:T(8,128)S(1)}, f32[2,256]{1,0:T(2,128)S(1)}) custom-call(f32[256,256]{1,0:T(8,128)S(1)} %get-tuple-element.92.edge, f32[4,256,256]{2,1,0:T(8,128)S(1)} %get-tuple-element.93.own.first_z, ...), custom_call_target="tpu_custom_call" | custom-call | tf_op jit(solution)/shard_map/pallas_call | solution.py:35
  44.7 2.5 %collective-permute-start.9 = (f32[352,256]{1,0:T(8,128)S(1)}, f32[352,256]{1,0:T(8,128)S(1)}, u32[]{:S(2)}, u32[]{:S(2)}) collective-permute-start(f32[352,256]{1,0:T(8,128)S(1)} %get-tuple-element.106), channel_id=1, source_target_pairs={{0,4},{4,0},{8,12},{12,8},{16,20},{20,16},{24,28},{28,24},{1,5},{5... | collective-permute-start | bytes 1081352 | tf_op jit(solution)/shard_map/ppermute | solution.py:474
  47.2 0.7 collective-permute-start.10
  47.9 15.9 %all_to_all.15.sums = f32[32,2,256]{2,1,0:T(2,128)S(1)} all-to-all(f32[32,2,256]{2,1,0:T(2,128)S(1)} %broadcast_in_dim.10), channel_id=1, replica_groups=mesh['sub'=8,'grp'=4] {'sub','grp'}, dimensions={0} | all-to-all | bytes 131072 | tf_op jit(solution)/shard_map/all_to_all | solution.py:482
  63.8 0.0 collective-permute-done.9.near
  63.8 0.0 collective-permute-done.10.far
  63.8 1.6 %shard_map.93 = (f32[4,256,256]{2,1,0:T(8,128)S(1)}, f32[256,256]{1,0:T(8,128)S(1)}, f32[256,256]{1,0:T(8,128)S(1)}, f32[4,256,256]{2,1,0:T(8,128)S(1)}, f32[256...) custom-call(f32[256,512]{1,0:T(8,128)S(1)} %get-tuple-element.104.fi, ...), custom_call_target="tpu_custom_call" | custom-call | tf_op jit(solution)/shard_map/pallas_call | solution.py:35
  65.4 2.8 %collective-permute-start.11 = (f32[256,256]{1,0:T(8,128)S(1)}, f32[256,256]{1,0:T(8,128)S(1)}, u32[]{:S(2)}, u32[]{:S(2)}) collective-permute-start(f32[256,256]{1,0:T(8,128)S(1)} %get-tuple-element.113), channel_id=1, source_target_pairs={{0,4},{4,0},{8,12},{12,8},{16,20},{20,16},{24,28},{28,24},{1,5},{5... | collective-permute-start | bytes 786440 | tf_op jit(solution)/shard_map/ppermute | solution.py:474
  68.1 0.7 collective-permute-start.12
  68.8 0.7 shard_map.94
  69.5 6.9 %all_gather.10.refs_8_ = f32[512,256]{1,0:T(8,128)S(1)} all-gather(f32[128,256]{1,0:T(8,128)S(1)} %shard_map.94), channel_id=1, replica_groups=mesh['sub'=8,'grp'=4] {'grp'}, dimensions={0}, use_global_device_ids=true | all-gather | bytes 655360 | tf_op jit(solution)/shard_map/all_gather | solution.py:596
  76.4 3.2 %collective-permute-done.11.refs_2_ = f32[256,256]{1,0:T(8,128)S(1)} collective-permute-done((f32[256,256]{1,0:T(8,128)S(1)}, f32[256,256]{1,0:T(8,128)S(1)}, u32[]{:S(2)}, u32[]{:S(2)}) %collective-permute-start.11) | collective-permute-done | bytes 262176 | tf_op jit(solution)/shard_map/ppermute | solution.py:474
  79.6 0.0 collective-permute-done.12.refs_3_
  79.6 2.2 %shard_map.95 = (f32[4,256,256]{2,1,0:T(8,128)S(1)}, f32[256,512]{1,0:T(8,128)S(1)}, f32[3,256,512]{2,1,0:T(8,128)S(1)}, f32[288,256]{1,0:T(8,128)S(1)}, f32[288,256]{1,0:T(8,128)S(1)}, /*index=5*/f32[2,256]{1,0:T(2,128)S(1)}) custom-call(f32[256,512]{1,0:T(8,128)S(1)} %get-tuple-element.111.refs_0_, f32[3,256,512]{2,1,0:T(8,128)S(1)} %get-tuple-element.112.refs_1_, ...), custom_call_target="tpu_custom_call" | custom-call | tf_op jit(solution)/shard_map/pallas_call | solution.py:35
  81.8 2.5 %collective-permute-start.13 = (f32[288,256]{1,0:T(8,128)S(1)}, f32[288,256]{1,0:T(8,128)S(1)}, u32[]{:S(2)}, u32[]{:S(2)}) collective-permute-start(f32[288,256]{1,0:T(8,128)S(1)} %get-tuple-element.122), channel_id=1, source_target_pairs={{0,4},{4,0},{8,12},{12,8},{16,20},{20,16},{24,28},{28,24},{1,5},{5... | collective-permute-start | bytes 884744 | tf_op jit(solution)/shard_map/ppermute | solution.py:474
  84.3 0.7 collective-permute-start.14
  85.0 14.4 %all_to_all.16.sums = f32[32,2,256]{2,1,0:T(2,128)S(1)} all-to-all(f32[32,2,256]{2,1,0:T(2,128)S(1)} %broadcast_in_dim.11), channel_id=1, replica_groups=mesh['sub'=8,'grp'=4] {'sub','grp'}, dimensions={0} | all-to-all | bytes 131072 | tf_op jit(solution)/shard_map/all_to_all | solution.py:482
  99.4 0.0 collective-permute-done.13.near
  99.4 0.0 collective-permute-done.14.far
  99.4 1.6 %shard_map.96 = (f32[4,256,256]{2,1,0:T(8,128)S(1)}, f32[256,256]{1,0:T(8,128)S(1)}, f32[4,256,256]{2,1,0:T(8,128)S(1)}, f32[256,512]{1,0:T(8,128)S(1)}, f32[3,2...) custom-call(f32[256,512]{1,0:T(8,128)S(1)} %get-tuple-element.120.fi, ...), custom_call_target="tpu_custom_call" | custom-call | tf_op jit(solution)/shard_map/pallas_call | solution.py:35
  101.1 0.8 collective-permute-start.15
  101.8 0.7 collective-permute-start.16
  102.5 0.7 shard_map.97
  103.2 6.8 %all_gather.11.refs_8_ = f32[512,256]{1,0:T(8,128)S(1)} all-gather(f32[128,256]{1,0:T(8,128)S(1)} %shard_map.97), channel_id=1, replica_groups=mesh['sub'=8,'grp'=4] {'grp'}, dimensions={0}, use_global_device_ids=true | all-gather | bytes 655360 | tf_op jit(solution)/shard_map/all_gather | solution.py:614
  110.0 3.3 %collective-permute-done.15.refs_2_ = f32[256,256]{1,0:T(8,128)S(1)} collective-permute-done((f32[256,256]{1,0:T(8,128)S(1)}, f32[256,256]{1,0:T(8,128)S(1)}, u32[]{:S(2)}, u32[]{:S(2)}) %collective-permute-start.15) | collective-permute-done | bytes 262176 | tf_op jit(solution)/shard_map/ppermute | solution.py:474
  113.3 0.0 collective-permute-done.16.refs_3_
  113.3 2.0 %shard_map.98 = (f32[4,256,256]{2,1,0:T(8,128)S(1)}, f32[256,512]{1,0:T(8,128)S(1)}, f32[3,256,512]{2,1,0:T(8,128)S(1)}, f32[256,256]{1,0:T(8,128)S(1)}, f32[2,256]{1,0:T(2,128)S(1)}) custom-call(f32[256,512]{1,0:T(8,128)S(1)} %get-tuple-element.129.refs_0_, f32[3,256,512]{2,1,0:T(8,128)S(1)} %get-tuple-element.130.refs_1_, ...), custom_call_target="tpu_custom_call" | custom-call | tf_op jit(solution)/shard_map/pallas_call | solution.py:35
  115.3 1.3 collective-permute-start.17
  116.6 15.2 %all_to_all.17.sums = f32[32,2,256]{2,1,0:T(2,128)S(1)} all-to-all(f32[32,2,256]{2,1,0:T(2,128)S(1)} %broadcast_in_dim.12), channel_id=1, replica_groups=mesh['sub'=8,'grp'=4] {'sub','grp'}, dimensions={0} | all-to-all | bytes 131072 | tf_op jit(solution)/shard_map/all_to_all | solution.py:482
  131.8 0.0 collective-permute-done.17.following
  131.8 1.9 %shard_map.99 = (f32[4,256,256]{2,1,0:T(8,128)}, f32[4,256,256]{2,1,0:T(8,128)}) custom-call(f32[256,512]{1,0:T(8,128)S(1)} %get-tuple-element.136.first, f32[3,256,512]{2,1,0:T(8,128)S(1)} %get-tuple-element.137.rest, f32[256,256]{1,0:T(8,128)S(1)} %collective-permute-done.17.following, f32[4,1,256]{2,1,0:T(1,128)S(1)} %get-tuple-element.85.live_rest.live_own.refs_5_.live, ...), custom_call_target="tpu_custom_call" | custom-call | tf_op jit(solution)/shard_map/pallas_call | solution.py:35
  (14 shorter events, 0.1 us)
Async XLA Ops:
  0.6 8.6 %copy-start.3 = (f32[1,4,256,256]{3,2,1,0:T(8,128)S(1)}, f32[1,4,256,256]{3,2,1,0:T(8,128)}, u32[]{:S(2)}) copy-start(f32[1,4,256,256]{3,2,1,0:T(8,128)} %rhs.1) | copy-start | bytes 3145732
  2.4 10.9 %collective-permute-start = (f32[264,256]{1,0:T(8,128)}, f32[264,256]{1,0:T(8,128)S(1)}, u32[]{:S(2)}, u32[]{:S(2)}) collective-permute-start(f32[264,256]{1,0:T(8,128)} %shard_map.86), channel_id=1, source_target_pairs={{0,4},{4,8},{8,12},{12,16},{16,20},{20,24},{24,28},{1,5},{5,9},{9,... | collective-permute-start | bytes 811016 | tf_op jit(solution)/shard_map/ppermute | solution.py:538
  7.3 6.4 %collective-permute-start.3 = (s32[4,32]{1,0:T(4,128)}, s32[4,32]{1,0:T(4,128)S(1)}, u32[]{:S(2)}, u32[]{:S(2)}) collective-permute-start(s32[4,32]{1,0:T(4,128)} %bitcast.22), channel_id=1, source_target_pairs={{0,3},{1,2},{2,1},{3,0},{4,7},{5,6},{6,5},{7,4},{8,11},{9,10},{10,... | collective-permute-start | bytes 1544 | tf_op jit(solution)/shard_map/ppermute | solution.py:490
  8.1 5.6 %collective-permute-start.2 = (s32[4,32]{1,0:T(4,128)}, s32[4,32]{1,0:T(4,128)S(1)}, u32[]{:S(2)}, u32[]{:S(2)}) collective-permute-start(s32[4,32]{1,0:T(4,128)} %bitcast.23), channel_id=1, source_target_pairs={{0,2},{1,3},{2,0},{3,1},{4,6},{5,7},{6,4},{7,5},{8,10},{9,11},{10,... | collective-permute-start | bytes 1544 | tf_op jit(solution)/shard_map/ppermute | solution.py:490
  9.0 4.7 %collective-permute-start.1 = (s32[4,32]{1,0:T(4,128)}, s32[4,32]{1,0:T(4,128)S(1)}, u32[]{:S(2)}, u32[]{:S(2)}) collective-permute-start(s32[4,32]{1,0:T(4,128)} %bitcast.24), channel_id=1, source_target_pairs={{0,1},{1,0},{2,3},{3,2},{4,5},{5,4},{6,7},{7,6},{8,9},{9,8},{10,11... | collective-permute-start | bytes 1544 | tf_op jit(solution)/shard_map/ppermute | solution.py:490
  9.2 1.6 %copy-start = (bf16[1,4,512,512]{3,2,1,0:T(8,128)(2,1)S(1)}, bf16[1,4,512,512]{3,2,1,0:T(8,128)(2,1)}, u32[]{:S(2)}) copy-start(bf16[1,4,512,512]{3,2,1,0:T(8,128)(2,1)} %param.10) | copy-start | bytes 6291460
  10.8 0.7 copy-start.7
  11.5 1.8 %copy-start.1 = (bf16[1,4,512,512]{3,2,1,0:T(8,128)(2,1)S(1)}, bf16[1,4,512,512]{3,2,1,0:T(8,128)(2,1)}, u32[]{:S(2)}) copy-start(bf16[1,4,512,512]{3,2,1,0:T(8,128)(2,1)} %param.10) | copy-start | bytes 6291460
  11.5 1.8 %copy-start.4 = (f32[1,4,32,512]{3,2,1,0:T(8,128)S(1)}, f32[1,4,32,512]{3,2,1,0:T(8,128)}, u32[]{:S(2)}) copy-start(f32[1,4,32,512]{3,2,1,0:T(8,128)} %param.11) | copy-start | bytes 786436
  13.3 1.2 copy-start.5
  13.3 1.2 copy-start.6
  14.6 19.3 %copy-start.2 = (bf16[1,4,512,512]{3,2,1,0:T(8,128)(2,1)S(1)}, bf16[1,4,512,512]{3,2,1,0:T(8,128)(2,1)}, u32[]{:S(2)}) copy-start(bf16[1,4,512,512]{3,2,1,0:T(8,128)(2,1)} %param.9) | copy-start | bytes 6291460
  16.5 5.0 %collective-permute-start.6 = (f32[128,512]{1,0:T(8,128)S(1)}, f32[128,512]{1,0:T(8,128)S(1)}, u32[]{:S(2)}, u32[]{:S(2)}) collective-permute-start(f32[128,512]{1,0:T(8,128)S(1)} %get-tuple-element.97), channel_id=1, source_target_pairs={{0,1},{1,0},{2,3},{3,2},{4,5},{5,4},{6,7},{7,6},{8,9},{9,8},{10,11... | collective-permute-start | bytes 786440 | tf_op jit(solution)/shard_map/ppermute | solution.py:499
  16.6 9.2 %collective-permute-start.7 = (f32[128,512]{1,0:T(8,128)S(1)}, f32[128,512]{1,0:T(8,128)S(1)}, u32[]{:S(2)}, u32[]{:S(2)}) collective-permute-start(f32[128,512]{1,0:T(8,128)S(1)} %get-tuple-element.98), channel_id=1, source_target_pairs={{0,2},{1,3},{2,0},{3,1},{4,6},{5,7},{6,4},{7,5},{8,10},{9,11},{10,... | collective-permute-start | bytes 786440 | tf_op jit(solution)/shard_map/ppermute | solution.py:499
  18.1 12.3 %collective-permute-start.8 = (f32[128,512]{1,0:T(8,128)S(1)}, f32[128,512]{1,0:T(8,128)S(1)}, u32[]{:S(2)}, u32[]{:S(2)}) collective-permute-start(f32[128,512]{1,0:T(8,128)S(1)} %get-tuple-element.99), channel_id=1, source_target_pairs={{0,3},{1,2},{2,1},{3,0},{4,7},{5,6},{6,5},{7,4},{8,11},{9,10},{10,... | collective-permute-start | bytes 786440 | tf_op jit(solution)/shard_map/ppermute | solution.py:499
  18.4 15.5 %collective-permute-start.4 = (f32[288,256]{1,0:T(8,128)S(1)}, f32[288,256]{1,0:T(8,128)S(1)}, u32[]{:S(2)}, u32[]{:S(2)}) collective-permute-start(f32[288,256]{1,0:T(8,128)S(1)} %get-tuple-element.82), channel_id=1, source_target_pairs={{0,4},{4,0},{8,12},{12,8},{16,20},{20,16},{24,28},{28,24},{1,5},{5... | collective-permute-start | bytes 884744 | tf_op jit(solution)/shard_map/ppermute | solution.py:474
  20.8 13.1 %collective-permute-start.5 = (f32[288,256]{1,0:T(8,128)S(1)}, f32[288,256]{1,0:T(8,128)S(1)}, u32[]{:S(2)}, u32[]{:S(2)}) collective-permute-start(f32[288,256]{1,0:T(8,128)S(1)} %get-tuple-element.83), channel_id=1, source_target_pairs={{4,8},{8,4},{12,16},{16,12},{20,24},{24,20},{5,9},{9,5},{13,17},{1... | collective-permute-start | bytes 884744 | tf_op jit(solution)/shard_map/ppermute | solution.py:475
  44.7 19.1 %collective-permute-start.9 = (f32[352,256]{1,0:T(8,128)S(1)}, f32[352,256]{1,0:T(8,128)S(1)}, u32[]{:S(2)}, u32[]{:S(2)}) collective-permute-start(f32[352,256]{1,0:T(8,128)S(1)} %get-tuple-element.106), channel_id=1, source_target_pairs={{0,4},{4,0},{8,12},{12,8},{16,20},{20,16},{24,28},{28,24},{1,5},{5... | collective-permute-start | bytes 1081352 | tf_op jit(solution)/shard_map/ppermute | solution.py:474
  47.2 16.6 %collective-permute-start.10 = (f32[352,256]{1,0:T(8,128)S(1)}, f32[352,256]{1,0:T(8,128)S(1)}, u32[]{:S(2)}, u32[]{:S(2)}) collective-permute-start(f32[352,256]{1,0:T(8,128)S(1)} %get-tuple-element.107), channel_id=1, source_target_pairs={{4,8},{8,4},{12,16},{16,12},{20,24},{24,20},{5,9},{9,5},{13,17},{1... | collective-permute-start | bytes 1081352 | tf_op jit(solution)/shard_map/ppermute | solution.py:475
  65.4 14.2 %collective-permute-start.11 = (f32[256,256]{1,0:T(8,128)S(1)}, f32[256,256]{1,0:T(8,128)S(1)}, u32[]{:S(2)}, u32[]{:S(2)}) collective-permute-start(f32[256,256]{1,0:T(8,128)S(1)} %get-tuple-element.113), channel_id=1, source_target_pairs={{0,4},{4,0},{8,12},{12,8},{16,20},{20,16},{24,28},{28,24},{1,5},{5... | collective-permute-start | bytes 786440 | tf_op jit(solution)/shard_map/ppermute | solution.py:474
  68.1 11.5 %collective-permute-start.12 = (f32[256,256]{1,0:T(8,128)S(1)}, f32[256,256]{1,0:T(8,128)S(1)}, u32[]{:S(2)}, u32[]{:S(2)}) collective-permute-start(f32[256,256]{1,0:T(8,128)S(1)} %get-tuple-element.114), channel_id=1, source_target_pairs={{4,8},{8,4},{12,16},{16,12},{20,24},{24,20},{5,9},{9,5},{13,17},{1... | collective-permute-start | bytes 786440 | tf_op jit(solution)/shard_map/ppermute | solution.py:475
  81.8 17.6 %collective-permute-start.13 = (f32[288,256]{1,0:T(8,128)S(1)}, f32[288,256]{1,0:T(8,128)S(1)}, u32[]{:S(2)}, u32[]{:S(2)}) collective-permute-start(f32[288,256]{1,0:T(8,128)S(1)} %get-tuple-element.122), channel_id=1, source_target_pairs={{0,4},{4,0},{8,12},{12,8},{16,20},{20,16},{24,28},{28,24},{1,5},{5... | collective-permute-start | bytes 884744 | tf_op jit(solution)/shard_map/ppermute | solution.py:474
  84.3 15.1 %collective-permute-start.14 = (f32[288,256]{1,0:T(8,128)S(1)}, f32[288,256]{1,0:T(8,128)S(1)}, u32[]{:S(2)}, u32[]{:S(2)}) collective-permute-start(f32[288,256]{1,0:T(8,128)S(1)} %get-tuple-element.123), channel_id=1, source_target_pairs={{4,8},{8,4},{12,16},{16,12},{20,24},{24,20},{5,9},{9,5},{13,17},{1... | collective-permute-start | bytes 884744 | tf_op jit(solution)/shard_map/ppermute | solution.py:475
  101.1 12.2 %collective-permute-start.15 = (f32[256,256]{1,0:T(8,128)S(1)}, f32[256,256]{1,0:T(8,128)S(1)}, u32[]{:S(2)}, u32[]{:S(2)}) collective-permute-start(f32[256,256]{1,0:T(8,128)S(1)} %get-tuple-element.131), channel_id=1, source_target_pairs={{0,4},{4,0},{8,12},{12,8},{16,20},{20,16},{24,28},{28,24},{1,5},{5... | collective-permute-start | bytes 786440 | tf_op jit(solution)/shard_map/ppermute | solution.py:474
  101.8 11.5 %collective-permute-start.16 = (f32[256,256]{1,0:T(8,128)S(1)}, f32[256,256]{1,0:T(8,128)S(1)}, u32[]{:S(2)}, u32[]{:S(2)}) collective-permute-start(f32[256,256]{1,0:T(8,128)S(1)} %get-tuple-element.132), channel_id=1, source_target_pairs={{4,8},{8,4},{12,16},{16,12},{20,24},{24,20},{5,9},{9,5},{13,17},{1... | collective-permute-start | bytes 786440 | tf_op jit(solution)/shard_map/ppermute | solution.py:475
  115.3 16.5 %collective-permute-start.17 = (f32[256,256]{1,0:T(8,128)S(1)}, f32[256,256]{1,0:T(8,128)S(1)}, u32[]{:S(2)}, u32[]{:S(2)}) collective-permute-start(f32[256,256]{1,0:T(8,128)S(1)} %get-tuple-element.138), channel_id=1, source_target_pairs={{4,0},{8,4},{12,8},{16,12},{20,16},{24,20},{28,24},{5,1},{9,5},{13... | collective-permute-start | bytes 786440 | tf_op jit(solution)/shard_map/ppermute | solution.py:621

commit v11 on v8

--- a/solution.py
+++ b/solution.py
@@ -203,7 +203,7 @@
         ) + lax.dot_general(chosen, low, dims, preferred_element_type=jnp.float32)
 
 
-def corner_kernel(first, rest, near, far, live_first, live_rest, coupling,
+def corner_kernel(first, rest, near, far, live_first, live_rest, coupling, _solve,
                   edge, own, corners):
     even = even_place()
     subs, rows = coupling.shape[0], coupling.shape[1] // 2
@@ -481,11 +481,11 @@
 
 def swap_blocks(picked):
     group = lax.axis_size("grp")
-    block = picked[0]
+    received = [picked[0]]
     for distance in range(1, group):
         routes = [(i, i ^ distance) for i in range(group)]
-        block = block + lax.ppermute(picked[distance], "grp", routes)
-    return block
+        received.append(lax.ppermute(picked[distance], "grp", routes))
+    return received
 
 
 def make_tail(counts, rhs):
@@ -540,14 +540,14 @@
         kinds=[jnp.float32] * group + [jnp.bfloat16] * 2,
         scratch=[pltpu.VMEM((group, 1, own), jnp.int32)],
     )
-    head, picked, rest = lax.optimization_barrier((head, picked, rest))
+    head, stacked = lax.optimization_barrier((head, stacked))
     live_edge, residual_edge, first, near, far = call(
         head_kernel,
         [(1, width), face_shape, first_shape, long_shape, long_shape],
         head, partial, rest, dirichlet, coupling[0],
     )
     near, far = swap(near, far)
-    block = jnp.concatenate(split_outside(swap_blocks(picked)), axis=0)
+    blocks = swap_blocks(picked)
     live, residual = (live_edge, live_own), (residual_edge, residual_own)
     taken, ends, for_next, for_prev, given = call(
         operators_kernel,
@@ -560,9 +560,11 @@
     edge, first_z, values = call(
         corner_kernel,
         edges_shapes + [(own, loads)],
-        first, rest, near, far, *live, stacked,
+        first, rest, near, far, *live, stacked, solve,
     )
     everyone = lax.all_gather(values, "grp", tiled=True)
+    everyone, blocks = lax.optimization_barrier((everyone, blocks))
+    block = jnp.concatenate(split_outside(sum(blocks[1:], blocks[0])), axis=0)
     first, rest, near, far, sums = call(
         first_dual_kernel,
         [first_shape, rest_shape, longer_shape, longer_shape, scalars_shape],

time: 133 us -> 130 us (0.977)
  waiting for transfers between devices: 19 us -> 16.8 us
    ppermute x3, waiting for transfers between devices: 9.2 us -> 0.01 us  [swap_blocks(): received.append(lax.ppermute(picked[distance], 'grp', routes))]
    ppermute x5, waiting for transfers between devices: 9.74 us -> 16.8 us  [swap(): lax.ppermute(near, 'sub', neighbour_pairs(size, 0))]
  transfers between devices with their start and end apart: 18 -> 18, of which waited for: 5 -> 3; matrix products, arithmetic and copies ran while one was open for 0% -> 0% of each run, Pallas kernels for 4% -> 4%
where the time goes in v11:
time: 130 us
  blocking collectives  64 us (49%)
  starting transfers between devices  24.9 us (19%)
  Pallas kernels  19.3 us (15%)
  waiting for transfers between devices  16.8 us (13%)
  local copies, waits for them, and re-layouts  3.54 us (3%)
    all_to_all x3, blocking collectives, from_all(): return lax.all_to_all(copies, ('sub', 'grp'), 0, 0)  43.3 us
    all_gather x3, blocking collectives, local(): everyone = lax.all_gather(values, 'grp', tiled=True)  20.8 us
    pallas_call x13, Pallas kernels, call(): pl.pallas_call(kernel, out_shape=[jax.ShapeDtypeStruct(*shape) for shape...  17.6 us
    ppermute x5, waiting for transfers between devices, swap(): lax.ppermute(near, 'sub', neighbour_pairs(size, 0))  16.8 us
    ppermute x5, starting transfers between devices, swap(): lax.ppermute(near, 'sub', neighbour_pairs(size, 0))  11.6 us
    ppermute x1, starting transfers between devices, local(): head = lax.ppermute(tail, 'sub', [(i, i + 1) for i in range(size - 1)])  4.86 us
    unnamed x16, local copies, waits for them, and re-layouts  3.49 us
    ppermute x5, starting transfers between devices, swap(): lax.ppermute(far, 'sub', neighbour_pairs(size, 1))  3.34 us
  transfers between devices with their start and end apart: 18, of which 3 were waited for; matrix products, arithmetic and copies ran while one was open for 0% of the time, Pallas kernels for 4%

profile of v11, /device:TPU:0, one launch (start us, length us, event | category | flops | bytes accessed | tf_op | source)
XLA Modules:
  0.0 129.7 jit_solution(18395352252130282863)
XLA Ops:
  0.6 0.0 copy-start.3
  0.6 1.8 %shard_map.86 = f32[264,256]{1,0:T(8,128)} custom-call(s32[1,4]{1,0:T(1,128)} %counts, f32[1,4,256,256]{3,2,1,0:T(8,128)} %rhs.1), custom_call_target="tpu_custom_call" | custom-call | tf_op jit(solution)/shard_map/pallas_call | solution.py:493
  2.4 4.9 %collective-permute-start = (f32[264,256]{1,0:T(8,128)}, f32[264,256]{1,0:T(8,128)S(1)}, u32[]{:S(2)}, u32[]{:S(2)}) collective-permute-start(f32[264,256]{1,0:T(8,128)} %shard_map.86), channel_id=1, source_target_pairs={{0,4},{4,8},{8,12},{12,16},{16,20},{20,24},{24,28},{1,5},{5,9},{9,... | collective-permute-start | bytes 811016 | tf_op jit(solution)/shard_map/ppermute | solution.py:526
  7.3 0.7 collective-permute-start.3
  8.1 0.9 collective-permute-start.2
  9.0 0.3 collective-permute-start.1
  9.2 1.6 %copy-done = bf16[1,4,512,512]{3,2,1,0:T(8,128)(2,1)S(1)} copy-done((bf16[1,4,512,512]{3,2,1,0:T(8,128)(2,1)S(1)}, bf16[1,4,512,512]{3,2,1,0:T(8,128)(2,1)}, u32[]{:S(2)}) %copy-start) | copy-done | bytes 2097176
  10.8 0.7 copy-done.7
  11.5 1.2 shard_map.88
  12.7 0.0 collective-permute-done.3.refs_3_
  12.7 0.0 collective-permute-done.2.refs_2_
  12.7 0.0 collective-permute-done.1.refs_1_
  12.7 0.0 copy-start.5
  12.8 1.2 copy-done.5
  14.0 1.9 %shard_map.87 = (f32[128,512]{1,0:T(8,128)S(1)}, f32[128,512]{1,0:T(8,128)S(1)}, f32[128,512]{1,0:T(8,128)S(1)}, f32[128,512]{1,0:T(8,128)S(1)}, bf16[4,64,512]{...) custom-call(s32[4,32]{1,0:T(4,128)S(1)} %bitcast.25, s32[4,32]{1,0:T(4,128)S(1)} %collective-permute-done.1.refs_1_, ...), custom_call_target="tpu_custom_call" | custom-call | tf_op jit(solution)/shard_map/pallas_call | solution.py:35
  15.9 0.0 collective-permute-done.head
  15.9 0.0 copy-done.1
  15.9 0.0 copy-start.2
  15.9 0.3 shard_map.89
  16.2 1.6 %collective-permute-start.4 = (f32[288,256]{1,0:T(8,128)S(1)}, f32[288,256]{1,0:T(8,128)S(1)}, u32[]{:S(2)}, u32[]{:S(2)}) collective-permute-start(f32[288,256]{1,0:T(8,128)S(1)} %get-tuple-element.82), channel_id=1, source_target_pairs={{0,4},{4,0},{8,12},{12,8},{16,20},{20,16},{24,28},{28,24},{1,5},{5... | collective-permute-start | bytes 884744 | tf_op jit(solution)/shard_map/ppermute | solution.py:462
  17.9 0.7 collective-permute-start.5
  18.5 0.1 collective-permute-start.6
  18.6 1.6 %collective-permute-start.7 = (f32[128,512]{1,0:T(8,128)S(1)}, f32[128,512]{1,0:T(8,128)S(1)}, u32[]{:S(2)}, u32[]{:S(2)}) collective-permute-start(f32[128,512]{1,0:T(8,128)S(1)} %get-tuple-element.93), channel_id=1, source_target_pairs={{0,2},{1,3},{2,0},{3,1},{4,6},{5,7},{6,4},{7,5},{8,10},{9,11},{10,... | collective-permute-start | bytes 786440 | tf_op jit(solution)/shard_map/ppermute | solution.py:487
  20.2 0.3 collective-permute-start.8
  20.5 10.4 %collective-permute-done.4.near = f32[288,256]{1,0:T(8,128)S(1)} collective-permute-done((f32[288,256]{1,0:T(8,128)S(1)}, f32[288,256]{1,0:T(8,128)S(1)}, u32[]{:S(2)}, u32[]{:S(2)}) %collective-permute-start.4) | collective-permute-done | bytes 294944 | tf_op jit(solution)/shard_map/ppermute | solution.py:462
  30.9 0.0 collective-permute-done.5.far
  30.9 0.8 shard_map.90
  31.6 6.9 %all_gather.9.everyone = f32[512,256]{1,0:T(8,128)S(1)} all-gather(f32[128,256]{1,0:T(8,128)S(1)} %get-tuple-element.90), channel_id=1, replica_groups=mesh['sub'=8,'grp'=4] {'grp'}, dimensions={0}, use_global_device_ids=true | all-gather | bytes 655360 | tf_op jit(solution)/shard_map/all_gather | solution.py:565
  38.6 0.0 collective-permute-done.6
  38.6 0.0 collective-permute-done.7
  38.6 0.0 collective-permute-done.8
  38.6 0.1 reduce-precision_convert_fusion
  38.7 0.6 shard_map.91
  39.3 2.2 %shard_map.92 = (f32[256,512]{1,0:T(8,128)S(1)}, f32[3,256,512]{2,1,0:T(8,128)S(1)}, f32[352,256]{1,0:T(8,128)S(1)}, f32[352,256]{1,0:T(8,128)S(1)}, f32[2,256]{1,0:T(2,128)S(1)}) custom-call(f32[256,256]{1,0:T(8,128)S(1)} %get-tuple-element.87.edge, f32[4,256,256]{2,1,0:T(8,128)S(1)} %get-tuple-element.88.own.first_z, ...), custom_call_target="tpu_custom_call" | custom-call | tf_op jit(solution)/shard_map/pallas_call | solution.py:35
  41.6 2.5 %collective-permute-start.9 = (f32[352,256]{1,0:T(8,128)S(1)}, f32[352,256]{1,0:T(8,128)S(1)}, u32[]{:S(2)}, u32[]{:S(2)}) collective-permute-start(f32[352,256]{1,0:T(8,128)S(1)} %get-tuple-element.106), channel_id=1, source_target_pairs={{0,4},{4,0},{8,12},{12,8},{16,20},{20,16},{24,28},{28,24},{1,5},{5... | collective-permute-start | bytes 1081352 | tf_op jit(solution)/shard_map/ppermute | solution.py:462
  44.1 0.7 collective-permute-start.10
  44.8 15.9 %all_to_all.15.sums = f32[32,2,256]{2,1,0:T(2,128)S(1)} all-to-all(f32[32,2,256]{2,1,0:T(2,128)S(1)} %broadcast_in_dim.10), channel_id=1, replica_groups=mesh['sub'=8,'grp'=4] {'sub','grp'}, dimensions={0} | all-to-all | bytes 131072 | tf_op jit(solution)/shard_map/all_to_all | solution.py:470
  60.7 0.0 collective-permute-done.9.near
  60.7 0.0 collective-permute-done.10.far
  60.7 1.6 %shard_map.93 = (f32[4,256,256]{2,1,0:T(8,128)S(1)}, f32[256,256]{1,0:T(8,128)S(1)}, f32[256,256]{1,0:T(8,128)S(1)}, f32[4,256,256]{2,1,0:T(8,128)S(1)}, f32[256...) custom-call(f32[256,512]{1,0:T(8,128)S(1)} %get-tuple-element.104.fi, ...), custom_call_target="tpu_custom_call" | custom-call | tf_op jit(solution)/shard_map/pallas_call | solution.py:35
  62.3 3.3 %collective-permute-start.11 = (f32[256,256]{1,0:T(8,128)S(1)}, f32[256,256]{1,0:T(8,128)S(1)}, u32[]{:S(2)}, u32[]{:S(2)}) collective-permute-start(f32[256,256]{1,0:T(8,128)S(1)} %get-tuple-element.113), channel_id=1, source_target_pairs={{0,4},{4,0},{8,12},{12,8},{16,20},{20,16},{24,28},{28,24},{1,5},{5... | collective-permute-start | bytes 786440 | tf_op jit(solution)/shard_map/ppermute | solution.py:462
  65.6 0.7 collective-permute-start.12
  66.3 0.7 shard_map.94
  67.0 6.8 %all_gather.10.refs_8_ = f32[512,256]{1,0:T(8,128)S(1)} all-gather(f32[128,256]{1,0:T(8,128)S(1)} %shard_map.94), channel_id=1, replica_groups=mesh['sub'=8,'grp'=4] {'grp'}, dimensions={0}, use_global_device_ids=true | all-gather | bytes 655360 | tf_op jit(solution)/shard_map/all_gather | solution.py:586
  73.7 3.3 %collective-permute-done.11.refs_2_ = f32[256,256]{1,0:T(8,128)S(1)} collective-permute-done((f32[256,256]{1,0:T(8,128)S(1)}, f32[256,256]{1,0:T(8,128)S(1)}, u32[]{:S(2)}, u32[]{:S(2)}) %collective-permute-start.11) | collective-permute-done | bytes 262176 | tf_op jit(solution)/shard_map/ppermute | solution.py:462
  77.0 0.0 collective-permute-done.12.refs_3_
  77.1 2.2 %shard_map.95 = (f32[4,256,256]{2,1,0:T(8,128)S(1)}, f32[256,512]{1,0:T(8,128)S(1)}, f32[3,256,512]{2,1,0:T(8,128)S(1)}, f32[288,256]{1,0:T(8,128)S(1)}, f32[288,256]{1,0:T(8,128)S(1)}, /*index=5*/f32[2,256]{1,0:T(2,128)S(1)}) custom-call(f32[256,512]{1,0:T(8,128)S(1)} %get-tuple-element.111.refs_0_, f32[3,256,512]{2,1,0:T(8,128)S(1)} %get-tuple-element.112.refs_1_, ...), custom_call_target="tpu_custom_call" | custom-call | tf_op jit(solution)/shard_map/pallas_call | solution.py:35
  79.3 2.5 %collective-permute-start.13 = (f32[288,256]{1,0:T(8,128)S(1)}, f32[288,256]{1,0:T(8,128)S(1)}, u32[]{:S(2)}, u32[]{:S(2)}) collective-permute-start(f32[288,256]{1,0:T(8,128)S(1)} %get-tuple-element.122), channel_id=1, source_target_pairs={{0,4},{4,0},{8,12},{12,8},{16,20},{20,16},{24,28},{28,24},{1,5},{5... | collective-permute-start | bytes 884744 | tf_op jit(solution)/shard_map/ppermute | solution.py:462
  81.8 0.7 collective-permute-start.14
  82.5 12.9 %all_to_all.16.sums = f32[32,2,256]{2,1,0:T(2,128)S(1)} all-to-all(f32[32,2,256]{2,1,0:T(2,128)S(1)} %broadcast_in_dim.11), channel_id=1, replica_groups=mesh['sub'=8,'grp'=4] {'sub','grp'}, dimensions={0} | all-to-all | bytes 131072 | tf_op jit(solution)/shard_map/all_to_all | solution.py:470
  95.4 0.0 collective-permute-done.13.near
  95.4 0.0 collective-permute-done.14.far
  95.4 1.7 %shard_map.96 = (f32[4,256,256]{2,1,0:T(8,128)S(1)}, f32[256,256]{1,0:T(8,128)S(1)}, f32[4,256,256]{2,1,0:T(8,128)S(1)}, f32[256,512]{1,0:T(8,128)S(1)}, f32[3,2...) custom-call(f32[256,512]{1,0:T(8,128)S(1)} %get-tuple-element.120.fi, ...), custom_call_target="tpu_custom_call" | custom-call | tf_op jit(solution)/shard_map/pallas_call | solution.py:35
  97.1 1.7 %collective-permute-start.15 = (f32[256,256]{1,0:T(8,128)S(1)}, f32[256,256]{1,0:T(8,128)S(1)}, u32[]{:S(2)}, u32[]{:S(2)}) collective-permute-start(f32[256,256]{1,0:T(8,128)S(1)} %get-tuple-element.131), channel_id=1, source_target_pairs={{0,4},{4,0},{8,12},{12,8},{16,20},{20,16},{24,28},{28,24},{1,5},{5... | collective-permute-start | bytes 786440 | tf_op jit(solution)/shard_map/ppermute | solution.py:462
  98.8 0.7 collective-permute-start.16
  99.4 0.7 shard_map.97
  100.1 7.0 %all_gather.11.refs_8_ = f32[512,256]{1,0:T(8,128)S(1)} all-gather(f32[128,256]{1,0:T(8,128)S(1)} %shard_map.97), channel_id=1, replica_groups=mesh['sub'=8,'grp'=4] {'grp'}, dimensions={0}, use_global_device_ids=true | all-gather | bytes 655360 | tf_op jit(solution)/shard_map/all_gather | solution.py:604
  107.2 3.1 %collective-permute-done.15.refs_2_ = f32[256,256]{1,0:T(8,128)S(1)} collective-permute-done((f32[256,256]{1,0:T(8,128)S(1)}, f32[256,256]{1,0:T(8,128)S(1)}, u32[]{:S(2)}, u32[]{:S(2)}) %collective-permute-start.15) | collective-permute-done | bytes 262176 | tf_op jit(solution)/shard_map/ppermute | solution.py:462
  110.2 0.0 collective-permute-done.16.refs_3_
  110.2 2.0 %shard_map.98 = (f32[4,256,256]{2,1,0:T(8,128)S(1)}, f32[256,512]{1,0:T(8,128)S(1)}, f32[3,256,512]{2,1,0:T(8,128)S(1)}, f32[256,256]{1,0:T(8,128)S(1)}, f32[2,256]{1,0:T(2,128)S(1)}) custom-call(f32[256,512]{1,0:T(8,128)S(1)} %get-tuple-element.129.refs_0_, f32[3,256,512]{2,1,0:T(8,128)S(1)} %get-tuple-element.130.refs_1_, ...), custom_call_target="tpu_custom_call" | custom-call | tf_op jit(solution)/shard_map/pallas_call | solution.py:35
  112.2 1.3 collective-permute-start.17
  113.5 14.4 %all_to_all.17.sums = f32[32,2,256]{2,1,0:T(2,128)S(1)} all-to-all(f32[32,2,256]{2,1,0:T(2,128)S(1)} %broadcast_in_dim.12), channel_id=1, replica_groups=mesh['sub'=8,'grp'=4] {'sub','grp'}, dimensions={0} | all-to-all | bytes 131072 | tf_op jit(solution)/shard_map/all_to_all | solution.py:470
  128.0 0.0 collective-permute-done.17.following
  128.0 1.8 %shard_map.99 = (f32[4,256,256]{2,1,0:T(8,128)}, f32[4,256,256]{2,1,0:T(8,128)}) custom-call(f32[256,512]{1,0:T(8,128)S(1)} %get-tuple-element.136.first, f32[3,256,512]{2,1,0:T(8,128)S(1)} %get-tuple-element.137.rest, f32[256,256]{1,0:T(8,128)S(1)} %collective-permute-done.17.following, f32[4,1,256]{2,1,0:T(1,128)S(1)} %get-tuple-element.85.live_rest.live_own.refs_5_.live, ...), custom_call_target="tpu_custom_call" | custom-call | tf_op jit(solution)/shard_map/pallas_call | solution.py:35
  (14 shorter events, 0.1 us)
Async XLA Ops:
  0.6 8.6 %copy-start.3 = (f32[1,4,256,256]{3,2,1,0:T(8,128)S(1)}, f32[1,4,256,256]{3,2,1,0:T(8,128)}, u32[]{:S(2)}) copy-start(f32[1,4,256,256]{3,2,1,0:T(8,128)} %rhs.1) | copy-start | bytes 3145732
  2.4 13.4 %collective-permute-start = (f32[264,256]{1,0:T(8,128)}, f32[264,256]{1,0:T(8,128)S(1)}, u32[]{:S(2)}, u32[]{:S(2)}) collective-permute-start(f32[264,256]{1,0:T(8,128)} %shard_map.86), channel_id=1, source_target_pairs={{0,4},{4,8},{8,12},{12,16},{16,20},{20,24},{24,28},{1,5},{5,9},{9,... | collective-permute-start | bytes 811016 | tf_op jit(solution)/shard_map/ppermute | solution.py:526
  7.3 5.4 %collective-permute-start.3 = (s32[4,32]{1,0:T(4,128)}, s32[4,32]{1,0:T(4,128)S(1)}, u32[]{:S(2)}, u32[]{:S(2)}) collective-permute-start(s32[4,32]{1,0:T(4,128)} %bitcast.22), channel_id=1, source_target_pairs={{0,3},{1,2},{2,1},{3,0},{4,7},{5,6},{6,5},{7,4},{8,11},{9,10},{10,... | collective-permute-start | bytes 1544 | tf_op jit(solution)/shard_map/ppermute | solution.py:478
  8.1 4.7 %collective-permute-start.2 = (s32[4,32]{1,0:T(4,128)}, s32[4,32]{1,0:T(4,128)S(1)}, u32[]{:S(2)}, u32[]{:S(2)}) collective-permute-start(s32[4,32]{1,0:T(4,128)} %bitcast.23), channel_id=1, source_target_pairs={{0,2},{1,3},{2,0},{3,1},{4,6},{5,7},{6,4},{7,5},{8,10},{9,11},{10,... | collective-permute-start | bytes 1544 | tf_op jit(solution)/shard_map/ppermute | solution.py:478
  9.0 3.7 %collective-permute-start.1 = (s32[4,32]{1,0:T(4,128)}, s32[4,32]{1,0:T(4,128)S(1)}, u32[]{:S(2)}, u32[]{:S(2)}) collective-permute-start(s32[4,32]{1,0:T(4,128)} %bitcast.24), channel_id=1, source_target_pairs={{0,1},{1,0},{2,3},{3,2},{4,5},{5,4},{6,7},{7,6},{8,9},{9,8},{10,11... | collective-permute-start | bytes 1544 | tf_op jit(solution)/shard_map/ppermute | solution.py:478
  9.2 1.6 %copy-start = (bf16[1,4,512,512]{3,2,1,0:T(8,128)(2,1)S(1)}, bf16[1,4,512,512]{3,2,1,0:T(8,128)(2,1)}, u32[]{:S(2)}) copy-start(bf16[1,4,512,512]{3,2,1,0:T(8,128)(2,1)} %param.10) | copy-start | bytes 6291460
  10.8 0.7 copy-start.7
  11.5 1.2 copy-start.4
  11.5 1.2 copy-start.6
  11.5 4.4 %copy-start.1 = (bf16[1,4,512,512]{3,2,1,0:T(8,128)(2,1)S(1)}, bf16[1,4,512,512]{3,2,1,0:T(8,128)(2,1)}, u32[]{:S(2)}) copy-start(bf16[1,4,512,512]{3,2,1,0:T(8,128)(2,1)} %param.10) | copy-start | bytes 6291460
  12.7 1.2 copy-start.5
  15.9 15.0 %copy-start.2 = (bf16[1,4,512,512]{3,2,1,0:T(8,128)(2,1)S(1)}, bf16[1,4,512,512]{3,2,1,0:T(8,128)(2,1)}, u32[]{:S(2)}) copy-start(bf16[1,4,512,512]{3,2,1,0:T(8,128)(2,1)} %param.9) | copy-start | bytes 6291460
  16.2 14.6 %collective-permute-start.4 = (f32[288,256]{1,0:T(8,128)S(1)}, f32[288,256]{1,0:T(8,128)S(1)}, u32[]{:S(2)}, u32[]{:S(2)}) collective-permute-start(f32[288,256]{1,0:T(8,128)S(1)} %get-tuple-element.82), channel_id=1, source_target_pairs={{0,4},{4,0},{8,12},{12,8},{16,20},{20,16},{24,28},{28,24},{1,5},{5... | collective-permute-start | bytes 884744 | tf_op jit(solution)/shard_map/ppermute | solution.py:462
  17.9 13.0 %collective-permute-start.5 = (f32[288,256]{1,0:T(8,128)S(1)}, f32[288,256]{1,0:T(8,128)S(1)}, u32[]{:S(2)}, u32[]{:S(2)}) collective-permute-start(f32[288,256]{1,0:T(8,128)S(1)} %get-tuple-element.83), channel_id=1, source_target_pairs={{4,8},{8,4},{12,16},{16,12},{20,24},{24,20},{5,9},{9,5},{13,17},{1... | collective-permute-start | bytes 884744 | tf_op jit(solution)/shard_map/ppermute | solution.py:463
  18.5 20.0 %collective-permute-start.6 = (f32[128,512]{1,0:T(8,128)S(1)}, f32[128,512]{1,0:T(8,128)S(1)}, u32[]{:S(2)}, u32[]{:S(2)}) collective-permute-start(f32[128,512]{1,0:T(8,128)S(1)} %get-tuple-element.92), channel_id=1, source_target_pairs={{0,1},{1,0},{2,3},{3,2},{4,5},{5,4},{6,7},{7,6},{8,9},{9,8},{10,11... | collective-permute-start | bytes 786440 | tf_op jit(solution)/shard_map/ppermute | solution.py:487
  18.6 20.0 %collective-permute-start.7 = (f32[128,512]{1,0:T(8,128)S(1)}, f32[128,512]{1,0:T(8,128)S(1)}, u32[]{:S(2)}, u32[]{:S(2)}) collective-permute-start(f32[128,512]{1,0:T(8,128)S(1)} %get-tuple-element.93), channel_id=1, source_target_pairs={{0,2},{1,3},{2,0},{3,1},{4,6},{5,7},{6,4},{7,5},{8,10},{9,11},{10,... | collective-permute-start | bytes 786440 | tf_op jit(solution)/shard_map/ppermute | solution.py:487
  20.2 18.4 %collective-permute-start.8 = (f32[128,512]{1,0:T(8,128)S(1)}, f32[128,512]{1,0:T(8,128)S(1)}, u32[]{:S(2)}, u32[]{:S(2)}) collective-permute-start(f32[128,512]{1,0:T(8,128)S(1)} %get-tuple-element.94), channel_id=1, source_target_pairs={{0,3},{1,2},{2,1},{3,0},{4,7},{5,6},{6,5},{7,4},{8,11},{9,10},{10,... | collective-permute-start | bytes 786440 | tf_op jit(solution)/shard_map/ppermute | solution.py:487
  41.6 19.1 %collective-permute-start.9 = (f32[352,256]{1,0:T(8,128)S(1)}, f32[352,256]{1,0:T(8,128)S(1)}, u32[]{:S(2)}, u32[]{:S(2)}) collective-permute-start(f32[352,256]{1,0:T(8,128)S(1)} %get-tuple-element.106), channel_id=1, source_target_pairs={{0,4},{4,0},{8,12},{12,8},{16,20},{20,16},{24,28},{28,24},{1,5},{5... | collective-permute-start | bytes 1081352 | tf_op jit(solution)/shard_map/ppermute | solution.py:462
  44.1 16.6 %collective-permute-start.10 = (f32[352,256]{1,0:T(8,128)S(1)}, f32[352,256]{1,0:T(8,128)S(1)}, u32[]{:S(2)}, u32[]{:S(2)}) collective-permute-start(f32[352,256]{1,0:T(8,128)S(1)} %get-tuple-element.107), channel_id=1, source_target_pairs={{4,8},{8,4},{12,16},{16,12},{20,24},{24,20},{5,9},{9,5},{13,17},{1... | collective-permute-start | bytes 1081352 | tf_op jit(solution)/shard_map/ppermute | solution.py:463
  62.3 14.8 %collective-permute-start.11 = (f32[256,256]{1,0:T(8,128)S(1)}, f32[256,256]{1,0:T(8,128)S(1)}, u32[]{:S(2)}, u32[]{:S(2)}) collective-permute-start(f32[256,256]{1,0:T(8,128)S(1)} %get-tuple-element.113), channel_id=1, source_target_pairs={{0,4},{4,0},{8,12},{12,8},{16,20},{20,16},{24,28},{28,24},{1,5},{5... | collective-permute-start | bytes 786440 | tf_op jit(solution)/shard_map/ppermute | solution.py:462
  65.6 11.5 %collective-permute-start.12 = (f32[256,256]{1,0:T(8,128)S(1)}, f32[256,256]{1,0:T(8,128)S(1)}, u32[]{:S(2)}, u32[]{:S(2)}) collective-permute-start(f32[256,256]{1,0:T(8,128)S(1)} %get-tuple-element.114), channel_id=1, source_target_pairs={{4,8},{8,4},{12,16},{16,12},{20,24},{24,20},{5,9},{9,5},{13,17},{1... | collective-permute-start | bytes 786440 | tf_op jit(solution)/shard_map/ppermute | solution.py:463
  79.3 16.1 %collective-permute-start.13 = (f32[288,256]{1,0:T(8,128)S(1)}, f32[288,256]{1,0:T(8,128)S(1)}, u32[]{:S(2)}, u32[]{:S(2)}) collective-permute-start(f32[288,256]{1,0:T(8,128)S(1)} %get-tuple-element.122), channel_id=1, source_target_pairs={{0,4},{4,0},{8,12},{12,8},{16,20},{20,16},{24,28},{28,24},{1,5},{5... | collective-permute-start | bytes 884744 | tf_op jit(solution)/shard_map/ppermute | solution.py:462
  81.8 13.6 %collective-permute-start.14 = (f32[288,256]{1,0:T(8,128)S(1)}, f32[288,256]{1,0:T(8,128)S(1)}, u32[]{:S(2)}, u32[]{:S(2)}) collective-permute-start(f32[288,256]{1,0:T(8,128)S(1)} %get-tuple-element.123), channel_id=1, source_target_pairs={{4,8},{8,4},{12,16},{16,12},{20,24},{24,20},{5,9},{9,5},{13,17},{1... | collective-permute-start | bytes 884744 | tf_op jit(solution)/shard_map/ppermute | solution.py:463
  97.1 13.1 %collective-permute-start.15 = (f32[256,256]{1,0:T(8,128)S(1)}, f32[256,256]{1,0:T(8,128)S(1)}, u32[]{:S(2)}, u32[]{:S(2)}) collective-permute-start(f32[256,256]{1,0:T(8,128)S(1)} %get-tuple-element.131), channel_id=1, source_target_pairs={{0,4},{4,0},{8,12},{12,8},{16,20},{20,16},{24,28},{28,24},{1,5},{5... | collective-permute-start | bytes 786440 | tf_op jit(solution)/shard_map/ppermute | solution.py:462
  98.8 11.5 %collective-permute-start.16 = (f32[256,256]{1,0:T(8,128)S(1)}, f32[256,256]{1,0:T(8,128)S(1)}, u32[]{:S(2)}, u32[]{:S(2)}) collective-permute-start(f32[256,256]{1,0:T(8,128)S(1)} %get-tuple-element.132), channel_id=1, source_target_pairs={{4,8},{8,4},{12,16},{16,12},{20,24},{24,20},{5,9},{9,5},{13,17},{1... | collective-permute-start | bytes 786440 | tf_op jit(solution)/shard_map/ppermute | solution.py:463
  112.2 15.8 %collective-permute-start.17 = (f32[256,256]{1,0:T(8,128)S(1)}, f32[256,256]{1,0:T(8,128)S(1)}, u32[]{:S(2)}, u32[]{:S(2)}) collective-permute-start(f32[256,256]{1,0:T(8,128)S(1)} %get-tuple-element.138), channel_id=1, source_target_pairs={{4,0},{8,4},{12,8},{16,12},{20,16},{24,20},{28,24},{5,1},{9,5},{13... | collective-permute-start | bytes 786440 | tf_op jit(solution)/shard_map/ppermute | solution.py:611

commit v12 on v11

--- a/solution.py
+++ b/solution.py
@@ -295,8 +295,8 @@
         )
 
 
-def dual_products(edges, residual, panel, everyone, block, lift, result, sums):
-    subs, width = panel.shape[0], panel.shape[1] // 2
+def coarse_lift(everyone, block, lift):
+    subs = lift.shape[0]
     rows = block.shape[0] // 2
     high, low = split(everyone[...])
     both = mul(block[...], high)
@@ -310,60 +310,121 @@
         spare = jnp.zeros((lift.shape[1] - 3 * corners, own.shape[1]), jnp.float32)
         return mul(jnp.concatenate(terms + [spare], axis=0).T.astype(jnp.bfloat16), lift[sub])
 
+    return lifted
+
+
+def on_subdomain(values, left, right):
+    width = left.shape[1]
+    return values[:, width:] * right - values[:, :width] * left
+
+
+def send_dual(even, inner, faces, for_next, for_prev, near_out, far_out, residual=None,
+              given=None):
+    to_next, to_prev = [faces[0]], [faces[1]]
+    count = inner.shape[0]
+    if given is not None:
+        to_next += [given[0], outer_rows(for_next, residual[count - 1])]
+        to_prev += [given[1], outer_rows(for_prev, residual[0])]
+    to_next.append(outer_rows(for_next, inner[count - 1]))
+    to_prev.append(outer_rows(for_prev, inner[0]))
+    send(even, to_next, to_prev, near_out, far_out)
+
+
+def inner_jump(result, live_own, inner):
+    width = inner.shape[2]
+    for place in range(inner.shape[0]):
+        inner[place] = live_own[place] * (result[place][:, width:] - result[place + 1][:, :width])
+
+
+def first_dual_kernel(edge, own, residual, panel, everyone, block, lift, live_own,
+                      for_next, for_prev, given, inner, near_out, far_out, sums, result):
+    subs, width = panel.shape[0], edge.shape[1]
+    edges = Joined(edge, own)
     parts = [split(edges[place]) for place in range(subs + 1)]
-    panel_products(parts, panel, result, lifted)
+    panel_products(parts, panel, result, coarse_lift(everyone, block, lift))
+    inner_jump(result, live_own, inner)
+    faces = [result[subs - 1][:, width:], result[0][:, :width]]
+    send_dual(even_place(), inner, faces, for_next, for_prev, near_out, far_out, residual, given)
     product = curvature = 0.0
     for sub in range(subs):
         product = product + residual[sub] * edges[sub + 1]
-        curvature = curvature + (
-            result[sub][:, width:] * edges[sub + 1] - result[sub][:, :width] * edges[sub]
-        )
+        curvature = curvature + on_subdomain(result[sub], edges[sub], edges[sub + 1])
     sums[...] = jnp.concatenate([row_sums(product), row_sums(curvature)], axis=0)
 
 
-def send_dual(result, live_own, subs, for_next, for_prev, near_out, far_out, residual=None,
-              given=None):
-    even = even_place()
-    width = near_out.shape[1]
-    to_next, to_prev = [result[subs - 1][:, width:]], [result[0][:, :width]]
-    if given is not None:
-        to_next += [given[0], outer_rows(for_next, residual[subs - 2])]
-        to_prev += [given[1], outer_rows(for_prev, residual[0])]
-    upper = live_own[subs - 2] * (result[subs - 2][:, width:] - result[subs - 1][:, :width])
-    lower = live_own[0] * (result[0][:, width:] - result[1][:, :width])
-    to_next.append(outer_rows(for_next, upper))
-    to_prev.append(outer_rows(for_prev, lower))
-    send(even, to_next, to_prev, near_out, far_out)
-
-
-def first_dual_kernel(edge, own, residual, panel, everyone, block, lift, live_own,
-                      for_next, for_prev, given, first, rest, near_out, far_out, sums):
-    result = Joined(first, rest)
-    dual_products(Joined(edge, own), residual, panel, everyone, block, lift, result, sums)
-    send_dual(result, live_own, panel.shape[0], for_next, for_prev, near_out, far_out,
-              residual, given)
-
-
-def dual_kernel(last, *refs):
-    first, rest, near, far, live_edge, live_own = refs[:6]
-    residual, panel, everyone, block, lift = refs[6:11]
-    even, subs = even_place(), panel.shape[0]
-    before, live = Joined(first, rest), Joined(live_edge, live_own)
-    edges = [
-        0.25 * jump_edge(even, before, near, far, live, place, subs) for place in range(subs + 1)
-    ]
-    if last:
-        own, first_new, rest_new, face, sums = refs[11:]
+def inner_edges_kernel(edge, own, panel, live_own, inner):
+    subs, width = panel.shape[0], edge.shape[1]
+    edges = Joined(edge, own)
+    parts = [split(edges[place]) for place in range(subs + 1)]
+
+    def half(sub, columns):
+        high = jnp.concatenate([-parts[sub][0], parts[sub + 1][0]], axis=1)
+        low = jnp.concatenate([-parts[sub][1], parts[sub + 1][1]], axis=1)
+        return mul(high, panel[sub, :, columns]) + mul(low, panel[sub, :, columns])
+
+    for place in range(subs - 1):
+        right = half(place, slice(width, 2 * width))
+        left = half(place + 1, slice(0, width))
+        inner[place] = (0.25 * live_own[place]) * (right - left)
+
+
+def inner_dual_kernel(inner, residual, panel, everyone, block, lift, result, partial):
+    subs, width = panel.shape[0], inner.shape[2]
+    lifted = coarse_lift(everyone, block, lift)
+    parts = [split(inner[place]) for place in range(subs - 1)]
+    high, low = parts[0]
+    result[0] = mul(high, panel[0, width:]) + mul(low, panel[0, width:]) + lifted(0)
+    product = residual[0] * inner[0]
+    curvature = jnp.zeros_like(product)
+    for sub in range(1, subs - 1):
+        high = jnp.concatenate([-parts[sub - 1][0], parts[sub][0]], axis=1)
+        low = jnp.concatenate([-parts[sub - 1][1], parts[sub][1]], axis=1)
+        result[sub] = mul(high, panel[sub]) + mul(low, panel[sub]) + lifted(sub)
+        product = product + residual[sub] * inner[sub]
+        curvature = curvature + on_subdomain(result[sub], inner[sub - 1], inner[sub])
+    high, low = parts[subs - 2]
+    result[subs - 1] = lifted(subs - 1) - (
+        mul(high, panel[subs - 1, :width]) + mul(low, panel[subs - 1, :width])
+    )
+    partial[0] = product
+    partial[1] = curvature
+
+
+def cut_edges(even, loads, near, far, near_sent, far_sent, live_first, live_last):
+    near, far, near_sent, far_sent = near[:loads], far[:loads], near_sent[:loads], far_sent[:loads]
+    first = live_first * jnp.where(even, far - far_sent, near - near_sent)
+    last = live_last * jnp.where(even, near_sent - near, far_sent - far)
+    return first, last
+
+
+def outer_dual_kernel(closing, *refs):
+    before, inner_z, partial, near, far, near_sent, far_sent, live_edge, live_own = refs[:9]
+    residual, panel = refs[9:11]
+    even, subs, width = even_place(), panel.shape[0], near_sent.shape[1]
+    edge, last = cut_edges(even, residual.shape[1], near, far, near_sent, far_sent,
+                           0.25 * live_edge[...], 0.25 * live_own[subs - 1])
+    if closing:
+        last_z, inner, to_next, to_prev, sums = refs[11:]
     else:
-        for_next, for_prev, own, first_new, rest_new, near_out, far_out, sums = refs[11:]
-    for sub in range(subs):
-        own[sub] = edges[sub + 1]
-    result = Joined(first_new, rest_new)
-    dual_products(edges, residual, panel, everyone, block, lift, result, sums)
-    if last:
-        face[...] = result[0][:, : face.shape[1]]
+        for_next, for_prev, last_z, inner, near_out, far_out, sums = refs[11:]
+    last_z[...] = last
+    high, low = split(edge)
+    result_first = before[0] - (mul(high, panel[0, :width]) + mul(low, panel[0, :width]))
+    high, low = split(last)
+    result_last = before[subs - 1] + (
+        mul(high, panel[subs - 1, width:]) + mul(low, panel[subs - 1, width:])
+    )
+    result = [result_first] + [before[sub] for sub in range(1, subs - 1)] + [result_last]
+    inner_jump(result, live_own, inner)
+    faces = [result_last[:, width:], result_first[:, :width]]
+    if closing:
+        to_next[...], to_prev[...] = faces
     else:
-        send_dual(result, live_own, subs, for_next, for_prev, near_out, far_out)
+        send_dual(even, inner, faces, for_next, for_prev, near_out, far_out)
+    product = partial[0] + residual[subs - 1] * last
+    curvature = partial[1] + on_subdomain(result_first, edge, inner_z[0])
+    curvature = curvature + on_subdomain(result_last, inner_z[subs - 2], last)
+    sums[...] = jnp.concatenate([row_sums(product), row_sums(curvature)], axis=0)
 
 
 def received(even, near, far, start, rows):
@@ -373,16 +434,34 @@
     )
 
 
-def first_update_kernel(first, rest, near, far, live_first, live_rest, sums,
+def send_outer(parts, panel, near_out, far_out):
+    subs, width = panel.shape[0], near_out.shape[1]
+
+    def half(sub, columns):
+        high = jnp.concatenate([-parts[sub][0], parts[sub + 1][0]], axis=1)
+        low = jnp.concatenate([-parts[sub][1], parts[sub + 1][1]], axis=1)
+        return mul(high, panel[sub, :, columns]) + mul(low, panel[sub, :, columns])
+
+    to_next = half(subs - 1, slice(width, 2 * width))
+    send(even_place(), [to_next], [half(0, slice(0, width))], near_out, far_out)
+
+
+def image_edges(even, inner, near, far, near_sent, far_sent, live_edge, live_own):
+    subs = live_own.shape[0]
+    edge, last = cut_edges(even, inner.shape[1], near, far, near_sent, far_sent, live_edge[...],
+                           live_own[subs - 1])
+    return [edge] + [inner[place] for place in range(subs - 1)] + [last]
+
+
+def first_update_kernel(inner, near, far, near_sent, far_sent, live_edge, live_own, sums,
                         residual_edge, residual_own, panel, ends,
-                        image_own, image_edge, new_edge, new_own, first_new, rest_new,
+                        image_own, image_edge, new_edge, new_own,
                         near_out, far_out, scalars, full_ends, outside_image, outside):
     even = even_place()
     loads, width = residual_edge.shape
     subs, rows = panel.shape[0], ends.shape[1]
-    result, live = Joined(first, rest), Joined(live_first, live_rest)
     residual, image = Joined(residual_edge, residual_own), Joined(image_edge, image_own)
-    residual_new, result_new = Joined(new_edge, new_own), Joined(first_new, rest_new)
+    residual_new = Joined(new_edge, new_own)
     rz_now, alpha, _ = step_scalars(0, sums, None)
     scalars[...] = jnp.concatenate([rz_now, alpha], axis=0)
     operators = received(even, near, far, loads, rows)
@@ -393,47 +472,43 @@
     outside[...] = received(even, near, far, loads + rows, rows) - alpha * values
     alpha_column = column(alpha, width)
     parts = []
-    for place in range(subs + 1):
-        value = jump_edge(even, result, near, far, live, place, subs)
+    edges = image_edges(even, inner, near, far, near_sent, far_sent, live_edge, live_own)
+    for place, value in enumerate(edges):
         image[place] = value
         residual_new[place] = residual[place] - alpha_column * value
         parts.append(split(residual_new[place]))
-    panel_products(parts, panel, result_new)
-    send_faces(even, result_new[0], result_new[subs - 1], near_out, far_out)
-
-
-def update_kernel(first, rest, near, far, live_first, live_rest, sums, before,
+    send_outer(parts, panel, near_out, far_out)
+
+
+def update_kernel(inner, near, far, near_sent, far_sent, live_edge, live_own, sums, before,
                   old_edge, old_own, residual_edge, residual_own, panel,
                   outside_image_old, outside_old,
-                  image_own, new_edge, new_own, first_new, rest_new,
-                  near_out, far_out, scalars, outside):
+                  image_own, new_edge, new_own, near_out, far_out, scalars, outside):
     even = even_place()
     loads, width = residual_edge.shape
-    subs, rows = panel.shape[0], outside.shape[0] // 2
-    result, live = Joined(first, rest), Joined(live_first, live_rest)
+    rows = outside.shape[0] // 2
     image_old, residual = Joined(old_edge, old_own), Joined(residual_edge, residual_own)
-    residual_new, result_new = Joined(new_edge, new_own), Joined(first_new, rest_new)
+    residual_new = Joined(new_edge, new_own)
     rz_now, alpha, beta = step_scalars(1, sums, before)
     scalars[...] = jnp.concatenate([rz_now, alpha], axis=0)
     values = received(even, near, far, loads, rows) + beta * outside_image_old[...]
     outside[...] = outside_old[...] - alpha * values
     alpha_column, beta_column = column(alpha, width), column(beta, width)
     parts = []
-    for place in range(subs + 1):
-        value = jump_edge(even, result, near, far, live, place, subs)
+    edges = image_edges(even, inner, near, far, near_sent, far_sent, live_edge, live_own)
+    for place, value in enumerate(edges):
         value = value + beta_column * image_old[place]
         if place > 0:
             image_own[place - 1] = value
         residual_new[place] = residual[place] - alpha_column * value
         parts.append(split(residual_new[place]))
-    panel_products(parts, panel, result_new)
-    send_faces(even, result_new[0], result_new[subs - 1], near_out, far_out)
-
-
-def last_kernel(first, rest, following, live, sums, before, older, image_old,
-                residual, first_z, second_z, third_z, multipliers, residual_new):
+    send_outer(parts, panel, near_out, far_out)
+
+
+def last_kernel(inner, to_next, following, live, sums, before, older, image_old,
+                residual, first_z, second_inner, second_last, third_inner, third_last,
+                multipliers, residual_new):
     subs, width = residual.shape[0], following.shape[1]
-    result = Joined(first, rest)
     rz_now, alpha, beta = step_scalars(2, sums, before)
     beta_before = before[0:1] / older[0:1]
     on_second = before[1:2] + alpha * beta
@@ -441,13 +516,15 @@
     alpha_column, beta_column = column(alpha, width), column(beta, width)
     second_column, first_column = column(on_second, width), column(on_first, width)
     for sub in range(subs):
-        left = following[...] if sub == subs - 1 else result[sub + 1][:, :width]
-        image = live[sub] * (result[sub][:, width:] - left) + beta_column * image_old[sub]
+        if sub == subs - 1:
+            image = live[sub] * (to_next[...] - following[...])
+            second_z, third_z = second_last[...], third_last[...]
+        else:
+            image, second_z, third_z = inner[sub], second_inner[sub], third_inner[sub]
+        image = image + beta_column * image_old[sub]
         residual_new[sub] = residual[sub] - alpha_column * image
         multipliers[sub] = (
-            first_column * first_z[sub]
-            + second_column * second_z[sub]
-            + alpha_column * third_z[sub]
+            first_column * first_z[sub] + second_column * second_z + alpha_column * third_z
         )
 
 
@@ -565,55 +642,69 @@
     everyone = lax.all_gather(values, "grp", tiled=True)
     everyone, blocks = lax.optimization_barrier((everyone, blocks))
     block = jnp.concatenate(split_outside(sum(blocks[1:], blocks[0])), axis=0)
-    first, rest, near, far, sums = call(
+    inner_shape, result_shape = (subs - 1, loads, width), (subs, loads, 2 * width)
+    inner, near, far, sums = call(
         first_dual_kernel,
-        [first_shape, rest_shape, longer_shape, longer_shape, scalars_shape],
+        [inner_shape, longer_shape, longer_shape, scalars_shape],
         edge, first_z, residual[1], solve, everyone, block, lift, live[1],
         for_next, for_prev, given,
+        scratch=[pltpu.VMEM(result_shape, jnp.float32)],
     )
     sums = from_all(sums)
+    sent = near, far
     near, far = swap(near, far)
-    (image_own, image_edge, *residual, first, rest, near, far, scalars_first, ends, outside_image,
-     outside) = call(
+    image_own, image_edge, *residual, near, far, scalars_first, ends, outside_image, outside = call(
         first_update_kernel,
-        [own_shape, face_shape] + edges_shapes + result_shapes
-        + [scalars_shape, (2,) + side_shape, outside_shape, outside_shape],
-        first, rest, near, far, *live, sums, *residual, dirichlet, ends,
-    )
-
+        [own_shape, face_shape] + edges_shapes
+        + [face_shape, face_shape, scalars_shape, (2,) + side_shape, outside_shape, outside_shape],
+        inner, near, far, *sent, *live, sums, *residual, dirichlet, ends,
+    )
+
+    def inside(residual, outside):
+        (values,) = call(early_corner_kernel, [(own, loads)], taken, ends, outside, *residual)
+        everyone = lax.all_gather(values, "grp", tiled=True)
+        (inner,) = call(inner_edges_kernel, [inner_shape], *residual, dirichlet, live[1])
+        result, partial = call(
+            inner_dual_kernel,
+            [result_shape, (2,) + face_shape],
+            inner, residual[1], solve, everyone, block, lift,
+        )
+        return result, inner, partial
+
+    sent = near, far
     near, far = swap(near, far)
-    (values,) = call(early_corner_kernel, [(own, loads)], taken, ends, outside, *residual)
-    everyone = lax.all_gather(values, "grp", tiled=True)
-    second_z, first, rest, near, far, sums = call(
-        functools.partial(dual_kernel, False),
-        [own_shape, first_shape, rest_shape, long_shape, long_shape, scalars_shape],
-        first, rest, near, far, *live, residual[1], solve, everyone, block, lift,
+    result, second_inner, partial = inside(residual, outside)
+    second_last, inner, near, far, sums = call(
+        functools.partial(outer_dual_kernel, False),
+        [face_shape, inner_shape, long_shape, long_shape, scalars_shape],
+        result, second_inner, partial, near, far, *sent, *live, residual[1], solve,
         for_next, for_prev,
     )
     sums = from_all(sums)
+    sent = near, far
     near, far = swap(near, far)
-    image_own, *residual, first, rest, near, far, scalars_second, outside = call(
+    image_own, *residual, near, far, scalars_second, outside = call(
         update_kernel,
-        [own_shape] + edges_shapes + result_shapes + [scalars_shape, outside_shape],
-        first, rest, near, far, *live, sums, scalars_first, image_edge, image_own, *residual,
+        [own_shape] + edges_shapes + [face_shape, face_shape, scalars_shape, outside_shape],
+        inner, near, far, *sent, *live, sums, scalars_first, image_edge, image_own, *residual,
         dirichlet, outside_image, outside,
     )
 
+    sent = near, far
     near, far = swap(near, far)
-    (values,) = call(early_corner_kernel, [(own, loads)], taken, ends, outside, *residual)
-    everyone = lax.all_gather(values, "grp", tiled=True)
-    third_z, first, rest, face, sums = call(
-        functools.partial(dual_kernel, True),
-        [own_shape, first_shape, rest_shape, face_shape, scalars_shape],
-        first, rest, near, far, *live, residual[1], solve, everyone, block, lift,
+    result, third_inner, partial = inside(residual, outside)
+    third_last, inner, to_next, to_prev, sums = call(
+        functools.partial(outer_dual_kernel, True),
+        [face_shape, inner_shape, face_shape, face_shape, scalars_shape],
+        result, third_inner, partial, near, far, *sent, *live, residual[1], solve,
     )
     sums = from_all(sums)
-    following = lax.ppermute(face, "sub", [(i + 1, i) for i in range(size - 1)])
+    following = lax.ppermute(to_prev, "sub", [(i + 1, i) for i in range(size - 1)])
     multipliers, residual = call(
         last_kernel,
         [own_shape] * 2,
-        first, rest, following, live[1], sums, scalars_second, scalars_first,
-        image_own, residual[1], first_z, second_z, third_z,
+        inner, to_next, following, live[1], sums, scalars_second, scalars_first,
+        image_own, residual[1], first_z, second_inner, second_last, third_inner, third_last,
     )
     return (multipliers[None], residual[None])
 

time: 130 us -> 127 us (0.977)
  waiting for transfers between devices: 16.8 us -> 12.2 us
  starting transfers between devices: 24.9 us -> 27 us
    all_gather x3 -> x1, blocking collectives: 20.8 us -> 6.96 us  [local(): everyone = lax.all_gather(values, 'grp', tiled=True)]
    all_gather x0 -> x2, blocking collectives: none -> 13.6 us  [inside(): everyone = lax.all_gather(values, 'grp', tiled=True)]
    ppermute x5, waiting for transfers between devices: 16.8 us -> 12.2 us  [swap(): lax.ppermute(near, 'sub', neighbour_pairs(size, 0))]
    ppermute x5, starting transfers between devices: 11.6 us -> 13.7 us  [swap(): lax.ppermute(near, 'sub', neighbour_pairs(size, 0))]
    pallas_call x13 -> x17, Pallas kernels: 17.6 us -> 17.9 us  [call(): pl.pallas_call(kernel, out_shape=[jax.ShapeDtypeStruct(*shape) for shape...]
  transfers between devices with their start and end apart: 18 -> 18, of which waited for: 3 -> 3; matrix products, arithmetic and copies ran while one was open for 0% -> 0% of each run, Pallas kernels for 4% -> 8%
where the time goes in v12:
time: 127 us; the launch traced here: 126 us
  blocking collectives  62.8 us (49%)
  starting transfers between devices  27 us (21%)
  Pallas kernels  19.7 us (16%)
  waiting for transfers between devices  12.2 us (10%)
  local copies, waits for them, and re-layouts  3.55 us (3%)
    all_to_all x3, blocking collectives, from_all(): return lax.all_to_all(copies, ('sub', 'grp'), 0, 0)  42.2 us
    pallas_call x17, Pallas kernels, call(): pl.pallas_call(kernel, out_shape=[jax.ShapeDtypeStruct(*shape) for shape...  17.9 us
    ppermute x5, starting transfers between devices, swap(): lax.ppermute(near, 'sub', neighbour_pairs(size, 0))  13.7 us
    all_gather x2, blocking collectives, inside(): everyone = lax.all_gather(values, 'grp', tiled=True)  13.6 us
    ppermute x5, waiting for transfers between devices, swap(): lax.ppermute(near, 'sub', neighbour_pairs(size, 0))  12.2 us
    all_gather x1, blocking collectives, local(): everyone = lax.all_gather(values, 'grp', tiled=True)  6.96 us
    ppermute x1, starting transfers between devices, local(): head = lax.ppermute(tail, 'sub', [(i, i + 1) for i in range(size - 1)])  4.86 us
    unnamed x16, local copies, waits for them, and re-layouts  3.49 us
  transfers between devices with their start and end apart: 18, of which 3 were waited for; matrix products, arithmetic and copies ran while one was open for 0% of the time, Pallas kernels for 8%

profile of v12, /device:TPU:0, one launch (start us, length us, event | category | flops | bytes accessed | tf_op | source)
XLA Modules:
  0.0 126.3 jit_solution(13334711728982872992)
XLA Ops:
  0.6 0.0 copy-start.6
  0.7 1.8 %shard_map.86 = f32[264,256]{1,0:T(8,128)} custom-call(s32[1,4]{1,0:T(1,128)} %counts, f32[1,4,256,256]{3,2,1,0:T(8,128)} %rhs.1), custom_call_target="tpu_custom_call" | custom-call | tf_op jit(solution)/shard_map/pallas_call | solution.py:570
  2.5 4.9 %collective-permute-start = (f32[264,256]{1,0:T(8,128)}, f32[264,256]{1,0:T(8,128)S(1)}, u32[]{:S(2)}, u32[]{:S(2)}) collective-permute-start(f32[264,256]{1,0:T(8,128)} %shard_map.86), channel_id=1, source_target_pairs={{0,4},{4,8},{8,12},{12,16},{16,20},{20,24},{24,28},{1,5},{5,9},{9,... | collective-permute-start | bytes 811016 | tf_op jit(solution)/shard_map/ppermute | solution.py:603
  7.3 0.7 collective-permute-start.3
  8.1 0.9 collective-permute-start.2
  9.0 0.3 collective-permute-start.1
  9.3 1.6 %copy-done = bf16[1,4,512,512]{3,2,1,0:T(8,128)(2,1)S(1)} copy-done((bf16[1,4,512,512]{3,2,1,0:T(8,128)(2,1)S(1)}, bf16[1,4,512,512]{3,2,1,0:T(8,128)(2,1)}, u32[]{:S(2)}) %copy-start) | copy-done | bytes 2097176
  10.9 1.2 copy-done.3
  12.1 0.7 copy-done.7
  12.7 1.2 shard_map.88
  13.9 0.0 collective-permute-done.3.refs_3_
  13.9 0.0 collective-permute-done.2.refs_2_
  14.0 0.0 collective-permute-done.1.refs_1_
  14.0 1.9 %shard_map.87 = (f32[128,512]{1,0:T(8,128)S(1)}, f32[128,512]{1,0:T(8,128)S(1)}, f32[128,512]{1,0:T(8,128)S(1)}, f32[128,512]{1,0:T(8,128)S(1)}, bf16[4,64,512]{...) custom-call(s32[4,32]{1,0:T(4,128)S(1)} %bitcast.29, s32[4,32]{1,0:T(4,128)S(1)} %collective-permute-done.1.refs_1_, ...), custom_call_target="tpu_custom_call" | custom-call | tf_op jit(solution)/shard_map/pallas_call | solution.py:35
  15.9 0.0 collective-permute-done.head
  15.9 0.0 copy-start.2
  15.9 0.3 shard_map.89
  16.3 1.6 %collective-permute-start.4 = (f32[288,256]{1,0:T(8,128)S(1)}, f32[288,256]{1,0:T(8,128)S(1)}, u32[]{:S(2)}, u32[]{:S(2)}) collective-permute-start(f32[288,256]{1,0:T(8,128)S(1)} %get-tuple-element.80), channel_id=1, source_target_pairs={{0,4},{4,0},{8,12},{12,8},{16,20},{20,16},{24,28},{28,24},{1,5},{5... | collective-permute-start | bytes 884744 | tf_op jit(solution)/shard_map/ppermute | solution.py:539
  17.9 0.7 collective-permute-start.5
  18.6 0.1 collective-permute-start.6
  18.6 1.6 %collective-permute-start.7 = (f32[128,512]{1,0:T(8,128)S(1)}, f32[128,512]{1,0:T(8,128)S(1)}, u32[]{:S(2)}, u32[]{:S(2)}) collective-permute-start(f32[128,512]{1,0:T(8,128)S(1)} %get-tuple-element.91), channel_id=1, source_target_pairs={{0,2},{1,3},{2,0},{3,1},{4,6},{5,7},{6,4},{7,5},{8,10},{9,11},{10,... | collective-permute-start | bytes 786440 | tf_op jit(solution)/shard_map/ppermute | solution.py:564
  20.2 0.3 collective-permute-start.8
  20.5 10.4 %collective-permute-done.4.near = f32[288,256]{1,0:T(8,128)S(1)} collective-permute-done((f32[288,256]{1,0:T(8,128)S(1)}, f32[288,256]{1,0:T(8,128)S(1)}, u32[]{:S(2)}, u32[]{:S(2)}) %collective-permute-start.4) | collective-permute-done | bytes 294944 | tf_op jit(solution)/shard_map/ppermute | solution.py:539
  30.9 0.0 collective-permute-done.5.far
  30.9 0.7 shard_map.90
  31.6 7.0 %all_gather.9.everyone = f32[512,256]{1,0:T(8,128)S(1)} all-gather(f32[128,256]{1,0:T(8,128)S(1)} %get-tuple-element.88), channel_id=1, replica_groups=mesh['sub'=8,'grp'=4] {'grp'}, dimensions={0}, use_global_device_ids=true | all-gather | bytes 655360 | tf_op jit(solution)/shard_map/all_gather | solution.py:642
  38.6 0.0 collective-permute-done.6
  38.6 0.0 collective-permute-done.7
  38.6 0.0 collective-permute-done.8
  38.6 0.1 reduce-precision_convert_fusion
  38.8 0.6 shard_map.91
  39.4 2.0 %shard_map.92 = (f32[3,256,256]{2,1,0:T(8,128)S(1)}, f32[352,256]{1,0:T(8,128)S(1)}, f32[352,256]{1,0:T(8,128)S(1)}, f32[2,256]{1,0:T(2,128)S(1)}) custom-call(f32[256,256]{1,0:T(8,128)S(1)} %get-tuple-element.85.edge, f32[4,256,256]{2,1,0:T(8,128)S(1)} %get-tuple-element.86.own.first_z, f32[4,256,256]{2,1,0:T(8,128)S(1)} %get-tuple-element.87.residual.residual_own, ...), custom_call_target="tpu_custom_call" | custom-call | tf_op jit(solution)/shard_map/pallas_call | solution.py:35
  41.4 2.5 %collective-permute-start.9 = (f32[352,256]{1,0:T(8,128)S(1)}, f32[352,256]{1,0:T(8,128)S(1)}, u32[]{:S(2)}, u32[]{:S(2)}) collective-permute-start(f32[352,256]{1,0:T(8,128)S(1)} %get-tuple-element.103.near_sent), channel_id=1, source_target_pairs={{0,4},{4,0},{8,12},{12,8},{16,20},{20,16},{24,28},{28,24},{1,5},{5... | collective-permute-start | bytes 1081352 | tf_op jit(solution)/shard_map/ppermute | solution.py:539
  43.9 0.7 collective-permute-start.10
  44.6 15.9 %all_to_all.15.sums = f32[32,2,256]{2,1,0:T(2,128)S(1)} all-to-all(f32[32,2,256]{2,1,0:T(2,128)S(1)} %broadcast_in_dim.10), channel_id=1, replica_groups=mesh['sub'=8,'grp'=4] {'sub','grp'}, dimensions={0} | all-to-all | bytes 131072 | tf_op jit(solution)/shard_map/all_to_all | solution.py:547
  60.5 0.0 collective-permute-done.9.near
  60.6 0.0 collective-permute-done.10.far
  60.6 0.8 shard_map.93
  61.3 3.3 %collective-permute-start.11 = (f32[256,256]{1,0:T(8,128)S(1)}, f32[256,256]{1,0:T(8,128)S(1)}, u32[]{:S(2)}, u32[]{:S(2)}) collective-permute-start(f32[256,256]{1,0:T(8,128)S(1)} %get-tuple-element.115.refs_5_), channel_id=1, source_target_pairs={{0,4},{4,0},{8,12},{12,8},{16,20},{20,16},{24,28},{28,24},{1,5},{5... | collective-permute-start | bytes 786440 | tf_op jit(solution)/shard_map/ppermute | solution.py:539
  64.6 0.7 collective-permute-start.12
  65.3 1.0 shard_map.94.inner.refs_1_.second_inner
  66.3 0.7 shard_map.95
  67.0 6.8 %all_gather.10.everyone = f32[512,256]{1,0:T(8,128)S(1)} all-gather(f32[128,256]{1,0:T(8,128)S(1)} %shard_map.95), channel_id=1, replica_groups=mesh['sub'=8,'grp'=4] {'grp'}, dimensions={0}, use_global_device_ids=true | all-gather | bytes 655360 | tf_op jit(solution)/shard_map/all_gather | solution.py:665
  73.8 1.4 %shard_map.96 = (f32[4,256,512]{2,1,0:T(8,128)S(1)}, f32[2,256,256]{2,1,0:T(8,128)S(1)}) custom-call(f32[3,256,256]{2,1,0:T(8,128)S(1)} %shard_map.94.inner.refs_1_.second_inner, f32[4,256,256]{2,1,0:T(8,128)S(1)} %get-tuple-element.109.own.residual.refs_9_.residual_own, bf16[4,512,512]{2,1,0:T(8,128)(2,1)S(1)} %bitcast.17, ...), custom_call_target="tpu_custom_call" | custom-call | tf_op jit(solution)/shard_map/pallas_call | solution.py:35
  75.2 0.9 collective-permute-done.11.refs_3_
  76.1 0.0 collective-permute-done.12.refs_4_
  76.1 0.9 shard_map.97
  77.0 3.1 %collective-permute-start.13 = (f32[288,256]{1,0:T(8,128)S(1)}, f32[288,256]{1,0:T(8,128)S(1)}, u32[]{:S(2)}, u32[]{:S(2)}) collective-permute-start(f32[288,256]{1,0:T(8,128)S(1)} %get-tuple-element.118.near_sent), channel_id=1, source_target_pairs={{0,4},{4,0},{8,12},{12,8},{16,20},{20,16},{24,28},{28,24},{1,5},{5... | collective-permute-start | bytes 884744 | tf_op jit(solution)/shard_map/ppermute | solution.py:539
  80.1 0.7 collective-permute-start.14
  80.8 13.1 %all_to_all.16.sums = f32[32,2,256]{2,1,0:T(2,128)S(1)} all-to-all(f32[32,2,256]{2,1,0:T(2,128)S(1)} %broadcast_in_dim.11), channel_id=1, replica_groups=mesh['sub'=8,'grp'=4] {'sub','grp'}, dimensions={0} | all-to-all | bytes 131072 | tf_op jit(solution)/shard_map/all_to_all | solution.py:547
  93.9 0.8 shard_map.98
  94.8 3.1 %collective-permute-start.15 = (f32[256,256]{1,0:T(8,128)S(1)}, f32[256,256]{1,0:T(8,128)S(1)}, u32[]{:S(2)}, u32[]{:S(2)}) collective-permute-start(f32[256,256]{1,0:T(8,128)S(1)} %get-tuple-element.130.refs_5_), channel_id=1, source_target_pairs={{0,4},{4,0},{8,12},{12,8},{16,20},{20,16},{24,28},{28,24},{1,5},{5... | collective-permute-start | bytes 786440 | tf_op jit(solution)/shard_map/ppermute | solution.py:539
  97.9 0.7 collective-permute-start.16
  98.6 1.0 shard_map.99.inner.refs_1_.third_inner
  99.6 0.7 shard_map.100
  100.3 6.8 %all_gather.11.everyone = f32[512,256]{1,0:T(8,128)S(1)} all-gather(f32[128,256]{1,0:T(8,128)S(1)} %shard_map.100), channel_id=1, replica_groups=mesh['sub'=8,'grp'=4] {'grp'}, dimensions={0}, use_global_device_ids=true | all-gather | bytes 655360 | tf_op jit(solution)/shard_map/all_gather | solution.py:665
  107.0 1.4 %shard_map.101 = (f32[4,256,512]{2,1,0:T(8,128)S(1)}, f32[2,256,256]{2,1,0:T(8,128)S(1)}) custom-call(f32[3,256,256]{2,1,0:T(8,128)S(1)} %shard_map.99.inner.refs_1_.third_inner, f32[4,256,256]{2,1,0:T(8,128)S(1)} %get-tuple-element.126.own.residual.refs_9_, bf16[4,512,512]{2,1,0:T(8,128)(2,1)S(1)} %bitcast.19, f32[512,256]{1,0:T(8,128)S(1)} %all_gather.11.everyone, ...), custom_call_target="tpu_custom_call" | custom-call | tf_op jit(solution)/shard_map/pallas_call | solution.py:35
  108.5 0.9 collective-permute-done.15.refs_3_
  109.4 0.0 collective-permute-done.16.refs_4_
  109.4 0.7 shard_map.102
  110.0 1.3 %collective-permute-start.17 = (f32[256,256]{1,0:T(8,128)S(1)}, f32[256,256]{1,0:T(8,128)S(1)}, u32[]{:S(2)}, u32[]{:S(2)}) collective-permute-start(f32[256,256]{1,0:T(8,128)S(1)} %get-tuple-element.134), channel_id=1, source_target_pairs={{4,0},{8,4},{12,8},{16,12},{20,16},{24,20},{28,24},{5,1},{9,5},{13... | collective-permute-start | bytes 786440 | tf_op jit(solution)/shard_map/ppermute | solution.py:702
  111.4 13.2 %all_to_all.17.sums = f32[32,2,256]{2,1,0:T(2,128)S(1)} all-to-all(f32[32,2,256]{2,1,0:T(2,128)S(1)} %broadcast_in_dim.12), channel_id=1, replica_groups=mesh['sub'=8,'grp'=4] {'sub','grp'}, dimensions={0} | all-to-all | bytes 131072 | tf_op jit(solution)/shard_map/all_to_all | solution.py:547
  124.6 0.0 collective-permute-done.17.following
  124.6 1.7 %shard_map.103 = (f32[4,256,256]{2,1,0:T(8,128)}, f32[4,256,256]{2,1,0:T(8,128)}) custom-call(f32[3,256,256]{2,1,0:T(8,128)S(1)} %get-tuple-element.132.inner, f32[256,256]{1,0:T(8,128)S(1)} %get-tuple-element.133.to_next, f32[256,256]{1,0:T(8,128)S(1)} %collective-permute-done.17.following, ...), custom_call_target="tpu_custom_call" | custom-call | tf_op jit(solution)/shard_map/pallas_call | solution.py:35
  (18 shorter events, 0.1 us)
Async XLA Ops:
  0.6 13.3 %copy-start.6 = (s32[1,4,32]{2,1,0:T(4,128)S(1)}, s32[1,4,32]{2,1,0:T(4,128)}, u32[]{:S(2)}) copy-start(s32[1,4,32]{2,1,0:T(4,128)} %param.12) | copy-start | bytes 1540
  0.6 13.3 %copy-start.5 = (f32[1,256,1024]{2,1,0:T(8,128)S(1)}, f32[1,256,1024]{2,1,0:T(8,128)}, u32[]{:S(2)}) copy-start(f32[1,256,1024]{2,1,0:T(8,128)} %param.13) | copy-start | bytes 3145732
  0.7 13.3 %copy-start.4 = (f32[1,4,32,512]{3,2,1,0:T(8,128)S(1)}, f32[1,4,32,512]{3,2,1,0:T(8,128)}, u32[]{:S(2)}) copy-start(f32[1,4,32,512]{3,2,1,0:T(8,128)} %param.11) | copy-start | bytes 786436
  2.5 13.4 %collective-permute-start = (f32[264,256]{1,0:T(8,128)}, f32[264,256]{1,0:T(8,128)S(1)}, u32[]{:S(2)}, u32[]{:S(2)}) collective-permute-start(f32[264,256]{1,0:T(8,128)} %shard_map.86), channel_id=1, source_target_pairs={{0,4},{4,8},{8,12},{12,16},{16,20},{20,24},{24,28},{1,5},{5,9},{9,... | collective-permute-start | bytes 811016 | tf_op jit(solution)/shard_map/ppermute | solution.py:603
  7.3 6.6 %collective-permute-start.3 = (s32[4,32]{1,0:T(4,128)}, s32[4,32]{1,0:T(4,128)S(1)}, u32[]{:S(2)}, u32[]{:S(2)}) collective-permute-start(s32[4,32]{1,0:T(4,128)} %bitcast.26), channel_id=1, source_target_pairs={{0,3},{1,2},{2,1},{3,0},{4,7},{5,6},{6,5},{7,4},{8,11},{9,10},{10,... | collective-permute-start | bytes 1544 | tf_op jit(solution)/shard_map/ppermute | solution.py:555
  8.1 5.9 %collective-permute-start.2 = (s32[4,32]{1,0:T(4,128)}, s32[4,32]{1,0:T(4,128)S(1)}, u32[]{:S(2)}, u32[]{:S(2)}) collective-permute-start(s32[4,32]{1,0:T(4,128)} %bitcast.27), channel_id=1, source_target_pairs={{0,2},{1,3},{2,0},{3,1},{4,6},{5,7},{6,4},{7,5},{8,10},{9,11},{10,... | collective-permute-start | bytes 1544 | tf_op jit(solution)/shard_map/ppermute | solution.py:555
  9.0 4.9 %collective-permute-start.1 = (s32[4,32]{1,0:T(4,128)}, s32[4,32]{1,0:T(4,128)S(1)}, u32[]{:S(2)}, u32[]{:S(2)}) collective-permute-start(s32[4,32]{1,0:T(4,128)} %bitcast.28), channel_id=1, source_target_pairs={{0,1},{1,0},{2,3},{3,2},{4,5},{5,4},{6,7},{7,6},{8,9},{9,8},{10,11... | collective-permute-start | bytes 1544 | tf_op jit(solution)/shard_map/ppermute | solution.py:555
  9.3 1.6 %copy-start = (bf16[1,4,512,512]{3,2,1,0:T(8,128)(2,1)S(1)}, bf16[1,4,512,512]{3,2,1,0:T(8,128)(2,1)}, u32[]{:S(2)}) copy-start(bf16[1,4,512,512]{3,2,1,0:T(8,128)(2,1)} %param.10) | copy-start | bytes 6291460
  10.9 1.2 copy-start.3
  12.1 0.7 copy-start.7
  12.7 3.2 %copy-start.1 = (bf16[1,4,512,512]{3,2,1,0:T(8,128)(2,1)S(1)}, bf16[1,4,512,512]{3,2,1,0:T(8,128)(2,1)}, u32[]{:S(2)}) copy-start(bf16[1,4,512,512]{3,2,1,0:T(8,128)(2,1)} %param.10) | copy-start | bytes 6291460
  15.9 14.9 %copy-start.2 = (bf16[1,4,512,512]{3,2,1,0:T(8,128)(2,1)S(1)}, bf16[1,4,512,512]{3,2,1,0:T(8,128)(2,1)}, u32[]{:S(2)}) copy-start(bf16[1,4,512,512]{3,2,1,0:T(8,128)(2,1)} %param.9) | copy-start | bytes 6291460
  16.3 14.6 %collective-permute-start.4 = (f32[288,256]{1,0:T(8,128)S(1)}, f32[288,256]{1,0:T(8,128)S(1)}, u32[]{:S(2)}, u32[]{:S(2)}) collective-permute-start(f32[288,256]{1,0:T(8,128)S(1)} %get-tuple-element.80), channel_id=1, source_target_pairs={{0,4},{4,0},{8,12},{12,8},{16,20},{20,16},{24,28},{28,24},{1,5},{5... | collective-permute-start | bytes 884744 | tf_op jit(solution)/shard_map/ppermute | solution.py:539
  17.9 13.0 %collective-permute-start.5 = (f32[288,256]{1,0:T(8,128)S(1)}, f32[288,256]{1,0:T(8,128)S(1)}, u32[]{:S(2)}, u32[]{:S(2)}) collective-permute-start(f32[288,256]{1,0:T(8,128)S(1)} %get-tuple-element.81), channel_id=1, source_target_pairs={{4,8},{8,4},{12,16},{16,12},{20,24},{24,20},{5,9},{9,5},{13,17},{1... | collective-permute-start | bytes 884744 | tf_op jit(solution)/shard_map/ppermute | solution.py:540
  18.6 20.0 %collective-permute-start.6 = (f32[128,512]{1,0:T(8,128)S(1)}, f32[128,512]{1,0:T(8,128)S(1)}, u32[]{:S(2)}, u32[]{:S(2)}) collective-permute-start(f32[128,512]{1,0:T(8,128)S(1)} %get-tuple-element.90), channel_id=1, source_target_pairs={{0,1},{1,0},{2,3},{3,2},{4,5},{5,4},{6,7},{7,6},{8,9},{9,8},{10,11... | collective-permute-start | bytes 786440 | tf_op jit(solution)/shard_map/ppermute | solution.py:564
  18.6 20.0 %collective-permute-start.7 = (f32[128,512]{1,0:T(8,128)S(1)}, f32[128,512]{1,0:T(8,128)S(1)}, u32[]{:S(2)}, u32[]{:S(2)}) collective-permute-start(f32[128,512]{1,0:T(8,128)S(1)} %get-tuple-element.91), channel_id=1, source_target_pairs={{0,2},{1,3},{2,0},{3,1},{4,6},{5,7},{6,4},{7,5},{8,10},{9,11},{10,... | collective-permute-start | bytes 786440 | tf_op jit(solution)/shard_map/ppermute | solution.py:564
  20.2 18.4 %collective-permute-start.8 = (f32[128,512]{1,0:T(8,128)S(1)}, f32[128,512]{1,0:T(8,128)S(1)}, u32[]{:S(2)}, u32[]{:S(2)}) collective-permute-start(f32[128,512]{1,0:T(8,128)S(1)} %get-tuple-element.92), channel_id=1, source_target_pairs={{0,3},{1,2},{2,1},{3,0},{4,7},{5,6},{6,5},{7,4},{8,11},{9,10},{10,... | collective-permute-start | bytes 786440 | tf_op jit(solution)/shard_map/ppermute | solution.py:564
  41.4 19.1 %collective-permute-start.9 = (f32[352,256]{1,0:T(8,128)S(1)}, f32[352,256]{1,0:T(8,128)S(1)}, u32[]{:S(2)}, u32[]{:S(2)}) collective-permute-start(f32[352,256]{1,0:T(8,128)S(1)} %get-tuple-element.103.near_sent), channel_id=1, source_target_pairs={{0,4},{4,0},{8,12},{12,8},{16,20},{20,16},{24,28},{28,24},{1,5},{5... | collective-permute-start | bytes 1081352 | tf_op jit(solution)/shard_map/ppermute | solution.py:539
  43.9 16.6 %collective-permute-start.10 = (f32[352,256]{1,0:T(8,128)S(1)}, f32[352,256]{1,0:T(8,128)S(1)}, u32[]{:S(2)}, u32[]{:S(2)}) collective-permute-start(f32[352,256]{1,0:T(8,128)S(1)} %get-tuple-element.104.far_sent), channel_id=1, source_target_pairs={{4,8},{8,4},{12,16},{16,12},{20,24},{24,20},{5,9},{9,5},{13,17},{1... | collective-permute-start | bytes 1081352 | tf_op jit(solution)/shard_map/ppermute | solution.py:540
  61.3 14.8 %collective-permute-start.11 = (f32[256,256]{1,0:T(8,128)S(1)}, f32[256,256]{1,0:T(8,128)S(1)}, u32[]{:S(2)}, u32[]{:S(2)}) collective-permute-start(f32[256,256]{1,0:T(8,128)S(1)} %get-tuple-element.115.refs_5_), channel_id=1, source_target_pairs={{0,4},{4,0},{8,12},{12,8},{16,20},{20,16},{24,28},{28,24},{1,5},{5... | collective-permute-start | bytes 786440 | tf_op jit(solution)/shard_map/ppermute | solution.py:539
  64.6 11.5 %collective-permute-start.12 = (f32[256,256]{1,0:T(8,128)S(1)}, f32[256,256]{1,0:T(8,128)S(1)}, u32[]{:S(2)}, u32[]{:S(2)}) collective-permute-start(f32[256,256]{1,0:T(8,128)S(1)} %get-tuple-element.116.refs_6_), channel_id=1, source_target_pairs={{4,8},{8,4},{12,16},{16,12},{20,24},{24,20},{5,9},{9,5},{13,17},{1... | collective-permute-start | bytes 786440 | tf_op jit(solution)/shard_map/ppermute | solution.py:540
  77.0 17.0 %collective-permute-start.13 = (f32[288,256]{1,0:T(8,128)S(1)}, f32[288,256]{1,0:T(8,128)S(1)}, u32[]{:S(2)}, u32[]{:S(2)}) collective-permute-start(f32[288,256]{1,0:T(8,128)S(1)} %get-tuple-element.118.near_sent), channel_id=1, source_target_pairs={{0,4},{4,0},{8,12},{12,8},{16,20},{20,16},{24,28},{28,24},{1,5},{5... | collective-permute-start | bytes 884744 | tf_op jit(solution)/shard_map/ppermute | solution.py:539
  80.1 13.8 %collective-permute-start.14 = (f32[288,256]{1,0:T(8,128)S(1)}, f32[288,256]{1,0:T(8,128)S(1)}, u32[]{:S(2)}, u32[]{:S(2)}) collective-permute-start(f32[288,256]{1,0:T(8,128)S(1)} %get-tuple-element.119.far_sent), channel_id=1, source_target_pairs={{4,8},{8,4},{12,16},{16,12},{20,24},{24,20},{5,9},{9,5},{13,17},{1... | collective-permute-start | bytes 884744 | tf_op jit(solution)/shard_map/ppermute | solution.py:540
  94.8 14.6 %collective-permute-start.15 = (f32[256,256]{1,0:T(8,128)S(1)}, f32[256,256]{1,0:T(8,128)S(1)}, u32[]{:S(2)}, u32[]{:S(2)}) collective-permute-start(f32[256,256]{1,0:T(8,128)S(1)} %get-tuple-element.130.refs_5_), channel_id=1, source_target_pairs={{0,4},{4,0},{8,12},{12,8},{16,20},{20,16},{24,28},{28,24},{1,5},{5... | collective-permute-start | bytes 786440 | tf_op jit(solution)/shard_map/ppermute | solution.py:539
  97.9 11.5 %collective-permute-start.16 = (f32[256,256]{1,0:T(8,128)S(1)}, f32[256,256]{1,0:T(8,128)S(1)}, u32[]{:S(2)}, u32[]{:S(2)}) collective-permute-start(f32[256,256]{1,0:T(8,128)S(1)} %get-tuple-element.131.refs_6_), channel_id=1, source_target_pairs={{4,8},{8,4},{12,16},{16,12},{20,24},{24,20},{5,9},{9,5},{13,17},{1... | collective-permute-start | bytes 786440 | tf_op jit(solution)/shard_map/ppermute | solution.py:540
  110.0 14.5 %collective-permute-start.17 = (f32[256,256]{1,0:T(8,128)S(1)}, f32[256,256]{1,0:T(8,128)S(1)}, u32[]{:S(2)}, u32[]{:S(2)}) collective-permute-start(f32[256,256]{1,0:T(8,128)S(1)} %get-tuple-element.134), channel_id=1, source_target_pairs={{4,0},{8,4},{12,8},{16,12},{20,16},{24,20},{28,24},{5,1},{9,5},{13... | collective-permute-start | bytes 786440 | tf_op jit(solution)/shard_map/ppermute | solution.py:702

commit v13 on v12

--- a/solution.py
+++ b/solution.py
@@ -56,19 +56,6 @@
             self.rest[place - 1] = value
 
 
-def jump_edge(even, result, near, far, live, edge, subs):
-    loads, width = result[0].shape[0], near.shape[1]
-    if edge == 0:
-        right = jnp.where(even, far[:loads], near[:loads])
-    else:
-        right = result[edge - 1][:, width:]
-    if edge == subs:
-        left = jnp.where(even, near[:loads], far[:loads])
-    else:
-        left = result[edge][:, :width]
-    return live[edge] * (right - left)
-
-
 def outer_rows(operator, edge):
     rows = operator.shape[0] // 2
     high, low = split(edge)
@@ -83,22 +70,6 @@
         near_out[rows, :] = jnp.where(even, ahead, behind)
         far_out[rows, :] = jnp.where(even, behind, ahead)
         row += ahead.shape[0]
-
-
-def send_faces(even, first, last, near_out, far_out):
-    width = first.shape[1] // 2
-    send(even, [last[:, width:]], [first[:, :width]], near_out, far_out)
-
-
-def panel_products(parts, panel, result, extra=None):
-    subs = panel.shape[0]
-    for sub in range(subs):
-        high = jnp.concatenate([-parts[sub][0], parts[sub + 1][0]], axis=1)
-        low = jnp.concatenate([-parts[sub][1], parts[sub + 1][1]], axis=1)
-        total = mul(high, panel[sub]) + mul(low, panel[sub])
-        if extra is not None:
-            total = total + extra(sub)
-        result[sub] = total
 
 
 def column(row, width):
@@ -145,30 +116,31 @@
     tail[:loads] = mask[:1] * face[...]
 
 
-def early_kernel(counts, rhs, panel, live, own, partial, rest):
+def early_kernel(counts, rhs, panel, live, own, to_next, partial):
     subs, loads, width = own.shape
-    parts = [None]
+    parts = []
     for sub in range(subs):
         mask = live_rows(counts, sub, 1, width)
         live[sub] = mask
         own[sub] = mask * rhs[sub]
         parts.append(split(own[sub]))
-    partial[...] = mul(parts[1][0], panel[0, width:]) + mul(parts[1][1], panel[0, width:])
-    for sub in range(1, subs):
-        high = jnp.concatenate([-parts[sub][0], parts[sub + 1][0]], axis=1)
-        low = jnp.concatenate([-parts[sub][1], parts[sub + 1][1]], axis=1)
-        rest[sub - 1] = mul(high, panel[sub]) + mul(low, panel[sub])
-
-
-def head_kernel(head, partial, rest, panel, coupling, live, edge, first, near_out, far_out):
+    high = jnp.concatenate([-parts[subs - 2][0], parts[subs - 1][0]], axis=1)
+    low = jnp.concatenate([-parts[subs - 2][1], parts[subs - 1][1]], axis=1)
+    to_next[...] = mul(high, panel[subs - 1, :, width:]) + mul(low, panel[subs - 1, :, width:])
+    high, low = parts[0]
+    partial[...] = mul(high, panel[0, width:, :width]) + mul(low, panel[0, width:, :width])
+
+
+def head_kernel(head, to_next, partial, panel, coupling, live, edge, near_out, far_out):
     loads, width = edge.shape
     live[...] = head[loads : loads + 1]
     edge[...] = head[:loads]
     high, low = split(head[:loads])
-    first[...] = partial[...] - mul(high, panel[0, :width]) - mul(low, panel[0, :width])
-    last = rest[rest.shape[0] - 1]
-    to_next = [last[:, width:], coupling[coupling.shape[0] - 1, :, width:]]
-    send(even_place(), to_next, [first[:, :width], coupling[0, :, :width]], near_out, far_out)
+    to_prev = partial[...] - (
+        mul(high, panel[0, :width, :width]) + mul(low, panel[0, :width, :width])
+    )
+    ahead = [to_next[...], coupling[coupling.shape[0] - 1, :, width:]]
+    send(even_place(), ahead, [to_prev, coupling[0, :, :width]], near_out, far_out)
 
 
 def setup_kernel(*refs):
@@ -203,44 +175,58 @@
         ) + lax.dot_general(chosen, low, dims, preferred_element_type=jnp.float32)
 
 
-def corner_kernel(first, rest, near, far, live_first, live_rest, coupling, _solve,
-                  edge, own, corners):
-    even = even_place()
+def start_kernel(inner, panel, coupling, result, corners):
     subs, rows = coupling.shape[0], coupling.shape[1] // 2
-    result, live, edges = Joined(first, rest), Joined(live_first, live_rest), Joined(edge, own)
-    parts = []
-    for place in range(subs + 1):
-        edges[place] = 0.25 * jump_edge(even, result, near, far, live, place, subs)
-        parts.append(split(edges[place]))
+    width = inner.shape[2]
+    parts = [split(inner[place]) for place in range(subs - 1)]
+    high, low = parts[0]
+    result[0] = mul(high, panel[0, width:]) + mul(low, panel[0, width:])
+    for sub in range(1, subs - 1):
+        high = jnp.concatenate([-parts[sub - 1][0], parts[sub][0]], axis=1)
+        low = jnp.concatenate([-parts[sub - 1][1], parts[sub][1]], axis=1)
+        result[sub] = mul(high, panel[sub]) + mul(low, panel[sub])
+    high, low = parts[subs - 2]
+    result[subs - 1] = -(mul(high, panel[subs - 1, :width]) + mul(low, panel[subs - 1, :width]))
     for sub in range(subs):
-        high = jnp.concatenate([-parts[sub][0], parts[sub + 1][0]], axis=1)
-        low = jnp.concatenate([-parts[sub][1], parts[sub + 1][1]], axis=1)
-        both = mul_rows(coupling[sub], high)
-        corners[sub * rows : (sub + 1) * rows, :] = (
-            both[:rows] + both[rows:] + mul_rows(coupling[sub, :rows], low)
-        )
-
-
-def operators_kernel(coupling, live_edge, live_own, near, far, panel,
-                     taken, ends, for_next, for_prev, given):
-    even = even_place()
+        values = jnp.zeros((rows, inner.shape[1]), jnp.float32)
+        if sub > 0:
+            values = values - outer_rows(coupling[sub, :, :width], inner[sub - 1])
+        if sub + 1 < subs:
+            values = values + outer_rows(coupling[sub, :, width:], inner[sub])
+        corners[sub * rows : (sub + 1) * rows, :] = values
+
+
+def corner_kernel(near, far, near_sent, far_sent, live_edge, live_own, coupling, partial,
+                  edge, last, corners):
+    subs, rows = coupling.shape[0], coupling.shape[1] // 2
+    loads, width = edge.shape
+    first_value, last_value = cut_edges(even_place(), loads, near, far, near_sent, far_sent,
+                                        0.25 * live_edge[...], 0.25 * live_own[subs - 1])
+    edge[...] = first_value
+    last[...] = last_value
+    corners[...] = partial[...]
+    corners[:rows, :] = partial[:rows, :] - outer_rows(coupling[0, :, :width], first_value)
+    corners[-rows:, :] = partial[-rows:, :] + outer_rows(
+        coupling[subs - 1, :, width:], last_value
+    )
+
+
+def operators_kernel(coupling, live_edge, live_own, panel, taken, ends):
     subs, rows = coupling.shape[0], coupling.shape[1]
     width = coupling.shape[2] // 2
     live = Joined(live_edge, live_own)
-    sides = received(even, near, far, near.shape[0] - rows, rows)
-    before, after = sides[:rows], sides[rows:]
     left = [coupling[sub, :, :width] * (0.25 * live[sub]) for sub in range(subs)]
-    left.append(after * (0.25 * live[subs]))
-    right = [before * (0.25 * live[0])]
-    right += [coupling[sub, :, width:] * (0.25 * live[sub + 1]) for sub in range(subs)]
+    right = [coupling[sub, :, width:] * (0.25 * live[sub + 1]) for sub in range(subs)]
     none = jnp.zeros((rows, width), jnp.float32)
     inner, ahead, behind = [], [], []
     for sub in range(subs):
+        above = left[sub + 1] if sub + 1 < subs else none
+        below = right[sub - 1] if sub > 0 else none
         factors = jnp.concatenate(
             [
-                jnp.concatenate([left[sub], right[sub + 1]], axis=1),
-                jnp.concatenate([none, left[sub + 1]], axis=1),
-                jnp.concatenate([right[sub], none], axis=1),
+                jnp.concatenate([left[sub], right[sub]], axis=1),
+                jnp.concatenate([none, above], axis=1),
+                jnp.concatenate([below, none], axis=1),
             ],
             axis=0,
         )
@@ -269,10 +255,6 @@
         high, low = split(jnp.concatenate(blocks, axis=1))
         taken[sub * rows : (sub + 1) * rows, :] = high
         taken[total + sub * rows : total + (sub + 1) * rows, :] = low
-    for_next[...] = jnp.concatenate(split(ahead[subs - 1][:, :width]), axis=0)
-    for_prev[...] = jnp.concatenate(split(-behind[0][:, width:]), axis=0)
-    given[0] = -ahead[subs - 1][:, width:]
-    given[1] = behind[0][:, :width]
 
 
 def early_corner_kernel(taken, ends, outside, edge, own, corners):
@@ -336,15 +318,37 @@
         inner[place] = live_own[place] * (result[place][:, width:] - result[place + 1][:, :width])
 
 
-def first_dual_kernel(edge, own, residual, panel, everyone, block, lift, live_own,
-                      for_next, for_prev, given, inner, near_out, far_out, sums, result):
-    subs, width = panel.shape[0], edge.shape[1]
-    edges = Joined(edge, own)
-    parts = [split(edges[place]) for place in range(subs + 1)]
-    panel_products(parts, panel, result, coarse_lift(everyone, block, lift))
+def first_dual_kernel(before, inner_z, edge, last_z, residual, panel, everyone, block, lift,
+                      near, far, live_edge, live_own, preconditioner,
+                      inner, near_out, far_out, sums, for_next, for_prev, result):
+    even = even_place()
+    subs, (loads, width) = panel.shape[0], edge.shape
+    rows = for_next.shape[0] // 2
+    sides = received(even, near, far, loads, rows)
+    after = sides[rows:] * (0.25 * live_own[subs - 1])
+    behind = sides[:rows] * (0.25 * live_edge[...])
+    both = mul(jnp.concatenate(split(after), axis=0), preconditioner[subs - 1, width:])
+    after = both[:rows] + both[rows:]
+    both = mul(jnp.concatenate(split(behind), axis=0), preconditioner[0, :width])
+    behind = both[:rows] + both[rows:]
+    for_next[...] = jnp.concatenate(split(after[:, :width]), axis=0)
+    for_prev[...] = jnp.concatenate(split(-behind[:, width:]), axis=0)
+    given = [-after[:, width:], behind[:, :width]]
+
+    lifted = coarse_lift(everyone, block, lift)
+    for sub in range(subs):
+        value = before[sub] + lifted(sub)
+        if sub == 0:
+            high, low = split(edge[...])
+            value = value - (mul(high, panel[0, :width]) + mul(low, panel[0, :width]))
+        if sub == subs - 1:
+            high, low = split(last_z[...])
+            value = value + (mul(high, panel[sub, width:]) + mul(low, panel[sub, width:]))
+        result[sub] = value
     inner_jump(result, live_own, inner)
     faces = [result[subs - 1][:, width:], result[0][:, :width]]
-    send_dual(even_place(), inner, faces, for_next, for_prev, near_out, far_out, residual, given)
+    send_dual(even, inner, faces, for_next, for_prev, near_out, far_out, residual, given)
+    edges = [edge[...]] + [inner_z[place] for place in range(subs - 1)] + [last_z[...]]
     product = curvature = 0.0
     for sub in range(subs):
         product = product + residual[sub] * edges[sub + 1]
@@ -506,7 +510,7 @@
 
 
 def last_kernel(inner, to_next, following, live, sums, before, older, image_old,
-                residual, first_z, second_inner, second_last, third_inner, third_last,
+                residual, first_inner, first_last, second_inner, second_last, third_inner, third_last,
                 multipliers, residual_new):
     subs, width = residual.shape[0], following.shape[1]
     rz_now, alpha, beta = step_scalars(2, sums, before)
@@ -518,13 +522,14 @@
     for sub in range(subs):
         if sub == subs - 1:
             image = live[sub] * (to_next[...] - following[...])
-            second_z, third_z = second_last[...], third_last[...]
+            first_z, second_z, third_z = first_last[...], second_last[...], third_last[...]
         else:
-            image, second_z, third_z = inner[sub], second_inner[sub], third_inner[sub]
+            image = inner[sub]
+            first_z, second_z, third_z = first_inner[sub], second_inner[sub], third_inner[sub]
         image = image + beta_column * image_old[sub]
         residual_new[sub] = residual[sub] - alpha_column * image
         multipliers[sub] = (
-            first_column * first_z[sub] + second_column * second_z + alpha_column * third_z
+            first_column * first_z + second_column * second_z + alpha_column * third_z
         )
 
 
@@ -592,19 +597,17 @@
     size = lax.axis_size("sub")
 
     face_shape, own_shape = (loads, width), (subs, loads, width)
-    first_shape, rest_shape = (loads, 2 * width), (subs - 1, loads, 2 * width)
     scalars_shape, outside_shape, side_shape = (2, loads), (2 * corners, loads), (corners, width)
     long_shape, longer_shape = (loads + corners, width), (loads + 3 * corners, width)
     edges_shapes = [face_shape, own_shape]
-    result_shapes = [first_shape, rest_shape, face_shape, face_shape]
 
     tail = make_tail(counts, rhs)
     tail, counts, corner_map = lax.optimization_barrier((tail, counts, corner_map))
     head = lax.ppermute(tail, "sub", [(i, i + 1) for i in range(size - 1)])
     maps = from_group(corner_map[0])
-    live_own, residual_own, partial, rest = call(
+    live_own, residual_own, to_next, partial = call(
         early_kernel,
-        [(subs, 1, width), own_shape, first_shape, rest_shape],
+        [(subs, 1, width), own_shape, face_shape, face_shape],
         counts, rhs[0], dirichlet,
     )
     group, own = len(maps), subs * corners
@@ -618,36 +621,43 @@
         scratch=[pltpu.VMEM((group, 1, own), jnp.int32)],
     )
     head, stacked = lax.optimization_barrier((head, stacked))
-    live_edge, residual_edge, first, near, far = call(
+    live_edge, residual_edge, near, far = call(
         head_kernel,
-        [(1, width), face_shape, first_shape, long_shape, long_shape],
-        head, partial, rest, dirichlet, coupling[0],
-    )
+        [(1, width), face_shape, long_shape, long_shape],
+        head, to_next, partial, dirichlet, coupling[0],
+    )
+    live, residual = (live_edge, live_own), (residual_edge, residual_own)
+    sent = near, far
     near, far = swap(near, far)
     blocks = swap_blocks(picked)
-    live, residual = (live_edge, live_own), (residual_edge, residual_own)
-    taken, ends, for_next, for_prev, given = call(
+    inner_shape, result_shape = (subs - 1, loads, width), (subs, loads, 2 * width)
+    (first_inner,) = call(inner_edges_kernel, [inner_shape], *residual, dirichlet, live[1])
+    result, partial = call(
+        start_kernel, [result_shape, (own, loads)], first_inner, solve, stacked
+    )
+    taken, ends = call(
         operators_kernel,
-        [(2 * own, (subs + 1) * width), (2,) + side_shape, (2 * corners, width),
-         (2 * corners, width), (2,) + side_shape],
-        coupling[0], *live, near, far, dirichlet,
-        kinds=[jnp.bfloat16, jnp.float32, jnp.bfloat16, jnp.bfloat16, jnp.float32],
-    )
-
-    edge, first_z, values = call(
+        [(2 * own, (subs + 1) * width), (2,) + side_shape],
+        coupling[0], *live, dirichlet,
+        kinds=[jnp.bfloat16, jnp.float32],
+    )
+    partial, taken, ends = lax.optimization_barrier((partial, taken, ends))
+
+    edge, first_last, values = call(
         corner_kernel,
-        edges_shapes + [(own, loads)],
-        first, rest, near, far, *live, stacked, solve,
+        [face_shape, face_shape, (own, loads)],
+        near, far, *sent, *live, stacked, partial,
     )
     everyone = lax.all_gather(values, "grp", tiled=True)
     everyone, blocks = lax.optimization_barrier((everyone, blocks))
     block = jnp.concatenate(split_outside(sum(blocks[1:], blocks[0])), axis=0)
-    inner_shape, result_shape = (subs - 1, loads, width), (subs, loads, 2 * width)
-    inner, near, far, sums = call(
+    inner, near, far, sums, for_next, for_prev = call(
         first_dual_kernel,
-        [inner_shape, longer_shape, longer_shape, scalars_shape],
-        edge, first_z, residual[1], solve, everyone, block, lift, live[1],
-        for_next, for_prev, given,
+        [inner_shape, longer_shape, longer_shape, scalars_shape]
+        + [(2 * corners, width), (2 * corners, width)],
+        result, first_inner, edge, first_last, residual[1], solve, everyone, block, lift,
+        near, far, *live, dirichlet,
+        kinds=[jnp.float32] * 4 + [jnp.bfloat16] * 2,
         scratch=[pltpu.VMEM(result_shape, jnp.float32)],
     )
     sums = from_all(sums)
@@ -704,7 +714,7 @@
         last_kernel,
         [own_shape] * 2,
         inner, to_next, following, live[1], sums, scalars_second, scalars_first,
-        image_own, residual[1], first_z, second_inner, second_last, third_inner, third_last,
+        image_own, residual[1], first_inner, first_last, second_inner, second_last, third_inner, third_last,
     )
     return (multipliers[None], residual[None])
 

time: 127 us -> 126 us (level)
  waiting for transfers between devices: 12.2 us -> 8.17 us
  Pallas kernels: 19.7 us -> 21.1 us
    ppermute x5, waiting for transfers between devices: 12.2 us -> 8.13 us  [swap(): lax.ppermute(near, 'sub', neighbour_pairs(size, 0))]
    pallas_call x17 -> x19, Pallas kernels: 17.9 us -> 19.3 us  [call(): pl.pallas_call(kernel, out_shape=[jax.ShapeDtypeStruct(*shape) for shape...]
  transfers between devices with their start and end apart: 18 -> 18, of which waited for: 3 -> 3; matrix products, arithmetic and copies ran while one was open for 0% -> 0% of each run, Pallas kernels for 8% -> 10%
where the time goes in v13:
time: 126 us; the launch traced here: 125 us
  blocking collectives  63 us (50%)
  starting transfers between devices  27.8 us (22%)
  Pallas kernels  21.1 us (17%)
  waiting for transfers between devices  8.17 us (6%)
  local copies, waits for them, and re-layouts  4.09 us (3%)
    all_to_all x3, blocking collectives, from_all(): return lax.all_to_all(copies, ('sub', 'grp'), 0, 0)  42.3 us
    pallas_call x19, Pallas kernels, call(): pl.pallas_call(kernel, out_shape=[jax.ShapeDtypeStruct(*shape) for shape...  19.3 us
    ppermute x5, starting transfers between devices, swap(): lax.ppermute(near, 'sub', neighbour_pairs(size, 0))  14.4 us
    all_gather x2, blocking collectives, inside(): everyone = lax.all_gather(values, 'grp', tiled=True)  13.7 us
    ppermute x5, waiting for transfers between devices, swap(): lax.ppermute(near, 'sub', neighbour_pairs(size, 0))  8.13 us
    all_gather x1, blocking collectives, local(): everyone = lax.all_gather(values, 'grp', tiled=True)  6.96 us
    ppermute x1, starting transfers between devices, local(): head = lax.ppermute(tail, 'sub', [(i, i + 1) for i in range(size - 1)])  4.86 us
    unnamed x16, local copies, waits for them, and re-layouts  4.04 us
  transfers between devices with their start and end apart: 18, of which 3 were waited for; matrix products, arithmetic and copies ran while one was open for 0% of the time, Pallas kernels for 10%

profile of v13, /device:TPU:0, one launch (start us, length us, event | category | flops | bytes accessed | tf_op | source)
XLA Modules:
  0.0 125.2 jit_solution(15739770457681287108)
XLA Ops:
  0.6 0.0 copy-start.6
  0.7 1.8 %shard_map.86 = f32[264,256]{1,0:T(8,128)} custom-call(s32[1,4]{1,0:T(1,128)} %counts, f32[1,4,256,256]{3,2,1,0:T(8,128)} %rhs.1), custom_call_target="tpu_custom_call" | custom-call | tf_op jit(solution)/shard_map/pallas_call | solution.py:575
  2.5 4.9 %collective-permute-start = (f32[264,256]{1,0:T(8,128)}, f32[264,256]{1,0:T(8,128)S(1)}, u32[]{:S(2)}, u32[]{:S(2)}) collective-permute-start(f32[264,256]{1,0:T(8,128)} %shard_map.86), channel_id=1, source_target_pairs={{0,4},{4,8},{8,12},{12,16},{16,20},{20,24},{24,28},{1,5},{5,9},{9,... | collective-permute-start | bytes 811016 | tf_op jit(solution)/shard_map/ppermute | solution.py:606
  7.3 0.7 collective-permute-start.3
  8.1 0.9 collective-permute-start.2
  9.0 0.3 collective-permute-start.1
  9.3 1.6 %copy-done = bf16[1,4,512,512]{3,2,1,0:T(8,128)(2,1)S(1)} copy-done((bf16[1,4,512,512]{3,2,1,0:T(8,128)(2,1)S(1)}, bf16[1,4,512,512]{3,2,1,0:T(8,128)(2,1)}, u32[]{:S(2)}) %copy-start) | copy-done | bytes 2097176
  10.9 1.2 copy-done.3
  12.1 0.7 copy-done.7
  12.7 0.4 shard_map.88
  13.2 0.0 collective-permute-done.3.refs_3_
  13.2 0.0 collective-permute-done.2.refs_2_
  13.2 1.9 %shard_map.87 = (f32[128,512]{1,0:T(8,128)S(1)}, f32[128,512]{1,0:T(8,128)S(1)}, f32[128,512]{1,0:T(8,128)S(1)}, f32[128,512]{1,0:T(8,128)S(1)}, bf16[4,64,512]{...) custom-call(s32[4,32]{1,0:T(4,128)S(1)} %bitcast.31, s32[4,32]{1,0:T(4,128)S(1)} %collective-permute-done.1.refs_1_, ...), custom_call_target="tpu_custom_call" | custom-call | tf_op jit(solution)/shard_map/pallas_call | solution.py:35
  15.2 0.0 collective-permute-done.head
  15.2 0.2 shard_map.89
  15.4 1.6 %collective-permute-start.4 = (f32[288,256]{1,0:T(8,128)S(1)}, f32[288,256]{1,0:T(8,128)S(1)}, u32[]{:S(2)}, u32[]{:S(2)}) collective-permute-start(f32[288,256]{1,0:T(8,128)S(1)} %get-tuple-element.87.near_sent), channel_id=1, source_target_pairs={{0,4},{4,0},{8,12},{12,8},{16,20},{20,16},{24,28},{28,24},{1,5},{5... | collective-permute-start | bytes 884744 | tf_op jit(solution)/shard_map/ppermute | solution.py:544
  17.0 0.7 collective-permute-start.5
  17.7 0.1 collective-permute-start.6
  17.8 1.6 %collective-permute-start.7 = (f32[128,512]{1,0:T(8,128)S(1)}, f32[128,512]{1,0:T(8,128)S(1)}, u32[]{:S(2)}, u32[]{:S(2)}) collective-permute-start(f32[128,512]{1,0:T(8,128)S(1)} %get-tuple-element.99), channel_id=1, source_target_pairs={{0,2},{1,3},{2,0},{3,1},{4,6},{5,7},{6,4},{7,5},{8,10},{9,11},{10,... | collective-permute-start | bytes 786440 | tf_op jit(solution)/shard_map/ppermute | solution.py:569
  19.4 0.3 collective-permute-start.8
  19.7 0.6 shard_map.92
  20.2 0.0 copy-start.2
  20.3 1.0 shard_map.90.inner.inner_z.first_inner
  21.3 0.5 copy-done.2
  21.8 1.4 %shard_map.91 = (f32[4,256,512]{2,1,0:T(8,128)S(1)}, f32[128,256]{1,0:T(8,128)S(1)}) custom-call(f32[3,256,256]{2,1,0:T(8,128)S(1)} %shard_map.90.inner.inner_z.first_inner, bf16[4,512,512]{2,1,0:T(8,128)(2,1)S(1)} %bitcast.17, bf16[4,64,512]{2,1,0:T(8,128)(2,1)S(1)} %get-tuple-element.85.coupling), custom_call_target="tpu_custom_call" | custom-call | tf_op jit(solution)/shard_map/pallas_call | solution.py:35
  23.2 6.8 %collective-permute-done.4.near = f32[288,256]{1,0:T(8,128)S(1)} collective-permute-done((f32[288,256]{1,0:T(8,128)S(1)}, f32[288,256]{1,0:T(8,128)S(1)}, u32[]{:S(2)}, u32[]{:S(2)}) %collective-permute-start.4) | collective-permute-done | bytes 294944 | tf_op jit(solution)/shard_map/ppermute | solution.py:544
  30.0 0.0 collective-permute-done.5.far
  30.0 0.3 shard_map.93
  30.3 7.0 %all_gather.9.everyone = f32[512,256]{1,0:T(8,128)S(1)} all-gather(f32[128,256]{1,0:T(8,128)S(1)} %get-tuple-element.96), channel_id=1, replica_groups=mesh['sub'=8,'grp'=4] {'grp'}, dimensions={0}, use_global_device_ids=true | all-gather | bytes 655360 | tf_op jit(solution)/shard_map/all_gather | solution.py:651
  37.3 0.0 collective-permute-done.6
  37.3 0.0 collective-permute-done.7
  37.3 0.0 collective-permute-done.8
  37.3 0.1 reduce-precision_convert_fusion
  37.5 2.0 %shard_map.94 = (f32[3,256,256]{2,1,0:T(8,128)S(1)}, f32[352,256]{1,0:T(8,128)S(1)}, f32[352,256]{1,0:T(8,128)S(1)}, f32[2,256]{1,0:T(2,128)S(1)}, bf16[64,256]{...) custom-call(f32[4,256,512]{2,1,0:T(8,128)S(1)} %get-tuple-element.86.before, ...), custom_call_target="tpu_custom_call" | custom-call | tf_op jit(solution)/shard_map/pallas_call | solution.py:35
  39.5 2.8 %collective-permute-start.9 = (f32[352,256]{1,0:T(8,128)S(1)}, f32[352,256]{1,0:T(8,128)S(1)}, u32[]{:S(2)}, u32[]{:S(2)}) collective-permute-start(f32[352,256]{1,0:T(8,128)S(1)} %get-tuple-element.108.near_sent), channel_id=1, source_target_pairs={{0,4},{4,0},{8,12},{12,8},{16,20},{20,16},{24,28},{28,24},{1,5},{5... | collective-permute-start | bytes 1081352 | tf_op jit(solution)/shard_map/ppermute | solution.py:544
  42.2 0.7 collective-permute-start.10
  42.9 15.9 %all_to_all.15.sums = f32[32,2,256]{2,1,0:T(2,128)S(1)} all-to-all(f32[32,2,256]{2,1,0:T(2,128)S(1)} %broadcast_in_dim.10), channel_id=1, replica_groups=mesh['sub'=8,'grp'=4] {'sub','grp'}, dimensions={0} | all-to-all | bytes 131072 | tf_op jit(solution)/shard_map/all_to_all | solution.py:552
  58.8 0.0 collective-permute-done.9.near
  58.8 0.0 collective-permute-done.10.far
  58.8 0.8 shard_map.95
  59.7 3.5 %collective-permute-start.11 = (f32[256,256]{1,0:T(8,128)S(1)}, f32[256,256]{1,0:T(8,128)S(1)}, u32[]{:S(2)}, u32[]{:S(2)}) collective-permute-start(f32[256,256]{1,0:T(8,128)S(1)} %get-tuple-element.119.refs_5_), channel_id=1, source_target_pairs={{0,4},{4,0},{8,12},{12,8},{16,20},{20,16},{24,28},{28,24},{1,5},{5... | collective-permute-start | bytes 786440 | tf_op jit(solution)/shard_map/ppermute | solution.py:544
  63.1 0.7 collective-permute-start.12
  63.8 1.0 shard_map.96.inner.refs_1_.second_inner
  64.8 0.7 shard_map.97
  65.6 7.0 %all_gather.10.everyone = f32[512,256]{1,0:T(8,128)S(1)} all-gather(f32[128,256]{1,0:T(8,128)S(1)} %shard_map.97), channel_id=1, replica_groups=mesh['sub'=8,'grp'=4] {'grp'}, dimensions={0}, use_global_device_ids=true | all-gather | bytes 655360 | tf_op jit(solution)/shard_map/all_gather | solution.py:675
  72.5 1.5 %shard_map.98 = (f32[4,256,512]{2,1,0:T(8,128)S(1)}, f32[2,256,256]{2,1,0:T(8,128)S(1)}) custom-call(f32[3,256,256]{2,1,0:T(8,128)S(1)} %shard_map.96.inner.refs_1_.second_inner, f32[4,256,256]{2,1,0:T(8,128)S(1)} %get-tuple-element.113.own.residual.refs_9_.residual_own, bf16[4,512,512]{2,1,0:T(8,128)(2,1)S(1)} %bitcast.19, ...), custom_call_target="tpu_custom_call" | custom-call | tf_op jit(solution)/shard_map/pallas_call | solution.py:35
  74.0 0.5 collective-permute-done.11.refs_3_
  74.6 0.9 shard_map.99
  75.5 3.5 %collective-permute-start.13 = (f32[288,256]{1,0:T(8,128)S(1)}, f32[288,256]{1,0:T(8,128)S(1)}, u32[]{:S(2)}, u32[]{:S(2)}) collective-permute-start(f32[288,256]{1,0:T(8,128)S(1)} %get-tuple-element.124.near_sent), channel_id=1, source_target_pairs={{0,4},{4,0},{8,12},{12,8},{16,20},{20,16},{24,28},{28,24},{1,5},{5... | collective-permute-start | bytes 884744 | tf_op jit(solution)/shard_map/ppermute | solution.py:544
  79.0 0.7 collective-permute-start.14
  79.7 13.1 %all_to_all.16.sums = f32[32,2,256]{2,1,0:T(2,128)S(1)} all-to-all(f32[32,2,256]{2,1,0:T(2,128)S(1)} %broadcast_in_dim.11), channel_id=1, replica_groups=mesh['sub'=8,'grp'=4] {'sub','grp'}, dimensions={0} | all-to-all | bytes 131072 | tf_op jit(solution)/shard_map/all_to_all | solution.py:552
  92.8 0.0 collective-permute-done.13.near
  92.8 0.9 shard_map.100
  93.7 3.1 %collective-permute-start.15 = (f32[256,256]{1,0:T(8,128)S(1)}, f32[256,256]{1,0:T(8,128)S(1)}, u32[]{:S(2)}, u32[]{:S(2)}) collective-permute-start(f32[256,256]{1,0:T(8,128)S(1)} %get-tuple-element.136.refs_5_), channel_id=1, source_target_pairs={{0,4},{4,0},{8,12},{12,8},{16,20},{20,16},{24,28},{28,24},{1,5},{5... | collective-permute-start | bytes 786440 | tf_op jit(solution)/shard_map/ppermute | solution.py:544
  96.8 0.7 collective-permute-start.16
  97.5 1.1 shard_map.101.inner.refs_1_.third_inner
  98.5 0.7 shard_map.102
  99.3 6.8 %all_gather.11.everyone = f32[512,256]{1,0:T(8,128)S(1)} all-gather(f32[128,256]{1,0:T(8,128)S(1)} %shard_map.102), channel_id=1, replica_groups=mesh['sub'=8,'grp'=4] {'grp'}, dimensions={0}, use_global_device_ids=true | all-gather | bytes 655360 | tf_op jit(solution)/shard_map/all_gather | solution.py:675
  106.0 1.5 %shard_map.103 = (f32[4,256,512]{2,1,0:T(8,128)S(1)}, f32[2,256,256]{2,1,0:T(8,128)S(1)}) custom-call(f32[3,256,256]{2,1,0:T(8,128)S(1)} %shard_map.101.inner.refs_1_.third_inner, f32[4,256,256]{2,1,0:T(8,128)S(1)} %get-tuple-element.132.own.residual.refs_9_, bf16[4,512,512]{2,1,0:T(8,128)(2,1)S(1)} %bitcast.21, f32[512,256]{1,0:T(8,128)S(1)} %all_gather.11.everyone, ...), custom_call_target="tpu_custom_call" | custom-call | tf_op jit(solution)/shard_map/pallas_call | solution.py:35
  107.5 0.8 collective-permute-done.15.refs_3_
  108.3 0.6 shard_map.104
  108.9 1.3 %collective-permute-start.17 = (f32[256,256]{1,0:T(8,128)S(1)}, f32[256,256]{1,0:T(8,128)S(1)}, u32[]{:S(2)}, u32[]{:S(2)}) collective-permute-start(f32[256,256]{1,0:T(8,128)S(1)} %get-tuple-element.140), channel_id=1, source_target_pairs={{4,0},{8,4},{12,8},{16,12},{20,16},{24,20},{28,24},{5,1},{9,5},{13... | collective-permute-start | bytes 786440 | tf_op jit(solution)/shard_map/ppermute | solution.py:712
  110.2 13.2 %all_to_all.17.sums = f32[32,2,256]{2,1,0:T(2,128)S(1)} all-to-all(f32[32,2,256]{2,1,0:T(2,128)S(1)} %broadcast_in_dim.12), channel_id=1, replica_groups=mesh['sub'=8,'grp'=4] {'sub','grp'}, dimensions={0} | all-to-all | bytes 131072 | tf_op jit(solution)/shard_map/all_to_all | solution.py:552
  123.5 1.7 %shard_map.105 = (f32[4,256,256]{2,1,0:T(8,128)}, f32[4,256,256]{2,1,0:T(8,128)}) custom-call(f32[3,256,256]{2,1,0:T(8,128)S(1)} %get-tuple-element.138.inner, f32[256,256]{1,0:T(8,128)S(1)} %get-tuple-element.139.to_next, f32[256,256]{1,0:T(8,128)S(1)} %collective-permute-done.17.following, f32[4,1,256]{2,1,0:T(1,128)S(1)} %get-tuple-element.84.live_own.refs_8_.live, ...), custom_call_target="tpu_custom_call" | custom-call | tf_op jit(solution)/shard_map/pallas_call | solution.py:35
  (20 shorter events, 0.1 us)
Async XLA Ops:
  0.6 12.6 %copy-start.6 = (s32[1,4,32]{2,1,0:T(4,128)S(1)}, s32[1,4,32]{2,1,0:T(4,128)}, u32[]{:S(2)}) copy-start(s32[1,4,32]{2,1,0:T(4,128)} %param.12) | copy-start | bytes 1540
  0.6 12.6 %copy-start.5 = (f32[1,256,1024]{2,1,0:T(8,128)S(1)}, f32[1,256,1024]{2,1,0:T(8,128)}, u32[]{:S(2)}) copy-start(f32[1,256,1024]{2,1,0:T(8,128)} %param.13) | copy-start | bytes 3145732
  0.7 12.6 %copy-start.4 = (f32[1,4,32,512]{3,2,1,0:T(8,128)S(1)}, f32[1,4,32,512]{3,2,1,0:T(8,128)}, u32[]{:S(2)}) copy-start(f32[1,4,32,512]{3,2,1,0:T(8,128)} %param.11) | copy-start | bytes 786436
  2.5 12.7 %collective-permute-start = (f32[264,256]{1,0:T(8,128)}, f32[264,256]{1,0:T(8,128)S(1)}, u32[]{:S(2)}, u32[]{:S(2)}) collective-permute-start(f32[264,256]{1,0:T(8,128)} %shard_map.86), channel_id=1, source_target_pairs={{0,4},{4,8},{8,12},{12,16},{16,20},{20,24},{24,28},{1,5},{5,9},{9,... | collective-permute-start | bytes 811016 | tf_op jit(solution)/shard_map/ppermute | solution.py:606
  7.3 5.8 %collective-permute-start.3 = (s32[4,32]{1,0:T(4,128)}, s32[4,32]{1,0:T(4,128)S(1)}, u32[]{:S(2)}, u32[]{:S(2)}) collective-permute-start(s32[4,32]{1,0:T(4,128)} %bitcast.28), channel_id=1, source_target_pairs={{0,3},{1,2},{2,1},{3,0},{4,7},{5,6},{6,5},{7,4},{8,11},{9,10},{10,... | collective-permute-start | bytes 1544 | tf_op jit(solution)/shard_map/ppermute | solution.py:560
  8.1 5.1 %collective-permute-start.2 = (s32[4,32]{1,0:T(4,128)}, s32[4,32]{1,0:T(4,128)S(1)}, u32[]{:S(2)}, u32[]{:S(2)}) collective-permute-start(s32[4,32]{1,0:T(4,128)} %bitcast.29), channel_id=1, source_target_pairs={{0,2},{1,3},{2,0},{3,1},{4,6},{5,7},{6,4},{7,5},{8,10},{9,11},{10,... | collective-permute-start | bytes 1544 | tf_op jit(solution)/shard_map/ppermute | solution.py:560
  9.0 4.2 %collective-permute-start.1 = (s32[4,32]{1,0:T(4,128)}, s32[4,32]{1,0:T(4,128)S(1)}, u32[]{:S(2)}, u32[]{:S(2)}) collective-permute-start(s32[4,32]{1,0:T(4,128)} %bitcast.30), channel_id=1, source_target_pairs={{0,1},{1,0},{2,3},{3,2},{4,5},{5,4},{6,7},{7,6},{8,9},{9,8},{10,11... | collective-permute-start | bytes 1544 | tf_op jit(solution)/shard_map/ppermute | solution.py:560
  9.3 1.6 %copy-start = (bf16[1,4,512,512]{3,2,1,0:T(8,128)(2,1)S(1)}, bf16[1,4,512,512]{3,2,1,0:T(8,128)(2,1)}, u32[]{:S(2)}) copy-start(bf16[1,4,512,512]{3,2,1,0:T(8,128)(2,1)} %param.10) | copy-start | bytes 6291460
  10.9 1.2 copy-start.3
  12.1 0.7 copy-start.7
  12.7 2.4 %copy-start.1 = (bf16[1,4,512,512]{3,2,1,0:T(8,128)(2,1)S(1)}, bf16[1,4,512,512]{3,2,1,0:T(8,128)(2,1)}, u32[]{:S(2)}) copy-start(bf16[1,4,512,512]{3,2,1,0:T(8,128)(2,1)} %param.10) | copy-start | bytes 6291460
  15.4 14.6 %collective-permute-start.4 = (f32[288,256]{1,0:T(8,128)S(1)}, f32[288,256]{1,0:T(8,128)S(1)}, u32[]{:S(2)}, u32[]{:S(2)}) collective-permute-start(f32[288,256]{1,0:T(8,128)S(1)} %get-tuple-element.87.near_sent), channel_id=1, source_target_pairs={{0,4},{4,0},{8,12},{12,8},{16,20},{20,16},{24,28},{28,24},{1,5},{5... | collective-permute-start | bytes 884744 | tf_op jit(solution)/shard_map/ppermute | solution.py:544
  17.0 13.0 %collective-permute-start.5 = (f32[288,256]{1,0:T(8,128)S(1)}, f32[288,256]{1,0:T(8,128)S(1)}, u32[]{:S(2)}, u32[]{:S(2)}) collective-permute-start(f32[288,256]{1,0:T(8,128)S(1)} %get-tuple-element.88.far_sent), channel_id=1, source_target_pairs={{4,8},{8,4},{12,16},{16,12},{20,24},{24,20},{5,9},{9,5},{13,17},{1... | collective-permute-start | bytes 884744 | tf_op jit(solution)/shard_map/ppermute | solution.py:545
  17.7 19.6 %collective-permute-start.6 = (f32[128,512]{1,0:T(8,128)S(1)}, f32[128,512]{1,0:T(8,128)S(1)}, u32[]{:S(2)}, u32[]{:S(2)}) collective-permute-start(f32[128,512]{1,0:T(8,128)S(1)} %get-tuple-element.98), channel_id=1, source_target_pairs={{0,1},{1,0},{2,3},{3,2},{4,5},{5,4},{6,7},{7,6},{8,9},{9,8},{10,11... | collective-permute-start | bytes 786440 | tf_op jit(solution)/shard_map/ppermute | solution.py:569
  17.8 19.5 %collective-permute-start.7 = (f32[128,512]{1,0:T(8,128)S(1)}, f32[128,512]{1,0:T(8,128)S(1)}, u32[]{:S(2)}, u32[]{:S(2)}) collective-permute-start(f32[128,512]{1,0:T(8,128)S(1)} %get-tuple-element.99), channel_id=1, source_target_pairs={{0,2},{1,3},{2,0},{3,1},{4,6},{5,7},{6,4},{7,5},{8,10},{9,11},{10,... | collective-permute-start | bytes 786440 | tf_op jit(solution)/shard_map/ppermute | solution.py:569
  19.4 17.9 %collective-permute-start.8 = (f32[128,512]{1,0:T(8,128)S(1)}, f32[128,512]{1,0:T(8,128)S(1)}, u32[]{:S(2)}, u32[]{:S(2)}) collective-permute-start(f32[128,512]{1,0:T(8,128)S(1)} %get-tuple-element.100), channel_id=1, source_target_pairs={{0,3},{1,2},{2,1},{3,0},{4,7},{5,6},{6,5},{7,4},{8,11},{9,10},{10,... | collective-permute-start | bytes 786440 | tf_op jit(solution)/shard_map/ppermute | solution.py:569
  20.2 1.6 %copy-start.2 = (bf16[1,4,512,512]{3,2,1,0:T(8,128)(2,1)S(1)}, bf16[1,4,512,512]{3,2,1,0:T(8,128)(2,1)}, u32[]{:S(2)}) copy-start(bf16[1,4,512,512]{3,2,1,0:T(8,128)(2,1)} %param.9) | copy-start | bytes 6291460
  39.5 19.4 %collective-permute-start.9 = (f32[352,256]{1,0:T(8,128)S(1)}, f32[352,256]{1,0:T(8,128)S(1)}, u32[]{:S(2)}, u32[]{:S(2)}) collective-permute-start(f32[352,256]{1,0:T(8,128)S(1)} %get-tuple-element.108.near_sent), channel_id=1, source_target_pairs={{0,4},{4,0},{8,12},{12,8},{16,20},{20,16},{24,28},{28,24},{1,5},{5... | collective-permute-start | bytes 1081352 | tf_op jit(solution)/shard_map/ppermute | solution.py:544
  42.2 16.6 %collective-permute-start.10 = (f32[352,256]{1,0:T(8,128)S(1)}, f32[352,256]{1,0:T(8,128)S(1)}, u32[]{:S(2)}, u32[]{:S(2)}) collective-permute-start(f32[352,256]{1,0:T(8,128)S(1)} %get-tuple-element.109.far_sent), channel_id=1, source_target_pairs={{4,8},{8,4},{12,16},{16,12},{20,24},{24,20},{5,9},{9,5},{13,17},{1... | collective-permute-start | bytes 1081352 | tf_op jit(solution)/shard_map/ppermute | solution.py:545
  59.7 14.9 %collective-permute-start.11 = (f32[256,256]{1,0:T(8,128)S(1)}, f32[256,256]{1,0:T(8,128)S(1)}, u32[]{:S(2)}, u32[]{:S(2)}) collective-permute-start(f32[256,256]{1,0:T(8,128)S(1)} %get-tuple-element.119.refs_5_), channel_id=1, source_target_pairs={{0,4},{4,0},{8,12},{12,8},{16,20},{20,16},{24,28},{28,24},{1,5},{5... | collective-permute-start | bytes 786440 | tf_op jit(solution)/shard_map/ppermute | solution.py:544
  63.1 11.5 %collective-permute-start.12 = (f32[256,256]{1,0:T(8,128)S(1)}, f32[256,256]{1,0:T(8,128)S(1)}, u32[]{:S(2)}, u32[]{:S(2)}) collective-permute-start(f32[256,256]{1,0:T(8,128)S(1)} %get-tuple-element.120.refs_6_), channel_id=1, source_target_pairs={{4,8},{8,4},{12,16},{16,12},{20,24},{24,20},{5,9},{9,5},{13,17},{1... | collective-permute-start | bytes 786440 | tf_op jit(solution)/shard_map/ppermute | solution.py:545
  75.5 17.3 %collective-permute-start.13 = (f32[288,256]{1,0:T(8,128)S(1)}, f32[288,256]{1,0:T(8,128)S(1)}, u32[]{:S(2)}, u32[]{:S(2)}) collective-permute-start(f32[288,256]{1,0:T(8,128)S(1)} %get-tuple-element.124.near_sent), channel_id=1, source_target_pairs={{0,4},{4,0},{8,12},{12,8},{16,20},{20,16},{24,28},{28,24},{1,5},{5... | collective-permute-start | bytes 884744 | tf_op jit(solution)/shard_map/ppermute | solution.py:544
  79.0 13.8 %collective-permute-start.14 = (f32[288,256]{1,0:T(8,128)S(1)}, f32[288,256]{1,0:T(8,128)S(1)}, u32[]{:S(2)}, u32[]{:S(2)}) collective-permute-start(f32[288,256]{1,0:T(8,128)S(1)} %get-tuple-element.125.far_sent), channel_id=1, source_target_pairs={{4,8},{8,4},{12,16},{16,12},{20,24},{24,20},{5,9},{9,5},{13,17},{1... | collective-permute-start | bytes 884744 | tf_op jit(solution)/shard_map/ppermute | solution.py:545
  93.7 14.6 %collective-permute-start.15 = (f32[256,256]{1,0:T(8,128)S(1)}, f32[256,256]{1,0:T(8,128)S(1)}, u32[]{:S(2)}, u32[]{:S(2)}) collective-permute-start(f32[256,256]{1,0:T(8,128)S(1)} %get-tuple-element.136.refs_5_), channel_id=1, source_target_pairs={{0,4},{4,0},{8,12},{12,8},{16,20},{20,16},{24,28},{28,24},{1,5},{5... | collective-permute-start | bytes 786440 | tf_op jit(solution)/shard_map/ppermute | solution.py:544
  96.8 11.5 %collective-permute-start.16 = (f32[256,256]{1,0:T(8,128)S(1)}, f32[256,256]{1,0:T(8,128)S(1)}, u32[]{:S(2)}, u32[]{:S(2)}) collective-permute-start(f32[256,256]{1,0:T(8,128)S(1)} %get-tuple-element.137.refs_6_), channel_id=1, source_target_pairs={{4,8},{8,4},{12,16},{16,12},{20,24},{24,20},{5,9},{9,5},{13,17},{1... | collective-permute-start | bytes 786440 | tf_op jit(solution)/shard_map/ppermute | solution.py:545
  108.9 14.6 %collective-permute-start.17 = (f32[256,256]{1,0:T(8,128)S(1)}, f32[256,256]{1,0:T(8,128)S(1)}, u32[]{:S(2)}, u32[]{:S(2)}) collective-permute-start(f32[256,256]{1,0:T(8,128)S(1)} %get-tuple-element.140), channel_id=1, source_target_pairs={{4,0},{8,4},{12,8},{16,12},{20,16},{24,20},{28,24},{5,1},{9,5},{13... | collective-permute-start | bytes 786440 | tf_op jit(solution)/shard_map/ppermute | solution.py:712

commit v14 on v13

--- a/solution.py
+++ b/solution.py
@@ -160,19 +160,26 @@
         unknowns = [maps[distance][sub : sub + 1, :] for sub in range(subs)]
         everyone[distance] = jnp.concatenate(unknowns, axis=1)
     high, low = split(coarse[...])
-    unknowns = lax.broadcasted_iota(jnp.int32, (size, own), 0)
+    together = max(1, 512 // own)
     columns = []
-    for member in range(group):
-        chosen = (unknowns == everyone[grp ^ member]).astype(jnp.bfloat16)
+    for start in range(0, group, together):
+        members = range(start, min(start + together, group))
+        wanted = jnp.concatenate([everyone[grp ^ member] for member in members], axis=1)
+        unknowns = lax.broadcasted_iota(jnp.int32, (size, wanted.shape[1]), 0)
+        chosen = (unknowns == wanted).astype(jnp.bfloat16)
         columns.append(mul(high, chosen) + mul(low, chosen))
     high, low = split(jnp.concatenate(columns, axis=1))
-    owned = lax.broadcasted_iota(jnp.int32, (rows, own), 0) + grp * rows
     dims = (((0,), (0,)), ((), ()))
-    for distance in range(group):
-        chosen = (owned == everyone[distance]).astype(jnp.bfloat16)
-        picked[distance][...] = lax.dot_general(
+    for start in range(0, group, together):
+        distances = range(start, min(start + together, group))
+        wanted = jnp.concatenate([everyone[distance] for distance in distances], axis=1)
+        owned = lax.broadcasted_iota(jnp.int32, (rows, wanted.shape[1]), 0) + grp * rows
+        chosen = (owned == wanted).astype(jnp.bfloat16)
+        values = lax.dot_general(
             chosen, high, dims, preferred_element_type=jnp.float32
         ) + lax.dot_general(chosen, low, dims, preferred_element_type=jnp.float32)
+        for place, distance in enumerate(distances):
+            picked[distance][...] = values[place * own : (place + 1) * own]
 
 
 def start_kernel(inner, panel, coupling, result, corners):
@@ -320,7 +327,7 @@
 
 def first_dual_kernel(before, inner_z, edge, last_z, residual, panel, everyone, block, lift,
                       near, far, live_edge, live_own, preconditioner,
-                      inner, near_out, far_out, sums, for_next, for_prev, result):
+                      inner, near_out, far_out, result, for_next, for_prev):
     even = even_place()
     subs, (loads, width) = panel.shape[0], edge.shape
     rows = for_next.shape[0] // 2
@@ -348,6 +355,10 @@
     inner_jump(result, live_own, inner)
     faces = [result[subs - 1][:, width:], result[0][:, :width]]
     send_dual(even, inner, faces, for_next, for_prev, near_out, far_out, residual, given)
+
+
+def sums_kernel(result, inner_z, edge, last_z, residual, sums):
+    subs = residual.shape[0]
     edges = [edge[...]] + [inner_z[place] for place in range(subs - 1)] + [last_z[...]]
     product = curvature = 0.0
     for sub in range(subs):
@@ -651,14 +662,16 @@
     everyone = lax.all_gather(values, "grp", tiled=True)
     everyone, blocks = lax.optimization_barrier((everyone, blocks))
     block = jnp.concatenate(split_outside(sum(blocks[1:], blocks[0])), axis=0)
-    inner, near, far, sums, for_next, for_prev = call(
+    inner, near, far, result, for_next, for_prev = call(
         first_dual_kernel,
-        [inner_shape, longer_shape, longer_shape, scalars_shape]
+        [inner_shape, longer_shape, longer_shape, result_shape]
         + [(2 * corners, width), (2 * corners, width)],
         result, first_inner, edge, first_last, residual[1], solve, everyone, block, lift,
         near, far, *live, dirichlet,
         kinds=[jnp.float32] * 4 + [jnp.bfloat16] * 2,
-        scratch=[pltpu.VMEM(result_shape, jnp.float32)],
+    )
+    (sums,) = call(
+        sums_kernel, [scalars_shape], result, first_inner, edge, first_last, residual[1]
     )
     sums = from_all(sums)
     sent = near, far

time: 126 us -> 124 us (0.984)
    pallas_call x19 -> x20, Pallas kernels: 19.3 us -> 18.4 us  [call(): pl.pallas_call(kernel, out_shape=[jax.ShapeDtypeStruct(*shape) for shape...]
  transfers between devices with their start and end apart: 18 -> 18, of which waited for: 3 -> 3; matrix products, arithmetic and copies ran while one was open for 0% -> 0% of each run, Pallas kernels for 10% -> 9%
where the time goes in v14:
time: 124 us
  blocking collectives  62.3 us (50%)
  starting transfers between devices  27.5 us (22%)
  Pallas kernels  20.2 us (16%)
  waiting for transfers between devices  8.58 us (7%)
  local copies, waits for them, and re-layouts  4.12 us (3%)
    all_to_all x3, blocking collectives, from_all(): return lax.all_to_all(copies, ('sub', 'grp'), 0, 0)  41.8 us
    pallas_call x20, Pallas kernels, call(): pl.pallas_call(kernel, out_shape=[jax.ShapeDtypeStruct(*shape) for shape...  18.4 us
    ppermute x5, starting transfers between devices, swap(): lax.ppermute(near, 'sub', neighbour_pairs(size, 0))  14.2 us
    all_gather x2, blocking collectives, inside(): everyone = lax.all_gather(values, 'grp', tiled=True)  13.6 us
    ppermute x5, waiting for transfers between devices, swap(): lax.ppermute(near, 'sub', neighbour_pairs(size, 0))  8.54 us
    all_gather x1, blocking collectives, local(): everyone = lax.all_gather(values, 'grp', tiled=True)  6.95 us
    ppermute x1, starting transfers between devices, local(): head = lax.ppermute(tail, 'sub', [(i, i + 1) for i in range(size - 1)])  4.86 us
    unnamed x16, local copies, waits for them, and re-layouts  4.07 us
  transfers between devices with their start and end apart: 18, of which 3 were waited for; matrix products, arithmetic and copies ran while one was open for 0% of the time, Pallas kernels for 9%

profile of v14, /device:TPU:0, one launch (start us, length us, event | category | flops | bytes accessed | tf_op | source)
XLA Modules:
  0.0 123.9 jit_solution(18002131678246960417)
XLA Ops:
  0.6 0.0 copy-start.6
  0.7 1.8 %shard_map.86 = f32[264,256]{1,0:T(8,128)} custom-call(s32[1,4]{1,0:T(1,128)} %counts, f32[1,4,256,256]{3,2,1,0:T(8,128)} %rhs.1), custom_call_target="tpu_custom_call" | custom-call | tf_op jit(solution)/shard_map/pallas_call | solution.py:586
  2.5 4.9 %collective-permute-start = (f32[264,256]{1,0:T(8,128)}, f32[264,256]{1,0:T(8,128)S(1)}, u32[]{:S(2)}, u32[]{:S(2)}) collective-permute-start(f32[264,256]{1,0:T(8,128)} %shard_map.86), channel_id=1, source_target_pairs={{0,4},{4,8},{8,12},{12,16},{16,20},{20,24},{24,28},{1,5},{5,9},{9,... | collective-permute-start | bytes 811016 | tf_op jit(solution)/shard_map/ppermute | solution.py:617
  7.3 0.7 collective-permute-start.3
  8.1 0.9 collective-permute-start.2
  9.0 0.3 collective-permute-start.1
  9.3 1.6 %copy-done = bf16[1,4,512,512]{3,2,1,0:T(8,128)(2,1)S(1)} copy-done((bf16[1,4,512,512]{3,2,1,0:T(8,128)(2,1)S(1)}, bf16[1,4,512,512]{3,2,1,0:T(8,128)(2,1)}, u32[]{:S(2)}) %copy-start) | copy-done | bytes 2097176
  10.9 1.2 copy-done.3
  12.1 0.7 copy-done.7
  12.7 0.4 shard_map.88
  13.2 0.0 collective-permute-done.3.refs_3_
  13.2 0.0 collective-permute-done.2.refs_2_
  13.2 0.0 collective-permute-done.1.refs_1_
  13.2 1.4 %shard_map.87 = (f32[128,512]{1,0:T(8,128)S(1)}, f32[128,512]{1,0:T(8,128)S(1)}, f32[128,512]{1,0:T(8,128)S(1)}, f32[128,512]{1,0:T(8,128)S(1)}, bf16[4,64,512]{...) custom-call(s32[4,32]{1,0:T(4,128)S(1)} %bitcast.31, s32[4,32]{1,0:T(4,128)S(1)} %collective-permute-done.1.refs_1_, ...), custom_call_target="tpu_custom_call" | custom-call | tf_op jit(solution)/shard_map/pallas_call | solution.py:35
  14.7 0.0 collective-permute-done.head
  14.7 0.2 shard_map.89
  14.9 1.6 %collective-permute-start.4 = (f32[288,256]{1,0:T(8,128)S(1)}, f32[288,256]{1,0:T(8,128)S(1)}, u32[]{:S(2)}, u32[]{:S(2)}) collective-permute-start(f32[288,256]{1,0:T(8,128)S(1)} %get-tuple-element.87.near_sent), channel_id=1, source_target_pairs={{0,4},{4,0},{8,12},{12,8},{16,20},{20,16},{24,28},{28,24},{1,5},{5... | collective-permute-start | bytes 884744 | tf_op jit(solution)/shard_map/ppermute | solution.py:555
  16.5 0.7 collective-permute-start.5
  17.2 0.1 collective-permute-start.6
  17.3 1.6 %collective-permute-start.7 = (f32[128,512]{1,0:T(8,128)S(1)}, f32[128,512]{1,0:T(8,128)S(1)}, u32[]{:S(2)}, u32[]{:S(2)}) collective-permute-start(f32[128,512]{1,0:T(8,128)S(1)} %get-tuple-element.99), channel_id=1, source_target_pairs={{0,2},{1,3},{2,0},{3,1},{4,6},{5,7},{6,4},{7,5},{8,10},{9,11},{10,... | collective-permute-start | bytes 786440 | tf_op jit(solution)/shard_map/ppermute | solution.py:580
  18.9 0.3 collective-permute-start.8
  19.2 0.6 shard_map.92
  19.8 0.0 copy-start.2
  19.8 1.0 shard_map.90.inner.inner_z.first_inner
  20.8 0.6 copy-done.2
  21.3 1.4 %shard_map.91 = (f32[4,256,512]{2,1,0:T(8,128)S(1)}, f32[128,256]{1,0:T(8,128)S(1)}) custom-call(f32[3,256,256]{2,1,0:T(8,128)S(1)} %shard_map.90.inner.inner_z.first_inner, bf16[4,512,512]{2,1,0:T(8,128)(2,1)S(1)} %bitcast.17, bf16[4,64,512]{2,1,0:T(8,128)(2,1)S(1)} %get-tuple-element.85.coupling), custom_call_target="tpu_custom_call" | custom-call | tf_op jit(solution)/shard_map/pallas_call | solution.py:35
  22.7 6.8 %collective-permute-done.4.near = f32[288,256]{1,0:T(8,128)S(1)} collective-permute-done((f32[288,256]{1,0:T(8,128)S(1)}, f32[288,256]{1,0:T(8,128)S(1)}, u32[]{:S(2)}, u32[]{:S(2)}) %collective-permute-start.4) | collective-permute-done | bytes 294944 | tf_op jit(solution)/shard_map/ppermute | solution.py:555
  29.5 0.0 collective-permute-done.5.far
  29.5 0.3 shard_map.93
  29.9 7.0 %all_gather.9.everyone = f32[512,256]{1,0:T(8,128)S(1)} all-gather(f32[128,256]{1,0:T(8,128)S(1)} %get-tuple-element.96), channel_id=1, replica_groups=mesh['sub'=8,'grp'=4] {'grp'}, dimensions={0}, use_global_device_ids=true | all-gather | bytes 655360 | tf_op jit(solution)/shard_map/all_gather | solution.py:662
  36.8 0.0 collective-permute-done.6
  36.8 0.0 collective-permute-done.7
  36.8 0.0 collective-permute-done.8
  36.8 0.1 reduce-precision_convert_fusion
  37.0 1.6 %shard_map.94 = (f32[3,256,256]{2,1,0:T(8,128)S(1)}, f32[352,256]{1,0:T(8,128)S(1)}, f32[352,256]{1,0:T(8,128)S(1)}, f32[4,256,512]{2,1,0:T(8,128)S(1)}, bf16[64...) custom-call(f32[4,256,512]{2,1,0:T(8,128)S(1)} %get-tuple-element.86.before, ...), custom_call_target="tpu_custom_call" | custom-call | tf_op jit(solution)/shard_map/pallas_call | solution.py:35
  38.6 2.8 %collective-permute-start.9 = (f32[352,256]{1,0:T(8,128)S(1)}, f32[352,256]{1,0:T(8,128)S(1)}, u32[]{:S(2)}, u32[]{:S(2)}) collective-permute-start(f32[352,256]{1,0:T(8,128)S(1)} %get-tuple-element.108.near_sent), channel_id=1, source_target_pairs={{0,4},{4,0},{8,12},{12,8},{16,20},{20,16},{24,28},{28,24},{1,5},{5... | collective-permute-start | bytes 1081352 | tf_op jit(solution)/shard_map/ppermute | solution.py:555
  41.3 0.7 collective-permute-start.10
  42.0 0.3 shard_map.95
  42.4 15.6 %all_to_all.15.sums = f32[32,2,256]{2,1,0:T(2,128)S(1)} all-to-all(f32[32,2,256]{2,1,0:T(2,128)S(1)} %broadcast_in_dim.10), channel_id=1, replica_groups=mesh['sub'=8,'grp'=4] {'sub','grp'}, dimensions={0} | all-to-all | bytes 131072 | tf_op jit(solution)/shard_map/all_to_all | solution.py:563
  58.0 0.8 shard_map.96
  58.7 3.5 %collective-permute-start.11 = (f32[256,256]{1,0:T(8,128)S(1)}, f32[256,256]{1,0:T(8,128)S(1)}, u32[]{:S(2)}, u32[]{:S(2)}) collective-permute-start(f32[256,256]{1,0:T(8,128)S(1)} %get-tuple-element.119.refs_5_), channel_id=1, source_target_pairs={{0,4},{4,0},{8,12},{12,8},{16,20},{20,16},{24,28},{28,24},{1,5},{5... | collective-permute-start | bytes 786440 | tf_op jit(solution)/shard_map/ppermute | solution.py:555
  62.2 0.7 collective-permute-start.12
  62.9 1.0 shard_map.97.inner.refs_1_.second_inner
  63.9 0.7 shard_map.98
  64.6 6.8 %all_gather.10.everyone = f32[512,256]{1,0:T(8,128)S(1)} all-gather(f32[128,256]{1,0:T(8,128)S(1)} %shard_map.98), channel_id=1, replica_groups=mesh['sub'=8,'grp'=4] {'grp'}, dimensions={0}, use_global_device_ids=true | all-gather | bytes 655360 | tf_op jit(solution)/shard_map/all_gather | solution.py:688
  71.4 1.4 %shard_map.99 = (f32[4,256,512]{2,1,0:T(8,128)S(1)}, f32[2,256,256]{2,1,0:T(8,128)S(1)}) custom-call(f32[3,256,256]{2,1,0:T(8,128)S(1)} %shard_map.97.inner.refs_1_.second_inner, f32[4,256,256]{2,1,0:T(8,128)S(1)} %get-tuple-element.113.own.residual.refs_9_.residual_own, bf16[4,512,512]{2,1,0:T(8,128)(2,1)S(1)} %bitcast.19, ...), custom_call_target="tpu_custom_call" | custom-call | tf_op jit(solution)/shard_map/pallas_call | solution.py:35
  72.8 0.8 collective-permute-done.11.refs_3_
  73.7 0.9 shard_map.100
  74.6 3.2 %collective-permute-start.13 = (f32[288,256]{1,0:T(8,128)S(1)}, f32[288,256]{1,0:T(8,128)S(1)}, u32[]{:S(2)}, u32[]{:S(2)}) collective-permute-start(f32[288,256]{1,0:T(8,128)S(1)} %get-tuple-element.124.near_sent), channel_id=1, source_target_pairs={{0,4},{4,0},{8,12},{12,8},{16,20},{20,16},{24,28},{28,24},{1,5},{5... | collective-permute-start | bytes 884744 | tf_op jit(solution)/shard_map/ppermute | solution.py:555
  77.8 0.7 collective-permute-start.14
  78.5 13.1 %all_to_all.16.sums = f32[32,2,256]{2,1,0:T(2,128)S(1)} all-to-all(f32[32,2,256]{2,1,0:T(2,128)S(1)} %broadcast_in_dim.11), channel_id=1, replica_groups=mesh['sub'=8,'grp'=4] {'sub','grp'}, dimensions={0} | all-to-all | bytes 131072 | tf_op jit(solution)/shard_map/all_to_all | solution.py:563
  91.6 0.8 shard_map.101
  92.4 3.1 %collective-permute-start.15 = (f32[256,256]{1,0:T(8,128)S(1)}, f32[256,256]{1,0:T(8,128)S(1)}, u32[]{:S(2)}, u32[]{:S(2)}) collective-permute-start(f32[256,256]{1,0:T(8,128)S(1)} %get-tuple-element.136.refs_5_), channel_id=1, source_target_pairs={{0,4},{4,0},{8,12},{12,8},{16,20},{20,16},{24,28},{28,24},{1,5},{5... | collective-permute-start | bytes 786440 | tf_op jit(solution)/shard_map/ppermute | solution.py:555
  95.5 0.7 collective-permute-start.16
  96.2 1.0 shard_map.102.inner.refs_1_.third_inner
  97.2 0.7 shard_map.103
  97.9 6.8 %all_gather.11.everyone = f32[512,256]{1,0:T(8,128)S(1)} all-gather(f32[128,256]{1,0:T(8,128)S(1)} %shard_map.103), channel_id=1, replica_groups=mesh['sub'=8,'grp'=4] {'grp'}, dimensions={0}, use_global_device_ids=true | all-gather | bytes 655360 | tf_op jit(solution)/shard_map/all_gather | solution.py:688
  104.7 1.4 %shard_map.104 = (f32[4,256,512]{2,1,0:T(8,128)S(1)}, f32[2,256,256]{2,1,0:T(8,128)S(1)}) custom-call(f32[3,256,256]{2,1,0:T(8,128)S(1)} %shard_map.102.inner.refs_1_.third_inner, f32[4,256,256]{2,1,0:T(8,128)S(1)} %get-tuple-element.132.own.residual.refs_9_, bf16[4,512,512]{2,1,0:T(8,128)(2,1)S(1)} %bitcast.21, f32[512,256]{1,0:T(8,128)S(1)} %all_gather.11.everyone, ...), custom_call_target="tpu_custom_call" | custom-call | tf_op jit(solution)/shard_map/pallas_call | solution.py:35
  106.1 0.9 collective-permute-done.15.refs_3_
  107.0 0.7 shard_map.105
  107.6 1.3 %collective-permute-start.17 = (f32[256,256]{1,0:T(8,128)S(1)}, f32[256,256]{1,0:T(8,128)S(1)}, u32[]{:S(2)}, u32[]{:S(2)}) collective-permute-start(f32[256,256]{1,0:T(8,128)S(1)} %get-tuple-element.140), channel_id=1, source_target_pairs={{4,0},{8,4},{12,8},{16,12},{20,16},{24,20},{28,24},{5,1},{9,5},{13... | collective-permute-start | bytes 786440 | tf_op jit(solution)/shard_map/ppermute | solution.py:725
  109.0 13.2 %all_to_all.17.sums = f32[32,2,256]{2,1,0:T(2,128)S(1)} all-to-all(f32[32,2,256]{2,1,0:T(2,128)S(1)} %broadcast_in_dim.12), channel_id=1, replica_groups=mesh['sub'=8,'grp'=4] {'sub','grp'}, dimensions={0} | all-to-all | bytes 131072 | tf_op jit(solution)/shard_map/all_to_all | solution.py:563
  122.2 0.0 collective-permute-done.17.following
  122.2 1.7 %shard_map.106 = (f32[4,256,256]{2,1,0:T(8,128)}, f32[4,256,256]{2,1,0:T(8,128)}) custom-call(f32[3,256,256]{2,1,0:T(8,128)S(1)} %get-tuple-element.138.inner, f32[256,256]{1,0:T(8,128)S(1)} %get-tuple-element.139.to_next, f32[256,256]{1,0:T(8,128)S(1)} %collective-permute-done.17.following, f32[4,1,256]{2,1,0:T(1,128)S(1)} %get-tuple-element.84.live_own.refs_8_.live, ...), custom_call_target="tpu_custom_call" | custom-call | tf_op jit(solution)/shard_map/pallas_call | solution.py:35
  (21 shorter events, 0.1 us)
Async XLA Ops:
  0.6 12.6 %copy-start.6 = (s32[1,4,32]{2,1,0:T(4,128)S(1)}, s32[1,4,32]{2,1,0:T(4,128)}, u32[]{:S(2)}) copy-start(s32[1,4,32]{2,1,0:T(4,128)} %param.12) | copy-start | bytes 1540
  0.6 12.6 %copy-start.5 = (f32[1,256,1024]{2,1,0:T(8,128)S(1)}, f32[1,256,1024]{2,1,0:T(8,128)}, u32[]{:S(2)}) copy-start(f32[1,256,1024]{2,1,0:T(8,128)} %param.13) | copy-start | bytes 3145732
  0.7 12.6 %copy-start.4 = (f32[1,4,32,512]{3,2,1,0:T(8,128)S(1)}, f32[1,4,32,512]{3,2,1,0:T(8,128)}, u32[]{:S(2)}) copy-start(f32[1,4,32,512]{3,2,1,0:T(8,128)} %param.11) | copy-start | bytes 786436
  2.5 12.2 %collective-permute-start = (f32[264,256]{1,0:T(8,128)}, f32[264,256]{1,0:T(8,128)S(1)}, u32[]{:S(2)}, u32[]{:S(2)}) collective-permute-start(f32[264,256]{1,0:T(8,128)} %shard_map.86), channel_id=1, source_target_pairs={{0,4},{4,8},{8,12},{12,16},{16,20},{20,24},{24,28},{1,5},{5,9},{9,... | collective-permute-start | bytes 811016 | tf_op jit(solution)/shard_map/ppermute | solution.py:617
  7.3 5.8 %collective-permute-start.3 = (s32[4,32]{1,0:T(4,128)}, s32[4,32]{1,0:T(4,128)S(1)}, u32[]{:S(2)}, u32[]{:S(2)}) collective-permute-start(s32[4,32]{1,0:T(4,128)} %bitcast.28), channel_id=1, source_target_pairs={{0,3},{1,2},{2,1},{3,0},{4,7},{5,6},{6,5},{7,4},{8,11},{9,10},{10,... | collective-permute-start | bytes 1544 | tf_op jit(solution)/shard_map/ppermute | solution.py:571
  8.1 5.1 %collective-permute-start.2 = (s32[4,32]{1,0:T(4,128)}, s32[4,32]{1,0:T(4,128)S(1)}, u32[]{:S(2)}, u32[]{:S(2)}) collective-permute-start(s32[4,32]{1,0:T(4,128)} %bitcast.29), channel_id=1, source_target_pairs={{0,2},{1,3},{2,0},{3,1},{4,6},{5,7},{6,4},{7,5},{8,10},{9,11},{10,... | collective-permute-start | bytes 1544 | tf_op jit(solution)/shard_map/ppermute | solution.py:571
  9.0 4.2 %collective-permute-start.1 = (s32[4,32]{1,0:T(4,128)}, s32[4,32]{1,0:T(4,128)S(1)}, u32[]{:S(2)}, u32[]{:S(2)}) collective-permute-start(s32[4,32]{1,0:T(4,128)} %bitcast.30), channel_id=1, source_target_pairs={{0,1},{1,0},{2,3},{3,2},{4,5},{5,4},{6,7},{7,6},{8,9},{9,8},{10,11... | collective-permute-start | bytes 1544 | tf_op jit(solution)/shard_map/ppermute | solution.py:571
  9.3 1.6 %copy-start = (bf16[1,4,512,512]{3,2,1,0:T(8,128)(2,1)S(1)}, bf16[1,4,512,512]{3,2,1,0:T(8,128)(2,1)}, u32[]{:S(2)}) copy-start(bf16[1,4,512,512]{3,2,1,0:T(8,128)(2,1)} %param.10) | copy-start | bytes 6291460
  10.9 1.2 copy-start.3
  12.1 0.7 copy-start.7
  12.7 1.9 %copy-start.1 = (bf16[1,4,512,512]{3,2,1,0:T(8,128)(2,1)S(1)}, bf16[1,4,512,512]{3,2,1,0:T(8,128)(2,1)}, u32[]{:S(2)}) copy-start(bf16[1,4,512,512]{3,2,1,0:T(8,128)(2,1)} %param.10) | copy-start | bytes 6291460
  14.9 14.6 %collective-permute-start.4 = (f32[288,256]{1,0:T(8,128)S(1)}, f32[288,256]{1,0:T(8,128)S(1)}, u32[]{:S(2)}, u32[]{:S(2)}) collective-permute-start(f32[288,256]{1,0:T(8,128)S(1)} %get-tuple-element.87.near_sent), channel_id=1, source_target_pairs={{0,4},{4,0},{8,12},{12,8},{16,20},{20,16},{24,28},{28,24},{1,5},{5... | collective-permute-start | bytes 884744 | tf_op jit(solution)/shard_map/ppermute | solution.py:555
  16.5 13.0 %collective-permute-start.5 = (f32[288,256]{1,0:T(8,128)S(1)}, f32[288,256]{1,0:T(8,128)S(1)}, u32[]{:S(2)}, u32[]{:S(2)}) collective-permute-start(f32[288,256]{1,0:T(8,128)S(1)} %get-tuple-element.88.far_sent), channel_id=1, source_target_pairs={{4,8},{8,4},{12,16},{16,12},{20,24},{24,20},{5,9},{9,5},{13,17},{1... | collective-permute-start | bytes 884744 | tf_op jit(solution)/shard_map/ppermute | solution.py:556
  17.2 19.6 %collective-permute-start.6 = (f32[128,512]{1,0:T(8,128)S(1)}, f32[128,512]{1,0:T(8,128)S(1)}, u32[]{:S(2)}, u32[]{:S(2)}) collective-permute-start(f32[128,512]{1,0:T(8,128)S(1)} %get-tuple-element.98), channel_id=1, source_target_pairs={{0,1},{1,0},{2,3},{3,2},{4,5},{5,4},{6,7},{7,6},{8,9},{9,8},{10,11... | collective-permute-start | bytes 786440 | tf_op jit(solution)/shard_map/ppermute | solution.py:580
  17.3 19.5 %collective-permute-start.7 = (f32[128,512]{1,0:T(8,128)S(1)}, f32[128,512]{1,0:T(8,128)S(1)}, u32[]{:S(2)}, u32[]{:S(2)}) collective-permute-start(f32[128,512]{1,0:T(8,128)S(1)} %get-tuple-element.99), channel_id=1, source_target_pairs={{0,2},{1,3},{2,0},{3,1},{4,6},{5,7},{6,4},{7,5},{8,10},{9,11},{10,... | collective-permute-start | bytes 786440 | tf_op jit(solution)/shard_map/ppermute | solution.py:580
  18.9 17.9 %collective-permute-start.8 = (f32[128,512]{1,0:T(8,128)S(1)}, f32[128,512]{1,0:T(8,128)S(1)}, u32[]{:S(2)}, u32[]{:S(2)}) collective-permute-start(f32[128,512]{1,0:T(8,128)S(1)} %get-tuple-element.100), channel_id=1, source_target_pairs={{0,3},{1,2},{2,1},{3,0},{4,7},{5,6},{6,5},{7,4},{8,11},{9,10},{10,... | collective-permute-start | bytes 786440 | tf_op jit(solution)/shard_map/ppermute | solution.py:580
  19.8 1.6 %copy-start.2 = (bf16[1,4,512,512]{3,2,1,0:T(8,128)(2,1)S(1)}, bf16[1,4,512,512]{3,2,1,0:T(8,128)(2,1)}, u32[]{:S(2)}) copy-start(bf16[1,4,512,512]{3,2,1,0:T(8,128)(2,1)} %param.9) | copy-start | bytes 6291460
  38.6 19.4 %collective-permute-start.9 = (f32[352,256]{1,0:T(8,128)S(1)}, f32[352,256]{1,0:T(8,128)S(1)}, u32[]{:S(2)}, u32[]{:S(2)}) collective-permute-start(f32[352,256]{1,0:T(8,128)S(1)} %get-tuple-element.108.near_sent), channel_id=1, source_target_pairs={{0,4},{4,0},{8,12},{12,8},{16,20},{20,16},{24,28},{28,24},{1,5},{5... | collective-permute-start | bytes 1081352 | tf_op jit(solution)/shard_map/ppermute | solution.py:555
  41.3 16.6 %collective-permute-start.10 = (f32[352,256]{1,0:T(8,128)S(1)}, f32[352,256]{1,0:T(8,128)S(1)}, u32[]{:S(2)}, u32[]{:S(2)}) collective-permute-start(f32[352,256]{1,0:T(8,128)S(1)} %get-tuple-element.109.far_sent), channel_id=1, source_target_pairs={{4,8},{8,4},{12,16},{16,12},{20,24},{24,20},{5,9},{9,5},{13,17},{1... | collective-permute-start | bytes 1081352 | tf_op jit(solution)/shard_map/ppermute | solution.py:556
  58.7 14.9 %collective-permute-start.11 = (f32[256,256]{1,0:T(8,128)S(1)}, f32[256,256]{1,0:T(8,128)S(1)}, u32[]{:S(2)}, u32[]{:S(2)}) collective-permute-start(f32[256,256]{1,0:T(8,128)S(1)} %get-tuple-element.119.refs_5_), channel_id=1, source_target_pairs={{0,4},{4,0},{8,12},{12,8},{16,20},{20,16},{24,28},{28,24},{1,5},{5... | collective-permute-start | bytes 786440 | tf_op jit(solution)/shard_map/ppermute | solution.py:555
  62.2 11.5 %collective-permute-start.12 = (f32[256,256]{1,0:T(8,128)S(1)}, f32[256,256]{1,0:T(8,128)S(1)}, u32[]{:S(2)}, u32[]{:S(2)}) collective-permute-start(f32[256,256]{1,0:T(8,128)S(1)} %get-tuple-element.120.refs_6_), channel_id=1, source_target_pairs={{4,8},{8,4},{12,16},{16,12},{20,24},{24,20},{5,9},{9,5},{13,17},{1... | collective-permute-start | bytes 786440 | tf_op jit(solution)/shard_map/ppermute | solution.py:556
  74.6 17.0 %collective-permute-start.13 = (f32[288,256]{1,0:T(8,128)S(1)}, f32[288,256]{1,0:T(8,128)S(1)}, u32[]{:S(2)}, u32[]{:S(2)}) collective-permute-start(f32[288,256]{1,0:T(8,128)S(1)} %get-tuple-element.124.near_sent), channel_id=1, source_target_pairs={{0,4},{4,0},{8,12},{12,8},{16,20},{20,16},{24,28},{28,24},{1,5},{5... | collective-permute-start | bytes 884744 | tf_op jit(solution)/shard_map/ppermute | solution.py:555
  77.8 13.8 %collective-permute-start.14 = (f32[288,256]{1,0:T(8,128)S(1)}, f32[288,256]{1,0:T(8,128)S(1)}, u32[]{:S(2)}, u32[]{:S(2)}) collective-permute-start(f32[288,256]{1,0:T(8,128)S(1)} %get-tuple-element.125.far_sent), channel_id=1, source_target_pairs={{4,8},{8,4},{12,16},{16,12},{20,24},{24,20},{5,9},{9,5},{13,17},{1... | collective-permute-start | bytes 884744 | tf_op jit(solution)/shard_map/ppermute | solution.py:556
  92.4 14.6 %collective-permute-start.15 = (f32[256,256]{1,0:T(8,128)S(1)}, f32[256,256]{1,0:T(8,128)S(1)}, u32[]{:S(2)}, u32[]{:S(2)}) collective-permute-start(f32[256,256]{1,0:T(8,128)S(1)} %get-tuple-element.136.refs_5_), channel_id=1, source_target_pairs={{0,4},{4,0},{8,12},{12,8},{16,20},{20,16},{24,28},{28,24},{1,5},{5... | collective-permute-start | bytes 786440 | tf_op jit(solution)/shard_map/ppermute | solution.py:555
  95.5 11.5 %collective-permute-start.16 = (f32[256,256]{1,0:T(8,128)S(1)}, f32[256,256]{1,0:T(8,128)S(1)}, u32[]{:S(2)}, u32[]{:S(2)}) collective-permute-start(f32[256,256]{1,0:T(8,128)S(1)} %get-tuple-element.137.refs_6_), channel_id=1, source_target_pairs={{4,8},{8,4},{12,16},{16,12},{20,24},{24,20},{5,9},{9,5},{13,17},{1... | collective-permute-start | bytes 786440 | tf_op jit(solution)/shard_map/ppermute | solution.py:556
  107.6 14.5 %collective-permute-start.17 = (f32[256,256]{1,0:T(8,128)S(1)}, f32[256,256]{1,0:T(8,128)S(1)}, u32[]{:S(2)}, u32[]{:S(2)}) collective-permute-start(f32[256,256]{1,0:T(8,128)S(1)} %get-tuple-element.140), channel_id=1, source_target_pairs={{4,0},{8,4},{12,8},{16,12},{20,16},{24,20},{28,24},{5,1},{9,5},{13... | collective-permute-start | bytes 786440 | tf_op jit(solution)/shard_map/ppermute | solution.py:725

commit v15 on v14

--- a/solution.py
+++ b/solution.py
@@ -307,13 +307,12 @@
     return values[:, width:] * right - values[:, :width] * left
 
 
-def send_dual(even, inner, faces, for_next, for_prev, near_out, far_out, residual=None,
-              given=None):
+def send_dual(even, inner, faces, for_next, for_prev, near_out, far_out, given=None):
     to_next, to_prev = [faces[0]], [faces[1]]
     count = inner.shape[0]
     if given is not None:
-        to_next += [given[0], outer_rows(for_next, residual[count - 1])]
-        to_prev += [given[1], outer_rows(for_prev, residual[0])]
+        to_next.append(given[0])
+        to_prev.append(given[1])
     to_next.append(outer_rows(for_next, inner[count - 1]))
     to_prev.append(outer_rows(for_prev, inner[0]))
     send(even, to_next, to_prev, near_out, far_out)
@@ -354,7 +353,7 @@
         result[sub] = value
     inner_jump(result, live_own, inner)
     faces = [result[subs - 1][:, width:], result[0][:, :width]]
-    send_dual(even, inner, faces, for_next, for_prev, near_out, far_out, residual, given)
+    send_dual(even, inner, faces, for_next, for_prev, near_out, far_out, given)
 
 
 def sums_kernel(result, inner_z, edge, last_z, residual, sums):
@@ -405,6 +404,12 @@
     partial[1] = curvature
 
 
+def inside_kernel(edge, own, preconditioner, live_own, panel, everyone, block, lift,
+                  inner, result, partial):
+    inner_edges_kernel(edge, own, preconditioner, live_own, inner)
+    inner_dual_kernel(inner, own, panel, everyone, block, lift, result, partial)
+
+
 def cut_edges(even, loads, near, far, near_sent, far_sent, live_first, live_last):
     near, far, near_sent, far_sent = near[:loads], far[:loads], near_sent[:loads], far_sent[:loads]
     first = live_first * jnp.where(even, far - far_sent, near - near_sent)
@@ -469,7 +474,7 @@
 
 
 def first_update_kernel(inner, near, far, near_sent, far_sent, live_edge, live_own, sums,
-                        residual_edge, residual_own, panel, ends,
+                        residual_edge, residual_own, panel, ends, start, own_start,
                         image_own, image_edge, new_edge, new_own,
                         near_out, far_out, scalars, full_ends, outside_image, outside):
     even = even_place()
@@ -482,9 +487,14 @@
     operators = received(even, near, far, loads, rows)
     full_ends[0] = ends[0] + operators[:rows]
     full_ends[1] = ends[1] + operators[rows:]
-    values = received(even, near, far, loads + 2 * rows, rows)
+    values = received(even, near, far, loads + rows, rows)
     outside_image[...] = values
-    outside[...] = received(even, near, far, loads + rows, rows) - alpha * values
+    for end, place in ((0, 0), (1, subs)):
+        part, row = slice(end * rows, (end + 1) * rows), end * (start.shape[0] - rows)
+        operator = jnp.concatenate(split(operators[part]), axis=0)
+        known = start[row : row + rows, :] - own_start[row : row + rows, :]
+        known = known - outer_rows(operator, residual[place])
+        outside[part, :] = known - alpha * values[part]
     alpha_column = column(alpha, width)
     parts = []
     edges = image_edges(even, inner, near, far, near_sent, far_sent, live_edge, live_own)
@@ -609,7 +619,7 @@
 
     face_shape, own_shape = (loads, width), (subs, loads, width)
     scalars_shape, outside_shape, side_shape = (2, loads), (2 * corners, loads), (corners, width)
-    long_shape, longer_shape = (loads + corners, width), (loads + 3 * corners, width)
+    long_shape, longer_shape = (loads + corners, width), (loads + 2 * corners, width)
     edges_shapes = [face_shape, own_shape]
 
     tail = make_tail(counts, rhs)
@@ -652,7 +662,12 @@
         coupling[0], *live, dirichlet,
         kinds=[jnp.bfloat16, jnp.float32],
     )
-    partial, taken, ends = lax.optimization_barrier((partial, taken, ends))
+    (own_start,) = call(
+        early_corner_kernel,
+        [(own, loads)],
+        taken, ends, jnp.zeros(outside_shape, jnp.float32), *residual,
+    )
+    partial, own_start = lax.optimization_barrier((partial, own_start))
 
     edge, first_last, values = call(
         corner_kernel,
@@ -680,17 +695,16 @@
         first_update_kernel,
         [own_shape, face_shape] + edges_shapes
         + [face_shape, face_shape, scalars_shape, (2,) + side_shape, outside_shape, outside_shape],
-        inner, near, far, *sent, *live, sums, *residual, dirichlet, ends,
+        inner, near, far, *sent, *live, sums, *residual, dirichlet, ends, values, own_start,
     )
 
     def inside(residual, outside):
         (values,) = call(early_corner_kernel, [(own, loads)], taken, ends, outside, *residual)
         everyone = lax.all_gather(values, "grp", tiled=True)
-        (inner,) = call(inner_edges_kernel, [inner_shape], *residual, dirichlet, live[1])
-        result, partial = call(
-            inner_dual_kernel,
-            [result_shape, (2,) + face_shape],
-            inner, residual[1], solve, everyone, block, lift,
+        inner, result, partial = call(
+            inside_kernel,
+            [inner_shape, result_shape, (2,) + face_shape],
+            *residual, dirichlet, live[1], solve, everyone, block, lift,
         )
         return result, inner, partial
 

time: 124 us -> 123 us (level)
  blocking collectives: 62.3 us -> 60.9 us
    all_to_all x3, blocking collectives: 41.8 us -> 40.4 us  [from_all(): return lax.all_to_all(copies, ('sub', 'grp'), 0, 0)]
    pallas_call x20 -> x19, Pallas kernels: 18.4 us -> 19.1 us  [call(): pl.pallas_call(kernel, out_shape=[jax.ShapeDtypeStruct(*shape) for shape...]
  transfers between devices with their start and end apart: 18 -> 18, of which waited for: 3 -> 3; matrix products, arithmetic and copies ran while one was open for 0% -> 0% of each run, Pallas kernels for 9% -> 10%
where the time goes in v15:
time: 123 us; the launch traced here: 122 us
  blocking collectives  60.9 us (50%)
  starting transfers between devices  27.5 us (22%)
  Pallas kernels  20.9 us (17%)
  waiting for transfers between devices  7.63 us (6%)
  local copies, waits for them, and re-layouts  4.41 us (4%)
    all_to_all x3, blocking collectives, from_all(): return lax.all_to_all(copies, ('sub', 'grp'), 0, 0)  40.4 us
    pallas_call x19, Pallas kernels, call(): pl.pallas_call(kernel, out_shape=[jax.ShapeDtypeStruct(*shape) for shape...  19.1 us
    ppermute x5, starting transfers between devices, swap(): lax.ppermute(near, 'sub', neighbour_pairs(size, 0))  14.1 us
    all_gather x2, blocking collectives, inside(): everyone = lax.all_gather(values, 'grp', tiled=True)  13.6 us
    ppermute x5, waiting for transfers between devices, swap(): lax.ppermute(near, 'sub', neighbour_pairs(size, 0))  7.6 us
    all_gather x1, blocking collectives, local(): everyone = lax.all_gather(values, 'grp', tiled=True)  6.95 us
    ppermute x1, starting transfers between devices, local(): head = lax.ppermute(tail, 'sub', [(i, i + 1) for i in range(size - 1)])  4.86 us
    unnamed x16, local copies, waits for them, and re-layouts  4.34 us
  transfers between devices with their start and end apart: 18, of which 3 were waited for; matrix products, arithmetic and copies ran while one was open for 0% of the time, Pallas kernels for 10%

profile of v15, /device:TPU:0, one launch (start us, length us, event | category | flops | bytes accessed | tf_op | source)
XLA Modules:
  0.0 122.4 jit_solution(13130385980193491032)
XLA Ops:
  0.6 0.0 copy-start.6
  0.7 1.8 %shard_map.86 = f32[264,256]{1,0:T(8,128)} custom-call(s32[1,4]{1,0:T(1,128)} %counts, f32[1,4,256,256]{3,2,1,0:T(8,128)} %rhs.1), custom_call_target="tpu_custom_call" | custom-call | tf_op jit(solution)/shard_map/pallas_call | solution.py:596
  2.5 4.9 %collective-permute-start = (f32[264,256]{1,0:T(8,128)}, f32[264,256]{1,0:T(8,128)S(1)}, u32[]{:S(2)}, u32[]{:S(2)}) collective-permute-start(f32[264,256]{1,0:T(8,128)} %shard_map.86), channel_id=1, source_target_pairs={{0,4},{4,8},{8,12},{12,16},{16,20},{20,24},{24,28},{1,5},{5,9},{9,... | collective-permute-start | bytes 811016 | tf_op jit(solution)/shard_map/ppermute | solution.py:627
  7.3 0.7 collective-permute-start.3
  8.1 0.9 collective-permute-start.2
  9.0 0.3 collective-permute-start.1
  9.3 1.6 %copy-done = bf16[1,4,512,512]{3,2,1,0:T(8,128)(2,1)S(1)} copy-done((bf16[1,4,512,512]{3,2,1,0:T(8,128)(2,1)S(1)}, bf16[1,4,512,512]{3,2,1,0:T(8,128)(2,1)}, u32[]{:S(2)}) %copy-start) | copy-done | bytes 2097176
  10.9 1.2 copy-done.3
  12.1 0.7 copy-done.7
  12.7 0.4 shard_map.88
  13.2 0.0 collective-permute-done.3.refs_3_
  13.2 0.0 collective-permute-done.2.refs_2_
  13.2 0.0 collective-permute-done.1.refs_1_
  13.2 1.4 %shard_map.87 = (f32[128,512]{1,0:T(8,128)S(1)}, f32[128,512]{1,0:T(8,128)S(1)}, f32[128,512]{1,0:T(8,128)S(1)}, f32[128,512]{1,0:T(8,128)S(1)}, bf16[4,64,512]{...) custom-call(s32[4,32]{1,0:T(4,128)S(1)} %bitcast.31, s32[4,32]{1,0:T(4,128)S(1)} %collective-permute-done.1.refs_1_, ...), custom_call_target="tpu_custom_call" | custom-call | tf_op jit(solution)/shard_map/pallas_call | solution.py:35
  14.7 0.0 collective-permute-done.head
  14.7 0.2 shard_map.89
  14.9 1.6 %collective-permute-start.4 = (f32[288,256]{1,0:T(8,128)S(1)}, f32[288,256]{1,0:T(8,128)S(1)}, u32[]{:S(2)}, u32[]{:S(2)}) collective-permute-start(f32[288,256]{1,0:T(8,128)S(1)} %get-tuple-element.88.near_sent), channel_id=1, source_target_pairs={{0,4},{4,0},{8,12},{12,8},{16,20},{20,16},{24,28},{28,24},{1,5},{5... | collective-permute-start | bytes 884744 | tf_op jit(solution)/shard_map/ppermute | solution.py:565
  16.5 0.7 collective-permute-start.5
  17.2 0.1 collective-permute-start.6
  17.3 1.6 %collective-permute-start.7 = (f32[128,512]{1,0:T(8,128)S(1)}, f32[128,512]{1,0:T(8,128)S(1)}, u32[]{:S(2)}, u32[]{:S(2)}) collective-permute-start(f32[128,512]{1,0:T(8,128)S(1)} %get-tuple-element.100), channel_id=1, source_target_pairs={{0,2},{1,3},{2,0},{3,1},{4,6},{5,7},{6,4},{7,5},{8,10},{9,11},{10,... | collective-permute-start | bytes 786440 | tf_op jit(solution)/shard_map/ppermute | solution.py:590
  18.9 0.3 collective-permute-start.8
  19.2 0.6 shard_map.92
  19.8 1.0 shard_map.90.inner.inner_z.first_inner
  20.8 0.0 copy-start.2
  20.8 0.7 shard_map.93.own_start
  21.5 0.9 copy-done.2
  22.4 1.4 %shard_map.91 = (f32[4,256,512]{2,1,0:T(8,128)S(1)}, f32[128,256]{1,0:T(8,128)S(1)}) custom-call(f32[3,256,256]{2,1,0:T(8,128)S(1)} %shard_map.90.inner.inner_z.first_inner, bf16[4,512,512]{2,1,0:T(8,128)(2,1)S(1)} %bitcast.17, bf16[4,64,512]{2,1,0:T(8,128)(2,1)S(1)} %get-tuple-element.86.coupling), custom_call_target="tpu_custom_call" | custom-call | tf_op jit(solution)/shard_map/pallas_call | solution.py:35
  23.7 5.8 %collective-permute-done.4.near = f32[288,256]{1,0:T(8,128)S(1)} collective-permute-done((f32[288,256]{1,0:T(8,128)S(1)}, f32[288,256]{1,0:T(8,128)S(1)}, u32[]{:S(2)}, u32[]{:S(2)}) %collective-permute-start.4) | collective-permute-done | bytes 294944 | tf_op jit(solution)/shard_map/ppermute | solution.py:565
  29.5 0.0 collective-permute-done.5.far
  29.5 0.3 shard_map.94
  29.9 7.0 %all_gather.9.everyone = f32[512,256]{1,0:T(8,128)S(1)} all-gather(f32[128,256]{1,0:T(8,128)S(1)} %get-tuple-element.97.start), channel_id=1, replica_groups=mesh['sub'=8,'grp'=4] {'grp'}, dimensions={0}, use_global_device_ids=true | all-gather | bytes 655360 | tf_op jit(solution)/shard_map/all_gather | solution.py:677
  36.8 0.0 collective-permute-done.6
  36.8 0.0 collective-permute-done.7
  36.8 0.0 collective-permute-done.8
  36.8 0.1 reduce-precision_convert_fusion
  37.0 1.4 %shard_map.95 = (f32[3,256,256]{2,1,0:T(8,128)S(1)}, f32[320,256]{1,0:T(8,128)S(1)}, f32[320,256]{1,0:T(8,128)S(1)}, f32[4,256,512]{2,1,0:T(8,128)S(1)}, bf16[64...) custom-call(f32[4,256,512]{2,1,0:T(8,128)S(1)} %get-tuple-element.87.before, ...), custom_call_target="tpu_custom_call" | custom-call | tf_op jit(solution)/shard_map/pallas_call | solution.py:35
  38.4 2.8 %collective-permute-start.9 = (f32[320,256]{1,0:T(8,128)S(1)}, f32[320,256]{1,0:T(8,128)S(1)}, u32[]{:S(2)}, u32[]{:S(2)}) collective-permute-start(f32[320,256]{1,0:T(8,128)S(1)} %get-tuple-element.109.near_sent), channel_id=1, source_target_pairs={{0,4},{4,0},{8,12},{12,8},{16,20},{20,16},{24,28},{28,24},{1,5},{5... | collective-permute-start | bytes 983048 | tf_op jit(solution)/shard_map/ppermute | solution.py:565
  41.2 0.7 collective-permute-start.10
  41.9 0.3 shard_map.96
  42.2 14.2 %all_to_all.15.sums = f32[32,2,256]{2,1,0:T(2,128)S(1)} all-to-all(f32[32,2,256]{2,1,0:T(2,128)S(1)} %broadcast_in_dim.13), channel_id=1, replica_groups=mesh['sub'=8,'grp'=4] {'sub','grp'}, dimensions={0} | all-to-all | bytes 131072 | tf_op jit(solution)/shard_map/all_to_all | solution.py:573
  56.4 0.0 collective-permute-done.9.near
  56.4 0.0 collective-permute-done.10.far
  56.4 0.9 shard_map.97
  57.3 3.5 %collective-permute-start.11 = (f32[256,256]{1,0:T(8,128)S(1)}, f32[256,256]{1,0:T(8,128)S(1)}, u32[]{:S(2)}, u32[]{:S(2)}) collective-permute-start(f32[256,256]{1,0:T(8,128)S(1)} %get-tuple-element.120.refs_5_), channel_id=1, source_target_pairs={{0,4},{4,0},{8,12},{12,8},{16,20},{20,16},{24,28},{28,24},{1,5},{5... | collective-permute-start | bytes 786440 | tf_op jit(solution)/shard_map/ppermute | solution.py:565
  60.8 0.7 collective-permute-start.12
  61.4 0.7 shard_map.98
  62.2 6.8 %all_gather.10.everyone = f32[512,256]{1,0:T(8,128)S(1)} all-gather(f32[128,256]{1,0:T(8,128)S(1)} %shard_map.98), channel_id=1, replica_groups=mesh['sub'=8,'grp'=4] {'grp'}, dimensions={0}, use_global_device_ids=true | all-gather | bytes 655360 | tf_op jit(solution)/shard_map/all_gather | solution.py:703
  69.0 2.4 %shard_map.99 = (f32[3,256,256]{2,1,0:T(8,128)S(1)}, f32[4,256,512]{2,1,0:T(8,128)S(1)}, f32[2,256,256]{2,1,0:T(8,128)S(1)}) custom-call(f32[256,256]{1,0:T(8,128)S(1)} %get-tuple-element.113.edge.residual_edge, f32[4,256,256]{2,1,0:T(8,128)S(1)} %get-tuple-element.114.own.refs_9_.residual_own, bf16[4,512,512]{2,1,0:T(8,128)(2,1)S(1)} %bitcast.14, ...), custom_call_target="tpu_custom_call" | custom-call | tf_op jit(solution)/shard_map/pallas_call | solution.py:35
  71.3 0.9 collective-permute-done.11.refs_3_
  72.2 0.9 shard_map.100
  73.1 3.1 %collective-permute-start.13 = (f32[288,256]{1,0:T(8,128)S(1)}, f32[288,256]{1,0:T(8,128)S(1)}, u32[]{:S(2)}, u32[]{:S(2)}) collective-permute-start(f32[288,256]{1,0:T(8,128)S(1)} %get-tuple-element.125.near_sent), channel_id=1, source_target_pairs={{0,4},{4,0},{8,12},{12,8},{16,20},{20,16},{24,28},{28,24},{1,5},{5... | collective-permute-start | bytes 884744 | tf_op jit(solution)/shard_map/ppermute | solution.py:565
  76.3 0.7 collective-permute-start.14
  77.0 13.1 %all_to_all.16.sums = f32[32,2,256]{2,1,0:T(2,128)S(1)} all-to-all(f32[32,2,256]{2,1,0:T(2,128)S(1)} %broadcast_in_dim.14), channel_id=1, replica_groups=mesh['sub'=8,'grp'=4] {'sub','grp'}, dimensions={0} | all-to-all | bytes 131072 | tf_op jit(solution)/shard_map/all_to_all | solution.py:573
  90.1 0.8 shard_map.101
  90.9 3.1 %collective-permute-start.15 = (f32[256,256]{1,0:T(8,128)S(1)}, f32[256,256]{1,0:T(8,128)S(1)}, u32[]{:S(2)}, u32[]{:S(2)}) collective-permute-start(f32[256,256]{1,0:T(8,128)S(1)} %get-tuple-element.138.refs_5_), channel_id=1, source_target_pairs={{0,4},{4,0},{8,12},{12,8},{16,20},{20,16},{24,28},{28,24},{1,5},{5... | collective-permute-start | bytes 786440 | tf_op jit(solution)/shard_map/ppermute | solution.py:565
  94.1 0.7 collective-permute-start.16
  94.7 0.7 shard_map.102
  95.5 6.8 %all_gather.11.everyone = f32[512,256]{1,0:T(8,128)S(1)} all-gather(f32[128,256]{1,0:T(8,128)S(1)} %shard_map.102), channel_id=1, replica_groups=mesh['sub'=8,'grp'=4] {'grp'}, dimensions={0}, use_global_device_ids=true | all-gather | bytes 655360 | tf_op jit(solution)/shard_map/all_gather | solution.py:703
  102.3 2.4 %shard_map.103 = (f32[3,256,256]{2,1,0:T(8,128)S(1)}, f32[4,256,512]{2,1,0:T(8,128)S(1)}, f32[2,256,256]{2,1,0:T(8,128)S(1)}) custom-call(f32[256,256]{1,0:T(8,128)S(1)} %get-tuple-element.132.edge, f32[4,256,256]{2,1,0:T(8,128)S(1)} %get-tuple-element.133.own.refs_9_.residual, bf16[4,512,512]{2,1,0:T(8,128)(2,1)S(1)} %bitcast.16, ...), custom_call_target="tpu_custom_call" | custom-call | tf_op jit(solution)/shard_map/pallas_call | solution.py:35
  104.7 0.9 collective-permute-done.15.refs_3_
  105.5 0.6 shard_map.104
  106.2 1.3 %collective-permute-start.17 = (f32[256,256]{1,0:T(8,128)S(1)}, f32[256,256]{1,0:T(8,128)S(1)}, u32[]{:S(2)}, u32[]{:S(2)}) collective-permute-start(f32[256,256]{1,0:T(8,128)S(1)} %get-tuple-element.142), channel_id=1, source_target_pairs={{4,0},{8,4},{12,8},{16,12},{20,16},{24,20},{28,24},{5,1},{9,5},{13... | collective-permute-start | bytes 786440 | tf_op jit(solution)/shard_map/ppermute | solution.py:739
  107.5 13.1 %all_to_all.17.sums = f32[32,2,256]{2,1,0:T(2,128)S(1)} all-to-all(f32[32,2,256]{2,1,0:T(2,128)S(1)} %broadcast_in_dim.30), channel_id=1, replica_groups=mesh['sub'=8,'grp'=4] {'sub','grp'}, dimensions={0} | all-to-all | bytes 131072 | tf_op jit(solution)/shard_map/all_to_all | solution.py:573
  120.6 1.8 %shard_map.105 = (f32[4,256,256]{2,1,0:T(8,128)}, f32[4,256,256]{2,1,0:T(8,128)}) custom-call(f32[3,256,256]{2,1,0:T(8,128)S(1)} %get-tuple-element.140.inner, f32[256,256]{1,0:T(8,128)S(1)} %get-tuple-element.141.to_next, f32[256,256]{1,0:T(8,128)S(1)} %collective-permute-done.17.following, f32[4,1,256]{2,1,0:T(1,128)S(1)} %get-tuple-element.85.live_own.refs_8_.live, ...), custom_call_target="tpu_custom_call" | custom-call | tf_op jit(solution)/shard_map/pallas_call | solution.py:35
  (21 shorter events, 0.1 us)
Async XLA Ops:
  0.6 12.6 %copy-start.6 = (s32[1,4,32]{2,1,0:T(4,128)S(1)}, s32[1,4,32]{2,1,0:T(4,128)}, u32[]{:S(2)}) copy-start(s32[1,4,32]{2,1,0:T(4,128)} %param.12) | copy-start | bytes 1540
  0.6 12.6 %copy-start.5 = (f32[1,256,1024]{2,1,0:T(8,128)S(1)}, f32[1,256,1024]{2,1,0:T(8,128)}, u32[]{:S(2)}) copy-start(f32[1,256,1024]{2,1,0:T(8,128)} %param.13) | copy-start | bytes 3145732
  0.7 12.6 %copy-start.4 = (f32[1,4,32,512]{3,2,1,0:T(8,128)S(1)}, f32[1,4,32,512]{3,2,1,0:T(8,128)}, u32[]{:S(2)}) copy-start(f32[1,4,32,512]{3,2,1,0:T(8,128)} %param.11) | copy-start | bytes 786436
  2.5 12.2 %collective-permute-start = (f32[264,256]{1,0:T(8,128)}, f32[264,256]{1,0:T(8,128)S(1)}, u32[]{:S(2)}, u32[]{:S(2)}) collective-permute-start(f32[264,256]{1,0:T(8,128)} %shard_map.86), channel_id=1, source_target_pairs={{0,4},{4,8},{8,12},{12,16},{16,20},{20,24},{24,28},{1,5},{5,9},{9,... | collective-permute-start | bytes 811016 | tf_op jit(solution)/shard_map/ppermute | solution.py:627
  7.3 5.8 %collective-permute-start.3 = (s32[4,32]{1,0:T(4,128)}, s32[4,32]{1,0:T(4,128)S(1)}, u32[]{:S(2)}, u32[]{:S(2)}) collective-permute-start(s32[4,32]{1,0:T(4,128)} %bitcast.28), channel_id=1, source_target_pairs={{0,3},{1,2},{2,1},{3,0},{4,7},{5,6},{6,5},{7,4},{8,11},{9,10},{10,... | collective-permute-start | bytes 1544 | tf_op jit(solution)/shard_map/ppermute | solution.py:581
  8.1 5.1 %collective-permute-start.2 = (s32[4,32]{1,0:T(4,128)}, s32[4,32]{1,0:T(4,128)S(1)}, u32[]{:S(2)}, u32[]{:S(2)}) collective-permute-start(s32[4,32]{1,0:T(4,128)} %bitcast.29), channel_id=1, source_target_pairs={{0,2},{1,3},{2,0},{3,1},{4,6},{5,7},{6,4},{7,5},{8,10},{9,11},{10,... | collective-permute-start | bytes 1544 | tf_op jit(solution)/shard_map/ppermute | solution.py:581
  9.0 4.2 %collective-permute-start.1 = (s32[4,32]{1,0:T(4,128)}, s32[4,32]{1,0:T(4,128)S(1)}, u32[]{:S(2)}, u32[]{:S(2)}) collective-permute-start(s32[4,32]{1,0:T(4,128)} %bitcast.30), channel_id=1, source_target_pairs={{0,1},{1,0},{2,3},{3,2},{4,5},{5,4},{6,7},{7,6},{8,9},{9,8},{10,11... | collective-permute-start | bytes 1544 | tf_op jit(solution)/shard_map/ppermute | solution.py:581
  9.3 1.6 %copy-start = (bf16[1,4,512,512]{3,2,1,0:T(8,128)(2,1)S(1)}, bf16[1,4,512,512]{3,2,1,0:T(8,128)(2,1)}, u32[]{:S(2)}) copy-start(bf16[1,4,512,512]{3,2,1,0:T(8,128)(2,1)} %param.10) | copy-start | bytes 6291460
  10.9 1.2 %copy-start.3 = (f32[1,4,256,256]{3,2,1,0:T(8,128)S(1)}, f32[1,4,256,256]{3,2,1,0:T(8,128)}, u32[]{:S(2)}) copy-start(f32[1,4,256,256]{3,2,1,0:T(8,128)} %rhs.1) | copy-start | bytes 3145732
  12.1 0.7 copy-start.7
  12.7 1.9 %copy-start.1 = (bf16[1,4,512,512]{3,2,1,0:T(8,128)(2,1)S(1)}, bf16[1,4,512,512]{3,2,1,0:T(8,128)(2,1)}, u32[]{:S(2)}) copy-start(bf16[1,4,512,512]{3,2,1,0:T(8,128)(2,1)} %param.10) | copy-start | bytes 6291460
  14.9 14.6 %collective-permute-start.4 = (f32[288,256]{1,0:T(8,128)S(1)}, f32[288,256]{1,0:T(8,128)S(1)}, u32[]{:S(2)}, u32[]{:S(2)}) collective-permute-start(f32[288,256]{1,0:T(8,128)S(1)} %get-tuple-element.88.near_sent), channel_id=1, source_target_pairs={{0,4},{4,0},{8,12},{12,8},{16,20},{20,16},{24,28},{28,24},{1,5},{5... | collective-permute-start | bytes 884744 | tf_op jit(solution)/shard_map/ppermute | solution.py:565
  16.5 13.0 %collective-permute-start.5 = (f32[288,256]{1,0:T(8,128)S(1)}, f32[288,256]{1,0:T(8,128)S(1)}, u32[]{:S(2)}, u32[]{:S(2)}) collective-permute-start(f32[288,256]{1,0:T(8,128)S(1)} %get-tuple-element.89.far_sent), channel_id=1, source_target_pairs={{4,8},{8,4},{12,16},{16,12},{20,24},{24,20},{5,9},{9,5},{13,17},{1... | collective-permute-start | bytes 884744 | tf_op jit(solution)/shard_map/ppermute | solution.py:566
  17.2 19.6 %collective-permute-start.6 = (f32[128,512]{1,0:T(8,128)S(1)}, f32[128,512]{1,0:T(8,128)S(1)}, u32[]{:S(2)}, u32[]{:S(2)}) collective-permute-start(f32[128,512]{1,0:T(8,128)S(1)} %get-tuple-element.99), channel_id=1, source_target_pairs={{0,1},{1,0},{2,3},{3,2},{4,5},{5,4},{6,7},{7,6},{8,9},{9,8},{10,11... | collective-permute-start | bytes 786440 | tf_op jit(solution)/shard_map/ppermute | solution.py:590
  17.3 19.5 %collective-permute-start.7 = (f32[128,512]{1,0:T(8,128)S(1)}, f32[128,512]{1,0:T(8,128)S(1)}, u32[]{:S(2)}, u32[]{:S(2)}) collective-permute-start(f32[128,512]{1,0:T(8,128)S(1)} %get-tuple-element.100), channel_id=1, source_target_pairs={{0,2},{1,3},{2,0},{3,1},{4,6},{5,7},{6,4},{7,5},{8,10},{9,11},{10,... | collective-permute-start | bytes 786440 | tf_op jit(solution)/shard_map/ppermute | solution.py:590
  18.9 17.9 %collective-permute-start.8 = (f32[128,512]{1,0:T(8,128)S(1)}, f32[128,512]{1,0:T(8,128)S(1)}, u32[]{:S(2)}, u32[]{:S(2)}) collective-permute-start(f32[128,512]{1,0:T(8,128)S(1)} %get-tuple-element.101), channel_id=1, source_target_pairs={{0,3},{1,2},{2,1},{3,0},{4,7},{5,6},{6,5},{7,4},{8,11},{9,10},{10,... | collective-permute-start | bytes 786440 | tf_op jit(solution)/shard_map/ppermute | solution.py:590
  20.8 1.6 %copy-start.2 = (bf16[1,4,512,512]{3,2,1,0:T(8,128)(2,1)S(1)}, bf16[1,4,512,512]{3,2,1,0:T(8,128)(2,1)}, u32[]{:S(2)}) copy-start(bf16[1,4,512,512]{3,2,1,0:T(8,128)(2,1)} %param.9) | copy-start | bytes 6291460
  38.4 18.0 %collective-permute-start.9 = (f32[320,256]{1,0:T(8,128)S(1)}, f32[320,256]{1,0:T(8,128)S(1)}, u32[]{:S(2)}, u32[]{:S(2)}) collective-permute-start(f32[320,256]{1,0:T(8,128)S(1)} %get-tuple-element.109.near_sent), channel_id=1, source_target_pairs={{0,4},{4,0},{8,12},{12,8},{16,20},{20,16},{24,28},{28,24},{1,5},{5... | collective-permute-start | bytes 983048 | tf_op jit(solution)/shard_map/ppermute | solution.py:565
  41.2 15.2 %collective-permute-start.10 = (f32[320,256]{1,0:T(8,128)S(1)}, f32[320,256]{1,0:T(8,128)S(1)}, u32[]{:S(2)}, u32[]{:S(2)}) collective-permute-start(f32[320,256]{1,0:T(8,128)S(1)} %get-tuple-element.110.far_sent), channel_id=1, source_target_pairs={{4,8},{8,4},{12,16},{16,12},{20,24},{24,20},{5,9},{9,5},{13,17},{1... | collective-permute-start | bytes 983048 | tf_op jit(solution)/shard_map/ppermute | solution.py:566
  57.3 14.9 %collective-permute-start.11 = (f32[256,256]{1,0:T(8,128)S(1)}, f32[256,256]{1,0:T(8,128)S(1)}, u32[]{:S(2)}, u32[]{:S(2)}) collective-permute-start(f32[256,256]{1,0:T(8,128)S(1)} %get-tuple-element.120.refs_5_), channel_id=1, source_target_pairs={{0,4},{4,0},{8,12},{12,8},{16,20},{20,16},{24,28},{28,24},{1,5},{5... | collective-permute-start | bytes 786440 | tf_op jit(solution)/shard_map/ppermute | solution.py:565
  60.8 11.5 %collective-permute-start.12 = (f32[256,256]{1,0:T(8,128)S(1)}, f32[256,256]{1,0:T(8,128)S(1)}, u32[]{:S(2)}, u32[]{:S(2)}) collective-permute-start(f32[256,256]{1,0:T(8,128)S(1)} %get-tuple-element.121.refs_6_), channel_id=1, source_target_pairs={{4,8},{8,4},{12,16},{16,12},{20,24},{24,20},{5,9},{9,5},{13,17},{1... | collective-permute-start | bytes 786440 | tf_op jit(solution)/shard_map/ppermute | solution.py:566
  73.1 16.9 %collective-permute-start.13 = (f32[288,256]{1,0:T(8,128)S(1)}, f32[288,256]{1,0:T(8,128)S(1)}, u32[]{:S(2)}, u32[]{:S(2)}) collective-permute-start(f32[288,256]{1,0:T(8,128)S(1)} %get-tuple-element.125.near_sent), channel_id=1, source_target_pairs={{0,4},{4,0},{8,12},{12,8},{16,20},{20,16},{24,28},{28,24},{1,5},{5... | collective-permute-start | bytes 884744 | tf_op jit(solution)/shard_map/ppermute | solution.py:565
  76.3 13.8 %collective-permute-start.14 = (f32[288,256]{1,0:T(8,128)S(1)}, f32[288,256]{1,0:T(8,128)S(1)}, u32[]{:S(2)}, u32[]{:S(2)}) collective-permute-start(f32[288,256]{1,0:T(8,128)S(1)} %get-tuple-element.126.far_sent), channel_id=1, source_target_pairs={{4,8},{8,4},{12,16},{16,12},{20,24},{24,20},{5,9},{9,5},{13,17},{1... | collective-permute-start | bytes 884744 | tf_op jit(solution)/shard_map/ppermute | solution.py:566
  90.9 14.6 %collective-permute-start.15 = (f32[256,256]{1,0:T(8,128)S(1)}, f32[256,256]{1,0:T(8,128)S(1)}, u32[]{:S(2)}, u32[]{:S(2)}) collective-permute-start(f32[256,256]{1,0:T(8,128)S(1)} %get-tuple-element.138.refs_5_), channel_id=1, source_target_pairs={{0,4},{4,0},{8,12},{12,8},{16,20},{20,16},{24,28},{28,24},{1,5},{5... | collective-permute-start | bytes 786440 | tf_op jit(solution)/shard_map/ppermute | solution.py:565
  94.1 11.5 %collective-permute-start.16 = (f32[256,256]{1,0:T(8,128)S(1)}, f32[256,256]{1,0:T(8,128)S(1)}, u32[]{:S(2)}, u32[]{:S(2)}) collective-permute-start(f32[256,256]{1,0:T(8,128)S(1)} %get-tuple-element.139.refs_6_), channel_id=1, source_target_pairs={{4,8},{8,4},{12,16},{16,12},{20,24},{24,20},{5,9},{9,5},{13,17},{1... | collective-permute-start | bytes 786440 | tf_op jit(solution)/shard_map/ppermute | solution.py:566
  106.2 14.5 %collective-permute-start.17 = (f32[256,256]{1,0:T(8,128)S(1)}, f32[256,256]{1,0:T(8,128)S(1)}, u32[]{:S(2)}, u32[]{:S(2)}) collective-permute-start(f32[256,256]{1,0:T(8,128)S(1)} %get-tuple-element.142), channel_id=1, source_target_pairs={{4,0},{8,4},{12,8},{16,12},{20,16},{24,20},{28,24},{5,1},{9,5},{13... | collective-permute-start | bytes 786440 | tf_op jit(solution)/shard_map/ppermute | solution.py:739

commit v16 on v15

--- a/solution.py
+++ b/solution.py
@@ -116,7 +116,7 @@
     tail[:loads] = mask[:1] * face[...]
 
 
-def early_kernel(counts, rhs, panel, live, own, to_next, partial):
+def early_kernel(counts, rhs, last_panel, first_panel, live, own, to_next, partial):
     subs, loads, width = own.shape
     parts = []
     for sub in range(subs):
@@ -126,18 +126,18 @@
         parts.append(split(own[sub]))
     high = jnp.concatenate([-parts[subs - 2][0], parts[subs - 1][0]], axis=1)
     low = jnp.concatenate([-parts[subs - 2][1], parts[subs - 1][1]], axis=1)
-    to_next[...] = mul(high, panel[subs - 1, :, width:]) + mul(low, panel[subs - 1, :, width:])
+    to_next[...] = mul(high, last_panel[...]) + mul(low, last_panel[...])
     high, low = parts[0]
-    partial[...] = mul(high, panel[0, width:, :width]) + mul(low, panel[0, width:, :width])
-
-
-def head_kernel(head, to_next, partial, panel, coupling, live, edge, near_out, far_out):
+    partial[...] = mul(high, first_panel[width:]) + mul(low, first_panel[width:])
+
+
+def head_kernel(head, to_next, partial, first_panel, coupling, live, edge, near_out, far_out):
     loads, width = edge.shape
     live[...] = head[loads : loads + 1]
     edge[...] = head[:loads]
     high, low = split(head[:loads])
     to_prev = partial[...] - (
-        mul(high, panel[0, :width, :width]) + mul(low, panel[0, :width, :width])
+        mul(high, first_panel[:width]) + mul(low, first_panel[:width])
     )
     ahead = [to_next[...], coupling[coupling.shape[0] - 1, :, width:]]
     send(even_place(), ahead, [to_prev, coupling[0, :, :width]], near_out, far_out)
@@ -629,7 +629,7 @@
     live_own, residual_own, to_next, partial = call(
         early_kernel,
         [(subs, 1, width), own_shape, face_shape, face_shape],
-        counts, rhs[0], dirichlet,
+        counts, rhs[0], dirichlet[subs - 1, :, width:], dirichlet[0, :, :width],
     )
     group, own = len(maps), subs * corners
     pair = [(corners, width)] * 2
@@ -645,7 +645,7 @@
     live_edge, residual_edge, near, far = call(
         head_kernel,
         [(1, width), face_shape, long_shape, long_shape],
-        head, to_next, partial, dirichlet, coupling[0],
+        head, to_next, partial, dirichlet[0, :, :width], coupling[0],
     )
     live, residual = (live_edge, live_own), (residual_edge, residual_own)
     sent = near, far

time: 123 us -> 123 us (level)
  local copies, waits for them, and re-layouts: 4.41 us -> 2 us
  starting transfers between devices: 27.5 us -> 29.4 us
    unnamed x16 -> x14, local copies, waits for them, and re-layouts: 4.34 us -> 0.87 us
    ppermute x5, starting transfers between devices: 14.1 us -> 16 us  [swap(): lax.ppermute(near, 'sub', neighbour_pairs(size, 0))]
  transfers between devices with their start and end apart: 18 -> 18, of which waited for: 3 -> 4; matrix products, arithmetic and copies ran while one was open for 0% -> 1% of each run, Pallas kernels for 10% -> 10%
where the time goes in v16:
time: 123 us; the launch traced here: 122 us
  blocking collectives  61.1 us (50%)
  starting transfers between devices  29.4 us (24%)
  Pallas kernels  20.8 us (17%)
  waiting for transfers between devices  7.74 us (6%)
  local copies, waits for them, and re-layouts  2 us (2%)
    all_to_all x3, blocking collectives, from_all(): return lax.all_to_all(copies, ('sub', 'grp'), 0, 0)  40.6 us
    pallas_call x19, Pallas kernels, call(): pl.pallas_call(kernel, out_shape=[jax.ShapeDtypeStruct(*shape) for shape...  19 us
    ppermute x5, starting transfers between devices, swap(): lax.ppermute(near, 'sub', neighbour_pairs(size, 0))  16 us
    all_gather x2, blocking collectives, inside(): everyone = lax.all_gather(values, 'grp', tiled=True)  13.6 us
    all_gather x1, blocking collectives, local(): everyone = lax.all_gather(values, 'grp', tiled=True)  6.92 us
    ppermute x5, waiting for transfers between devices, swap(): lax.ppermute(near, 'sub', neighbour_pairs(size, 0))  6.62 us
    ppermute x1, starting transfers between devices, local(): head = lax.ppermute(tail, 'sub', [(i, i + 1) for i in range(size - 1)])  4.99 us
    ppermute x5, starting transfers between devices, swap(): lax.ppermute(far, 'sub', neighbour_pairs(size, 1))  3.33 us
  transfers between devices with their start and end apart: 18, of which 4 were waited for; matrix products, arithmetic and copies ran while one was open for 1% of the time, Pallas kernels for 10%

profile of v16, /device:TPU:0, one launch (start us, length us, event | category | flops | bytes accessed | tf_op | source)
XLA Modules:
  0.0 122.2 jit_solution(3024169194509692617)
XLA Ops:
  0.6 0.0 copy-start.5
  0.7 1.8 %shard_map.86 = f32[264,256]{1,0:T(8,128)} custom-call(s32[1,4]{1,0:T(1,128)} %counts, f32[1,4,256,256]{3,2,1,0:T(8,128)} %rhs.1), custom_call_target="tpu_custom_call" | custom-call | tf_op jit(solution)/shard_map/pallas_call | solution.py:596
  2.5 0.0 copy-start.4
  2.5 5.0 %collective-permute-start = (f32[264,256]{1,0:T(8,128)}, f32[264,256]{1,0:T(8,128)S(1)}, u32[]{:S(2)}, u32[]{:S(2)}) collective-permute-start(f32[264,256]{1,0:T(8,128)} %shard_map.86), channel_id=1, source_target_pairs={{0,4},{4,8},{8,12},{12,16},{16,20},{20,24},{24,28},{1,5},{5,9},{9,... | collective-permute-start | bytes 811016 | tf_op jit(solution)/shard_map/ppermute | solution.py:627
  7.5 0.7 collective-permute-start.3
  8.2 0.9 collective-permute-start.2
  9.2 0.3 collective-permute-start.1
  9.4 1.1 slice_bitcast_fusion
  10.5 0.0 copy-start
  10.5 0.4 shard_map.88
  11.0 0.0 collective-permute-done.3.refs_3_
  11.0 1.1 collective-permute-done.2.refs_2_
  12.0 0.0 collective-permute-done.1.refs_1_
  12.1 1.4 %shard_map.87 = (f32[128,512]{1,0:T(8,128)S(1)}, f32[128,512]{1,0:T(8,128)S(1)}, f32[128,512]{1,0:T(8,128)S(1)}, f32[128,512]{1,0:T(8,128)S(1)}, bf16[4,64,512]{...) custom-call(s32[4,32]{1,0:T(4,128)S(1)} %bitcast.34, s32[4,32]{1,0:T(4,128)S(1)} %collective-permute-done.1.refs_1_, ...), custom_call_target="tpu_custom_call" | custom-call | tf_op jit(solution)/shard_map/pallas_call | solution.py:35
  13.5 0.0 collective-permute-done.head
  13.5 0.2 shard_map.89
  13.8 2.4 %collective-permute-start.4 = (f32[288,256]{1,0:T(8,128)S(1)}, f32[288,256]{1,0:T(8,128)S(1)}, u32[]{:S(2)}, u32[]{:S(2)}) collective-permute-start(f32[288,256]{1,0:T(8,128)S(1)} %get-tuple-element.88.near_sent), channel_id=1, source_target_pairs={{0,4},{4,0},{8,12},{12,8},{16,20},{20,16},{24,28},{28,24},{1,5},{5... | collective-permute-start | bytes 884744 | tf_op jit(solution)/shard_map/ppermute | solution.py:565
  16.2 0.7 collective-permute-start.5
  16.9 0.1 collective-permute-start.6
  17.0 1.6 %collective-permute-start.7 = (f32[128,512]{1,0:T(8,128)S(1)}, f32[128,512]{1,0:T(8,128)S(1)}, u32[]{:S(2)}, u32[]{:S(2)}) collective-permute-start(f32[128,512]{1,0:T(8,128)S(1)} %get-tuple-element.100), channel_id=1, source_target_pairs={{0,2},{1,3},{2,0},{3,1},{4,6},{5,7},{6,4},{7,5},{8,10},{9,11},{10,... | collective-permute-start | bytes 786440 | tf_op jit(solution)/shard_map/ppermute | solution.py:590
  18.5 0.3 collective-permute-start.8
  18.8 0.6 shard_map.92
  19.4 1.0 shard_map.90.inner.inner_z.first_inner
  20.4 0.0 copy-start.1
  20.5 0.7 shard_map.93.own_start
  21.2 0.8 copy-done.1
  22.0 1.4 %shard_map.91 = (f32[4,256,512]{2,1,0:T(8,128)S(1)}, f32[128,256]{1,0:T(8,128)S(1)}) custom-call(f32[3,256,256]{2,1,0:T(8,128)S(1)} %shard_map.90.inner.inner_z.first_inner, bf16[4,512,512]{2,1,0:T(8,128)(2,1)S(1)} %bitcast.20, bf16[4,64,512]{2,1,0:T(8,128)(2,1)S(1)} %get-tuple-element.86.coupling), custom_call_target="tpu_custom_call" | custom-call | tf_op jit(solution)/shard_map/pallas_call | solution.py:35
  23.4 4.8 %collective-permute-done.4.near = f32[288,256]{1,0:T(8,128)S(1)} collective-permute-done((f32[288,256]{1,0:T(8,128)S(1)}, f32[288,256]{1,0:T(8,128)S(1)}, u32[]{:S(2)}, u32[]{:S(2)}) %collective-permute-start.4) | collective-permute-done | bytes 294944 | tf_op jit(solution)/shard_map/ppermute | solution.py:565
  28.2 0.3 shard_map.94
  28.5 6.9 %all_gather.9.everyone = f32[512,256]{1,0:T(8,128)S(1)} all-gather(f32[128,256]{1,0:T(8,128)S(1)} %get-tuple-element.97.start), channel_id=1, replica_groups=mesh['sub'=8,'grp'=4] {'grp'}, dimensions={0}, use_global_device_ids=true | all-gather | bytes 655360 | tf_op jit(solution)/shard_map/all_gather | solution.py:677
  35.4 0.0 collective-permute-done.6
  35.4 0.0 collective-permute-done.7
  35.4 0.0 collective-permute-done.8
  35.4 0.1 reduce-precision_convert_fusion
  35.6 1.4 %shard_map.95 = (f32[3,256,256]{2,1,0:T(8,128)S(1)}, f32[320,256]{1,0:T(8,128)S(1)}, f32[320,256]{1,0:T(8,128)S(1)}, f32[4,256,512]{2,1,0:T(8,128)S(1)}, bf16[64...) custom-call(f32[4,256,512]{2,1,0:T(8,128)S(1)} %get-tuple-element.87.before, ...), custom_call_target="tpu_custom_call" | custom-call | tf_op jit(solution)/shard_map/pallas_call | solution.py:35
  37.0 3.8 %collective-permute-start.9 = (f32[320,256]{1,0:T(8,128)S(1)}, f32[320,256]{1,0:T(8,128)S(1)}, u32[]{:S(2)}, u32[]{:S(2)}) collective-permute-start(f32[320,256]{1,0:T(8,128)S(1)} %get-tuple-element.109.near_sent), channel_id=1, source_target_pairs={{0,4},{4,0},{8,12},{12,8},{16,20},{20,16},{24,28},{28,24},{1,5},{5... | collective-permute-start | bytes 983048 | tf_op jit(solution)/shard_map/ppermute | solution.py:565
  40.9 0.7 collective-permute-start.10
  41.5 0.4 shard_map.96
  42.0 14.1 %all_to_all.15.sums = f32[32,2,256]{2,1,0:T(2,128)S(1)} all-to-all(f32[32,2,256]{2,1,0:T(2,128)S(1)} %broadcast_in_dim.13), channel_id=1, replica_groups=mesh['sub'=8,'grp'=4] {'sub','grp'}, dimensions={0} | all-to-all | bytes 131072 | tf_op jit(solution)/shard_map/all_to_all | solution.py:573
  56.1 0.0 collective-permute-done.10.far
  56.1 0.9 shard_map.97
  57.0 3.5 %collective-permute-start.11 = (f32[256,256]{1,0:T(8,128)S(1)}, f32[256,256]{1,0:T(8,128)S(1)}, u32[]{:S(2)}, u32[]{:S(2)}) collective-permute-start(f32[256,256]{1,0:T(8,128)S(1)} %get-tuple-element.120.refs_5_), channel_id=1, source_target_pairs={{0,4},{4,0},{8,12},{12,8},{16,20},{20,16},{24,28},{28,24},{1,5},{5... | collective-permute-start | bytes 786440 | tf_op jit(solution)/shard_map/ppermute | solution.py:565
  60.4 0.7 collective-permute-start.12
  61.1 0.7 shard_map.98
  61.8 6.8 %all_gather.10.everyone = f32[512,256]{1,0:T(8,128)S(1)} all-gather(f32[128,256]{1,0:T(8,128)S(1)} %shard_map.98), channel_id=1, replica_groups=mesh['sub'=8,'grp'=4] {'grp'}, dimensions={0}, use_global_device_ids=true | all-gather | bytes 655360 | tf_op jit(solution)/shard_map/all_gather | solution.py:703
  68.6 2.4 %shard_map.99 = (f32[3,256,256]{2,1,0:T(8,128)S(1)}, f32[4,256,512]{2,1,0:T(8,128)S(1)}, f32[2,256,256]{2,1,0:T(8,128)S(1)}) custom-call(f32[256,256]{1,0:T(8,128)S(1)} %get-tuple-element.113.edge.residual_edge, f32[4,256,256]{2,1,0:T(8,128)S(1)} %get-tuple-element.114.own.refs_9_.residual_own, bf16[4,512,512]{2,1,0:T(8,128)(2,1)S(1)} %bitcast.17, ...), custom_call_target="tpu_custom_call" | custom-call | tf_op jit(solution)/shard_map/pallas_call | solution.py:35
  71.0 0.9 collective-permute-done.11.refs_3_
  71.9 0.0 collective-permute-done.12.refs_4_
  71.9 0.9 shard_map.100
  72.7 3.1 %collective-permute-start.13 = (f32[288,256]{1,0:T(8,128)S(1)}, f32[288,256]{1,0:T(8,128)S(1)}, u32[]{:S(2)}, u32[]{:S(2)}) collective-permute-start(f32[288,256]{1,0:T(8,128)S(1)} %get-tuple-element.125.near_sent), channel_id=1, source_target_pairs={{0,4},{4,0},{8,12},{12,8},{16,20},{20,16},{24,28},{28,24},{1,5},{5... | collective-permute-start | bytes 884744 | tf_op jit(solution)/shard_map/ppermute | solution.py:565
  75.9 0.7 collective-permute-start.14
  76.6 13.1 %all_to_all.16.sums = f32[32,2,256]{2,1,0:T(2,128)S(1)} all-to-all(f32[32,2,256]{2,1,0:T(2,128)S(1)} %broadcast_in_dim.14), channel_id=1, replica_groups=mesh['sub'=8,'grp'=4] {'sub','grp'}, dimensions={0} | all-to-all | bytes 131072 | tf_op jit(solution)/shard_map/all_to_all | solution.py:573
  89.7 0.0 collective-permute-done.13.near
  89.7 0.8 shard_map.101
  90.5 3.1 %collective-permute-start.15 = (f32[256,256]{1,0:T(8,128)S(1)}, f32[256,256]{1,0:T(8,128)S(1)}, u32[]{:S(2)}, u32[]{:S(2)}) collective-permute-start(f32[256,256]{1,0:T(8,128)S(1)} %get-tuple-element.138.refs_5_), channel_id=1, source_target_pairs={{0,4},{4,0},{8,12},{12,8},{16,20},{20,16},{24,28},{28,24},{1,5},{5... | collective-permute-start | bytes 786440 | tf_op jit(solution)/shard_map/ppermute | solution.py:565
  93.6 0.7 collective-permute-start.16
  94.3 0.7 shard_map.102
  95.0 6.8 %all_gather.11.everyone = f32[512,256]{1,0:T(8,128)S(1)} all-gather(f32[128,256]{1,0:T(8,128)S(1)} %shard_map.102), channel_id=1, replica_groups=mesh['sub'=8,'grp'=4] {'grp'}, dimensions={0}, use_global_device_ids=true | all-gather | bytes 655360 | tf_op jit(solution)/shard_map/all_gather | solution.py:703
  101.8 2.4 %shard_map.103 = (f32[3,256,256]{2,1,0:T(8,128)S(1)}, f32[4,256,512]{2,1,0:T(8,128)S(1)}, f32[2,256,256]{2,1,0:T(8,128)S(1)}) custom-call(f32[256,256]{1,0:T(8,128)S(1)} %get-tuple-element.132.edge, f32[4,256,256]{2,1,0:T(8,128)S(1)} %get-tuple-element.133.own.refs_9_.residual, bf16[4,512,512]{2,1,0:T(8,128)(2,1)S(1)} %bitcast.19, ...), custom_call_target="tpu_custom_call" | custom-call | tf_op jit(solution)/shard_map/pallas_call | solution.py:35
  104.2 0.9 collective-permute-done.15.refs_3_
  105.1 0.6 shard_map.104
  105.7 1.3 %collective-permute-start.17 = (f32[256,256]{1,0:T(8,128)S(1)}, f32[256,256]{1,0:T(8,128)S(1)}, u32[]{:S(2)}, u32[]{:S(2)}) collective-permute-start(f32[256,256]{1,0:T(8,128)S(1)} %get-tuple-element.142), channel_id=1, source_target_pairs={{4,0},{8,4},{12,8},{16,12},{20,16},{24,20},{28,24},{5,1},{9,5},{13... | collective-permute-start | bytes 786440 | tf_op jit(solution)/shard_map/ppermute | solution.py:739
  107.1 13.4 %all_to_all.17.sums = f32[32,2,256]{2,1,0:T(2,128)S(1)} all-to-all(f32[32,2,256]{2,1,0:T(2,128)S(1)} %broadcast_in_dim.30), channel_id=1, replica_groups=mesh['sub'=8,'grp'=4] {'sub','grp'}, dimensions={0} | all-to-all | bytes 131072 | tf_op jit(solution)/shard_map/all_to_all | solution.py:573
  120.5 1.7 %shard_map.105 = (f32[4,256,256]{2,1,0:T(8,128)}, f32[4,256,256]{2,1,0:T(8,128)}) custom-call(f32[3,256,256]{2,1,0:T(8,128)S(1)} %get-tuple-element.140.inner, f32[256,256]{1,0:T(8,128)S(1)} %get-tuple-element.141.to_next, f32[256,256]{1,0:T(8,128)S(1)} %collective-permute-done.17.following, f32[4,1,256]{2,1,0:T(1,128)S(1)} %get-tuple-element.85.live_own.refs_8_.live, ...), custom_call_target="tpu_custom_call" | custom-call | tf_op jit(solution)/shard_map/pallas_call | solution.py:35
  (20 shorter events, 0.1 us)
Async XLA Ops:
  0.6 9.9 %copy-start.6 = (s32[1,4]{1,0:T(1,128)S(1)}, s32[1,4]{1,0:T(1,128)}, u32[]{:S(2)}) copy-start(s32[1,4]{1,0:T(1,128)} %counts) | copy-start | bytes 52
  0.6 9.9 %copy-start.2 = (f32[1,4,256,256]{3,2,1,0:T(8,128)S(1)}, f32[1,4,256,256]{3,2,1,0:T(8,128)}, u32[]{:S(2)}) copy-start(f32[1,4,256,256]{3,2,1,0:T(8,128)} %rhs.1) | copy-start | bytes 3145732
  0.6 11.4 %copy-start.5 = (s32[1,4,32]{2,1,0:T(4,128)S(1)}, s32[1,4,32]{2,1,0:T(4,128)}, u32[]{:S(2)}) copy-start(s32[1,4,32]{2,1,0:T(4,128)} %param.12) | copy-start | bytes 1540
  0.7 11.4 %copy-start.3 = (f32[1,4,32,512]{3,2,1,0:T(8,128)S(1)}, f32[1,4,32,512]{3,2,1,0:T(8,128)}, u32[]{:S(2)}) copy-start(f32[1,4,32,512]{3,2,1,0:T(8,128)} %param.11) | copy-start | bytes 786436
  2.5 9.6 %copy-start.4 = (f32[1,256,1024]{2,1,0:T(8,128)S(1)}, f32[1,256,1024]{2,1,0:T(8,128)}, u32[]{:S(2)}) copy-start(f32[1,256,1024]{2,1,0:T(8,128)} %param.13) | copy-start | bytes 3145732
  2.5 11.0 %collective-permute-start = (f32[264,256]{1,0:T(8,128)}, f32[264,256]{1,0:T(8,128)S(1)}, u32[]{:S(2)}, u32[]{:S(2)}) collective-permute-start(f32[264,256]{1,0:T(8,128)} %shard_map.86), channel_id=1, source_target_pairs={{0,4},{4,8},{8,12},{12,16},{16,20},{20,24},{24,28},{1,5},{5,9},{9,... | collective-permute-start | bytes 811016 | tf_op jit(solution)/shard_map/ppermute | solution.py:627
  7.5 3.5 %collective-permute-start.3 = (s32[4,32]{1,0:T(4,128)}, s32[4,32]{1,0:T(4,128)S(1)}, u32[]{:S(2)}, u32[]{:S(2)}) collective-permute-start(s32[4,32]{1,0:T(4,128)} %bitcast.31), channel_id=1, source_target_pairs={{0,3},{1,2},{2,1},{3,0},{4,7},{5,6},{6,5},{7,4},{8,11},{9,10},{10,... | collective-permute-start | bytes 1544 | tf_op jit(solution)/shard_map/ppermute | solution.py:581
  8.2 3.8 %collective-permute-start.2 = (s32[4,32]{1,0:T(4,128)}, s32[4,32]{1,0:T(4,128)S(1)}, u32[]{:S(2)}, u32[]{:S(2)}) collective-permute-start(s32[4,32]{1,0:T(4,128)} %bitcast.32), channel_id=1, source_target_pairs={{0,2},{1,3},{2,0},{3,1},{4,6},{5,7},{6,4},{7,5},{8,10},{9,11},{10,... | collective-permute-start | bytes 1544 | tf_op jit(solution)/shard_map/ppermute | solution.py:581
  9.2 2.9 %collective-permute-start.1 = (s32[4,32]{1,0:T(4,128)}, s32[4,32]{1,0:T(4,128)S(1)}, u32[]{:S(2)}, u32[]{:S(2)}) collective-permute-start(s32[4,32]{1,0:T(4,128)} %bitcast.33), channel_id=1, source_target_pairs={{0,1},{1,0},{2,3},{3,2},{4,5},{5,4},{6,7},{7,6},{8,9},{9,8},{10,11... | collective-permute-start | bytes 1544 | tf_op jit(solution)/shard_map/ppermute | solution.py:581
  10.5 8.3 %copy-start = (bf16[1,4,512,512]{3,2,1,0:T(8,128)(2,1)S(1)}, bf16[1,4,512,512]{3,2,1,0:T(8,128)(2,1)}, u32[]{:S(2)}) copy-start(bf16[1,4,512,512]{3,2,1,0:T(8,128)(2,1)} %param.10) | copy-start | bytes 6291460
  13.8 14.4 %collective-permute-start.4 = (f32[288,256]{1,0:T(8,128)S(1)}, f32[288,256]{1,0:T(8,128)S(1)}, u32[]{:S(2)}, u32[]{:S(2)}) collective-permute-start(f32[288,256]{1,0:T(8,128)S(1)} %get-tuple-element.88.near_sent), channel_id=1, source_target_pairs={{0,4},{4,0},{8,12},{12,8},{16,20},{20,16},{24,28},{28,24},{1,5},{5... | collective-permute-start | bytes 884744 | tf_op jit(solution)/shard_map/ppermute | solution.py:565
  16.2 12.0 %collective-permute-start.5 = (f32[288,256]{1,0:T(8,128)S(1)}, f32[288,256]{1,0:T(8,128)S(1)}, u32[]{:S(2)}, u32[]{:S(2)}) collective-permute-start(f32[288,256]{1,0:T(8,128)S(1)} %get-tuple-element.89.far_sent), channel_id=1, source_target_pairs={{4,8},{8,4},{12,16},{16,12},{20,24},{24,20},{5,9},{9,5},{13,17},{1... | collective-permute-start | bytes 884744 | tf_op jit(solution)/shard_map/ppermute | solution.py:566
  16.9 18.5 %collective-permute-start.6 = (f32[128,512]{1,0:T(8,128)S(1)}, f32[128,512]{1,0:T(8,128)S(1)}, u32[]{:S(2)}, u32[]{:S(2)}) collective-permute-start(f32[128,512]{1,0:T(8,128)S(1)} %get-tuple-element.99), channel_id=1, source_target_pairs={{0,1},{1,0},{2,3},{3,2},{4,5},{5,4},{6,7},{7,6},{8,9},{9,8},{10,11... | collective-permute-start | bytes 786440 | tf_op jit(solution)/shard_map/ppermute | solution.py:590
  17.0 18.5 %collective-permute-start.7 = (f32[128,512]{1,0:T(8,128)S(1)}, f32[128,512]{1,0:T(8,128)S(1)}, u32[]{:S(2)}, u32[]{:S(2)}) collective-permute-start(f32[128,512]{1,0:T(8,128)S(1)} %get-tuple-element.100), channel_id=1, source_target_pairs={{0,2},{1,3},{2,0},{3,1},{4,6},{5,7},{6,4},{7,5},{8,10},{9,11},{10,... | collective-permute-start | bytes 786440 | tf_op jit(solution)/shard_map/ppermute | solution.py:590
  18.5 16.9 %collective-permute-start.8 = (f32[128,512]{1,0:T(8,128)S(1)}, f32[128,512]{1,0:T(8,128)S(1)}, u32[]{:S(2)}, u32[]{:S(2)}) collective-permute-start(f32[128,512]{1,0:T(8,128)S(1)} %get-tuple-element.101), channel_id=1, source_target_pairs={{0,3},{1,2},{2,1},{3,0},{4,7},{5,6},{6,5},{7,4},{8,11},{9,10},{10,... | collective-permute-start | bytes 786440 | tf_op jit(solution)/shard_map/ppermute | solution.py:590
  20.4 1.6 %copy-start.1 = (bf16[1,4,512,512]{3,2,1,0:T(8,128)(2,1)S(1)}, bf16[1,4,512,512]{3,2,1,0:T(8,128)(2,1)}, u32[]{:S(2)}) copy-start(bf16[1,4,512,512]{3,2,1,0:T(8,128)(2,1)} %param.9) | copy-start | bytes 6291460
  37.0 19.0 %collective-permute-start.9 = (f32[320,256]{1,0:T(8,128)S(1)}, f32[320,256]{1,0:T(8,128)S(1)}, u32[]{:S(2)}, u32[]{:S(2)}) collective-permute-start(f32[320,256]{1,0:T(8,128)S(1)} %get-tuple-element.109.near_sent), channel_id=1, source_target_pairs={{0,4},{4,0},{8,12},{12,8},{16,20},{20,16},{24,28},{28,24},{1,5},{5... | collective-permute-start | bytes 983048 | tf_op jit(solution)/shard_map/ppermute | solution.py:565
  40.9 15.2 %collective-permute-start.10 = (f32[320,256]{1,0:T(8,128)S(1)}, f32[320,256]{1,0:T(8,128)S(1)}, u32[]{:S(2)}, u32[]{:S(2)}) collective-permute-start(f32[320,256]{1,0:T(8,128)S(1)} %get-tuple-element.110.far_sent), channel_id=1, source_target_pairs={{4,8},{8,4},{12,16},{16,12},{20,24},{24,20},{5,9},{9,5},{13,17},{1... | collective-permute-start | bytes 983048 | tf_op jit(solution)/shard_map/ppermute | solution.py:566
  57.0 14.9 %collective-permute-start.11 = (f32[256,256]{1,0:T(8,128)S(1)}, f32[256,256]{1,0:T(8,128)S(1)}, u32[]{:S(2)}, u32[]{:S(2)}) collective-permute-start(f32[256,256]{1,0:T(8,128)S(1)} %get-tuple-element.120.refs_5_), channel_id=1, source_target_pairs={{0,4},{4,0},{8,12},{12,8},{16,20},{20,16},{24,28},{28,24},{1,5},{5... | collective-permute-start | bytes 786440 | tf_op jit(solution)/shard_map/ppermute | solution.py:565
  60.4 11.5 %collective-permute-start.12 = (f32[256,256]{1,0:T(8,128)S(1)}, f32[256,256]{1,0:T(8,128)S(1)}, u32[]{:S(2)}, u32[]{:S(2)}) collective-permute-start(f32[256,256]{1,0:T(8,128)S(1)} %get-tuple-element.121.refs_6_), channel_id=1, source_target_pairs={{4,8},{8,4},{12,16},{16,12},{20,24},{24,20},{5,9},{9,5},{13,17},{1... | collective-permute-start | bytes 786440 | tf_op jit(solution)/shard_map/ppermute | solution.py:566
  72.7 16.9 %collective-permute-start.13 = (f32[288,256]{1,0:T(8,128)S(1)}, f32[288,256]{1,0:T(8,128)S(1)}, u32[]{:S(2)}, u32[]{:S(2)}) collective-permute-start(f32[288,256]{1,0:T(8,128)S(1)} %get-tuple-element.125.near_sent), channel_id=1, source_target_pairs={{0,4},{4,0},{8,12},{12,8},{16,20},{20,16},{24,28},{28,24},{1,5},{5... | collective-permute-start | bytes 884744 | tf_op jit(solution)/shard_map/ppermute | solution.py:565
  75.9 13.8 %collective-permute-start.14 = (f32[288,256]{1,0:T(8,128)S(1)}, f32[288,256]{1,0:T(8,128)S(1)}, u32[]{:S(2)}, u32[]{:S(2)}) collective-permute-start(f32[288,256]{1,0:T(8,128)S(1)} %get-tuple-element.126.far_sent), channel_id=1, source_target_pairs={{4,8},{8,4},{12,16},{16,12},{20,24},{24,20},{5,9},{9,5},{13,17},{1... | collective-permute-start | bytes 884744 | tf_op jit(solution)/shard_map/ppermute | solution.py:566
  90.5 14.6 %collective-permute-start.15 = (f32[256,256]{1,0:T(8,128)S(1)}, f32[256,256]{1,0:T(8,128)S(1)}, u32[]{:S(2)}, u32[]{:S(2)}) collective-permute-start(f32[256,256]{1,0:T(8,128)S(1)} %get-tuple-element.138.refs_5_), channel_id=1, source_target_pairs={{0,4},{4,0},{8,12},{12,8},{16,20},{20,16},{24,28},{28,24},{1,5},{5... | collective-permute-start | bytes 786440 | tf_op jit(solution)/shard_map/ppermute | solution.py:565
  93.6 11.5 %collective-permute-start.16 = (f32[256,256]{1,0:T(8,128)S(1)}, f32[256,256]{1,0:T(8,128)S(1)}, u32[]{:S(2)}, u32[]{:S(2)}) collective-permute-start(f32[256,256]{1,0:T(8,128)S(1)} %get-tuple-element.139.refs_6_), channel_id=1, source_target_pairs={{4,8},{8,4},{12,16},{16,12},{20,24},{24,20},{5,9},{9,5},{13,17},{1... | collective-permute-start | bytes 786440 | tf_op jit(solution)/shard_map/ppermute | solution.py:566
  105.7 14.8 %collective-permute-start.17 = (f32[256,256]{1,0:T(8,128)S(1)}, f32[256,256]{1,0:T(8,128)S(1)}, u32[]{:S(2)}, u32[]{:S(2)}) collective-permute-start(f32[256,256]{1,0:T(8,128)S(1)} %get-tuple-element.142), channel_id=1, source_target_pairs={{4,0},{8,4},{12,8},{16,12},{20,16},{24,20},{28,24},{5,1},{9,5},{13... | collective-permute-start | bytes 786440 | tf_op jit(solution)/shard_map/ppermute | solution.py:739
